TPU v7x, 32 devices: a whole 2x2x4 slice. The times are simulated.
32 devices in a mesh: groups: 2 (over y), blk: 4 (over z), mpo: 2 (over x), rep: 2 (over core).
Axes of the slice: x: 2, y: 2, z: 4, core: 2. Of those that a mesh axis runs over, the one named last changes fastest.
Arguments:
- wavefunction: bfloat16 [16, 256, 256], P(('groups', 'blk', 'rep')), parts along dimension 0
- env_left: bfloat16 [48, 16, 256, 256], P('mpo', ('groups', 'blk', 'rep')), parts along dimension 1
- env_right: bfloat16 [48, 16, 256, 256], P('mpo', ('groups', 'blk', 'rep')), parts along dimension 1
- channel_class: int32 [48], P('mpo'), may hold values from 0 to 4
Outputs:
- basis: bfloat16 [3, 16, 256, 256], P(None, ('groups', 'blk', 'rep'), 'mpo'), parts along dimension 1
- coeffs: float32 [4, 3], P('groups'), parts along dimension 0
There are 2 independent parts, one for each index of `groups`. A program takes and returns all parts, laid end to end along the dimension named above; an argument that names none is the same for every part. Nothing has to cross between parts.
Inputs may be any that keep to these rules, and one draw needn't show every extreme that they name: `channel_class`: class 0 keeps both quantum numbers; classes 1 and 2 raise the particle number with spin up and down; classes 3 and 4 lower it with spin up and down.
All inputs are finite; a program needn't handle non-finite values.
Results may differ from a plain program's by a relative error of at most 0.018.
Values may be sent and summed in bfloat16 or wider, within the bound.
No kernel may reach another device: no remote copies, remote signals or barrier semaphores. Data moves between devices by JAX's collectives and lax.ppermute only.
A program may use at most 64 MiB of HBM per device.

v0:
```python
import jax
import jax.numpy as jnp
from jax import lax
from jax.sharding import PartitionSpec as P

NS = 4
STEPS = 3


epsilon = 1e-06


def shifted(block, axis, distance):
    devices = range(lax.axis_size(axis))
    route = [(i - distance, i) for i in devices if i - distance in devices]
    return lax.ppermute(block, axis, route)


def fetch(vector, offset):
    return shifted(vector, ("blk", "rep"), offset)


def spin_masks(sector):
    spin_index = sector % NS
    keep_low = (spin_index >= 1).astype(jnp.bfloat16)
    keep_high = (spin_index <= NS - 2).astype(jnp.bfloat16)
    return (keep_low, keep_high)


def whole_sources(vector, sector):
    keep_low, keep_high = spin_masks(sector)
    return jnp.stack(
        [
            vector,
            fetch(vector, NS + 1) * keep_low,
            fetch(vector, NS - 1) * keep_high,
            fetch(vector, -(NS + 1)) * keep_high,
            fetch(vector, -(NS - 1)) * keep_low,
        ]
    )


def apply_hamiltonian(candidates, env_left, env_right, channel_class):
    picker = (channel_class[:, None] == jnp.arange(5, dtype=jnp.int32)[None, :]).astype(
        jnp.bfloat16
    )
    picked = jnp.einsum(
        "kc,cnij->knij", picker, candidates, preferred_element_type=jnp.float32
    ).astype(jnp.bfloat16)
    partial_value = jnp.einsum(
        "knij,knjl->knil", env_left, picked, preferred_element_type=jnp.float32
    ).astype(jnp.bfloat16)
    return jnp.einsum(
        "knij,knlj->nil", partial_value, env_right, preferred_element_type=jnp.float32
    )


def coefficients(current, product, previous, beta_prev, entries):
    alpha_now = lax.psum(jnp.sum(current * product), ("blk", "mpo", "rep")) / entries
    residue = product - alpha_now * current - beta_prev * previous
    square_mean = lax.psum(jnp.sum(residue * residue), ("blk", "mpo", "rep")) / entries
    return (alpha_now, jnp.sqrt(square_mean + epsilon), residue)


def shards(wavefunction, env_left, env_right, channel_class):
    width = wavefunction.shape[1]
    entries = wavefunction.shape[0] * lax.axis_size("blk") * lax.axis_size("rep") * width * width
    sector = lax.axis_index("blk") * lax.axis_size("rep") + lax.axis_index("rep")
    share_rows = width // lax.axis_size("mpo")
    row_start = lax.axis_index("mpo") * share_rows
    initial = wavefunction.astype(jnp.float32)
    start_value = jnp.sqrt(lax.psum(jnp.sum(initial * initial), ("blk", "rep")) / entries + epsilon)
    vector = (initial / start_value).astype(jnp.bfloat16)
    share = lax.dynamic_slice_in_dim(vector, row_start, share_rows, 1)
    previous = jnp.zeros((wavefunction.shape[0], share_rows, width), jnp.float32)
    beta_prev = jnp.zeros((), jnp.float32)
    basis_list, alphas, beta_list = ([], [], [])
    for iteration in range(STEPS):
        if iteration > 0:
            candidates = whole_sources(vector, sector)
        else:
            candidates = whole_sources(vector, sector)
        terms = apply_hamiltonian(candidates, env_left, env_right, channel_class)
        product = lax.psum_scatter(
            terms.astype(jnp.bfloat16), "mpo", scatter_dimension=1, tiled=True
        ).astype(jnp.float32)
        current = share.astype(jnp.float32)
        alpha_now, beta_now, residue = coefficients(current, product, previous, beta_prev, entries)
        upcoming = (residue / beta_now).astype(jnp.bfloat16)
        basis_list.append(upcoming)
        alphas.append(alpha_now)
        beta_list.append(beta_now)
        if iteration + 1 < STEPS:
            vector = lax.all_gather(upcoming, "mpo", axis=1, tiled=True)
        share = upcoming
        previous = current
        beta_prev = beta_now
    return (jnp.stack(basis_list), jnp.stack([jnp.stack(alphas), jnp.stack(beta_list)]))


def solution(mesh):
    return jax.shard_map(
        shards,
        mesh=mesh,
        in_specs=(
            P(("groups", "blk", "rep"), None, None),
            P("mpo", ("groups", "blk", "rep"), None, None),
            P("mpo", ("groups", "blk", "rep"), None, None),
            P("mpo"),
        ),
        out_specs=(P(None, ("groups", "blk", "rep"), "mpo", None), P("groups", None)),
        check_vma=False,
    )
```

profile of v0, /device:TPU:0, one launch (start us, length us, event | category | flops | bytes accessed | tf_op | source)
XLA Modules:
  0.0 356.3 jit_solution(15724699546207158484)
XLA Ops:
  9.0 18.7 %psum.49 = f32[]{:T(128)} all-reduce(f32[]{:T(128)} %fusion.99), channel_id=1, replica_groups=mesh['groups'=2,'blk'=4,'mpo'=2,'rep'=2] {'blk','rep'}, use_global_device_ids=true, to_apply=%region_1.0 | all-reduce | flops 1 | bytes 8 | tf_op jit(solution)/shard_map/psum | solution.py:72
  34.4 4.3 %collective-permute-start.1 = (bf16[1,256,256]{2,1,0:T(8,128)(2,1)S(1)}, bf16[1,256,256]{2,1,0:T(8,128)(2,1)}, u32[]{:S(2)}, u32[]{:S(2)}) collective-permute-start(bf16[1,256,256]{2,1,0:T(8,128)(2,1)S(1)} %get-tuple-element.3), channel_id=1, source_target_pairs={{0,5},{1,8},{4,9},{5,12},{8,13},{2,7},{3,10},{6,11},{7,14},{10,15}... | collective-permute-start | bytes 393224 | tf_op jit(solution)/shard_map/ppermute | solution.py:16
  44.9 3.8 %fusion.97 = bf16[24,256,256]{2,0,1:T(8,128)(2,1)} fusion(bf16[5,256,256]{2,1,0:T(8,128)(2,1)} %bitcast.167, s32[24]{0:T(128)} %param.7), kind=kOutput, calls=%fused_computation.34 | convolution fusion | flops 15728760 | bytes 3801184 | tf_op jit(solution)/shard_map/kc,cnij->knij/dot_general | solution.py:47
  48.7 5.4 %fusion.72 = bf16[1,256,256]{2,1,0:T(8,128)(2,1)} fusion(bf16[24,1,256,256]{3,2,1,0:T(8,128)(2,1)S(1)} %copy-done, bf16[24,256,256]{2,0,1:T(8,128)(2,1)} %fusion.97, bf16[24,1,256,256]{3,2,1,0:T(8,128)(2,1)} %param.5), kind=kOutput, calls=%fused_computation.27 | convolution fusion | flops 1612251136 | bytes 9568256 | tf_op jit(solution)/shard_map/knij,knlj->nil/dot_general | solution.py:53
  54.2 12.4 %reduce-scatter.4.cloned.1.call-done = bf16[1,128,256]{2,1,0:T(8,128)(2,1)} async-done(((bf16[1,256,256]{2,1,0:T(8,128)(2,1)}), bf16[1,128,256]{2,1,0:T(8,128)(2,1)}) %reduce-scatter.4.cloned.1.call-update) | async-done | bytes 65552 | tf_op jit(solution)/shard_map/reduce_scatter | solution.py:84
  68.1 32.8 %psum.50 = f32[]{:T(128)} all-reduce(f32[]{:T(128)} %fusion.104), channel_id=1, replica_groups=mesh['groups'=2,'blk'=4,'mpo'=2,'rep'=2] {'blk','mpo','rep'}, use_global_device_ids=true, to_apply=%region_4.5 | all-reduce | flops 1 | bytes 8 | tf_op jit(solution)/shard_map/psum | solution.py:59
  103.0 30.1 %psum.51 = f32[]{:T(128)} all-reduce(f32[]{:T(128)} %multiply_reduce_fusion.2), channel_id=1, replica_groups=mesh['groups'=2,'blk'=4,'mpo'=2,'rep'=2] {'blk','mpo','rep'}, use_global_device_ids=true, to_apply=%region_6.7 | all-reduce | flops 1 | bytes 8 | tf_op jit(solution)/shard_map/psum | solution.py:61
  134.7 4.9 %all_gather.6 = bf16[1,256,256]{2,1,0:T(8,128)(2,1)S(1)} all-gather(bf16[1,128,256]{2,1,0:T(8,128)(2,1)S(1)} %divide_convert_fusion.2), channel_id=1, replica_groups=mesh['groups'=2,'blk'=4,'mpo'=2,'rep'=2] {'mpo'}, dimensions={1}, use_global_device_ids=true | all-gather | bytes 196608 | tf_op jit(solution)/shard_map/all_gather | solution.py:94
  142.2 3.7 %collective-permute-start.5 = (bf16[1,256,256]{2,1,0:T(8,128)(2,1)S(1)}, bf16[1,256,256]{2,1,0:T(8,128)(2,1)S(1)}, u32[]{:S(2)}, u32[]{:S(2)}) collective-permute-start(bf16[1,256,256]{2,1,0:T(8,128)(2,1)S(1)} %all_gather.6), channel_id=1, source_target_pairs={{0,5},{1,8},{4,9},{5,12},{8,13},{2,7},{3,10},{6,11},{7,14},{10,15}... | collective-permute-start | bytes 393224 | tf_op jit(solution)/shard_map/ppermute | solution.py:16
  145.9 2.8 collective-permute-start.4
  148.7 2.8 collective-permute-done.4
  151.7 2.7 fusion.95
  154.4 5.4 %fusion.79 = bf16[1,256,256]{2,1,0:T(8,128)(2,1)} fusion(bf16[24,1,256,256]{3,2,1,0:T(8,128)(2,1)S(1)} %copy-done, bf16[24,256,256]{2,0,1:T(8,128)(2,1)} %fusion.95, bf16[24,1,256,256]{3,2,1,0:T(8,128)(2,1)} %param.5), kind=kOutput, calls=%fused_computation.28 | convolution fusion | flops 1612251136 | bytes 9568256 | tf_op jit(solution)/shard_map/knij,knlj->nil/dot_general | solution.py:53
  159.9 13.5 %reduce-scatter.6.cloned.1.call-done = bf16[1,128,256]{2,1,0:T(8,128)(2,1)} async-done(((bf16[1,256,256]{2,1,0:T(8,128)(2,1)}), bf16[1,128,256]{2,1,0:T(8,128)(2,1)}) %reduce-scatter.6.cloned.1.call-update) | async-done | bytes 65552 | tf_op jit(solution)/shard_map/reduce_scatter | solution.py:84
  174.9 32.8 %psum.52 = f32[]{:T(128)} all-reduce(f32[]{:T(128)} %fusion.105), channel_id=1, replica_groups=mesh['groups'=2,'blk'=4,'mpo'=2,'rep'=2] {'blk','mpo','rep'}, use_global_device_ids=true, to_apply=%region_9.10 | all-reduce | flops 1 | bytes 8 | tf_op jit(solution)/shard_map/psum | solution.py:59
  209.8 30.1 %psum.53 = f32[]{:T(128)} all-reduce(f32[]{:T(128)} %multiply_reduce_fusion.1), channel_id=1, replica_groups=mesh['groups'=2,'blk'=4,'mpo'=2,'rep'=2] {'blk','mpo','rep'}, use_global_device_ids=true, to_apply=%region_11.12 | all-reduce | flops 1 | bytes 8 | tf_op jit(solution)/shard_map/psum | solution.py:61
  241.5 4.9 %all_gather.7 = bf16[1,256,256]{2,1,0:T(8,128)(2,1)S(1)} all-gather(bf16[1,128,256]{2,1,0:T(8,128)(2,1)S(1)} %divide_convert_fusion.1), channel_id=1, replica_groups=mesh['groups'=2,'blk'=4,'mpo'=2,'rep'=2] {'mpo'}, dimensions={1}, use_global_device_ids=true | all-gather | bytes 196608 | tf_op jit(solution)/shard_map/all_gather | solution.py:94
  249.1 3.7 %collective-permute-start.9 = (bf16[1,256,256]{2,1,0:T(8,128)(2,1)S(1)}, bf16[1,256,256]{2,1,0:T(8,128)(2,1)S(1)}, u32[]{:S(2)}, u32[]{:S(2)}) collective-permute-start(bf16[1,256,256]{2,1,0:T(8,128)(2,1)S(1)} %all_gather.7), channel_id=1, source_target_pairs={{0,5},{1,8},{4,9},{5,12},{8,13},{2,7},{3,10},{6,11},{7,14},{10,15}... | collective-permute-start | bytes 393224 | tf_op jit(solution)/shard_map/ppermute | solution.py:16
  252.7 2.8 collective-permute-start.8
  255.6 2.8 collective-permute-done.8
  261.2 5.4 %fusion.86 = bf16[1,256,256]{2,1,0:T(8,128)(2,1)} fusion(bf16[24,1,256,256]{3,2,1,0:T(8,128)(2,1)S(1)} %copy-done, bf16[24,256,256]{2,0,1:T(8,128)(2,1)} %fusion.93, bf16[24,1,256,256]{3,2,1,0:T(8,128)(2,1)} %param.5), kind=kOutput, calls=%fused_computation.29 | convolution fusion | flops 1612251136 | bytes 9568256 | tf_op jit(solution)/shard_map/knij,knlj->nil/dot_general | solution.py:53
  266.7 13.6 %reduce-scatter.8.cloned.1.call-done = bf16[1,128,256]{2,1,0:T(8,128)(2,1)} async-done(((bf16[1,256,256]{2,1,0:T(8,128)(2,1)}), bf16[1,128,256]{2,1,0:T(8,128)(2,1)}) %reduce-scatter.8.cloned.1.call-update) | async-done | bytes 65552 | tf_op jit(solution)/shard_map/reduce_scatter | solution.py:84
  281.7 32.8 %psum.54 = f32[]{:T(128)} all-reduce(f32[]{:T(128)} %fusion.103), channel_id=1, replica_groups=mesh['groups'=2,'blk'=4,'mpo'=2,'rep'=2] {'blk','mpo','rep'}, use_global_device_ids=true, to_apply=%region_14.15 | all-reduce | flops 1 | bytes 8 | tf_op jit(solution)/shard_map/psum | solution.py:59
  316.7 30.1 %psum.55 = f32[]{:T(128)} all-reduce(f32[]{:T(128)} %multiply_reduce_fusion), channel_id=1, replica_groups=mesh['groups'=2,'blk'=4,'mpo'=2,'rep'=2] {'blk','mpo','rep'}, use_global_device_ids=true, to_apply=%region_16.17 | all-reduce | flops 1 | bytes 8 | tf_op jit(solution)/shard_map/psum | solution.py:61
  (57 shorter events, 35.2 us)
Async XLA Ops:
  7.2 41.5 %copy-start = (bf16[24,1,256,256]{3,2,1,0:T(8,128)(2,1)S(1)}, bf16[24,1,256,256]{3,2,1,0:T(8,128)(2,1)}, u32[]{:S(2)}) copy-start(bf16[24,1,256,256]{3,2,1,0:T(8,128)(2,1)} %param.6) | copy-start | bytes 9437188
  7.2 59.4 %reduce-scatter.4.cloned.1.call-start = ((), (), s32[]{:S(2)}) async-start(), calls=%async_computation.3 | async-start | bytes 196608 | tf_op jit(solution)/shard_map/reduce_scatter | solution.py:84
  29.9 8.8 %collective-permute-start = (bf16[1,256,256]{2,1,0:T(8,128)(2,1)S(1)}, bf16[1,256,256]{2,1,0:T(8,128)(2,1)}, u32[]{:S(2)}, u32[]{:S(2)}) collective-permute-start(bf16[1,256,256]{2,1,0:T(8,128)(2,1)S(1)} %get-tuple-element.3), channel_id=1, source_target_pairs={{0,9},{1,12},{4,13},{2,11},{3,14},{6,15},{16,25},{17,28},{20,29},{... | collective-permute-start | bytes 393224 | tf_op jit(solution)/shard_map/ppermute | solution.py:16
  31.9 12.3 %collective-permute-start.3 = (bf16[1,256,256]{2,1,0:T(8,128)(2,1)S(1)}, bf16[1,256,256]{2,1,0:T(8,128)(2,1)S(1)}, u32[]{:S(2)}, u32[]{:S(2)}) collective-permute-start(bf16[1,256,256]{2,1,0:T(8,128)(2,1)S(1)} %get-tuple-element.3), channel_id=1, source_target_pairs={{5,0},{8,1},{9,4},{12,5},{13,8},{7,2},{10,3},{11,6},{14,7},{15,10}... | collective-permute-start | bytes 393224 | tf_op jit(solution)/shard_map/ppermute | solution.py:16
  33.1 10.4 %collective-permute-start.2 = (bf16[1,256,256]{2,1,0:T(8,128)(2,1)S(1)}, bf16[1,256,256]{2,1,0:T(8,128)(2,1)S(1)}, u32[]{:S(2)}, u32[]{:S(2)}) collective-permute-start(bf16[1,256,256]{2,1,0:T(8,128)(2,1)S(1)} %get-tuple-element.3), channel_id=1, source_target_pairs={{9,0},{12,1},{13,4},{11,2},{14,3},{15,6},{25,16},{28,17},{29,20},{... | collective-permute-start | bytes 393224 | tf_op jit(solution)/shard_map/ppermute | solution.py:16
  34.4 6.4 %collective-permute-start.1 = (bf16[1,256,256]{2,1,0:T(8,128)(2,1)S(1)}, bf16[1,256,256]{2,1,0:T(8,128)(2,1)}, u32[]{:S(2)}, u32[]{:S(2)}) collective-permute-start(bf16[1,256,256]{2,1,0:T(8,128)(2,1)S(1)} %get-tuple-element.3), channel_id=1, source_target_pairs={{0,5},{1,8},{4,9},{5,12},{8,13},{2,7},{3,10},{6,11},{7,14},{10,15}... | collective-permute-start | bytes 393224 | tf_op jit(solution)/shard_map/ppermute | solution.py:16
  48.7 103.0 %copy-start.1 = (s32[24]{0:T(128)S(1)}, s32[24]{0:T(128)}, u32[]{:S(2)}) copy-start(s32[24]{0:T(128)} %param.7) | copy-start | bytes 292
  54.1 119.3 %reduce-scatter.6.cloned.1.call-start = ((), (), s32[]{:S(2)}) async-start(), calls=%async_computation.4 | async-start | bytes 196608 | tf_op jit(solution)/shard_map/reduce_scatter | solution.py:84
  139.6 12.0 %collective-permute-start.7 = (bf16[1,256,256]{2,1,0:T(8,128)(2,1)S(1)}, bf16[1,256,256]{2,1,0:T(8,128)(2,1)S(1)}, u32[]{:S(2)}, u32[]{:S(2)}) collective-permute-start(bf16[1,256,256]{2,1,0:T(8,128)(2,1)S(1)} %all_gather.6), channel_id=1, source_target_pairs={{5,0},{8,1},{9,4},{12,5},{13,8},{7,2},{10,3},{11,6},{14,7},{15,10}... | collective-permute-start | bytes 393224 | tf_op jit(solution)/shard_map/ppermute | solution.py:16
  140.9 10.7 %collective-permute-start.6 = (bf16[1,256,256]{2,1,0:T(8,128)(2,1)S(1)}, bf16[1,256,256]{2,1,0:T(8,128)(2,1)S(1)}, u32[]{:S(2)}, u32[]{:S(2)}) collective-permute-start(bf16[1,256,256]{2,1,0:T(8,128)(2,1)S(1)} %all_gather.6), channel_id=1, source_target_pairs={{9,0},{12,1},{13,4},{11,2},{14,3},{15,6},{25,16},{28,17},{29,20},{... | collective-permute-start | bytes 393224 | tf_op jit(solution)/shard_map/ppermute | solution.py:16
  142.2 9.3 %collective-permute-start.5 = (bf16[1,256,256]{2,1,0:T(8,128)(2,1)S(1)}, bf16[1,256,256]{2,1,0:T(8,128)(2,1)S(1)}, u32[]{:S(2)}, u32[]{:S(2)}) collective-permute-start(bf16[1,256,256]{2,1,0:T(8,128)(2,1)S(1)} %all_gather.6), channel_id=1, source_target_pairs={{0,5},{1,8},{4,9},{5,12},{8,13},{2,7},{3,10},{6,11},{7,14},{10,15}... | collective-permute-start | bytes 393224 | tf_op jit(solution)/shard_map/ppermute | solution.py:16
  145.9 5.7 %collective-permute-start.4 = (bf16[1,256,256]{2,1,0:T(8,128)(2,1)S(1)}, bf16[1,256,256]{2,1,0:T(8,128)(2,1)S(1)}, u32[]{:S(2)}, u32[]{:S(2)}) collective-permute-start(bf16[1,256,256]{2,1,0:T(8,128)(2,1)S(1)} %all_gather.6), channel_id=1, source_target_pairs={{0,9},{1,12},{4,13},{2,11},{3,14},{6,15},{16,25},{17,28},{20,29},{... | collective-permute-start | bytes 393224 | tf_op jit(solution)/shard_map/ppermute | solution.py:16
  159.9 120.4 %reduce-scatter.8.cloned.1.call-start = ((), (), s32[]{:S(2)}) async-start(), calls=%async_computation.5 | async-start | bytes 196608 | tf_op jit(solution)/shard_map/reduce_scatter | solution.py:84
  246.5 12.0 %collective-permute-start.11 = (bf16[1,256,256]{2,1,0:T(8,128)(2,1)S(1)}, bf16[1,256,256]{2,1,0:T(8,128)(2,1)S(1)}, u32[]{:S(2)}, u32[]{:S(2)}) collective-permute-start(bf16[1,256,256]{2,1,0:T(8,128)(2,1)S(1)} %all_gather.7), channel_id=1, source_target_pairs={{5,0},{8,1},{9,4},{12,5},{13,8},{7,2},{10,3},{11,6},{14,7},{15,10}... | collective-permute-start | bytes 393224 | tf_op jit(solution)/shard_map/ppermute | solution.py:16
  247.8 10.7 %collective-permute-start.10 = (bf16[1,256,256]{2,1,0:T(8,128)(2,1)S(1)}, bf16[1,256,256]{2,1,0:T(8,128)(2,1)S(1)}, u32[]{:S(2)}, u32[]{:S(2)}) collective-permute-start(bf16[1,256,256]{2,1,0:T(8,128)(2,1)S(1)} %all_gather.7), channel_id=1, source_target_pairs={{9,0},{12,1},{13,4},{11,2},{14,3},{15,6},{25,16},{28,17},{29,20},{... | collective-permute-start | bytes 393224 | tf_op jit(solution)/shard_map/ppermute | solution.py:16
  249.1 9.3 %collective-permute-start.9 = (bf16[1,256,256]{2,1,0:T(8,128)(2,1)S(1)}, bf16[1,256,256]{2,1,0:T(8,128)(2,1)S(1)}, u32[]{:S(2)}, u32[]{:S(2)}) collective-permute-start(bf16[1,256,256]{2,1,0:T(8,128)(2,1)S(1)} %all_gather.7), channel_id=1, source_target_pairs={{0,5},{1,8},{4,9},{5,12},{8,13},{2,7},{3,10},{6,11},{7,14},{10,15}... | collective-permute-start | bytes 393224 | tf_op jit(solution)/shard_map/ppermute | solution.py:16
  252.7 5.7 %collective-permute-start.8 = (bf16[1,256,256]{2,1,0:T(8,128)(2,1)S(1)}, bf16[1,256,256]{2,1,0:T(8,128)(2,1)S(1)}, u32[]{:S(2)}, u32[]{:S(2)}) collective-permute-start(bf16[1,256,256]{2,1,0:T(8,128)(2,1)S(1)} %all_gather.7), channel_id=1, source_target_pairs={{0,9},{1,12},{4,13},{2,11},{3,14},{6,15},{16,25},{17,28},{20,29},{... | collective-permute-start | bytes 393224 | tf_op jit(solution)/shard_map/ppermute | solution.py:16
Sparse Core Ops, SparseCore 0:
  54.2 12.3 reduce-scatter.3
  160.0 13.4 reduce-scatter.5
  266.8 13.4 reduce-scatter.7
where the time goes:
time: 357 us; the launch traced here: 356 us
  blocking collectives  217 us (61%)
  waiting for transfers between devices  46.8 us (13%)
  starting transfers between devices  27 us (8%)
  matrix products  25.5 us (7%)
  other arithmetic  21 us (6%)
  between operations  18.7 us (5%)
    psum x3, blocking collectives, coefficients(): lax.psum(jnp.sum(current * product), ('blk', 'mpo', 'rep')) / entries  98.4 us
    psum x3, blocking collectives, coefficients(): lax.psum(jnp.sum(residue * residue), ('blk', 'mpo', 'rep')) / entries  90.3 us
    reduce_scatter x3, waiting for transfers between devices, shards(): lax.psum_scatter(terms.astype(jnp.bfloat16), 'mpo', scatter_dimension=1,...  39.5 us
    ppermute x12, starting transfers between devices, shifted(): return lax.ppermute(block, axis, route)  26.9 us
    psum x1, blocking collectives, shards(): lax.psum(jnp.sum(initial * initial), ('blk', 'rep')) / entries + epsilon  18.7 us
    dot_general x3, matrix products, apply_hamiltonian(): jnp.einsum('knij,knlj->nil', partial_value, env_right, preferred_element_...  16.3 us
    all_gather x2, blocking collectives, shards(): vector = lax.all_gather(upcoming, 'mpo', axis=1, tiled=True)  9.89 us
    dot_general x3, matrix products, apply_hamiltonian(): jnp.einsum('kc,cnij->knij', picker, candidates, preferred_element_type=jn...  9.2 us
  transfers between devices with their start and end apart: 15, of which 7 were waited for; matrix products, arithmetic and copies ran while one was open for 1% of the time, Pallas kernels for 0%

commit v1 on v0

v1 whole, which is shorter than its diff:
```python
import functools

import jax
import jax.numpy as jnp
from jax import lax
from jax.experimental import pallas as pl
from jax.experimental.pallas import tpu as pltpu
from jax.sharding import PartitionSpec as P

NS = 4
STEPS = 3
OFFSETS = (0, NS + 1, NS - 1, -(NS + 1), -(NS - 1))
EPSILON = 1e-06
UNROLL = 2
VMEM = pl.BlockSpec(memory_space=pltpu.VMEM)
SMEM = pl.BlockSpec(memory_space=pltpu.SMEM)
ANY = pl.BlockSpec(memory_space=pl.ANY)


def reaches(kind, sector, blocks):
    source = sector - OFFSETS[kind]
    spin = sector % NS
    inside = (source >= 0) & (source < blocks)
    if kind in (1, 4):
        return inside & (spin >= 1)
    if kind in (2, 3):
        return inside & (spin <= NS - 2)
    return inside


def routes(blocks):
    lists = {}
    for kind in range(1, 5):
        lists[kind] = [
            (k - OFFSETS[kind], k) for k in range(blocks) if bool(reaches(kind, k, blocks))
        ]
    permutes, place = [], {}
    for up, down in ((1, 3), (2, 4)):
        both = lists[up] + lists[down]
        disjoint = len({a for a, _ in both}) == len(both) == len({b for _, b in both})
        groups = ((up, down),) if disjoint else ((up,), (down,))
        for group in groups:
            for kind in group:
                place[kind] = len(permutes)
            permutes.append([pair for kind in group for pair in lists[kind]])
    return permutes, place


def lane_of(rows, lane):
    return rows[:, lane : lane + 1]


def pack(values, shape):
    lanes = lax.broadcasted_iota(jnp.int32, shape, 1)
    out = jnp.zeros(shape, jnp.float32)
    for place, value in enumerate(values):
        out = jnp.where(lanes == place, value, out)
    return out


def total(x):
    return jnp.sum(jnp.sum(x, axis=0, keepdims=True), axis=1, keepdims=True)


def norm_kernel(psi_ref, rows_ref):
    psi = psi_ref[0].astype(jnp.float32)
    rows_ref[...] = pack([total(psi * psi)], rows_ref.shape)


def sum_parts(parts_ref):
    w = parts_ref[0].astype(jnp.float32)
    for part in range(1, parts_ref.shape[0]):
        w += parts_ref[part].astype(jnp.float32)
    return w


def middle_kernel(first, last, *refs):
    parts, (v_ref, vp_ref, scal_ref, w_ref, rows_ref) = refs[:-5], refs[-5:]
    w = parts[0][...].astype(jnp.float32)
    for part in parts[1:]:
        w += part[...].astype(jnp.float32)
    if not last:
        w_ref[...] = w.astype(jnp.bfloat16)
    v = v_ref[0].astype(jnp.float32)
    a = total(v * w)
    d = total(v * v)
    local = a / jnp.maximum(d, 1e-30)
    r = w - local * v
    if not first:
        r -= lane_of(scal_ref[0:1, :], 1) * vp_ref[0].astype(jnp.float32)
    if last:
        w_ref[...] = w
    rows_ref[...] = pack([a, d, local, total(r * v), total(r * r)], rows_ref.shape)


def coefficients(rows, entries):
    a, d, local, p, q = (lane_of(rows, lane) for lane in range(5))
    alpha = jnp.sum(a, axis=0, keepdims=True) / entries
    off = local - alpha
    square = jnp.sum(q + off * (2.0 * p + off * d), axis=0, keepdims=True)
    beta = jnp.sqrt(jnp.maximum(square, 0.0) / entries + EPSILON)
    return alpha, beta


def product_kernel(step, slots, place, blocks, entries, *refs):
    refs = list(refs)
    kinds_ref, left_hbm, right_hbm, rows_ref = refs[:4]
    refs = refs[4:]
    fresh, refs = refs[:slots], refs[slots:]
    if step >= 1:
        v_ref, refs = refs[0], refs[1:]
    if step >= 2:
        vp_ref, scal_ref, refs = refs[0], refs[1], refs[2:]
    t_ref, v_out, scal_out, left, right, acc, order, slot_of, sems = refs
    channels = left_hbm.shape[0]
    sector = lax.axis_index("blk") * lax.axis_size("rep") + lax.axis_index("rep")

    def list_channel(b, count):
        kind = kinds_ref[b]
        live = kind == 0
        slot = jnp.int32(0)
        for c in range(1, 5):
            live = live | ((kind == c) & reaches(c, sector, blocks))
            slot = jnp.where(kind == c, 1 + place[c], slot)

        @pl.when(live)
        def _():
            order[count] = b
            slot_of[count] = slot
            pltpu.make_async_copy(left_hbm.at[b], left.at[count], sems.at[0, count]).start()
            pltpu.make_async_copy(right_hbm.at[b], right.at[count], sems.at[1, count]).start()

        return count + live.astype(jnp.int32)

    count = lax.fori_loop(0, channels, list_channel, jnp.int32(0))
    for extra in range(UNROLL - 1):
        order[count + extra] = 0
        slot_of[count + extra] = slots

    rows = rows_ref[...]
    if step == 0:
        beta = jnp.sqrt(jnp.sum(lane_of(rows, 0), axis=0, keepdims=True) / entries + EPSILON)
        alpha = jnp.zeros_like(beta)
    else:
        alpha, beta = coefficients(rows, entries)
    scal_out[...] = pack([alpha, beta], scal_out.shape)
    for slot in range(slots):
        block = fresh[slot][0] if step == 0 else fresh[slot][...]
        r = block.astype(jnp.float32)
        if step >= 1:
            r -= alpha * v_ref[slot].astype(jnp.float32)
        if step >= 2:
            r -= lane_of(scal_ref[0:1, :], 1) * vp_ref[slot].astype(jnp.float32)
        v_out[slot] = (r / beta).astype(jnp.bfloat16)
    v_out[slots] = jnp.zeros(v_out.shape[1:], jnp.bfloat16)
    acc[...] = jnp.zeros_like(acc)

    def multiply(group, carry):
        result = None
        for inner in range(UNROLL):
            at = group * UNROLL + inner
            live = at < count

            @pl.when(live)
            def _():
                pltpu.make_async_copy(left_hbm.at[0], left.at[at], sems.at[0, at]).wait()
                pltpu.make_async_copy(right_hbm.at[0], right.at[at], sems.at[1, at]).wait()

        for inner in range(UNROLL):
            at = group * UNROLL + inner
            held = jnp.where(at < count, at, 0)
            piece = jnp.dot(
                left[held], v_out[slot_of[at]], preferred_element_type=jnp.float32
            ).astype(jnp.bfloat16)
            term = lax.dot_general(
                piece, right[held], (((1,), (1,)), ((), ())), preferred_element_type=jnp.float32
            )
            result = term if result is None else result + term
        acc[...] += result
        return carry

    lax.fori_loop(0, (count + UNROLL - 1) // UNROLL, multiply, 0)
    t_ref[...] = acc[...].astype(jnp.bfloat16)


def final_kernel(entries, rows_ref, w_ref, v3_ref, v2_ref, scal1_ref, scal2_ref, basis_ref, coef_ref):
    share = basis_ref.shape[2]
    start = pl.multiple_of(lax.axis_index("mpo") * share, share)
    mine = pl.ds(start, share)
    alpha, beta = coefficients(rows_ref[...], entries)
    v3, v2 = v3_ref[0, mine, :], v2_ref[0, mine, :]
    r = w_ref[mine, :] - alpha * v3.astype(jnp.float32)
    r -= lane_of(scal2_ref[0:1, :], 1) * v2.astype(jnp.float32)
    basis_ref[0, 0] = v2
    basis_ref[1, 0] = v3
    basis_ref[2, 0] = (r / beta).astype(jnp.bfloat16)
    row = lax.broadcasted_iota(jnp.int32, coef_ref.shape, 0)
    column = lax.broadcasted_iota(jnp.int32, coef_ref.shape, 1)
    out = jnp.zeros(coef_ref.shape, jnp.float32)
    pairs = [(lane_of(s[0:1, :], 0), lane_of(s[0:1, :], 1)) for s in (scal1_ref, scal2_ref)]
    for step, (a, b) in enumerate(pairs + [(alpha, beta)]):
        out = jnp.where(column == step, jnp.where(row == 0, a, b), out)
    coef_ref[...] = out


def shards(wavefunction, env_left, env_right, channel_class):
    width = wavefunction.shape[1]
    ring = ("blk", "rep")
    parts = lax.axis_size("mpo")
    blocks = lax.axis_size("blk") * lax.axis_size("rep")
    entries = blocks * width * width
    permutes, place = routes(blocks)
    slots = 1 + len(permutes)
    channels = channel_class.shape[0]
    left, right = env_left[:, 0], env_right[:, 0]
    rows_shape = jax.ShapeDtypeStruct((blocks, 128), jnp.float32)
    block_f32 = jax.ShapeDtypeStruct((width, width), jnp.float32)
    block_bf16 = jax.ShapeDtypeStruct((width, width), jnp.bfloat16)

    def exchange(rows):
        return lax.all_to_all(rows, ring, 0, 0, tiled=True)

    def gather_parts(t):
        if parts == 2:
            return [t, lax.ppermute(t, "mpo", [(0, 1), (1, 0)])]
        held = lax.all_gather(t, "mpo")
        return [held[i] for i in range(parts)]

    def product(step, fresh, rows, *old):
        return pl.pallas_call(
            functools.partial(product_kernel, step, slots, place, blocks, entries),
            out_shape=(
                block_bf16,
                jax.ShapeDtypeStruct((slots + 1, width, width), jnp.bfloat16),
                jax.ShapeDtypeStruct((8, 128), jnp.float32),
            ),
            in_specs=[SMEM, ANY, ANY] + [VMEM] * (1 + len(fresh) + len(old)),
            out_specs=(VMEM,) * 3,
            scratch_shapes=[
                pltpu.VMEM((channels, width, width), jnp.bfloat16),
                pltpu.VMEM((channels, width, width), jnp.bfloat16),
                pltpu.VMEM((width, width), jnp.float32),
                pltpu.SMEM((channels + UNROLL,), jnp.int32),
                pltpu.SMEM((channels + UNROLL,), jnp.int32),
                pltpu.SemaphoreType.DMA((2, channels)),
            ],
            compiler_params=pltpu.CompilerParams(vmem_limit_bytes=32 * 1024 * 1024),
            name="product",
        )(channel_class, left, right, rows, *fresh, *old)

    def middle(first, last, t, v, vp, scal):
        pieces = gather_parts(t)
        return pl.pallas_call(
            functools.partial(middle_kernel, first, last),
            out_shape=(block_f32 if last else block_bf16, rows_shape),
            in_specs=[VMEM] * (len(pieces) + 3),
            out_specs=(VMEM, VMEM),
            name="middle",
        )(*pieces, v, vp, scal)

    def spread(block):
        return [block] + [lax.ppermute(block, ring, pairs) for pairs in permutes]

    fresh = spread(wavefunction)
    rows = pl.pallas_call(norm_kernel, out_shape=rows_shape, in_specs=[VMEM], out_specs=VMEM, name="norm")(
        wavefunction
    )
    t, v1, scal0 = product(0, fresh, exchange(rows))
    w, rows = middle(True, False, t, v1, v1, scal0)
    fresh = spread(w)
    t, v2, scal1 = product(1, fresh, exchange(rows), v1)
    w, rows = middle(False, False, t, v2, v1, scal1)
    fresh = spread(w)
    t, v3, scal2 = product(2, fresh, exchange(rows), v2, v1, scal1)
    w, rows = middle(False, True, t, v3, v2, scal2)
    basis, coefs = pl.pallas_call(
        functools.partial(final_kernel, entries),
        out_shape=(
            jax.ShapeDtypeStruct((STEPS, 1, width // parts, width), jnp.bfloat16),
            jax.ShapeDtypeStruct((2, STEPS), jnp.float32),
        ),
        in_specs=[VMEM] * 6,
        out_specs=(VMEM, VMEM),
        name="final",
    )(exchange(rows), w, v3, v2, scal1, scal2)
    return basis, coefs


def solution(mesh):
    return jax.shard_map(
        shards,
        mesh=mesh,
        in_specs=(
            P(("groups", "blk", "rep"), None, None),
            P("mpo", ("groups", "blk", "rep"), None, None),
            P("mpo", ("groups", "blk", "rep"), None, None),
            P("mpo"),
        ),
        out_specs=(P(None, ("groups", "blk", "rep"), "mpo", None), P("groups", None)),
        check_vma=False,
    )
```

time: 357 us -> 135 us (0.38)
  blocking collectives: 217 us -> 40 us
  Pallas kernels: 0 us -> 35.8 us
  waiting for transfers between devices: 46.8 us -> 11.5 us
  matrix products: 25.5 us -> 0 us
  other arithmetic: 21 us -> 0 us
  local copies, waits for them, and re-layouts: 0.03 us -> 20.8 us
  between operations: 18.7 us -> 0.78 us
    psum x7 -> x0, blocking collectives: 207 us -> none  [the longest x3 98.4 us: coefficients(): lax.psum(jnp.sum(current * product), ('blk', 'mpo', 'rep')) / entries]
    all_to_all x0 -> x4, blocking collectives: none -> 40 us  [exchange(): return lax.all_to_all(rows, ring, 0, 0, tiled=True)]
    reduce_scatter x3 -> x0, waiting for transfers between devices: 39.5 us -> none  [shards(): lax.psum_scatter(terms.astype(jnp.bfloat16), 'mpo', scatter_dimension=1,...]
    pallas_call x0 -> x8, Pallas kernels: none -> 35.8 us  [the longest x3 25.2 us: product(): pl.pallas_call(functools.partial(product_kernel, step, slots, place, bloc...]
    dot_general x6 -> x0, matrix products: 25.5 us -> none  [the longest x3 16.3 us: apply_hamiltonian(): jnp.einsum('knij,knlj->nil', partial_value, env_right, preferred_element_...]
    unnamed x6 -> x52, local copies, waits for them, and re-layouts: 0.03 us -> 20.8 us
    reduce_sum x7 -> x0, other arithmetic: 10.7 us -> none  [the longest x3 4.5 us: coefficients(): jnp.sum(residue * residue)]
    all_gather x2 -> x0, blocking collectives: 9.89 us -> none  [shards(): vector = lax.all_gather(upcoming, 'mpo', axis=1, tiled=True)]
  transfers between devices with their start and end apart: 15 -> 9, of which waited for: 7 -> 3; matrix products, arithmetic and copies ran while one was open for 1% -> 0% of each run, Pallas kernels for 0% -> 1%
where the time goes in v1:
time: 135 us
  blocking collectives  40 us (30%)
  Pallas kernels  35.8 us (27%)
  starting transfers between devices  26.2 us (19%)
  local copies, waits for them, and re-layouts  20.8 us (15%)
  waiting for transfers between devices  11.5 us (9%)
    all_to_all x4, blocking collectives, exchange(): return lax.all_to_all(rows, ring, 0, 0, tiled=True)  40 us
    pallas_call x3, Pallas kernels, product(): pl.pallas_call(functools.partial(product_kernel, step, slots, place, bloc...  25.2 us
    ppermute x6, starting transfers between devices, spread(): return [block] + [lax.ppermute(block, ring, pairs) for pairs in permutes]  22.8 us
    unnamed x52, local copies, waits for them, and re-layouts  20.8 us
    ppermute x3, waiting for transfers between devices, gather_parts(): return [t, lax.ppermute(t, 'mpo', [(0, 1), (1, 0)])]  11.4 us
    pallas_call x3, Pallas kernels, middle(): pl.pallas_call(functools.partial(middle_kernel, first, last), out_shape=(...  6.66 us
    ppermute x3, starting transfers between devices, gather_parts(): return [t, lax.ppermute(t, 'mpo', [(0, 1), (1, 0)])]  3.46 us
  transfers between devices with their start and end apart: 9, of which 3 were waited for; matrix products, arithmetic and copies ran while one was open for 0% of the time, Pallas kernels for 1%

profile of v1, /device:TPU:0, one launch (start us, length us, event | category | flops | bytes accessed | tf_op | source)
XLA Modules:
  0.0 135.0 jit_solution(12932244815051228249)
XLA Ops:
  0.6 5.4 %collective-permute-start = (bf16[1,256,256]{2,1,0:T(8,128)(2,1)}, bf16[1,256,256]{2,1,0:T(8,128)(2,1)S(1)}, u32[]{:S(2)}, u32[]{:S(2)}) collective-permute-start(bf16[1,256,256]{2,1,0:T(8,128)(2,1)} %refs_4_.1), channel_id=1, source_target_pairs={{0,9},{1,12},{4,13},{9,0},{12,1},{13,4},{2,11},{3,14},{6,15},{11,2... | collective-permute-start | bytes 393224 | tf_op jit(solution)/shard_map/ppermute | solution.py:262
  6.7 1.6 %norm.1 = f32[8,128]{1,0:T(8,128)} custom-call(bf16[1,256,256]{2,1,0:T(8,128)(2,1)} %refs_4_.1), custom_call_target="tpu_custom_call" | custom-call | tf_op jit(solution)/shard_map/norm/pallas_call | solution.py:265
  8.3 12.2 %all_to_all.44 = f32[8,1,128]{2,1,0:T(1,128)S(1)} all-to-all(f32[8,1,128]{2,1,0:T(1,128)} %bitcast.28), channel_id=1, replica_groups=mesh['groups'=2,'blk'=4,'mpo'=2,'rep'=2] {'blk','rep'}, dimensions={0} | all-to-all | bytes 8192 | tf_op jit(solution)/shard_map/all_to_all | solution.py:221
  20.5 1.9 %copy-done = bf16[24,1,256,256]{3,2,1,0:T(8,128)(2,1)S(1)} copy-done((bf16[24,1,256,256]{3,2,1,0:T(8,128)(2,1)S(1)}, bf16[24,1,256,256]{3,2,1,0:T(8,128)(2,1)}, u32[]{:S(2)}) %copy-start) | copy-done | bytes 3145752
  22.4 1.9 %copy-done.2 = bf16[24,1,256,256]{3,2,1,0:T(8,128)(2,1)S(1)} copy-done((bf16[24,1,256,256]{3,2,1,0:T(8,128)(2,1)S(1)}, bf16[24,1,256,256]{3,2,1,0:T(8,128)(2,1)}, u32[]{:S(2)}) %copy-start.2) | copy-done | bytes 3145752
  25.9 8.1 %product.3 = (bf16[256,256]{1,0:T(8,128)(2,1)S(1)}, bf16[4,256,256]{2,1,0:T(8,128)(2,1)S(1)}, f32[8,128]{1,0:T(8,128)S(1)}) custom-call(s32[24]{0:T(128)S(1)} %copy-done.20, bf16[24,256,256]{2,1,0:T(8,128)(2,1)S(1)} %bitcast.18, bf16[24,256,256]{2,1,0:T(8,128)(2,1)S(1)} %bitcast.21, f32[8,128]{1,0:T(8,128)S(1)} %bitcast.26, ...), custom_call_target="tpu_custom_call" | custom-call | tf_op jit(solution)/shard_map/product/pallas_call | solution.py:230
  35.4 1.2 collective-permute-start.2
  36.5 3.8 %collective-permute-done.2.refs_1_ = bf16[256,256]{1,0:T(8,128)(2,1)S(1)} collective-permute-done((bf16[256,256]{1,0:T(8,128)(2,1)S(1)}, bf16[256,256]{1,0:T(8,128)(2,1)S(1)}, u32[]{:S(2)}, u32[]{:S(2)}) %collective-permute-start.2) | collective-permute-done | bytes 131104 | tf_op jit(solution)/shard_map/ppermute | solution.py:225
  41.0 2.2 %middle.3 = (bf16[256,256]{1,0:T(8,128)(2,1)}, f32[8,128]{1,0:T(8,128)}) custom-call(bf16[256,256]{1,0:T(8,128)(2,1)} %copy-done.16, bf16[256,256]{1,0:T(8,128)(2,1)} %copy-done.23, bf16[4,256,256]{2,1,0:T(8,128)(2,1)} %copy-done.5, bf16[4,256,256]{2,1,0:T(8,128)(2,1)} %copy-done.5, f32[8,128]{1,0:T(8,128)} %copy-done.22), custom_call_target="tpu_custom_call" | custom-call | tf_op jit(solution)/shard_map/middle/pallas_call | solution.py:253
  43.9 7.7 %collective-permute-start.3 = (bf16[256,256]{1,0:T(8,128)(2,1)}, bf16[256,256]{1,0:T(8,128)(2,1)S(1)}, u32[]{:S(2)}, u32[]{:S(2)}) collective-permute-start(bf16[256,256]{1,0:T(8,128)(2,1)} %get-tuple-element.21.refs_4_), channel_id=1, source_target_pairs={{0,9},{1,12},{4,13},{9,0},{12,1},{13,4},{2,11},{3,14},{6,15},{11,2... | collective-permute-start | bytes 393224 | tf_op jit(solution)/shard_map/ppermute | solution.py:262
  51.6 8.8 %all_to_all.45 = f32[8,1,128]{2,1,0:T(1,128)S(1)} all-to-all(f32[8,1,128]{2,1,0:T(1,128)} %bitcast.29), channel_id=1, replica_groups=mesh['groups'=2,'blk'=4,'mpo'=2,'rep'=2] {'blk','rep'}, dimensions={0} | all-to-all | bytes 8192 | tf_op jit(solution)/shard_map/all_to_all | solution.py:221
  60.4 1.9 %copy-done.3 = bf16[24,1,256,256]{3,2,1,0:T(8,128)(2,1)S(1)} copy-done((bf16[24,1,256,256]{3,2,1,0:T(8,128)(2,1)S(1)}, bf16[24,1,256,256]{3,2,1,0:T(8,128)(2,1)}, u32[]{:S(2)}) %copy-start.3) | copy-done | bytes 3145752
  64.2 8.5 %product.4 = (bf16[256,256]{1,0:T(8,128)(2,1)S(1)}, bf16[4,256,256]{2,1,0:T(8,128)(2,1)S(1)}, f32[8,128]{1,0:T(8,128)S(1)}) custom-call(s32[24]{0:T(128)S(1)} %copy-done.21, bf16[24,256,256]{2,1,0:T(8,128)(2,1)S(1)} %bitcast.19, bf16[24,256,256]{2,1,0:T(8,128)(2,1)S(1)} %bitcast.22, f32[8,128]{1,0:T(8,128)S(1)} %bitcast.25, bf16[256,256]{1,0:T(8,128)(2,1)S(1)} %copy-done.12, ...), custom_call_target="tpu_custom_call" | custom-call | tf_op jit(solution)/shard_map/product/pallas_call | solution.py:230
  74.1 1.2 collective-permute-start.5
  75.2 3.8 %collective-permute-done.5.refs_1_ = bf16[256,256]{1,0:T(8,128)(2,1)S(1)} collective-permute-done((bf16[256,256]{1,0:T(8,128)(2,1)S(1)}, bf16[256,256]{1,0:T(8,128)(2,1)S(1)}, u32[]{:S(2)}, u32[]{:S(2)}) %collective-permute-start.5) | collective-permute-done | bytes 131104 | tf_op jit(solution)/shard_map/ppermute | solution.py:225
  79.7 2.2 %middle.4 = (bf16[256,256]{1,0:T(8,128)(2,1)}, f32[8,128]{1,0:T(8,128)}) custom-call(bf16[256,256]{1,0:T(8,128)(2,1)} %copy-done.15, bf16[256,256]{1,0:T(8,128)(2,1)} %copy-done.24, bf16[4,256,256]{2,1,0:T(8,128)(2,1)} %copy-done.8, bf16[4,256,256]{2,1,0:T(8,128)(2,1)} %copy-done.5, f32[8,128]{1,0:T(8,128)} %copy-done.17), custom_call_target="tpu_custom_call" | custom-call | tf_op jit(solution)/shard_map/middle/pallas_call | solution.py:253
  82.6 7.7 %collective-permute-start.6 = (bf16[256,256]{1,0:T(8,128)(2,1)}, bf16[256,256]{1,0:T(8,128)(2,1)S(1)}, u32[]{:S(2)}, u32[]{:S(2)}) collective-permute-start(bf16[256,256]{1,0:T(8,128)(2,1)} %get-tuple-element.26.refs_4_), channel_id=1, source_target_pairs={{0,9},{1,12},{4,13},{9,0},{12,1},{13,4},{2,11},{3,14},{6,15},{11,2... | collective-permute-start | bytes 393224 | tf_op jit(solution)/shard_map/ppermute | solution.py:262
  90.3 8.8 %all_to_all.46 = f32[8,1,128]{2,1,0:T(1,128)S(1)} all-to-all(f32[8,1,128]{2,1,0:T(1,128)} %bitcast.30), channel_id=1, replica_groups=mesh['groups'=2,'blk'=4,'mpo'=2,'rep'=2] {'blk','rep'}, dimensions={0} | all-to-all | bytes 8192 | tf_op jit(solution)/shard_map/all_to_all | solution.py:221
  99.1 1.9 %copy-done.4 = bf16[24,1,256,256]{3,2,1,0:T(8,128)(2,1)S(1)} copy-done((bf16[24,1,256,256]{3,2,1,0:T(8,128)(2,1)S(1)}, bf16[24,1,256,256]{3,2,1,0:T(8,128)(2,1)}, u32[]{:S(2)}) %copy-start.4) | copy-done | bytes 3145752
  104.6 8.6 %product.5 = (bf16[256,256]{1,0:T(8,128)(2,1)S(1)}, bf16[4,256,256]{2,1,0:T(8,128)(2,1)S(1)}, f32[8,128]{1,0:T(8,128)S(1)}) custom-call(s32[24]{0:T(128)S(1)} %copy-done.21, bf16[24,256,256]{2,1,0:T(8,128)(2,1)S(1)} %bitcast.20, bf16[24,256,256]{2,1,0:T(8,128)(2,1)S(1)} %bitcast.23, f32[8,128]{1,0:T(8,128)S(1)} %bitcast.24, bf16[256,256]{1,0:T(8,128)(2,1)S(1)} %copy-done.13, ...), custom_call_target="tpu_custom_call" | custom-call | tf_op jit(solution)/shard_map/product/pallas_call | solution.py:230
  115.8 3.8 %collective-permute-done.8.refs_1_ = bf16[256,256]{1,0:T(8,128)(2,1)S(1)} collective-permute-done((bf16[256,256]{1,0:T(8,128)(2,1)S(1)}, bf16[256,256]{1,0:T(8,128)(2,1)S(1)}, u32[]{:S(2)}, u32[]{:S(2)}) %collective-permute-start.8) | collective-permute-done | bytes 131104 | tf_op jit(solution)/shard_map/ppermute | solution.py:225
  120.3 2.2 %middle.5 = (f32[256,256]{1,0:T(8,128)}, f32[8,128]{1,0:T(8,128)}) custom-call(bf16[256,256]{1,0:T(8,128)(2,1)} %copy-done.14, bf16[256,256]{1,0:T(8,128)(2,1)} %copy-done.25, bf16[4,256,256]{2,1,0:T(8,128)(2,1)} %copy-done.10, bf16[4,256,256]{2,1,0:T(8,128)(2,1)} %copy-done.8, f32[8,128]{1,0:T(8,128)} %copy-done.19), custom_call_target="tpu_custom_call" | custom-call | tf_op jit(solution)/shard_map/middle/pallas_call | solution.py:253
  122.5 10.1 %all_to_all.47 = f32[8,1,128]{2,1,0:T(1,128)} all-to-all(f32[8,1,128]{2,1,0:T(1,128)} %bitcast.31), channel_id=1, replica_groups=mesh['groups'=2,'blk'=4,'mpo'=2,'rep'=2] {'blk','rep'}, dimensions={0} | all-to-all | bytes 8192 | tf_op jit(solution)/shard_map/all_to_all | solution.py:221
  132.7 2.4 %final.1 = (bf16[3,1,128,256]{3,2,1,0:T(8,128)(2,1)}, f32[2,3]{1,0:T(2,128)}) custom-call(f32[8,128]{1,0:T(8,128)} %bitcast.27, f32[256,256]{1,0:T(8,128)} %get-tuple-element.31.w_ref, bf16[4,256,256]{2,1,0:T(8,128)(2,1)} %copy-done.10, bf16[4,256,256]{2,1,0:T(8,128)(2,1)} %copy-done.8, f32[8,128]{1,0:T(8,128)} %copy-done.17, f32[8,128]{1,0:T(8,128)} %copy-done.19), custom_call_target="tpu_custom_call" | custom-call | tf_op jit(solution)/shard_map/final/pallas_call | solution.py:276
  (58 shorter events, 16.4 us)
Async XLA Ops:
  0.6 19.9 %collective-permute-start = (bf16[1,256,256]{2,1,0:T(8,128)(2,1)}, bf16[1,256,256]{2,1,0:T(8,128)(2,1)S(1)}, u32[]{:S(2)}, u32[]{:S(2)}) collective-permute-start(bf16[1,256,256]{2,1,0:T(8,128)(2,1)} %refs_4_.1), channel_id=1, source_target_pairs={{0,9},{1,12},{4,13},{9,0},{12,1},{13,4},{2,11},{3,14},{6,15},{11,2... | collective-permute-start | bytes 393224 | tf_op jit(solution)/shard_map/ppermute | solution.py:262
  6.0 14.5 %collective-permute-start.1 = (bf16[1,256,256]{2,1,0:T(8,128)(2,1)}, bf16[1,256,256]{2,1,0:T(8,128)(2,1)S(1)}, u32[]{:S(2)}, u32[]{:S(2)}) collective-permute-start(bf16[1,256,256]{2,1,0:T(8,128)(2,1)} %refs_4_.1), channel_id=1, source_target_pairs={{1,8},{4,9},{5,12},{8,1},{9,4},{12,5},{3,10},{6,11},{7,14},{10,3},... | collective-permute-start | bytes 393224 | tf_op jit(solution)/shard_map/ppermute | solution.py:262
  20.5 1.9 %copy-start = (bf16[24,1,256,256]{3,2,1,0:T(8,128)(2,1)S(1)}, bf16[24,1,256,256]{3,2,1,0:T(8,128)(2,1)}, u32[]{:S(2)}) copy-start(bf16[24,1,256,256]{3,2,1,0:T(8,128)(2,1)} %param.5) | copy-start | bytes 9437188
  22.4 1.9 %copy-start.2 = (bf16[24,1,256,256]{3,2,1,0:T(8,128)(2,1)S(1)}, bf16[24,1,256,256]{3,2,1,0:T(8,128)(2,1)}, u32[]{:S(2)}) copy-start(bf16[24,1,256,256]{3,2,1,0:T(8,128)(2,1)} %param.6) | copy-start | bytes 9437188
  24.3 0.9 copy-start.11
  25.9 34.5 %copy-start.1 = (bf16[24,1,256,256]{3,2,1,0:T(8,128)(2,1)S(1)}, bf16[24,1,256,256]{3,2,1,0:T(8,128)(2,1)}, u32[]{:S(2)}) copy-start(bf16[24,1,256,256]{3,2,1,0:T(8,128)(2,1)} %param.5) | copy-start | bytes 9437188
  25.9 34.5 %copy-start.21 = (s32[24]{0:T(128)S(1)}, s32[24]{0:T(128)}, u32[]{:S(2)}) copy-start(s32[24]{0:T(128)} %refs_0_.5) | copy-start | bytes 292
  35.4 5.0 %copy-start.16 = (bf16[256,256]{1,0:T(8,128)(2,1)}, bf16[256,256]{1,0:T(8,128)(2,1)S(1)}, u32[]{:S(2)}) copy-start(bf16[256,256]{1,0:T(8,128)(2,1)S(1)} %get-tuple-element.17.refs_0_) | copy-start | bytes 393220
  35.4 5.0 %collective-permute-start.2 = (bf16[256,256]{1,0:T(8,128)(2,1)S(1)}, bf16[256,256]{1,0:T(8,128)(2,1)S(1)}, u32[]{:S(2)}, u32[]{:S(2)}) collective-permute-start(bf16[256,256]{1,0:T(8,128)(2,1)S(1)} %get-tuple-element.17.refs_0_), channel_id=1, source_target_pairs={{0,2},{2,0},{1,3},{3,1},{4,6},{6,4},{5,7},{7,5},{8,10},{10,8},{9,1... | collective-permute-start | bytes 393224 | tf_op jit(solution)/shard_map/ppermute | solution.py:225
  43.2 17.2 %collective-permute-start.4 = (bf16[256,256]{1,0:T(8,128)(2,1)}, bf16[256,256]{1,0:T(8,128)(2,1)S(1)}, u32[]{:S(2)}, u32[]{:S(2)}) collective-permute-start(bf16[256,256]{1,0:T(8,128)(2,1)} %get-tuple-element.21.refs_4_), channel_id=1, source_target_pairs={{1,8},{4,9},{5,12},{8,1},{9,4},{12,5},{3,10},{6,11},{7,14},{10,3},... | collective-permute-start | bytes 393224 | tf_op jit(solution)/shard_map/ppermute | solution.py:262
  43.9 16.5 %collective-permute-start.3 = (bf16[256,256]{1,0:T(8,128)(2,1)}, bf16[256,256]{1,0:T(8,128)(2,1)S(1)}, u32[]{:S(2)}, u32[]{:S(2)}) collective-permute-start(bf16[256,256]{1,0:T(8,128)(2,1)} %get-tuple-element.21.refs_4_), channel_id=1, source_target_pairs={{0,9},{1,12},{4,13},{9,0},{12,1},{13,4},{2,11},{3,14},{6,15},{11,2... | collective-permute-start | bytes 393224 | tf_op jit(solution)/shard_map/ppermute | solution.py:262
  60.4 1.9 %copy-start.3 = (bf16[24,1,256,256]{3,2,1,0:T(8,128)(2,1)S(1)}, bf16[24,1,256,256]{3,2,1,0:T(8,128)(2,1)}, u32[]{:S(2)}) copy-start(bf16[24,1,256,256]{3,2,1,0:T(8,128)(2,1)} %param.6) | copy-start | bytes 9437188
  62.3 1.0 copy-start.6
  63.3 0.9 copy-start.12
  74.1 5.0 %copy-start.15 = (bf16[256,256]{1,0:T(8,128)(2,1)}, bf16[256,256]{1,0:T(8,128)(2,1)S(1)}, u32[]{:S(2)}) copy-start(bf16[256,256]{1,0:T(8,128)(2,1)S(1)} %get-tuple-element.22.refs_0_) | copy-start | bytes 393220
  74.1 5.0 %collective-permute-start.5 = (bf16[256,256]{1,0:T(8,128)(2,1)S(1)}, bf16[256,256]{1,0:T(8,128)(2,1)S(1)}, u32[]{:S(2)}, u32[]{:S(2)}) collective-permute-start(bf16[256,256]{1,0:T(8,128)(2,1)S(1)} %get-tuple-element.22.refs_0_), channel_id=1, source_target_pairs={{0,2},{2,0},{1,3},{3,1},{4,6},{6,4},{5,7},{7,5},{8,10},{10,8},{9,1... | collective-permute-start | bytes 393224 | tf_op jit(solution)/shard_map/ppermute | solution.py:225
  81.9 17.2 %collective-permute-start.7 = (bf16[256,256]{1,0:T(8,128)(2,1)}, bf16[256,256]{1,0:T(8,128)(2,1)S(1)}, u32[]{:S(2)}, u32[]{:S(2)}) collective-permute-start(bf16[256,256]{1,0:T(8,128)(2,1)} %get-tuple-element.26.refs_4_), channel_id=1, source_target_pairs={{1,8},{4,9},{5,12},{8,1},{9,4},{12,5},{3,10},{6,11},{7,14},{10,3},... | collective-permute-start | bytes 393224 | tf_op jit(solution)/shard_map/ppermute | solution.py:262
  82.6 16.5 %collective-permute-start.6 = (bf16[256,256]{1,0:T(8,128)(2,1)}, bf16[256,256]{1,0:T(8,128)(2,1)S(1)}, u32[]{:S(2)}, u32[]{:S(2)}) collective-permute-start(bf16[256,256]{1,0:T(8,128)(2,1)} %get-tuple-element.26.refs_4_), channel_id=1, source_target_pairs={{0,9},{1,12},{4,13},{9,0},{12,1},{13,4},{2,11},{3,14},{6,15},{11,2... | collective-permute-start | bytes 393224 | tf_op jit(solution)/shard_map/ppermute | solution.py:262
  99.1 1.9 %copy-start.4 = (bf16[24,1,256,256]{3,2,1,0:T(8,128)(2,1)S(1)}, bf16[24,1,256,256]{3,2,1,0:T(8,128)(2,1)}, u32[]{:S(2)}) copy-start(bf16[24,1,256,256]{3,2,1,0:T(8,128)(2,1)} %param.6) | copy-start | bytes 9437188
  101.0 1.0 copy-start.7
  102.0 1.0 copy-start.9
  103.1 0.9 copy-start.13
  114.7 5.0 %copy-start.14 = (bf16[256,256]{1,0:T(8,128)(2,1)}, bf16[256,256]{1,0:T(8,128)(2,1)S(1)}, u32[]{:S(2)}) copy-start(bf16[256,256]{1,0:T(8,128)(2,1)S(1)} %get-tuple-element.27.refs_0_) | copy-start | bytes 393220
  114.7 5.0 %collective-permute-start.8 = (bf16[256,256]{1,0:T(8,128)(2,1)S(1)}, bf16[256,256]{1,0:T(8,128)(2,1)S(1)}, u32[]{:S(2)}, u32[]{:S(2)}) collective-permute-start(bf16[256,256]{1,0:T(8,128)(2,1)S(1)} %get-tuple-element.27.refs_0_), channel_id=1, source_target_pairs={{0,2},{2,0},{1,3},{3,1},{4,6},{6,4},{5,7},{7,5},{8,10},{10,8},{9,1... | collective-permute-start | bytes 393224 | tf_op jit(solution)/shard_map/ppermute | solution.py:225
  (11 other events, 7.5 us)

commit v2 on v1

--- a/solution.py
+++ b/solution.py
@@ -11,10 +11,10 @@
 STEPS = 3
 OFFSETS = (0, NS + 1, NS - 1, -(NS + 1), -(NS - 1))
 EPSILON = 1e-06
-UNROLL = 2
+WIDE = 8
 VMEM = pl.BlockSpec(memory_space=pltpu.VMEM)
 SMEM = pl.BlockSpec(memory_space=pltpu.SMEM)
-ANY = pl.BlockSpec(memory_space=pl.ANY)
+MIB = 1024 * 1024
 
 
 def reaches(kind, sector, blocks):
@@ -104,36 +104,30 @@
 
 def product_kernel(step, slots, place, blocks, entries, *refs):
     refs = list(refs)
-    kinds_ref, left_hbm, right_hbm, rows_ref = refs[:4]
+    kinds_ref, left_ref, right_ref, rows_ref = refs[:4]
     refs = refs[4:]
     fresh, refs = refs[:slots], refs[slots:]
     if step >= 1:
         v_ref, refs = refs[0], refs[1:]
     if step >= 2:
         vp_ref, scal_ref, refs = refs[0], refs[1], refs[2:]
-    t_ref, v_out, scal_out, left, right, acc, order, slot_of, sems = refs
-    channels = left_hbm.shape[0]
+    t_ref, v_out, scal_out, acc, order, slot_of = refs
+    channels = kinds_ref.shape[0]
     sector = lax.axis_index("blk") * lax.axis_size("rep") + lax.axis_index("rep")
+    reached = [jnp.int32(1)] + [reaches(c, sector, blocks).astype(jnp.int32) for c in range(1, 5)]
 
     def list_channel(b, count):
         kind = kinds_ref[b]
-        live = kind == 0
-        slot = jnp.int32(0)
+        live, slot = reached[0], jnp.int32(0)
         for c in range(1, 5):
-            live = live | ((kind == c) & reaches(c, sector, blocks))
+            live = jnp.where(kind == c, reached[c], live)
             slot = jnp.where(kind == c, 1 + place[c], slot)
-
-        @pl.when(live)
-        def _():
-            order[count] = b
-            slot_of[count] = slot
-            pltpu.make_async_copy(left_hbm.at[b], left.at[count], sems.at[0, count]).start()
-            pltpu.make_async_copy(right_hbm.at[b], right.at[count], sems.at[1, count]).start()
-
-        return count + live.astype(jnp.int32)
+        order[count] = b
+        slot_of[count] = slot
+        return count + live
 
     count = lax.fori_loop(0, channels, list_channel, jnp.int32(0))
-    for extra in range(UNROLL - 1):
+    for extra in range(WIDE):
         order[count + extra] = 0
         slot_of[count + extra] = slots
 
@@ -144,6 +138,7 @@
     else:
         alpha, beta = coefficients(rows, entries)
     scal_out[...] = pack([alpha, beta], scal_out.shape)
+    inverse = 1.0 / beta
     for slot in range(slots):
         block = fresh[slot][0] if step == 0 else fresh[slot][...]
         r = block.astype(jnp.float32)
@@ -151,35 +146,38 @@
             r -= alpha * v_ref[slot].astype(jnp.float32)
         if step >= 2:
             r -= lane_of(scal_ref[0:1, :], 1) * vp_ref[slot].astype(jnp.float32)
-        v_out[slot] = (r / beta).astype(jnp.bfloat16)
+        v_out[slot] = (r * inverse).astype(jnp.bfloat16)
     v_out[slots] = jnp.zeros(v_out.shape[1:], jnp.bfloat16)
     acc[...] = jnp.zeros_like(acc)
 
-    def multiply(group, carry):
-        result = None
-        for inner in range(UNROLL):
-            at = group * UNROLL + inner
-            live = at < count
-
-            @pl.when(live)
-            def _():
-                pltpu.make_async_copy(left_hbm.at[0], left.at[at], sems.at[0, at]).wait()
-                pltpu.make_async_copy(right_hbm.at[0], right.at[at], sems.at[1, at]).wait()
-
-        for inner in range(UNROLL):
-            at = group * UNROLL + inner
-            held = jnp.where(at < count, at, 0)
-            piece = jnp.dot(
-                left[held], v_out[slot_of[at]], preferred_element_type=jnp.float32
+    def multiply(start, wide):
+        held = [order[start + inner] for inner in range(wide)]
+        pieces = [
+            jnp.dot(
+                left_ref[b], v_out[slot_of[start + inner]], preferred_element_type=jnp.float32
             ).astype(jnp.bfloat16)
-            term = lax.dot_general(
-                piece, right[held], (((1,), (1,)), ((), ())), preferred_element_type=jnp.float32
-            )
-            result = term if result is None else result + term
-        acc[...] += result
+            for inner, b in enumerate(held)
+        ]
+        acc[...] += lax.dot_general(
+            jnp.concatenate(pieces, axis=1),
+            jnp.concatenate([right_ref[b] for b in held], axis=1),
+            (((1,), (1,)), ((), ())),
+            preferred_element_type=jnp.float32,
+        )
+
+    def full(group, carry):
+        multiply(group * WIDE, WIDE)
         return carry
 
-    lax.fori_loop(0, (count + UNROLL - 1) // UNROLL, multiply, 0)
+    groups = count // WIDE
+    lax.fori_loop(0, groups, full, 0)
+    rest = count - groups * WIDE
+    for low, wide in ((0, 2), (2, 4), (4, WIDE)):
+
+        @pl.when((rest > low) & (rest <= wide))
+        def _():
+            multiply(groups * WIDE, wide)
+
     t_ref[...] = acc[...].astype(jnp.bfloat16)
 
 
@@ -234,17 +232,14 @@
                 jax.ShapeDtypeStruct((slots + 1, width, width), jnp.bfloat16),
                 jax.ShapeDtypeStruct((8, 128), jnp.float32),
             ),
-            in_specs=[SMEM, ANY, ANY] + [VMEM] * (1 + len(fresh) + len(old)),
+            in_specs=[SMEM] + [VMEM] * (3 + len(fresh) + len(old)),
             out_specs=(VMEM,) * 3,
             scratch_shapes=[
-                pltpu.VMEM((channels, width, width), jnp.bfloat16),
-                pltpu.VMEM((channels, width, width), jnp.bfloat16),
                 pltpu.VMEM((width, width), jnp.float32),
-                pltpu.SMEM((channels + UNROLL,), jnp.int32),
-                pltpu.SMEM((channels + UNROLL,), jnp.int32),
-                pltpu.SemaphoreType.DMA((2, channels)),
+                pltpu.SMEM((channels + WIDE,), jnp.int32),
+                pltpu.SMEM((channels + WIDE,), jnp.int32),
             ],
-            compiler_params=pltpu.CompilerParams(vmem_limit_bytes=32 * 1024 * 1024),
+            compiler_params=pltpu.CompilerParams(vmem_limit_bytes=16 * MIB),
             name="product",
         )(channel_class, left, right, rows, *fresh, *old)
 
@@ -255,6 +250,7 @@
             out_shape=(block_f32 if last else block_bf16, rows_shape),
             in_specs=[VMEM] * (len(pieces) + 3),
             out_specs=(VMEM, VMEM),
+            compiler_params=pltpu.CompilerParams(vmem_limit_bytes=4 * MIB),
             name="middle",
         )(*pieces, v, vp, scal)
 
@@ -262,9 +258,14 @@
         return [block] + [lax.ppermute(block, ring, pairs) for pairs in permutes]
 
     fresh = spread(wavefunction)
-    rows = pl.pallas_call(norm_kernel, out_shape=rows_shape, in_specs=[VMEM], out_specs=VMEM, name="norm")(
-        wavefunction
-    )
+    rows = pl.pallas_call(
+        norm_kernel,
+        out_shape=rows_shape,
+        in_specs=[VMEM],
+        out_specs=VMEM,
+        compiler_params=pltpu.CompilerParams(vmem_limit_bytes=4 * MIB),
+        name="norm",
+    )(wavefunction)
     t, v1, scal0 = product(0, fresh, exchange(rows))
     w, rows = middle(True, False, t, v1, v1, scal0)
     fresh = spread(w)
@@ -281,6 +282,7 @@
         ),
         in_specs=[VMEM] * 6,
         out_specs=(VMEM, VMEM),
+        compiler_params=pltpu.CompilerParams(vmem_limit_bytes=4 * MIB),
         name="final",
     )(exchange(rows), w, v3, v2, scal1, scal2)
     return basis, coefs

time: 135 us -> 89.8 us (0.67)
  Pallas kernels: 35.8 us -> 8.39 us
  local copies, waits for them, and re-layouts: 20.8 us -> 6.25 us
  starting transfers between devices: 26.2 us -> 20.6 us
  waiting for transfers between devices: 11.5 us -> 12.9 us
    pallas_call x3, Pallas kernels: 25.2 us -> 6.26 us  [product(): pl.pallas_call(functools.partial(product_kernel, step, slots, place, bloc...]
    unnamed x52 -> x16, local copies, waits for them, and re-layouts: 20.8 us -> 6.25 us
    ppermute x6, starting transfers between devices: 22.8 us -> 16.3 us  [spread(): return [block] + [lax.ppermute(block, ring, pairs) for pairs in permutes]]
    pallas_call x3, Pallas kernels: 6.66 us -> 0.96 us  [middle(): pl.pallas_call(functools.partial(middle_kernel, first, last), out_shape=(...]
    pallas_call x1, Pallas kernels: 1.6 us -> 0.11 us  [shards(): pl.pallas_call(norm_kernel, out_shape=rows_shape, in_specs=[VMEM], out_sp...]
    ppermute x3, waiting for transfers between devices: 11.4 us -> 12.9 us  [gather_parts(): return [t, lax.ppermute(t, 'mpo', [(0, 1), (1, 0)])]]
  transfers between devices with their start and end apart: 9 -> 9, of which waited for: 3 -> 3; matrix products, arithmetic and copies ran while one was open for 0% -> 0% of each run, Pallas kernels for 1% -> 0%
where the time goes in v2:
time: 89.8 us; the launch traced here: 88.7 us
  blocking collectives  39.8 us (44%)
  starting transfers between devices  20.6 us (23%)
  waiting for transfers between devices  12.9 us (14%)
  Pallas kernels  8.39 us (9%)
  local copies, waits for them, and re-layouts  6.25 us (7%)
    all_to_all x4, blocking collectives, exchange(): return lax.all_to_all(rows, ring, 0, 0, tiled=True)  39.8 us
    ppermute x6, starting transfers between devices, spread(): return [block] + [lax.ppermute(block, ring, pairs) for pairs in permutes]  16.3 us
    ppermute x3, waiting for transfers between devices, gather_parts(): return [t, lax.ppermute(t, 'mpo', [(0, 1), (1, 0)])]  12.9 us
    pallas_call x3, Pallas kernels, product(): pl.pallas_call(functools.partial(product_kernel, step, slots, place, bloc...  6.26 us
    unnamed x16, local copies, waits for them, and re-layouts  6.25 us
    ppermute x3, starting transfers between devices, gather_parts(): return [t, lax.ppermute(t, 'mpo', [(0, 1), (1, 0)])]  4.31 us
  transfers between devices with their start and end apart: 9, of which 3 were waited for; matrix products, arithmetic and copies ran while one was open for 0% of the time, Pallas kernels for 0%

profile of v2, /device:TPU:0, one launch (start us, length us, event | category | flops | bytes accessed | tf_op | source)
XLA Modules:
  0.0 88.7 jit_solution(15728420994273765397)
XLA Ops:
  0.6 5.4 %collective-permute-start = (bf16[1,256,256]{2,1,0:T(8,128)(2,1)}, bf16[1,256,256]{2,1,0:T(8,128)(2,1)S(1)}, u32[]{:S(2)}, u32[]{:S(2)}) collective-permute-start(bf16[1,256,256]{2,1,0:T(8,128)(2,1)} %refs_4_.1), channel_id=1, source_target_pairs={{0,9},{1,12},{4,13},{9,0},{12,1},{13,4},{2,11},{3,14},{6,15},{11,2... | collective-permute-start | bytes 393224 | tf_op jit(solution)/shard_map/ppermute | solution.py:258
  6.0 0.7 collective-permute-start.1
  6.7 0.9 %copy-done.4 = bf16[1,256,256]{2,1,0:T(8,128)(2,1)S(1)} copy-done((bf16[1,256,256]{2,1,0:T(8,128)(2,1)S(1)}, bf16[1,256,256]{2,1,0:T(8,128)(2,1)}, u32[]{:S(2)}) %copy-start.4) | copy-done | bytes 131096
  7.7 12.1 %all_to_all.44 = f32[8,1,128]{2,1,0:T(1,128)S(1)} all-to-all(f32[8,1,128]{2,1,0:T(1,128)S(1)} %bitcast.28), channel_id=1, replica_groups=mesh['groups'=2,'blk'=4,'mpo'=2,'rep'=2] {'blk','rep'}, dimensions={0} | all-to-all | bytes 8192 | tf_op jit(solution)/shard_map/all_to_all | solution.py:219
  19.8 1.9 %copy-done = bf16[24,1,256,256]{3,2,1,0:T(8,128)(2,1)S(1)} copy-done((bf16[24,1,256,256]{3,2,1,0:T(8,128)(2,1)S(1)}, bf16[24,1,256,256]{3,2,1,0:T(8,128)(2,1)}, u32[]{:S(2)}) %copy-start) | copy-done | bytes 3145752
  21.7 1.9 %copy-done.2 = bf16[24,1,256,256]{3,2,1,0:T(8,128)(2,1)S(1)} copy-done((bf16[24,1,256,256]{3,2,1,0:T(8,128)(2,1)S(1)}, bf16[24,1,256,256]{3,2,1,0:T(8,128)(2,1)}, u32[]{:S(2)}) %copy-start.2) | copy-done | bytes 3145752
  23.6 0.9 %copy-done.5 = bf16[1,256,256]{2,1,0:T(8,128)(2,1)S(1)} copy-done((bf16[1,256,256]{2,1,0:T(8,128)(2,1)S(1)}, bf16[1,256,256]{2,1,0:T(8,128)(2,1)}, u32[]{:S(2)}) %copy-start.5) | copy-done | bytes 131096
  25.2 1.8 %product.3 = (bf16[256,256]{1,0:T(8,128)(2,1)S(1)}, bf16[4,256,256]{2,1,0:T(8,128)(2,1)S(1)}, f32[8,128]{1,0:T(8,128)S(1)}) custom-call(s32[24]{0:T(128)S(1)} %copy-done.6, bf16[24,256,256]{2,1,0:T(8,128)(2,1)S(1)} %bitcast.18, bf16[24,256,256]{2,1,0:T(8,128)(2,1)S(1)} %bitcast.21, f32[8,128]{1,0:T(8,128)S(1)} %bitcast.26, ...), custom_call_target="tpu_custom_call" | custom-call | tf_op jit(solution)/shard_map/product/pallas_call | solution.py:228
  27.0 1.6 %collective-permute-start.2 = (bf16[256,256]{1,0:T(8,128)(2,1)S(1)}, bf16[256,256]{1,0:T(8,128)(2,1)S(1)}, u32[]{:S(2)}, u32[]{:S(2)}) collective-permute-start(bf16[256,256]{1,0:T(8,128)(2,1)S(1)} %get-tuple-element.17.refs_0_), channel_id=1, source_target_pairs={{0,2},{2,0},{1,3},{3,1},{4,6},{6,4},{5,7},{7,5},{8,10},{10,8},{9,1... | collective-permute-start | bytes 393224 | tf_op jit(solution)/shard_map/ppermute | solution.py:223
  28.5 4.3 %collective-permute-done.2.refs_1_ = bf16[256,256]{1,0:T(8,128)(2,1)S(1)} collective-permute-done((bf16[256,256]{1,0:T(8,128)(2,1)S(1)}, bf16[256,256]{1,0:T(8,128)(2,1)S(1)}, u32[]{:S(2)}, u32[]{:S(2)}) %collective-permute-start.2) | collective-permute-done | bytes 131104 | tf_op jit(solution)/shard_map/ppermute | solution.py:223
  33.1 0.7 collective-permute-start.4
  33.8 4.4 %collective-permute-start.3 = (bf16[256,256]{1,0:T(8,128)(2,1)S(1)}, bf16[256,256]{1,0:T(8,128)(2,1)S(1)}, u32[]{:S(2)}, u32[]{:S(2)}) collective-permute-start(bf16[256,256]{1,0:T(8,128)(2,1)S(1)} %get-tuple-element.21.refs_4_), channel_id=1, source_target_pairs={{0,9},{1,12},{4,13},{9,0},{12,1},{13,4},{2,11},{3,14},{6,15},{11,2... | collective-permute-start | bytes 393224 | tf_op jit(solution)/shard_map/ppermute | solution.py:258
  38.3 9.8 %all_to_all.45 = f32[8,1,128]{2,1,0:T(1,128)S(1)} all-to-all(f32[8,1,128]{2,1,0:T(1,128)S(1)} %bitcast.29), channel_id=1, replica_groups=mesh['groups'=2,'blk'=4,'mpo'=2,'rep'=2] {'blk','rep'}, dimensions={0} | all-to-all | bytes 8192 | tf_op jit(solution)/shard_map/all_to_all | solution.py:219
  48.1 2.2 %product.4 = (bf16[256,256]{1,0:T(8,128)(2,1)S(1)}, bf16[4,256,256]{2,1,0:T(8,128)(2,1)S(1)}, f32[8,128]{1,0:T(8,128)S(1)}) custom-call(s32[24]{0:T(128)S(1)} %copy-done.7, bf16[24,256,256]{2,1,0:T(8,128)(2,1)S(1)} %bitcast.19, bf16[24,256,256]{2,1,0:T(8,128)(2,1)S(1)} %bitcast.22, f32[8,128]{1,0:T(8,128)S(1)} %bitcast.25, ...), custom_call_target="tpu_custom_call" | custom-call | tf_op jit(solution)/shard_map/product/pallas_call | solution.py:228
  50.3 1.4 %collective-permute-start.5 = (bf16[256,256]{1,0:T(8,128)(2,1)S(1)}, bf16[256,256]{1,0:T(8,128)(2,1)S(1)}, u32[]{:S(2)}, u32[]{:S(2)}) collective-permute-start(bf16[256,256]{1,0:T(8,128)(2,1)S(1)} %get-tuple-element.22.refs_0_), channel_id=1, source_target_pairs={{0,2},{2,0},{1,3},{3,1},{4,6},{6,4},{5,7},{7,5},{8,10},{10,8},{9,1... | collective-permute-start | bytes 393224 | tf_op jit(solution)/shard_map/ppermute | solution.py:223
  51.7 4.3 %collective-permute-done.5.refs_1_ = bf16[256,256]{1,0:T(8,128)(2,1)S(1)} collective-permute-done((bf16[256,256]{1,0:T(8,128)(2,1)S(1)}, bf16[256,256]{1,0:T(8,128)(2,1)S(1)}, u32[]{:S(2)}, u32[]{:S(2)}) %collective-permute-start.5) | collective-permute-done | bytes 131104 | tf_op jit(solution)/shard_map/ppermute | solution.py:223
  56.3 0.7 collective-permute-start.7
  57.0 4.4 %collective-permute-start.6 = (bf16[256,256]{1,0:T(8,128)(2,1)S(1)}, bf16[256,256]{1,0:T(8,128)(2,1)S(1)}, u32[]{:S(2)}, u32[]{:S(2)}) collective-permute-start(bf16[256,256]{1,0:T(8,128)(2,1)S(1)} %get-tuple-element.26.refs_4_), channel_id=1, source_target_pairs={{0,9},{1,12},{4,13},{9,0},{12,1},{13,4},{2,11},{3,14},{6,15},{11,2... | collective-permute-start | bytes 393224 | tf_op jit(solution)/shard_map/ppermute | solution.py:258
  61.5 9.9 %all_to_all.46 = f32[8,1,128]{2,1,0:T(1,128)S(1)} all-to-all(f32[8,1,128]{2,1,0:T(1,128)S(1)} %bitcast.30), channel_id=1, replica_groups=mesh['groups'=2,'blk'=4,'mpo'=2,'rep'=2] {'blk','rep'}, dimensions={0} | all-to-all | bytes 8192 | tf_op jit(solution)/shard_map/all_to_all | solution.py:219
  71.4 2.3 %product.5 = (bf16[256,256]{1,0:T(8,128)(2,1)S(1)}, bf16[4,256,256]{2,1,0:T(8,128)(2,1)S(1)}, f32[8,128]{1,0:T(8,128)S(1)}) custom-call(s32[24]{0:T(128)S(1)} %copy-done.7, bf16[24,256,256]{2,1,0:T(8,128)(2,1)S(1)} %bitcast.20, bf16[24,256,256]{2,1,0:T(8,128)(2,1)S(1)} %bitcast.23, f32[8,128]{1,0:T(8,128)S(1)} %bitcast.24, ...), custom_call_target="tpu_custom_call" | custom-call | tf_op jit(solution)/shard_map/product/pallas_call | solution.py:228
  73.7 1.3 %collective-permute-start.8 = (bf16[256,256]{1,0:T(8,128)(2,1)S(1)}, bf16[256,256]{1,0:T(8,128)(2,1)S(1)}, u32[]{:S(2)}, u32[]{:S(2)}) collective-permute-start(bf16[256,256]{1,0:T(8,128)(2,1)S(1)} %get-tuple-element.27.refs_0_), channel_id=1, source_target_pairs={{0,2},{2,0},{1,3},{3,1},{4,6},{6,4},{5,7},{7,5},{8,10},{10,8},{9,1... | collective-permute-start | bytes 393224 | tf_op jit(solution)/shard_map/ppermute | solution.py:223
  75.0 4.3 %collective-permute-done.8.refs_1_ = bf16[256,256]{1,0:T(8,128)(2,1)S(1)} collective-permute-done((bf16[256,256]{1,0:T(8,128)(2,1)S(1)}, bf16[256,256]{1,0:T(8,128)(2,1)S(1)}, u32[]{:S(2)}, u32[]{:S(2)}) %collective-permute-start.8) | collective-permute-done | bytes 131104 | tf_op jit(solution)/shard_map/ppermute | solution.py:223
  79.6 8.0 %all_to_all.47 = f32[8,1,128]{2,1,0:T(1,128)S(1)} all-to-all(f32[8,1,128]{2,1,0:T(1,128)S(1)} %bitcast.31), channel_id=1, replica_groups=mesh['groups'=2,'blk'=4,'mpo'=2,'rep'=2] {'blk','rep'}, dimensions={0} | all-to-all | bytes 8192 | tf_op jit(solution)/shard_map/all_to_all | solution.py:219
  87.6 1.1 %final.1 = (bf16[3,1,128,256]{3,2,1,0:T(8,128)(2,1)}, f32[2,3]{1,0:T(2,128)}) custom-call(f32[8,128]{1,0:T(8,128)S(1)} %bitcast.27, f32[256,256]{1,0:T(8,128)S(1)} %get-tuple-element.31.w_ref, bf16[4,256,256]{2,1,0:T(8,128)(2,1)S(1)} %get-tuple-element.28.refs_2_.v3_ref, bf16[4,256,256]{2,1,0:T(8,128)(2,1)S(1)} %get-tuple-element.23.refs_2_.refs_7_.refs_3_.v2_ref, ...), custom_call_target="tpu_custom_call" | custom-call | tf_op jit(solution)/shard_map/final/pallas_call | solution.py:277
  (22 shorter events, 1.8 us)
Async XLA Ops:
  0.6 19.2 %collective-permute-start = (bf16[1,256,256]{2,1,0:T(8,128)(2,1)}, bf16[1,256,256]{2,1,0:T(8,128)(2,1)S(1)}, u32[]{:S(2)}, u32[]{:S(2)}) collective-permute-start(bf16[1,256,256]{2,1,0:T(8,128)(2,1)} %refs_4_.1), channel_id=1, source_target_pairs={{0,9},{1,12},{4,13},{9,0},{12,1},{13,4},{2,11},{3,14},{6,15},{11,2... | collective-permute-start | bytes 393224 | tf_op jit(solution)/shard_map/ppermute | solution.py:258
  6.0 13.8 %collective-permute-start.1 = (bf16[1,256,256]{2,1,0:T(8,128)(2,1)}, bf16[1,256,256]{2,1,0:T(8,128)(2,1)S(1)}, u32[]{:S(2)}, u32[]{:S(2)}) collective-permute-start(bf16[1,256,256]{2,1,0:T(8,128)(2,1)} %refs_4_.1), channel_id=1, source_target_pairs={{1,8},{4,9},{5,12},{8,1},{9,4},{12,5},{3,10},{6,11},{7,14},{10,3},... | collective-permute-start | bytes 393224 | tf_op jit(solution)/shard_map/ppermute | solution.py:258
  6.7 0.9 %copy-start.4 = (bf16[1,256,256]{2,1,0:T(8,128)(2,1)S(1)}, bf16[1,256,256]{2,1,0:T(8,128)(2,1)}, u32[]{:S(2)}) copy-start(bf16[1,256,256]{2,1,0:T(8,128)(2,1)} %refs_4_.1) | copy-start | bytes 393220
  19.8 1.9 %copy-start = (bf16[24,1,256,256]{3,2,1,0:T(8,128)(2,1)S(1)}, bf16[24,1,256,256]{3,2,1,0:T(8,128)(2,1)}, u32[]{:S(2)}) copy-start(bf16[24,1,256,256]{3,2,1,0:T(8,128)(2,1)} %param.5) | copy-start | bytes 9437188
  21.7 1.9 %copy-start.2 = (bf16[24,1,256,256]{3,2,1,0:T(8,128)(2,1)S(1)}, bf16[24,1,256,256]{3,2,1,0:T(8,128)(2,1)}, u32[]{:S(2)}) copy-start(bf16[24,1,256,256]{3,2,1,0:T(8,128)(2,1)} %param.6) | copy-start | bytes 9437188
  23.6 0.9 %copy-start.5 = (bf16[1,256,256]{2,1,0:T(8,128)(2,1)S(1)}, bf16[1,256,256]{2,1,0:T(8,128)(2,1)}, u32[]{:S(2)}) copy-start(bf16[1,256,256]{2,1,0:T(8,128)(2,1)} %refs_4_.1) | copy-start | bytes 393220
  24.5 0.7 copy-start.6
  25.2 22.9 %copy-start.1 = (bf16[24,1,256,256]{3,2,1,0:T(8,128)(2,1)S(1)}, bf16[24,1,256,256]{3,2,1,0:T(8,128)(2,1)}, u32[]{:S(2)}) copy-start(bf16[24,1,256,256]{3,2,1,0:T(8,128)(2,1)} %param.5) | copy-start | bytes 9437188
  25.2 22.9 %copy-start.3 = (bf16[24,1,256,256]{3,2,1,0:T(8,128)(2,1)S(1)}, bf16[24,1,256,256]{3,2,1,0:T(8,128)(2,1)}, u32[]{:S(2)}) copy-start(bf16[24,1,256,256]{3,2,1,0:T(8,128)(2,1)} %param.6) | copy-start | bytes 9437188
  25.2 22.9 %copy-start.7 = (s32[24]{0:T(128)S(1)}, s32[24]{0:T(128)}, u32[]{:S(2)}) copy-start(s32[24]{0:T(128)} %refs_0_.5) | copy-start | bytes 292
  27.0 5.9 %collective-permute-start.2 = (bf16[256,256]{1,0:T(8,128)(2,1)S(1)}, bf16[256,256]{1,0:T(8,128)(2,1)S(1)}, u32[]{:S(2)}, u32[]{:S(2)}) collective-permute-start(bf16[256,256]{1,0:T(8,128)(2,1)S(1)} %get-tuple-element.17.refs_0_), channel_id=1, source_target_pairs={{0,2},{2,0},{1,3},{3,1},{4,6},{6,4},{5,7},{7,5},{8,10},{10,8},{9,1... | collective-permute-start | bytes 393224 | tf_op jit(solution)/shard_map/ppermute | solution.py:223
  33.1 14.9 %collective-permute-start.4 = (bf16[256,256]{1,0:T(8,128)(2,1)S(1)}, bf16[256,256]{1,0:T(8,128)(2,1)S(1)}, u32[]{:S(2)}, u32[]{:S(2)}) collective-permute-start(bf16[256,256]{1,0:T(8,128)(2,1)S(1)} %get-tuple-element.21.refs_4_), channel_id=1, source_target_pairs={{1,8},{4,9},{5,12},{8,1},{9,4},{12,5},{3,10},{6,11},{7,14},{10,3},... | collective-permute-start | bytes 393224 | tf_op jit(solution)/shard_map/ppermute | solution.py:258
  33.8 14.3 %collective-permute-start.3 = (bf16[256,256]{1,0:T(8,128)(2,1)S(1)}, bf16[256,256]{1,0:T(8,128)(2,1)S(1)}, u32[]{:S(2)}, u32[]{:S(2)}) collective-permute-start(bf16[256,256]{1,0:T(8,128)(2,1)S(1)} %get-tuple-element.21.refs_4_), channel_id=1, source_target_pairs={{0,9},{1,12},{4,13},{9,0},{12,1},{13,4},{2,11},{3,14},{6,15},{11,2... | collective-permute-start | bytes 393224 | tf_op jit(solution)/shard_map/ppermute | solution.py:258
  50.3 5.7 %collective-permute-start.5 = (bf16[256,256]{1,0:T(8,128)(2,1)S(1)}, bf16[256,256]{1,0:T(8,128)(2,1)S(1)}, u32[]{:S(2)}, u32[]{:S(2)}) collective-permute-start(bf16[256,256]{1,0:T(8,128)(2,1)S(1)} %get-tuple-element.22.refs_0_), channel_id=1, source_target_pairs={{0,2},{2,0},{1,3},{3,1},{4,6},{6,4},{5,7},{7,5},{8,10},{10,8},{9,1... | collective-permute-start | bytes 393224 | tf_op jit(solution)/shard_map/ppermute | solution.py:223
  56.3 15.0 %collective-permute-start.7 = (bf16[256,256]{1,0:T(8,128)(2,1)S(1)}, bf16[256,256]{1,0:T(8,128)(2,1)S(1)}, u32[]{:S(2)}, u32[]{:S(2)}) collective-permute-start(bf16[256,256]{1,0:T(8,128)(2,1)S(1)} %get-tuple-element.26.refs_4_), channel_id=1, source_target_pairs={{1,8},{4,9},{5,12},{8,1},{9,4},{12,5},{3,10},{6,11},{7,14},{10,3},... | collective-permute-start | bytes 393224 | tf_op jit(solution)/shard_map/ppermute | solution.py:258
  57.0 14.4 %collective-permute-start.6 = (bf16[256,256]{1,0:T(8,128)(2,1)S(1)}, bf16[256,256]{1,0:T(8,128)(2,1)S(1)}, u32[]{:S(2)}, u32[]{:S(2)}) collective-permute-start(bf16[256,256]{1,0:T(8,128)(2,1)S(1)} %get-tuple-element.26.refs_4_), channel_id=1, source_target_pairs={{0,9},{1,12},{4,13},{9,0},{12,1},{13,4},{2,11},{3,14},{6,15},{11,2... | collective-permute-start | bytes 393224 | tf_op jit(solution)/shard_map/ppermute | solution.py:258
  73.7 5.6 %collective-permute-start.8 = (bf16[256,256]{1,0:T(8,128)(2,1)S(1)}, bf16[256,256]{1,0:T(8,128)(2,1)S(1)}, u32[]{:S(2)}, u32[]{:S(2)}) collective-permute-start(bf16[256,256]{1,0:T(8,128)(2,1)S(1)} %get-tuple-element.27.refs_0_), channel_id=1, source_target_pairs={{0,2},{2,0},{1,3},{3,1},{4,6},{6,4},{5,7},{7,5},{8,10},{10,8},{9,1... | collective-permute-start | bytes 393224 | tf_op jit(solution)/shard_map/ppermute | solution.py:223

commit v3 on v2

v3 whole, which is shorter than its diff:
```python
import functools

import jax
import jax.numpy as jnp
from jax import lax
from jax.experimental import pallas as pl
from jax.experimental.pallas import tpu as pltpu
from jax.sharding import PartitionSpec as P

NS = 4
STEPS = 3
OFFSETS = (0, NS + 1, NS - 1, -(NS + 1), -(NS - 1))
EPSILON = 1e-06
WIDE = 8
SMALLEST = 1e-30
MIB = 1024 * 1024
VMEM = pl.BlockSpec(memory_space=pltpu.VMEM)
SMEM = pl.BlockSpec(memory_space=pltpu.SMEM)


def reaches(kind, sector, blocks):
    source = sector - OFFSETS[kind]
    spin = sector % NS
    inside = (source >= 0) & (source < blocks)
    if kind in (1, 4):
        return inside & (spin >= 1)
    if kind in (2, 3):
        return inside & (spin <= NS - 2)
    return inside


def routes(blocks):
    lists = {}
    for kind in range(1, 5):
        lists[kind] = [
            (k - OFFSETS[kind], k) for k in range(blocks) if bool(reaches(kind, k, blocks))
        ]
    permutes, place = [], {}
    for up, down in ((1, 3), (2, 4)):
        both = lists[up] + lists[down]
        disjoint = len({a for a, _ in both}) == len(both) == len({b for _, b in both})
        groups = ((up, down),) if disjoint else ((up,), (down,))
        for group in groups:
            for kind in group:
                place[kind] = len(permutes)
            permutes.append([pair for kind in group for pair in lists[kind]])
    return permutes, place


def here():
    return lax.axis_index("blk") * lax.axis_size("rep") + lax.axis_index("rep")


def lane_of(rows, lane):
    return rows[:, lane : lane + 1]


def pack(values, shape):
    lanes = lax.broadcasted_iota(jnp.int32, shape, 1)
    out = jnp.zeros(shape, jnp.float32)
    for place, value in enumerate(values):
        out = jnp.where(lanes == place, value, out)
    return out


def total(x):
    return jnp.sum(jnp.sum(x, axis=0, keepdims=True), axis=1, keepdims=True)


def column_sum(x):
    return jnp.sum(x, axis=0, keepdims=True)


def peak(x):
    return jnp.max(jnp.max(jnp.abs(x), axis=0, keepdims=True), axis=1, keepdims=True)


def wide_float(ref):
    return ref[...].astype(jnp.float32)


def sum_parts(parts):
    w = wide_float(parts[0])
    for part in parts[1:]:
        w += wide_float(part)
    return w


def first_row(ref):
    return ref[0:1, :]


def list_channels(which, place, blocks, kinds_ref, order, slot_of, idle):
    sector = here()
    use_own = 0 if which == "rest" else 1
    reached = [jnp.int32(use_own)]
    for c in range(1, 5):
        reach = reaches(c, sector, blocks).astype(jnp.int32)
        reached.append(reach if which != "own" else jnp.int32(0))

    def list_channel(b, count):
        kind = kinds_ref[b]
        live, slot = reached[0], jnp.int32(0)
        for c in range(1, 5):
            live = jnp.where(kind == c, reached[c], live)
            slot = jnp.where(kind == c, 1 + place[c], slot)
        order[count] = b
        slot_of[count] = slot
        return count + live

    count = lax.fori_loop(0, kinds_ref.shape[0], list_channel, jnp.int32(0))
    for extra in range(WIDE):
        order[count + extra] = 0
        slot_of[count + extra] = idle
    return count


def multiply_listed(count, left_ref, right_ref, source, acc, order, slot_of):
    def multiply(start, wide):
        held = [order[start + inner] for inner in range(wide)]
        pieces = [
            jnp.dot(
                left_ref[b], source[slot_of[start + inner]], preferred_element_type=jnp.float32
            ).astype(jnp.bfloat16)
            for inner, b in enumerate(held)
        ]
        acc[...] += lax.dot_general(
            jnp.concatenate(pieces, axis=1),
            jnp.concatenate([right_ref[b] for b in held], axis=1),
            (((1,), (1,)), ((), ())),
            preferred_element_type=jnp.float32,
        )

    def full(group, carry):
        multiply(group * WIDE, WIDE)
        return carry

    groups = count // WIDE
    lax.fori_loop(0, groups, full, 0)
    rest = count - groups * WIDE
    for low, wide in ((0, 2), (2, 4), (4, WIDE)):

        @pl.when((rest > low) & (rest <= wide))
        def _():
            multiply(groups * WIDE, wide)


def own_kernel(scaled, place, blocks, kinds_ref, left_ref, right_ref, block_ref, acc, source, order, slot_of):
    count = list_channels("own", place, blocks, kinds_ref, order, slot_of, 1)
    if scaled:
        block = wide_float(block_ref)
        inverse = 1.0 / jnp.maximum(peak(block), SMALLEST)
        source[0] = (block * inverse).astype(jnp.bfloat16)
    else:
        source[0] = block_ref[...]
    source[1] = jnp.zeros(source.shape[1:], jnp.bfloat16)
    acc[...] = jnp.zeros_like(acc)
    multiply_listed(count, left_ref, right_ref, source, acc, order, slot_of)


def rest_kernel(scaled, slots, place, blocks, *refs):
    kinds_ref, left_ref, right_ref, own_ref = refs[:4]
    held, refs = refs[4 : 4 + slots], refs[4 + slots :]
    if scaled:
        t_ref, unit_ref, acc, source, order, slot_of = refs
    else:
        t_ref, acc, source, order, slot_of = refs
    count = list_channels("rest", place, blocks, kinds_ref, order, slot_of, slots)
    if scaled:
        peaks = [jnp.maximum(peak(wide_float(block)), SMALLEST) for block in held]
        unit = functools.reduce(jnp.maximum, peaks)
        unit_ref[...] = jnp.broadcast_to(unit, unit_ref.shape)
        inverse = 1.0 / unit
        for slot in range(1, slots):
            source[slot] = (wide_float(held[slot]) * inverse).astype(jnp.bfloat16)
        acc[...] = own_ref[...] * (peaks[0] * inverse)
    else:
        for slot in range(1, slots):
            source[slot] = held[slot][...]
        acc[...] = own_ref[...]
    source[slots] = jnp.zeros(source.shape[1:], jnp.bfloat16)
    multiply_listed(count, left_ref, right_ref, source, acc, order, slot_of)
    t_ref[...] = acc[...].astype(jnp.bfloat16)


def second_kernel(slots, place, blocks, entries, *refs):
    kinds_ref, left_ref, right_ref, rows_ref = refs[:4]
    products, psis = refs[4 : 4 + slots], refs[4 + slots : 4 + 2 * slots]
    t_ref, v_ref, scal_ref, acc, source, order, slot_of = refs[4 + 2 * slots :]
    count = list_channels("all", place, blocks, kinds_ref, order, slot_of, slots)
    rows = rows_ref[...]
    a, d, local, p, q, unit = (lane_of(rows, lane) for lane in range(6))
    beta_0 = jnp.sqrt(column_sum(unit * unit * d) / entries + EPSILON)
    start_inverse = 1.0 / beta_0
    gain = unit * start_inverse
    alpha = column_sum(gain * (gain * a)) / entries
    off = local - alpha
    square = column_sum(gain * (gain * (q + off * (2.0 * p + off * d))))
    beta = jnp.sqrt(jnp.maximum(square, 0.0) / entries + EPSILON)
    inverse = 1.0 / beta
    sector = here()
    row_of = lax.broadcasted_iota(jnp.int32, gain.shape, 0)
    for slot in range(slots):
        origin = sector
        for kind in range(1, 5):
            if 1 + place[kind] == slot:
                origin = jnp.where(reaches(kind, sector, blocks), sector - OFFSETS[kind], origin)
        gain_here = column_sum(jnp.where(row_of == origin, gain, 0.0))
        r = gain_here * wide_float(products[slot]) - (alpha * start_inverse) * wide_float(psis[slot])
        source[slot] = (r * inverse).astype(jnp.bfloat16)
        if slot == 0:
            scal_ref[...] = pack([alpha, beta, start_inverse, gain_here], scal_ref.shape)
            v_ref[...] = source[0]
    source[slots] = jnp.zeros(source.shape[1:], jnp.bfloat16)
    acc[...] = jnp.zeros_like(acc)
    multiply_listed(count, left_ref, right_ref, source, acc, order, slot_of)
    t_ref[...] = acc[...].astype(jnp.bfloat16)


def first_sums_kernel(*refs):
    parts, (psi_ref, unit_ref, w_ref, rows_ref) = refs[:-4], refs[-4:]
    w = sum_parts(parts)
    w_ref[...] = w.astype(jnp.bfloat16)
    unit = lane_of(first_row(unit_ref), 0)
    v = wide_float(psi_ref) * (1.0 / unit)
    a = total(v * w)
    d = total(v * v)
    local = a / jnp.maximum(d, SMALLEST)
    r = w - local * v
    rows_ref[...] = pack([a, d, local, total(r * v), total(r * r), unit], rows_ref.shape)


def shrink(scal):
    return 1.0 / (jnp.abs(lane_of(scal, 0)) + lane_of(scal, 1))


def second_sums_kernel(*refs):
    parts, (scal_ref, wide_ref, w_ref) = refs[:-3], refs[-3:]
    w = sum_parts(parts) * shrink(first_row(scal_ref))
    wide_ref[...] = w
    w_ref[...] = w.astype(jnp.bfloat16)


def third_sums_kernel(*refs):
    parts, refs = refs[:-8], refs[-8:]
    psi_ref, first_ref, v_ref, w_ref, scal_ref, r_ref, z_ref, rows_ref = refs
    scal = first_row(scal_ref)
    beta, start_inverse, gain = (lane_of(scal, lane) for lane in range(1, 4))
    scale = shrink(scal)
    v, w = wide_float(v_ref), w_ref[...]
    vv, vw = total(v * v), total(v * w)
    local = vw / jnp.maximum(vv, SMALLEST)
    r = w - local * v - (scale * beta * start_inverse) * wide_float(psi_ref)
    z = sum_parts(parts) - (local / scale) * w - (scale * beta * gain) * wide_float(first_ref)
    r_ref[...] = r
    z_ref[...] = z
    sums = [total(r * r), total(r * v), total(r * z), total(r * w)]
    sums += [total(z * v), total(z * w), total(z * z), total(w * w)]
    rows_ref[...] = pack([vv, vw, local] + sums, rows_ref.shape)


def final_kernel(entries, rows_ref, r_ref, z_ref, w_ref, v_ref, scal_ref, basis_ref, coef_ref):
    share = basis_ref.shape[2]
    mine = pl.ds(pl.multiple_of(lax.axis_index("mpo") * share, share), share)
    vv, vw, local, rr, rv, rz, rw, zv, zw, zz, ww = (lane_of(rows_ref[...], i) for i in range(11))
    scal = first_row(scal_ref)
    scale = shrink(scal)
    inverse_scale = 1.0 / scale
    alpha_scaled = column_sum(vw) / entries
    off = local - alpha_scaled
    lift = off * inverse_scale
    square = column_sum(rr + off * (2.0 * rv + off * vv)) / entries
    beta_scaled = jnp.sqrt(jnp.maximum(square, 0.0) + scale * scale * EPSILON)
    inverse = 1.0 / beta_scaled
    mixed = column_sum(rz + lift * rw + off * (zv + lift * vw)) / entries
    alpha_3 = mixed * inverse * inverse
    r_v = column_sum(rv + off * vv) / entries
    z_v = column_sum(zv + lift * vw) / entries
    z_z = column_sum(zz + lift * (2.0 * zw + lift * ww)) / entries
    v_v = column_sum(vv) / entries
    beta_2 = beta_scaled * inverse_scale
    third = (z_z - 2.0 * alpha_3 * mixed + alpha_3 * alpha_3 * square) * inverse * inverse
    third += beta_2 * (beta_2 * v_v - 2.0 * inverse * (z_v - alpha_3 * r_v))
    beta_3 = jnp.sqrt(jnp.maximum(third, 0.0) + EPSILON)

    sector = here()
    row_of = lax.broadcasted_iota(jnp.int32, off.shape, 0)
    off_here = column_sum(jnp.where(row_of == sector, off, 0.0))
    v = v_ref[mine, :]
    v_wide = v.astype(jnp.float32)
    v_3 = (r_ref[mine, :] + off_here * v_wide) * inverse
    image = (z_ref[mine, :] + (off_here * inverse_scale) * w_ref[mine, :]) * inverse
    basis_ref[0, 0] = v
    basis_ref[1, 0] = v_3.astype(jnp.bfloat16)
    residual = image - alpha_3 * v_3 - beta_2 * v_wide
    basis_ref[2, 0] = (residual * (1.0 / beta_3)).astype(jnp.bfloat16)

    row = lax.broadcasted_iota(jnp.int32, coef_ref.shape, 0)
    column = lax.broadcasted_iota(jnp.int32, coef_ref.shape, 1)
    out = jnp.zeros(coef_ref.shape, jnp.float32)
    pairs = [(lane_of(scal, 0), lane_of(scal, 1)), (alpha_scaled * inverse_scale, beta_2), (alpha_3, beta_3)]
    for step, (a, b) in enumerate(pairs):
        out = jnp.where(column == step, jnp.where(row == 0, a, b), out)
    coef_ref[...] = out


def shards(wavefunction, env_left, env_right, channel_class):
    width = wavefunction.shape[1]
    ring = ("blk", "rep")
    parts = lax.axis_size("mpo")
    blocks = lax.axis_size("blk") * lax.axis_size("rep")
    entries = blocks * width * width
    permutes, place = routes(blocks)
    slots = 1 + len(permutes)
    channels = channel_class.shape[0]
    psi, left, right = wavefunction[0], env_left[:, 0], env_right[:, 0]
    rows_shape = jax.ShapeDtypeStruct((blocks, 128), jnp.float32)
    scalars = jax.ShapeDtypeStruct((8, 128), jnp.float32)
    wide = jax.ShapeDtypeStruct((width, width), jnp.float32)
    narrow = jax.ShapeDtypeStruct((width, width), jnp.bfloat16)
    lists = [pltpu.SMEM((channels + WIDE,), jnp.int32)] * 2

    def call(kernel, name, outs, args, scratch=(), share=0, limit=4):
        flops = int(4 * channels * share * width**3)
        cost = pl.CostEstimate(flops=flops, bytes_accessed=4 * width * width, transcendentals=0)
        listed = outs if isinstance(outs, tuple) else (outs,)
        first = SMEM if share else VMEM
        return pl.pallas_call(
            kernel,
            out_shape=outs,
            in_specs=[first] + [VMEM] * (len(args) - 1),
            out_specs=tuple(VMEM for _ in listed) if isinstance(outs, tuple) else VMEM,
            scratch_shapes=list(scratch),
            compiler_params=pltpu.CompilerParams(vmem_limit_bytes=limit * MIB),
            cost_estimate=cost,
            name=name,
        )(*args)

    def sources(count):
        return pltpu.VMEM((count + 1, width, width), jnp.bfloat16)

    def own(scaled, block):
        return call(
            functools.partial(own_kernel, scaled, place, blocks),
            "own",
            wide,
            (channel_class, left, right, block),
            [sources(1)] + lists,
            0.2,
            16,
        )

    def rest(scaled, mine, held):
        return call(
            functools.partial(rest_kernel, scaled, slots, place, blocks),
            "rest",
            (narrow, scalars) if scaled else narrow,
            (channel_class, left, right, mine, *held),
            [pltpu.VMEM((width, width), jnp.float32), sources(slots)] + lists,
            0.4,
            16,
        )

    def spread(block):
        return [block] + [lax.ppermute(block, ring, pairs) for pairs in permutes]

    def gather_parts(t):
        if parts == 2:
            return [t, lax.ppermute(t, "mpo", [(0, 1), (1, 0)])]
        held = lax.all_gather(t, "mpo")
        return [held[i] for i in range(parts)]

    def exchange(rows):
        return lax.all_to_all(rows, ring, 0, 0, tiled=True)

    psis = spread(psi)
    t, unit = rest(True, own(True, psi), psis)
    w_1, rows = call(first_sums_kernel, "sums", (narrow, rows_shape), (*gather_parts(t), psi, unit))
    products = spread(w_1)
    t, v_2, scal = call(
        functools.partial(second_kernel, slots, place, blocks, entries),
        "second",
        (narrow, narrow, scalars),
        (channel_class, left, right, exchange(rows), *products, *psis),
        [pltpu.VMEM((width, width), jnp.float32), sources(slots)] + lists,
        0.6,
        16,
    )
    w_wide, w_2 = call(second_sums_kernel, "sums", (wide, narrow), (*gather_parts(t), scal))
    t = rest(False, own(False, w_2), spread(w_2))
    r, z, rows = call(
        third_sums_kernel,
        "sums",
        (wide, wide, rows_shape),
        (*gather_parts(t), psi, w_1, v_2, w_wide, scal),
        limit=8,
    )
    return call(
        functools.partial(final_kernel, entries),
        "final",
        (
            jax.ShapeDtypeStruct((STEPS, 1, width // parts, width), jnp.bfloat16),
            jax.ShapeDtypeStruct((2, STEPS), jnp.float32),
        ),
        (exchange(rows), r, z, w_wide, v_2, scal),
    )


def solution(mesh):
    return jax.shard_map(
        shards,
        mesh=mesh,
        in_specs=(
            P(("groups", "blk", "rep"), None, None),
            P("mpo", ("groups", "blk", "rep"), None, None),
            P("mpo", ("groups", "blk", "rep"), None, None),
            P("mpo"),
        ),
        out_specs=(P(None, ("groups", "blk", "rep"), "mpo", None), P("groups", None)),
        check_vma=False,
    )
```

time: 89.8 us -> 77.3 us (0.86)
  blocking collectives: 39.8 us -> 18.6 us
  waiting for transfers between devices: 12.9 us -> 19.6 us
  Pallas kernels: 8.39 us -> 10.4 us
  starting transfers between devices: 20.6 us -> 22.4 us
  local copies, waits for them, and re-layouts: 6.25 us -> 5.34 us
    all_to_all x4 -> x2, blocking collectives: 39.8 us -> 18.6 us  [exchange(): return lax.all_to_all(rows, ring, 0, 0, tiled=True)]
    ppermute x6, waiting for transfers between devices: 0.02 us -> 7.22 us  [spread(): return [block] + [lax.ppermute(block, ring, pairs) for pairs in permutes]]
    pallas_call x8 -> x9, Pallas kernels: 8.39 us -> 10.4 us  [call(): pl.pallas_call(kernel, out_shape=outs, in_specs=[first] + [VMEM] * (len(a...]
    ppermute x6, starting transfers between devices: 16.3 us -> 18 us  [spread(): return [block] + [lax.ppermute(block, ring, pairs) for pairs in permutes]]
    unnamed x16 -> x10, local copies, waits for them, and re-layouts: 6.25 us -> 5.34 us
  transfers between devices with their start and end apart: 9 -> 9, of which waited for: 3 -> 5; matrix products, arithmetic and copies ran while one was open for 0% -> 0% of each run, Pallas kernels for 0% -> 4%
where the time goes in v3:
time: 77.3 us; the launch traced here: 77 us
  starting transfers between devices  22.4 us (29%)
  waiting for transfers between devices  19.6 us (25%)
  blocking collectives  18.6 us (24%)
  Pallas kernels  10.4 us (13%)
  local copies, waits for them, and re-layouts  5.34 us (7%)
    all_to_all x2, blocking collectives, exchange(): return lax.all_to_all(rows, ring, 0, 0, tiled=True)  18.6 us
    ppermute x6, starting transfers between devices, spread(): return [block] + [lax.ppermute(block, ring, pairs) for pairs in permutes]  18 us
    ppermute x3, waiting for transfers between devices, gather_parts(): return [t, lax.ppermute(t, 'mpo', [(0, 1), (1, 0)])]  12.3 us
    pallas_call x9, Pallas kernels, call(): pl.pallas_call(kernel, out_shape=outs, in_specs=[first] + [VMEM] * (len(a...  10.4 us
    ppermute x6, waiting for transfers between devices, spread(): return [block] + [lax.ppermute(block, ring, pairs) for pairs in permutes]  7.22 us
    unnamed x10, local copies, waits for them, and re-layouts  5.34 us
    ppermute x3, starting transfers between devices, gather_parts(): return [t, lax.ppermute(t, 'mpo', [(0, 1), (1, 0)])]  4.37 us
  transfers between devices with their start and end apart: 9, of which 5 were waited for; matrix products, arithmetic and copies ran while one was open for 0% of the time, Pallas kernels for 4%

profile of v3, /device:TPU:0, one launch (start us, length us, event | category | flops | bytes accessed | tf_op | source)
XLA Modules:
  0.0 77.0 jit_solution(8746149650220173587)
XLA Ops:
  0.6 0.7 collective-permute-start.1
  1.3 7.4 %collective-permute-start = (bf16[256,256]{1,0:T(8,128)(2,1)}, bf16[256,256]{1,0:T(8,128)(2,1)S(1)}, u32[]{:S(2)}, u32[]{:S(2)}) collective-permute-start(bf16[256,256]{1,0:T(8,128)(2,1)} %bitcast.22), channel_id=1, source_target_pairs={{0,9},{1,12},{4,13},{9,0},{12,1},{13,4},{2,11},{3,14},{6,15},{11,2... | collective-permute-start | bytes 393224 | tf_op jit(solution)/shard_map/ppermute | solution.py:365
  8.7 1.9 %copy-done = bf16[24,1,256,256]{3,2,1,0:T(8,128)(2,1)S(1)} copy-done((bf16[24,1,256,256]{3,2,1,0:T(8,128)(2,1)S(1)}, bf16[24,1,256,256]{3,2,1,0:T(8,128)(2,1)}, u32[]{:S(2)}) %copy-start) | copy-done | bytes 3145752
  10.6 1.9 %copy-done.1 = bf16[24,1,256,256]{3,2,1,0:T(8,128)(2,1)S(1)} copy-done((bf16[24,1,256,256]{3,2,1,0:T(8,128)(2,1)S(1)}, bf16[24,1,256,256]{3,2,1,0:T(8,128)(2,1)}, u32[]{:S(2)}) %copy-start.1) | copy-done | bytes 3145752
  12.5 0.9 %copy-done.2 = bf16[1,256,256]{2,1,0:T(8,128)(2,1)S(1)} copy-done((bf16[1,256,256]{2,1,0:T(8,128)(2,1)S(1)}, bf16[1,256,256]{2,1,0:T(8,128)(2,1)}, u32[]{:S(2)}) %copy-start.2) | copy-done | bytes 131096
  14.0 1.5 %own.2.refs_3_ = f32[256,256]{1,0:T(8,128)S(1)} custom-call(s32[24]{0:T(128)S(1)} %copy-done.4, bf16[24,256,256]{2,1,0:T(8,128)(2,1)S(1)} %bitcast.11, bf16[24,256,256]{2,1,0:T(8,128)(2,1)S(1)} %bitcast.16, bf16[256,256]{1,0:T(8,128)(2,1)S(1)} %bitcast.23), custom_call_target="tpu_custom_call" | custom-call | flops 322122560 | bytes 262144 | tf_op jit(solution)/shard_map/own/pallas_call | solution.py:328
  15.6 1.1 %collective-permute-done.refs_5_.refs_8_ = bf16[256,256]{1,0:T(8,128)(2,1)S(1)} collective-permute-done((bf16[256,256]{1,0:T(8,128)(2,1)}, bf16[256,256]{1,0:T(8,128)(2,1)S(1)}, u32[]{:S(2)}, u32[]{:S(2)}) %collective-permute-start) | collective-permute-done | bytes 131104 | tf_op jit(solution)/shard_map/ppermute | solution.py:365
  16.6 1.4 %rest.2 = (bf16[256,256]{1,0:T(8,128)(2,1)S(1)}, f32[8,128]{1,0:T(8,128)S(1)}) custom-call(s32[24]{0:T(128)S(1)} %copy-done.4, bf16[24,256,256]{2,1,0:T(8,128)(2,1)S(1)} %bitcast.12, bf16[24,256,256]{2,1,0:T(8,128)(2,1)S(1)} %bitcast.17, f32[256,256]{1,0:T(8,128)S(1)} %own.2.refs_3_, bf16[256,256]{1,0:T(8,128)(2,1)S(1)} %bitcast.24, ...), custom_call_target="tpu_custom_call" | custom-call | flops 644245120 | bytes 262144 | tf_op jit(solution)/shard_map/rest/pallas_call | solution.py:328
  18.0 1.2 %collective-permute-start.2 = (bf16[256,256]{1,0:T(8,128)(2,1)S(1)}, bf16[256,256]{1,0:T(8,128)(2,1)S(1)}, u32[]{:S(2)}, u32[]{:S(2)}) collective-permute-start(bf16[256,256]{1,0:T(8,128)(2,1)S(1)} %get-tuple-element.14.refs_0_), channel_id=1, source_target_pairs={{0,2},{2,0},{1,3},{3,1},{4,6},{6,4},{5,7},{7,5},{8,10},{10,8},{9,1... | collective-permute-start | bytes 393224 | tf_op jit(solution)/shard_map/ppermute | solution.py:369
  19.2 4.7 %collective-permute-done.2.refs_1_ = bf16[256,256]{1,0:T(8,128)(2,1)S(1)} collective-permute-done((bf16[256,256]{1,0:T(8,128)(2,1)S(1)}, bf16[256,256]{1,0:T(8,128)(2,1)S(1)}, u32[]{:S(2)}, u32[]{:S(2)}) %collective-permute-start.2) | collective-permute-done | bytes 131104 | tf_op jit(solution)/shard_map/ppermute | solution.py:369
  24.9 3.9 %collective-permute-start.3 = (bf16[256,256]{1,0:T(8,128)(2,1)S(1)}, bf16[256,256]{1,0:T(8,128)(2,1)S(1)}, u32[]{:S(2)}, u32[]{:S(2)}) collective-permute-start(bf16[256,256]{1,0:T(8,128)(2,1)S(1)} %get-tuple-element.17.refs_4_.refs_3_), channel_id=1, source_target_pairs={{0,9},{1,12},{4,13},{9,0},{12,1},{13,4},{2,11},{3,14},{6,15},{11,2... | collective-permute-start | bytes 393224 | tf_op jit(solution)/shard_map/ppermute | solution.py:365
  28.8 8.9 %all_to_all.22 = f32[8,1,128]{2,1,0:T(1,128)S(1)} all-to-all(f32[8,1,128]{2,1,0:T(1,128)S(1)} %bitcast.30), channel_id=1, replica_groups=mesh['groups'=2,'blk'=4,'mpo'=2,'rep'=2] {'blk','rep'}, dimensions={0} | all-to-all | bytes 8192 | tf_op jit(solution)/shard_map/all_to_all | solution.py:374
  37.7 2.4 %second.1 = (bf16[256,256]{1,0:T(8,128)(2,1)S(1)}, bf16[256,256]{1,0:T(8,128)(2,1)S(1)}, f32[8,128]{1,0:T(8,128)S(1)}) custom-call(s32[24]{0:T(128)S(1)} %copy-done.4, bf16[24,256,256]{2,1,0:T(8,128)(2,1)S(1)} %bitcast.13, bf16[24,256,256]{2,1,0:T(8,128)(2,1)S(1)} %bitcast.18, f32[8,128]{1,0:T(8,128)S(1)} %bitcast.28, ...), custom_call_target="tpu_custom_call" | custom-call | flops 966367616 | bytes 262144 | tf_op jit(solution)/shard_map/second/pallas_call | solution.py:328
  40.1 1.6 %collective-permute-start.5 = (bf16[256,256]{1,0:T(8,128)(2,1)S(1)}, bf16[256,256]{1,0:T(8,128)(2,1)S(1)}, u32[]{:S(2)}, u32[]{:S(2)}) collective-permute-start(bf16[256,256]{1,0:T(8,128)(2,1)S(1)} %get-tuple-element.18.refs_0_), channel_id=1, source_target_pairs={{0,2},{2,0},{1,3},{3,1},{4,6},{6,4},{5,7},{7,5},{8,10},{10,8},{9,1... | collective-permute-start | bytes 393224 | tf_op jit(solution)/shard_map/ppermute | solution.py:369
  41.7 4.2 %collective-permute-done.5.refs_1_ = bf16[256,256]{1,0:T(8,128)(2,1)S(1)} collective-permute-done((bf16[256,256]{1,0:T(8,128)(2,1)S(1)}, bf16[256,256]{1,0:T(8,128)(2,1)S(1)}, u32[]{:S(2)}, u32[]{:S(2)}) %collective-permute-start.5) | collective-permute-done | bytes 131104 | tf_op jit(solution)/shard_map/ppermute | solution.py:369
  46.0 0.7 collective-permute-start.7
  46.7 4.8 %collective-permute-start.6 = (bf16[256,256]{1,0:T(8,128)(2,1)S(1)}, bf16[256,256]{1,0:T(8,128)(2,1)S(1)}, u32[]{:S(2)}, u32[]{:S(2)}) collective-permute-start(bf16[256,256]{1,0:T(8,128)(2,1)S(1)} %get-tuple-element.20.block_ref.refs_4_), channel_id=1, source_target_pairs={{0,9},{1,12},{4,13},{9,0},{12,1},{13,4},{2,11},{3,14},{6,15},{11,2... | collective-permute-start | bytes 393224 | tf_op jit(solution)/shard_map/ppermute | solution.py:365
  51.5 1.4 %own.3.refs_3_ = f32[256,256]{1,0:T(8,128)S(1)} custom-call(s32[24]{0:T(128)S(1)} %copy-done.4, bf16[24,256,256]{2,1,0:T(8,128)(2,1)S(1)} %bitcast.14, bf16[24,256,256]{2,1,0:T(8,128)(2,1)S(1)} %bitcast.19, bf16[256,256]{1,0:T(8,128)(2,1)S(1)} %get-tuple-element.20.block_ref.refs_4_), custom_call_target="tpu_custom_call" | custom-call | flops 322122560 | bytes 262144 | tf_op jit(solution)/shard_map/own/pallas_call | solution.py:328
  53.0 6.1 %collective-permute-done.6.refs_5_ = bf16[256,256]{1,0:T(8,128)(2,1)S(1)} collective-permute-done((bf16[256,256]{1,0:T(8,128)(2,1)S(1)}, bf16[256,256]{1,0:T(8,128)(2,1)S(1)}, u32[]{:S(2)}, u32[]{:S(2)}) %collective-permute-start.6) | collective-permute-done | bytes 131104 | tf_op jit(solution)/shard_map/ppermute | solution.py:365
  59.1 1.2 %rest.3.refs_0_ = bf16[256,256]{1,0:T(8,128)(2,1)S(1)} custom-call(s32[24]{0:T(128)S(1)} %copy-done.4, bf16[24,256,256]{2,1,0:T(8,128)(2,1)S(1)} %bitcast.15, bf16[24,256,256]{2,1,0:T(8,128)(2,1)S(1)} %bitcast.20, f32[256,256]{1,0:T(8,128)S(1)} %own.3.refs_3_, bf16[256,256]{1,0:T(8,128)(2,1)S(1)} %get-tuple-element.20.block_ref.refs_4_, ...), custom_call_target="tpu_custom_call" | custom-call | flops 644245120 | bytes 262144 | tf_op jit(solution)/shard_map/rest/pallas_call | solution.py:328
  60.3 1.6 %collective-permute-start.8 = (bf16[256,256]{1,0:T(8,128)(2,1)S(1)}, bf16[256,256]{1,0:T(8,128)(2,1)S(1)}, u32[]{:S(2)}, u32[]{:S(2)}) collective-permute-start(bf16[256,256]{1,0:T(8,128)(2,1)S(1)} %rest.3.refs_0_), channel_id=1, source_target_pairs={{0,2},{2,0},{1,3},{3,1},{4,6},{6,4},{5,7},{7,5},{8,10},{10,8},{9,1... | collective-permute-start | bytes 393224 | tf_op jit(solution)/shard_map/ppermute | solution.py:369
  61.9 3.5 %collective-permute-done.8.refs_1_ = bf16[256,256]{1,0:T(8,128)(2,1)S(1)} collective-permute-done((bf16[256,256]{1,0:T(8,128)(2,1)S(1)}, bf16[256,256]{1,0:T(8,128)(2,1)S(1)}, u32[]{:S(2)}, u32[]{:S(2)}) %collective-permute-start.8) | collective-permute-done | bytes 131104 | tf_op jit(solution)/shard_map/ppermute | solution.py:369
  66.0 9.7 %all_to_all.23 = f32[8,1,128]{2,1,0:T(1,128)S(1)} all-to-all(f32[8,1,128]{2,1,0:T(1,128)S(1)} %bitcast.31), channel_id=1, replica_groups=mesh['groups'=2,'blk'=4,'mpo'=2,'rep'=2] {'blk','rep'}, dimensions={0} | all-to-all | bytes 8192 | tf_op jit(solution)/shard_map/all_to_all | solution.py:374
  75.6 1.4 %final.1 = (bf16[3,1,128,256]{3,2,1,0:T(8,128)(2,1)}, f32[2,3]{1,0:T(2,128)}) custom-call(f32[8,128]{1,0:T(8,128)S(1)} %bitcast.29, f32[256,256]{1,0:T(8,128)S(1)} %get-tuple-element.24.r_ref, f32[256,256]{1,0:T(8,128)S(1)} %get-tuple-element.25.z_ref, f32[256,256]{1,0:T(8,128)S(1)} %get-tuple-element.22.refs_5_.w_ref, ...), custom_call_target="tpu_custom_call" | custom-call | bytes 262144 | tf_op jit(solution)/shard_map/final/pallas_call | solution.py:328
  (15 shorter events, 2.4 us)
Async XLA Ops:
  0.6 14.9 %collective-permute-start.1 = (bf16[256,256]{1,0:T(8,128)(2,1)}, bf16[256,256]{1,0:T(8,128)(2,1)S(1)}, u32[]{:S(2)}, u32[]{:S(2)}) collective-permute-start(bf16[256,256]{1,0:T(8,128)(2,1)} %bitcast.21), channel_id=1, source_target_pairs={{1,8},{4,9},{5,12},{8,1},{9,4},{12,5},{3,10},{6,11},{7,14},{10,3},... | collective-permute-start | bytes 393224 | tf_op jit(solution)/shard_map/ppermute | solution.py:365
  1.3 15.3 %collective-permute-start = (bf16[256,256]{1,0:T(8,128)(2,1)}, bf16[256,256]{1,0:T(8,128)(2,1)S(1)}, u32[]{:S(2)}, u32[]{:S(2)}) collective-permute-start(bf16[256,256]{1,0:T(8,128)(2,1)} %bitcast.22), channel_id=1, source_target_pairs={{0,9},{1,12},{4,13},{9,0},{12,1},{13,4},{2,11},{3,14},{6,15},{11,2... | collective-permute-start | bytes 393224 | tf_op jit(solution)/shard_map/ppermute | solution.py:365
  8.7 1.9 %copy-start = (bf16[24,1,256,256]{3,2,1,0:T(8,128)(2,1)S(1)}, bf16[24,1,256,256]{3,2,1,0:T(8,128)(2,1)}, u32[]{:S(2)}) copy-start(bf16[24,1,256,256]{3,2,1,0:T(8,128)(2,1)} %param.5) | copy-start | bytes 9437188
  10.6 1.9 %copy-start.1 = (bf16[24,1,256,256]{3,2,1,0:T(8,128)(2,1)S(1)}, bf16[24,1,256,256]{3,2,1,0:T(8,128)(2,1)}, u32[]{:S(2)}) copy-start(bf16[24,1,256,256]{3,2,1,0:T(8,128)(2,1)} %param.6) | copy-start | bytes 9437188
  12.5 0.9 %copy-start.2 = (bf16[1,256,256]{2,1,0:T(8,128)(2,1)S(1)}, bf16[1,256,256]{2,1,0:T(8,128)(2,1)}, u32[]{:S(2)}) copy-start(bf16[1,256,256]{2,1,0:T(8,128)(2,1)} %param.4) | copy-start | bytes 393220
  13.4 0.7 copy-start.4
  18.0 5.9 %collective-permute-start.2 = (bf16[256,256]{1,0:T(8,128)(2,1)S(1)}, bf16[256,256]{1,0:T(8,128)(2,1)S(1)}, u32[]{:S(2)}, u32[]{:S(2)}) collective-permute-start(bf16[256,256]{1,0:T(8,128)(2,1)S(1)} %get-tuple-element.14.refs_0_), channel_id=1, source_target_pairs={{0,2},{2,0},{1,3},{3,1},{4,6},{6,4},{5,7},{7,5},{8,10},{10,8},{9,1... | collective-permute-start | bytes 393224 | tf_op jit(solution)/shard_map/ppermute | solution.py:369
  24.2 13.5 %collective-permute-start.4 = (bf16[256,256]{1,0:T(8,128)(2,1)S(1)}, bf16[256,256]{1,0:T(8,128)(2,1)S(1)}, u32[]{:S(2)}, u32[]{:S(2)}) collective-permute-start(bf16[256,256]{1,0:T(8,128)(2,1)S(1)} %get-tuple-element.17.refs_4_.refs_3_), channel_id=1, source_target_pairs={{1,8},{4,9},{5,12},{8,1},{9,4},{12,5},{3,10},{6,11},{7,14},{10,3},... | collective-permute-start | bytes 393224 | tf_op jit(solution)/shard_map/ppermute | solution.py:365
  24.9 12.8 %collective-permute-start.3 = (bf16[256,256]{1,0:T(8,128)(2,1)S(1)}, bf16[256,256]{1,0:T(8,128)(2,1)S(1)}, u32[]{:S(2)}, u32[]{:S(2)}) collective-permute-start(bf16[256,256]{1,0:T(8,128)(2,1)S(1)} %get-tuple-element.17.refs_4_.refs_3_), channel_id=1, source_target_pairs={{0,9},{1,12},{4,13},{9,0},{12,1},{13,4},{2,11},{3,14},{6,15},{11,2... | collective-permute-start | bytes 393224 | tf_op jit(solution)/shard_map/ppermute | solution.py:365
  40.1 5.8 %collective-permute-start.5 = (bf16[256,256]{1,0:T(8,128)(2,1)S(1)}, bf16[256,256]{1,0:T(8,128)(2,1)S(1)}, u32[]{:S(2)}, u32[]{:S(2)}) collective-permute-start(bf16[256,256]{1,0:T(8,128)(2,1)S(1)} %get-tuple-element.18.refs_0_), channel_id=1, source_target_pairs={{0,2},{2,0},{1,3},{3,1},{4,6},{6,4},{5,7},{7,5},{8,10},{10,8},{9,1... | collective-permute-start | bytes 393224 | tf_op jit(solution)/shard_map/ppermute | solution.py:369
  46.0 6.9 %collective-permute-start.7 = (bf16[256,256]{1,0:T(8,128)(2,1)S(1)}, bf16[256,256]{1,0:T(8,128)(2,1)S(1)}, u32[]{:S(2)}, u32[]{:S(2)}) collective-permute-start(bf16[256,256]{1,0:T(8,128)(2,1)S(1)} %get-tuple-element.20.block_ref.refs_4_), channel_id=1, source_target_pairs={{1,8},{4,9},{5,12},{8,1},{9,4},{12,5},{3,10},{6,11},{7,14},{10,3},... | collective-permute-start | bytes 393224 | tf_op jit(solution)/shard_map/ppermute | solution.py:365
  46.7 12.4 %collective-permute-start.6 = (bf16[256,256]{1,0:T(8,128)(2,1)S(1)}, bf16[256,256]{1,0:T(8,128)(2,1)S(1)}, u32[]{:S(2)}, u32[]{:S(2)}) collective-permute-start(bf16[256,256]{1,0:T(8,128)(2,1)S(1)} %get-tuple-element.20.block_ref.refs_4_), channel_id=1, source_target_pairs={{0,9},{1,12},{4,13},{9,0},{12,1},{13,4},{2,11},{3,14},{6,15},{11,2... | collective-permute-start | bytes 393224 | tf_op jit(solution)/shard_map/ppermute | solution.py:365
  52.9 12.4 %copy-start.3 = (bf16[1,256,256]{2,1,0:T(8,128)(2,1)S(1)}, bf16[1,256,256]{2,1,0:T(8,128)(2,1)}, u32[]{:S(2)}) copy-start(bf16[1,256,256]{2,1,0:T(8,128)(2,1)} %param.4) | copy-start | bytes 393220
  60.3 5.0 %collective-permute-start.8 = (bf16[256,256]{1,0:T(8,128)(2,1)S(1)}, bf16[256,256]{1,0:T(8,128)(2,1)S(1)}, u32[]{:S(2)}, u32[]{:S(2)}) collective-permute-start(bf16[256,256]{1,0:T(8,128)(2,1)S(1)} %rest.3.refs_0_), channel_id=1, source_target_pairs={{0,2},{2,0},{1,3},{3,1},{4,6},{6,4},{5,7},{7,5},{8,10},{10,8},{9,1... | collective-permute-start | bytes 393224 | tf_op jit(solution)/shard_map/ppermute | solution.py:369

commit v4 on v3

--- a/solution.py
+++ b/solution.py
@@ -98,20 +98,19 @@
         reach = reaches(c, sector, blocks).astype(jnp.int32)
         reached.append(reach if which != "own" else jnp.int32(0))
 
-    def list_channel(b, count):
+    count = jnp.int32(0)
+    for b in range(kinds_ref.shape[0]):
         kind = kinds_ref[b]
         live, slot = reached[0], jnp.int32(0)
         for c in range(1, 5):
             live = jnp.where(kind == c, reached[c], live)
             slot = jnp.where(kind == c, 1 + place[c], slot)
-        order[count] = b
+        order[count] = jnp.int32(b)
         slot_of[count] = slot
-        return count + live
-
-    count = lax.fori_loop(0, kinds_ref.shape[0], list_channel, jnp.int32(0))
+        count += live
     for extra in range(WIDE):
-        order[count + extra] = 0
-        slot_of[count + extra] = idle
+        order[count + extra] = jnp.int32(0)
+        slot_of[count + extra] = jnp.int32(idle)
     return count
 
 
@@ -135,10 +134,10 @@
         multiply(group * WIDE, WIDE)
         return carry
 
-    groups = count // WIDE
+    groups = (count + WIDE // 2 - 1) // WIDE
     lax.fori_loop(0, groups, full, 0)
     rest = count - groups * WIDE
-    for low, wide in ((0, 2), (2, 4), (4, WIDE)):
+    for low, wide in ((0, 2), (2, 4)):
 
         @pl.when((rest > low) & (rest <= wide))
         def _():

time: 77.3 us -> 76.4 us (0.988)
  waiting for transfers between devices: 19.6 us -> 18.3 us
  Pallas kernels: 10.4 us -> 11.6 us
  blocking collectives: 18.6 us -> 17.8 us
    pallas_call x9, Pallas kernels: 10.4 us -> 11.6 us  [call(): pl.pallas_call(kernel, out_shape=outs, in_specs=[first] + [VMEM] * (len(a...]
    all_to_all x2, blocking collectives: 18.6 us -> 17.8 us  [exchange(): return lax.all_to_all(rows, ring, 0, 0, tiled=True)]
    ppermute x6, waiting for transfers between devices: 7.22 us -> 6.44 us  [spread(): return [block] + [lax.ppermute(block, ring, pairs) for pairs in permutes]]
where the time goes in v4:
time: 76.4 us; the launch traced here: 76.2 us
  starting transfers between devices  22.3 us (29%)
  waiting for transfers between devices  18.3 us (24%)
  blocking collectives  17.8 us (23%)
  Pallas kernels  11.6 us (15%)
  local copies, waits for them, and re-layouts  5.34 us (7%)
  between operations  0.77 us (1%)
    all_to_all x2, blocking collectives, exchange(): return lax.all_to_all(rows, ring, 0, 0, tiled=True)  17.8 us
    ppermute x6, starting transfers between devices, spread(): return [block] + [lax.ppermute(block, ring, pairs) for pairs in permutes]  17.6 us
    ppermute x3, waiting for transfers between devices, gather_parts(): return [t, lax.ppermute(t, 'mpo', [(0, 1), (1, 0)])]  11.9 us
    pallas_call x9, Pallas kernels, call(): pl.pallas_call(kernel, out_shape=outs, in_specs=[first] + [VMEM] * (len(a...  11.6 us
    ppermute x6, waiting for transfers between devices, spread(): return [block] + [lax.ppermute(block, ring, pairs) for pairs in permutes]  6.44 us
    unnamed x10, local copies, waits for them, and re-layouts  5.34 us
    ppermute x3, starting transfers between devices, gather_parts(): return [t, lax.ppermute(t, 'mpo', [(0, 1), (1, 0)])]  4.64 us
  transfers between devices with their start and end apart: 9, of which 5 were waited for; matrix products, arithmetic and copies ran while one was open for 0% of the time, Pallas kernels for 4%

profile of v4, /device:TPU:0, one launch (start us, length us, event | category | flops | bytes accessed | tf_op | source)
XLA Modules:
  0.0 76.2 jit_solution(4750722090686987653)
XLA Ops:
  0.6 0.7 collective-permute-start.1
  1.3 7.4 %collective-permute-start = (bf16[256,256]{1,0:T(8,128)(2,1)}, bf16[256,256]{1,0:T(8,128)(2,1)S(1)}, u32[]{:S(2)}, u32[]{:S(2)}) collective-permute-start(bf16[256,256]{1,0:T(8,128)(2,1)} %bitcast.22), channel_id=1, source_target_pairs={{0,9},{1,12},{4,13},{9,0},{12,1},{13,4},{2,11},{3,14},{6,15},{11,2... | collective-permute-start | bytes 393224 | tf_op jit(solution)/shard_map/ppermute | solution.py:364
  8.7 1.9 %copy-done = bf16[24,1,256,256]{3,2,1,0:T(8,128)(2,1)S(1)} copy-done((bf16[24,1,256,256]{3,2,1,0:T(8,128)(2,1)S(1)}, bf16[24,1,256,256]{3,2,1,0:T(8,128)(2,1)}, u32[]{:S(2)}) %copy-start) | copy-done | bytes 3145752
  10.6 1.9 %copy-done.1 = bf16[24,1,256,256]{3,2,1,0:T(8,128)(2,1)S(1)} copy-done((bf16[24,1,256,256]{3,2,1,0:T(8,128)(2,1)S(1)}, bf16[24,1,256,256]{3,2,1,0:T(8,128)(2,1)}, u32[]{:S(2)}) %copy-start.1) | copy-done | bytes 3145752
  12.5 0.9 %copy-done.2 = bf16[1,256,256]{2,1,0:T(8,128)(2,1)S(1)} copy-done((bf16[1,256,256]{2,1,0:T(8,128)(2,1)S(1)}, bf16[1,256,256]{2,1,0:T(8,128)(2,1)}, u32[]{:S(2)}) %copy-start.2) | copy-done | bytes 131096
  14.0 1.5 %own.2.refs_3_ = f32[256,256]{1,0:T(8,128)S(1)} custom-call(s32[24]{0:T(128)S(1)} %copy-done.4, bf16[24,256,256]{2,1,0:T(8,128)(2,1)S(1)} %bitcast.11, bf16[24,256,256]{2,1,0:T(8,128)(2,1)S(1)} %bitcast.16, bf16[256,256]{1,0:T(8,128)(2,1)S(1)} %bitcast.23), custom_call_target="tpu_custom_call" | custom-call | flops 322122560 | bytes 262144 | tf_op jit(solution)/shard_map/own/pallas_call | solution.py:327
  15.6 1.0 %collective-permute-done.refs_5_.refs_8_ = bf16[256,256]{1,0:T(8,128)(2,1)S(1)} collective-permute-done((bf16[256,256]{1,0:T(8,128)(2,1)}, bf16[256,256]{1,0:T(8,128)(2,1)S(1)}, u32[]{:S(2)}, u32[]{:S(2)}) %collective-permute-start) | collective-permute-done | bytes 131104 | tf_op jit(solution)/shard_map/ppermute | solution.py:364
  16.6 1.6 %rest.2 = (bf16[256,256]{1,0:T(8,128)(2,1)S(1)}, f32[8,128]{1,0:T(8,128)S(1)}) custom-call(s32[24]{0:T(128)S(1)} %copy-done.4, bf16[24,256,256]{2,1,0:T(8,128)(2,1)S(1)} %bitcast.12, bf16[24,256,256]{2,1,0:T(8,128)(2,1)S(1)} %bitcast.17, f32[256,256]{1,0:T(8,128)S(1)} %own.2.refs_3_, bf16[256,256]{1,0:T(8,128)(2,1)S(1)} %bitcast.24, ...), custom_call_target="tpu_custom_call" | custom-call | flops 644245120 | bytes 262144 | tf_op jit(solution)/shard_map/rest/pallas_call | solution.py:327
  18.2 1.6 %collective-permute-start.2 = (bf16[256,256]{1,0:T(8,128)(2,1)S(1)}, bf16[256,256]{1,0:T(8,128)(2,1)S(1)}, u32[]{:S(2)}, u32[]{:S(2)}) collective-permute-start(bf16[256,256]{1,0:T(8,128)(2,1)S(1)} %get-tuple-element.14.refs_0_), channel_id=1, source_target_pairs={{0,2},{2,0},{1,3},{3,1},{4,6},{6,4},{5,7},{7,5},{8,10},{10,8},{9,1... | collective-permute-start | bytes 393224 | tf_op jit(solution)/shard_map/ppermute | solution.py:368
  19.8 4.4 %collective-permute-done.2.refs_1_ = bf16[256,256]{1,0:T(8,128)(2,1)S(1)} collective-permute-done((bf16[256,256]{1,0:T(8,128)(2,1)S(1)}, bf16[256,256]{1,0:T(8,128)(2,1)S(1)}, u32[]{:S(2)}, u32[]{:S(2)}) %collective-permute-start.2) | collective-permute-done | bytes 131104 | tf_op jit(solution)/shard_map/ppermute | solution.py:368
  25.2 3.7 %collective-permute-start.3 = (bf16[256,256]{1,0:T(8,128)(2,1)S(1)}, bf16[256,256]{1,0:T(8,128)(2,1)S(1)}, u32[]{:S(2)}, u32[]{:S(2)}) collective-permute-start(bf16[256,256]{1,0:T(8,128)(2,1)S(1)} %get-tuple-element.17.refs_4_.refs_3_), channel_id=1, source_target_pairs={{0,9},{1,12},{4,13},{9,0},{12,1},{13,4},{2,11},{3,14},{6,15},{11,2... | collective-permute-start | bytes 393224 | tf_op jit(solution)/shard_map/ppermute | solution.py:364
  28.9 9.2 %all_to_all.22 = f32[8,1,128]{2,1,0:T(1,128)S(1)} all-to-all(f32[8,1,128]{2,1,0:T(1,128)S(1)} %bitcast.30), channel_id=1, replica_groups=mesh['groups'=2,'blk'=4,'mpo'=2,'rep'=2] {'blk','rep'}, dimensions={0} | all-to-all | bytes 8192 | tf_op jit(solution)/shard_map/all_to_all | solution.py:373
  38.1 2.9 %second.1 = (bf16[256,256]{1,0:T(8,128)(2,1)S(1)}, bf16[256,256]{1,0:T(8,128)(2,1)S(1)}, f32[8,128]{1,0:T(8,128)S(1)}) custom-call(s32[24]{0:T(128)S(1)} %copy-done.4, bf16[24,256,256]{2,1,0:T(8,128)(2,1)S(1)} %bitcast.13, bf16[24,256,256]{2,1,0:T(8,128)(2,1)S(1)} %bitcast.18, f32[8,128]{1,0:T(8,128)S(1)} %bitcast.28, ...), custom_call_target="tpu_custom_call" | custom-call | flops 966367616 | bytes 262144 | tf_op jit(solution)/shard_map/second/pallas_call | solution.py:327
  41.1 1.3 %collective-permute-start.5 = (bf16[256,256]{1,0:T(8,128)(2,1)S(1)}, bf16[256,256]{1,0:T(8,128)(2,1)S(1)}, u32[]{:S(2)}, u32[]{:S(2)}) collective-permute-start(bf16[256,256]{1,0:T(8,128)(2,1)S(1)} %get-tuple-element.18.refs_0_), channel_id=1, source_target_pairs={{0,2},{2,0},{1,3},{3,1},{4,6},{6,4},{5,7},{7,5},{8,10},{10,8},{9,1... | collective-permute-start | bytes 393224 | tf_op jit(solution)/shard_map/ppermute | solution.py:368
  42.3 4.1 %collective-permute-done.5.refs_1_ = bf16[256,256]{1,0:T(8,128)(2,1)S(1)} collective-permute-done((bf16[256,256]{1,0:T(8,128)(2,1)S(1)}, bf16[256,256]{1,0:T(8,128)(2,1)S(1)}, u32[]{:S(2)}, u32[]{:S(2)}) %collective-permute-start.5) | collective-permute-done | bytes 131104 | tf_op jit(solution)/shard_map/ppermute | solution.py:368
  46.6 0.7 collective-permute-start.7
  47.3 4.6 %collective-permute-start.6 = (bf16[256,256]{1,0:T(8,128)(2,1)S(1)}, bf16[256,256]{1,0:T(8,128)(2,1)S(1)}, u32[]{:S(2)}, u32[]{:S(2)}) collective-permute-start(bf16[256,256]{1,0:T(8,128)(2,1)S(1)} %get-tuple-element.20.block_ref.refs_4_), channel_id=1, source_target_pairs={{0,9},{1,12},{4,13},{9,0},{12,1},{13,4},{2,11},{3,14},{6,15},{11,2... | collective-permute-start | bytes 393224 | tf_op jit(solution)/shard_map/ppermute | solution.py:364
  51.8 1.5 %own.3.refs_3_ = f32[256,256]{1,0:T(8,128)S(1)} custom-call(s32[24]{0:T(128)S(1)} %copy-done.4, bf16[24,256,256]{2,1,0:T(8,128)(2,1)S(1)} %bitcast.14, bf16[24,256,256]{2,1,0:T(8,128)(2,1)S(1)} %bitcast.19, bf16[256,256]{1,0:T(8,128)(2,1)S(1)} %get-tuple-element.20.block_ref.refs_4_), custom_call_target="tpu_custom_call" | custom-call | flops 322122560 | bytes 262144 | tf_op jit(solution)/shard_map/own/pallas_call | solution.py:327
  53.4 5.4 %collective-permute-done.6.refs_5_ = bf16[256,256]{1,0:T(8,128)(2,1)S(1)} collective-permute-done((bf16[256,256]{1,0:T(8,128)(2,1)S(1)}, bf16[256,256]{1,0:T(8,128)(2,1)S(1)}, u32[]{:S(2)}, u32[]{:S(2)}) %collective-permute-start.6) | collective-permute-done | bytes 131104 | tf_op jit(solution)/shard_map/ppermute | solution.py:364
  58.8 1.6 %rest.3.refs_0_ = bf16[256,256]{1,0:T(8,128)(2,1)S(1)} custom-call(s32[24]{0:T(128)S(1)} %copy-done.4, bf16[24,256,256]{2,1,0:T(8,128)(2,1)S(1)} %bitcast.15, bf16[24,256,256]{2,1,0:T(8,128)(2,1)S(1)} %bitcast.20, f32[256,256]{1,0:T(8,128)S(1)} %own.3.refs_3_, bf16[256,256]{1,0:T(8,128)(2,1)S(1)} %get-tuple-element.20.block_ref.refs_4_, ...), custom_call_target="tpu_custom_call" | custom-call | flops 644245120 | bytes 262144 | tf_op jit(solution)/shard_map/rest/pallas_call | solution.py:327
  60.4 1.8 %collective-permute-start.8 = (bf16[256,256]{1,0:T(8,128)(2,1)S(1)}, bf16[256,256]{1,0:T(8,128)(2,1)S(1)}, u32[]{:S(2)}, u32[]{:S(2)}) collective-permute-start(bf16[256,256]{1,0:T(8,128)(2,1)S(1)} %rest.3.refs_0_), channel_id=1, source_target_pairs={{0,2},{2,0},{1,3},{3,1},{4,6},{6,4},{5,7},{7,5},{8,10},{10,8},{9,1... | collective-permute-start | bytes 393224 | tf_op jit(solution)/shard_map/ppermute | solution.py:368
  62.2 3.4 %collective-permute-done.8.refs_1_ = bf16[256,256]{1,0:T(8,128)(2,1)S(1)} collective-permute-done((bf16[256,256]{1,0:T(8,128)(2,1)S(1)}, bf16[256,256]{1,0:T(8,128)(2,1)S(1)}, u32[]{:S(2)}, u32[]{:S(2)}) %collective-permute-start.8) | collective-permute-done | bytes 131104 | tf_op jit(solution)/shard_map/ppermute | solution.py:368
  66.1 8.6 %all_to_all.23 = f32[8,1,128]{2,1,0:T(1,128)S(1)} all-to-all(f32[8,1,128]{2,1,0:T(1,128)S(1)} %bitcast.31), channel_id=1, replica_groups=mesh['groups'=2,'blk'=4,'mpo'=2,'rep'=2] {'blk','rep'}, dimensions={0} | all-to-all | bytes 8192 | tf_op jit(solution)/shard_map/all_to_all | solution.py:373
  74.8 1.4 %final.1 = (bf16[3,1,128,256]{3,2,1,0:T(8,128)(2,1)}, f32[2,3]{1,0:T(2,128)}) custom-call(f32[8,128]{1,0:T(8,128)S(1)} %bitcast.29, f32[256,256]{1,0:T(8,128)S(1)} %get-tuple-element.24.r_ref, f32[256,256]{1,0:T(8,128)S(1)} %get-tuple-element.25.z_ref, f32[256,256]{1,0:T(8,128)S(1)} %get-tuple-element.22.refs_5_.w_ref, ...), custom_call_target="tpu_custom_call" | custom-call | bytes 262144 | tf_op jit(solution)/shard_map/final/pallas_call | solution.py:327
  (15 shorter events, 2.4 us)
Async XLA Ops:
  0.6 14.9 %collective-permute-start.1 = (bf16[256,256]{1,0:T(8,128)(2,1)}, bf16[256,256]{1,0:T(8,128)(2,1)S(1)}, u32[]{:S(2)}, u32[]{:S(2)}) collective-permute-start(bf16[256,256]{1,0:T(8,128)(2,1)} %bitcast.21), channel_id=1, source_target_pairs={{1,8},{4,9},{5,12},{8,1},{9,4},{12,5},{3,10},{6,11},{7,14},{10,3},... | collective-permute-start | bytes 393224 | tf_op jit(solution)/shard_map/ppermute | solution.py:364
  1.3 15.3 %collective-permute-start = (bf16[256,256]{1,0:T(8,128)(2,1)}, bf16[256,256]{1,0:T(8,128)(2,1)S(1)}, u32[]{:S(2)}, u32[]{:S(2)}) collective-permute-start(bf16[256,256]{1,0:T(8,128)(2,1)} %bitcast.22), channel_id=1, source_target_pairs={{0,9},{1,12},{4,13},{9,0},{12,1},{13,4},{2,11},{3,14},{6,15},{11,2... | collective-permute-start | bytes 393224 | tf_op jit(solution)/shard_map/ppermute | solution.py:364
  8.7 1.9 %copy-start = (bf16[24,1,256,256]{3,2,1,0:T(8,128)(2,1)S(1)}, bf16[24,1,256,256]{3,2,1,0:T(8,128)(2,1)}, u32[]{:S(2)}) copy-start(bf16[24,1,256,256]{3,2,1,0:T(8,128)(2,1)} %param.5) | copy-start | bytes 9437188
  10.6 1.9 %copy-start.1 = (bf16[24,1,256,256]{3,2,1,0:T(8,128)(2,1)S(1)}, bf16[24,1,256,256]{3,2,1,0:T(8,128)(2,1)}, u32[]{:S(2)}) copy-start(bf16[24,1,256,256]{3,2,1,0:T(8,128)(2,1)} %param.6) | copy-start | bytes 9437188
  12.5 0.9 %copy-start.2 = (bf16[1,256,256]{2,1,0:T(8,128)(2,1)S(1)}, bf16[1,256,256]{2,1,0:T(8,128)(2,1)}, u32[]{:S(2)}) copy-start(bf16[1,256,256]{2,1,0:T(8,128)(2,1)} %param.4) | copy-start | bytes 393220
  13.4 0.7 copy-start.4
  18.2 5.9 %collective-permute-start.2 = (bf16[256,256]{1,0:T(8,128)(2,1)S(1)}, bf16[256,256]{1,0:T(8,128)(2,1)S(1)}, u32[]{:S(2)}, u32[]{:S(2)}) collective-permute-start(bf16[256,256]{1,0:T(8,128)(2,1)S(1)} %get-tuple-element.14.refs_0_), channel_id=1, source_target_pairs={{0,2},{2,0},{1,3},{3,1},{4,6},{6,4},{5,7},{7,5},{8,10},{10,8},{9,1... | collective-permute-start | bytes 393224 | tf_op jit(solution)/shard_map/ppermute | solution.py:368
  24.5 13.6 %collective-permute-start.4 = (bf16[256,256]{1,0:T(8,128)(2,1)S(1)}, bf16[256,256]{1,0:T(8,128)(2,1)S(1)}, u32[]{:S(2)}, u32[]{:S(2)}) collective-permute-start(bf16[256,256]{1,0:T(8,128)(2,1)S(1)} %get-tuple-element.17.refs_4_.refs_3_), channel_id=1, source_target_pairs={{1,8},{4,9},{5,12},{8,1},{9,4},{12,5},{3,10},{6,11},{7,14},{10,3},... | collective-permute-start | bytes 393224 | tf_op jit(solution)/shard_map/ppermute | solution.py:364
  25.2 12.9 %collective-permute-start.3 = (bf16[256,256]{1,0:T(8,128)(2,1)S(1)}, bf16[256,256]{1,0:T(8,128)(2,1)S(1)}, u32[]{:S(2)}, u32[]{:S(2)}) collective-permute-start(bf16[256,256]{1,0:T(8,128)(2,1)S(1)} %get-tuple-element.17.refs_4_.refs_3_), channel_id=1, source_target_pairs={{0,9},{1,12},{4,13},{9,0},{12,1},{13,4},{2,11},{3,14},{6,15},{11,2... | collective-permute-start | bytes 393224 | tf_op jit(solution)/shard_map/ppermute | solution.py:364
  41.1 5.4 %collective-permute-start.5 = (bf16[256,256]{1,0:T(8,128)(2,1)S(1)}, bf16[256,256]{1,0:T(8,128)(2,1)S(1)}, u32[]{:S(2)}, u32[]{:S(2)}) collective-permute-start(bf16[256,256]{1,0:T(8,128)(2,1)S(1)} %get-tuple-element.18.refs_0_), channel_id=1, source_target_pairs={{0,2},{2,0},{1,3},{3,1},{4,6},{6,4},{5,7},{7,5},{8,10},{10,8},{9,1... | collective-permute-start | bytes 393224 | tf_op jit(solution)/shard_map/ppermute | solution.py:368
  46.6 6.8 %collective-permute-start.7 = (bf16[256,256]{1,0:T(8,128)(2,1)S(1)}, bf16[256,256]{1,0:T(8,128)(2,1)S(1)}, u32[]{:S(2)}, u32[]{:S(2)}) collective-permute-start(bf16[256,256]{1,0:T(8,128)(2,1)S(1)} %get-tuple-element.20.block_ref.refs_4_), channel_id=1, source_target_pairs={{1,8},{4,9},{5,12},{8,1},{9,4},{12,5},{3,10},{6,11},{7,14},{10,3},... | collective-permute-start | bytes 393224 | tf_op jit(solution)/shard_map/ppermute | solution.py:364
  47.3 11.5 %collective-permute-start.6 = (bf16[256,256]{1,0:T(8,128)(2,1)S(1)}, bf16[256,256]{1,0:T(8,128)(2,1)S(1)}, u32[]{:S(2)}, u32[]{:S(2)}) collective-permute-start(bf16[256,256]{1,0:T(8,128)(2,1)S(1)} %get-tuple-element.20.block_ref.refs_4_), channel_id=1, source_target_pairs={{0,9},{1,12},{4,13},{9,0},{12,1},{13,4},{2,11},{3,14},{6,15},{11,2... | collective-permute-start | bytes 393224 | tf_op jit(solution)/shard_map/ppermute | solution.py:364
  53.4 12.2 %copy-start.3 = (bf16[1,256,256]{2,1,0:T(8,128)(2,1)S(1)}, bf16[1,256,256]{2,1,0:T(8,128)(2,1)}, u32[]{:S(2)}) copy-start(bf16[1,256,256]{2,1,0:T(8,128)(2,1)} %param.4) | copy-start | bytes 393220
  60.4 5.2 %collective-permute-start.8 = (bf16[256,256]{1,0:T(8,128)(2,1)S(1)}, bf16[256,256]{1,0:T(8,128)(2,1)S(1)}, u32[]{:S(2)}, u32[]{:S(2)}) collective-permute-start(bf16[256,256]{1,0:T(8,128)(2,1)S(1)} %rest.3.refs_0_), channel_id=1, source_target_pairs={{0,2},{2,0},{1,3},{3,1},{4,6},{6,4},{5,7},{7,5},{8,10},{10,8},{9,1... | collective-permute-start | bytes 393224 | tf_op jit(solution)/shard_map/ppermute | solution.py:368

commit v5 on v4

--- a/solution.py
+++ b/solution.py
@@ -30,21 +30,58 @@
 
 
 def routes(blocks):
-    lists = {}
-    for kind in range(1, 5):
-        lists[kind] = [
-            (k - OFFSETS[kind], k) for k in range(blocks) if bool(reaches(kind, k, blocks))
-        ]
-    permutes, place = [], {}
-    for up, down in ((1, 3), (2, 4)):
-        both = lists[up] + lists[down]
-        disjoint = len({a for a, _ in both}) == len(both) == len({b for _, b in both})
-        groups = ((up, down),) if disjoint else ((up,), (down,))
-        for group in groups:
-            for kind in group:
-                place[kind] = len(permutes)
-            permutes.append([pair for kind in group for pair in lists[kind]])
-    return permutes, place
+    degree, edges = [0] * blocks, []
+    for kind in (1, 2):
+        for k in range(blocks):
+            if reaches(kind, k, blocks):
+                edges.append((k - OFFSETS[kind], k))
+                degree[k - OFFSETS[kind]] += 1
+                degree[k] += 1
+    edges.sort(key=lambda edge: degree[edge[0]] + degree[edge[1]])
+    partner = [{} for _ in range(blocks)]
+
+    def lowest(block):
+        return next(c for c in range(len(edges)) if c not in partner[block])
+
+    for a, b in edges:
+        here_free, there_free = lowest(a), lowest(b)
+        if here_free in partner[b]:
+            path, block, colour = [b], b, here_free
+            while colour in partner[block]:
+                block = partner[block][colour]
+                path.append(block)
+                colour = there_free if colour == here_free else here_free
+            for block in path:
+                moved = {}
+                for old, new in ((here_free, there_free), (there_free, here_free)):
+                    if old in partner[block]:
+                        moved[new] = partner[block].pop(old)
+                partner[block].update(moved)
+        partner[a][here_free], partner[b][here_free] = b, a
+    colours = sorted({c for held in partner for c in held})
+    permutes = [[(held[c], k) for k, held in enumerate(partner) if c in held] for c in colours]
+    return sorted(permutes, key=len, reverse=True)
+
+
+def slot_tables(permutes, blocks):
+    origins = [{k: k for k in range(blocks)}] + [{k: s for s, k in pairs} for pairs in permutes]
+    places = []
+    for kind in range(5):
+        place = {}
+        for slot, origin in enumerate(origins):
+            for k, source in origin.items():
+                if source == k - OFFSETS[kind] and reaches(kind, k, blocks):
+                    place[k] = slot
+        places.append(place)
+    return places, origins
+
+
+def look_up(table, sector, default):
+    out = jnp.int32(default)
+    for k, value in table.items():
+        if value != default:
+            out = jnp.where(sector == k, jnp.int32(value), out)
+    return out
 
 
 def here():
@@ -90,24 +127,19 @@
     return ref[0:1, :]
 
 
-def list_channels(which, place, blocks, kinds_ref, order, slot_of, idle):
+def list_channels(which, places, kinds_ref, order, slot_of, idle):
     sector = here()
-    use_own = 0 if which == "rest" else 1
-    reached = [jnp.int32(use_own)]
-    for c in range(1, 5):
-        reach = reaches(c, sector, blocks).astype(jnp.int32)
-        reached.append(reach if which != "own" else jnp.int32(0))
-
+    slots = [jnp.int32(-1 if which == "rest" else 0)]
+    slots += [look_up(places[c], sector, -1) if which != "own" else jnp.int32(-1) for c in range(1, 5)]
     count = jnp.int32(0)
     for b in range(kinds_ref.shape[0]):
         kind = kinds_ref[b]
-        live, slot = reached[0], jnp.int32(0)
+        slot = slots[0]
         for c in range(1, 5):
-            live = jnp.where(kind == c, reached[c], live)
-            slot = jnp.where(kind == c, 1 + place[c], slot)
+            slot = jnp.where(kind == c, slots[c], slot)
         order[count] = jnp.int32(b)
         slot_of[count] = slot
-        count += live
+        count += jnp.where(slot >= 0, 1, 0)
     for extra in range(WIDE):
         order[count + extra] = jnp.int32(0)
         slot_of[count + extra] = jnp.int32(idle)
@@ -144,8 +176,8 @@
             multiply(groups * WIDE, wide)
 
 
-def own_kernel(scaled, place, blocks, kinds_ref, left_ref, right_ref, block_ref, acc, source, order, slot_of):
-    count = list_channels("own", place, blocks, kinds_ref, order, slot_of, 1)
+def own_kernel(scaled, places, kinds_ref, left_ref, right_ref, block_ref, acc, source, order, slot_of):
+    count = list_channels("own", places, kinds_ref, order, slot_of, 1)
     if scaled:
         block = wide_float(block_ref)
         inverse = 1.0 / jnp.maximum(peak(block), SMALLEST)
@@ -157,36 +189,47 @@
     multiply_listed(count, left_ref, right_ref, source, acc, order, slot_of)
 
 
-def rest_kernel(scaled, slots, place, blocks, *refs):
+def scaled_rest_kernel(slots, places, *refs):
     kinds_ref, left_ref, right_ref, own_ref = refs[:4]
-    held, refs = refs[4 : 4 + slots], refs[4 + slots :]
-    if scaled:
-        t_ref, unit_ref, acc, source, order, slot_of = refs
-    else:
-        t_ref, acc, source, order, slot_of = refs
-    count = list_channels("rest", place, blocks, kinds_ref, order, slot_of, slots)
-    if scaled:
-        peaks = [jnp.maximum(peak(wide_float(block)), SMALLEST) for block in held]
-        unit = functools.reduce(jnp.maximum, peaks)
-        unit_ref[...] = jnp.broadcast_to(unit, unit_ref.shape)
-        inverse = 1.0 / unit
-        for slot in range(1, slots):
-            source[slot] = (wide_float(held[slot]) * inverse).astype(jnp.bfloat16)
-        acc[...] = own_ref[...] * (peaks[0] * inverse)
-    else:
-        for slot in range(1, slots):
-            source[slot] = held[slot][...]
-        acc[...] = own_ref[...]
+    held, (t_ref, unit_ref, acc, source, order, slot_of) = refs[4 : 4 + slots], refs[4 + slots :]
+    count = list_channels("rest", places, kinds_ref, order, slot_of, slots)
+    peaks = [jnp.maximum(peak(wide_float(block)), SMALLEST) for block in held]
+    unit = functools.reduce(jnp.maximum, peaks)
+    unit_ref[...] = jnp.broadcast_to(unit, unit_ref.shape)
+    inverse = 1.0 / unit
+    for slot in range(1, slots):
+        source[slot] = (wide_float(held[slot]) * inverse).astype(jnp.bfloat16)
+    acc[...] = own_ref[...] * (peaks[0] * inverse)
     source[slots] = jnp.zeros(source.shape[1:], jnp.bfloat16)
     multiply_listed(count, left_ref, right_ref, source, acc, order, slot_of)
     t_ref[...] = acc[...].astype(jnp.bfloat16)
 
 
-def second_kernel(slots, place, blocks, entries, *refs):
+def rest_kernel(slots, places, *refs):
+    kinds_ref, left_ref, right_ref, own_ref = refs[:4]
+    t_ref, acc, source, order, slot_of = refs[-5:]
+    shares, held = refs[4 : -5 - (slots - 2)], refs[-5 - (slots - 2) : -5]
+    count = list_channels("rest", places, kinds_ref, order, slot_of, slots)
+    share = source.shape[1] // lax.axis_size("mpo")
+    for step, block in enumerate(shares):
+        if len(shares) == 1:
+            source[1] = block[...]
+        else:
+            at = lax.axis_index("mpo") if step == 0 else 1 - lax.axis_index("mpo")
+            source[1, pl.ds(pl.multiple_of(at * share, share), share), :] = block[...]
+    for slot in range(2, slots):
+        source[slot] = held[slot - 2][...]
+    acc[...] = own_ref[...]
+    source[slots] = jnp.zeros(source.shape[1:], jnp.bfloat16)
+    multiply_listed(count, left_ref, right_ref, source, acc, order, slot_of)
+    t_ref[...] = acc[...].astype(jnp.bfloat16)
+
+
+def second_kernel(slots, places, origins, entries, *refs):
     kinds_ref, left_ref, right_ref, rows_ref = refs[:4]
     products, psis = refs[4 : 4 + slots], refs[4 + slots : 4 + 2 * slots]
     t_ref, v_ref, scal_ref, acc, source, order, slot_of = refs[4 + 2 * slots :]
-    count = list_channels("all", place, blocks, kinds_ref, order, slot_of, slots)
+    count = list_channels("all", places, kinds_ref, order, slot_of, slots)
     rows = rows_ref[...]
     a, d, local, p, q, unit = (lane_of(rows, lane) for lane in range(6))
     beta_0 = jnp.sqrt(column_sum(unit * unit * d) / entries + EPSILON)
@@ -200,10 +243,7 @@
     sector = here()
     row_of = lax.broadcasted_iota(jnp.int32, gain.shape, 0)
     for slot in range(slots):
-        origin = sector
-        for kind in range(1, 5):
-            if 1 + place[kind] == slot:
-                origin = jnp.where(reaches(kind, sector, blocks), sector - OFFSETS[kind], origin)
+        origin = sector if slot == 0 else look_up(origins[slot], sector, 0)
         gain_here = column_sum(jnp.where(row_of == origin, gain, 0.0))
         r = gain_here * wide_float(products[slot]) - (alpha * start_inverse) * wide_float(psis[slot])
         source[slot] = (r * inverse).astype(jnp.bfloat16)
@@ -234,10 +274,13 @@
 
 
 def second_sums_kernel(*refs):
-    parts, (scal_ref, wide_ref, w_ref) = refs[:-3], refs[-3:]
+    parts, (scal_ref, wide_ref, w_ref, share_ref) = refs[:-4], refs[-4:]
     w = sum_parts(parts) * shrink(first_row(scal_ref))
     wide_ref[...] = w
     w_ref[...] = w.astype(jnp.bfloat16)
+    share = share_ref.shape[0]
+    mine = pl.ds(pl.multiple_of(lax.axis_index("mpo") * share, share), share)
+    share_ref[...] = wide_ref[mine, :].astype(jnp.bfloat16)
 
 
 def third_sums_kernel(*refs):
@@ -309,7 +352,8 @@
     parts = lax.axis_size("mpo")
     blocks = lax.axis_size("blk") * lax.axis_size("rep")
     entries = blocks * width * width
-    permutes, place = routes(blocks)
+    permutes = routes(blocks)
+    places, origins = slot_tables(permutes, blocks)
     slots = 1 + len(permutes)
     channels = channel_class.shape[0]
     psi, left, right = wavefunction[0], env_left[:, 0], env_right[:, 0]
@@ -340,7 +384,7 @@
 
     def own(scaled, block):
         return call(
-            functools.partial(own_kernel, scaled, place, blocks),
+            functools.partial(own_kernel, scaled, places),
             "own",
             wide,
             (channel_class, left, right, block),
@@ -349,9 +393,9 @@
             16,
         )
 
-    def rest(scaled, mine, held):
+    def rest(scaled, mine, *held):
         return call(
-            functools.partial(rest_kernel, scaled, slots, place, blocks),
+            functools.partial(scaled_rest_kernel if scaled else rest_kernel, slots, places),
             "rest",
             (narrow, scalars) if scaled else narrow,
             (channel_class, left, right, mine, *held),
@@ -360,8 +404,19 @@
             16,
         )
 
+    def shift(block, pairs):
+        return lax.ppermute(block, ring, pairs)
+
     def spread(block):
-        return [block] + [lax.ppermute(block, ring, pairs) for pairs in permutes]
+        return [block] + [shift(block, pairs) for pairs in permutes]
+
+    def spread_shared(block, share):
+        piece = shift(share, permutes[0])
+        if parts == 2:
+            first = [piece, lax.ppermute(piece, "mpo", [(0, 1), (1, 0)])]
+        else:
+            first = [lax.all_gather(piece, "mpo", axis=0, tiled=True)]
+        return first + [shift(block, pairs) for pairs in permutes[1:]]
 
     def gather_parts(t):
         if parts == 2:
@@ -373,11 +428,11 @@
         return lax.all_to_all(rows, ring, 0, 0, tiled=True)
 
     psis = spread(psi)
-    t, unit = rest(True, own(True, psi), psis)
+    t, unit = rest(True, own(True, psi), *psis)
     w_1, rows = call(first_sums_kernel, "sums", (narrow, rows_shape), (*gather_parts(t), psi, unit))
     products = spread(w_1)
     t, v_2, scal = call(
-        functools.partial(second_kernel, slots, place, blocks, entries),
+        functools.partial(second_kernel, slots, places, origins, entries),
         "second",
         (narrow, narrow, scalars),
         (channel_class, left, right, exchange(rows), *products, *psis),
@@ -385,8 +440,11 @@
         0.6,
         16,
     )
-    w_wide, w_2 = call(second_sums_kernel, "sums", (wide, narrow), (*gather_parts(t), scal))
-    t = rest(False, own(False, w_2), spread(w_2))
+    share = jax.ShapeDtypeStruct((width // parts, width), jnp.bfloat16)
+    w_wide, w_2, share_2 = call(
+        second_sums_kernel, "sums", (wide, narrow, share), (*gather_parts(t), scal)
+    )
+    t = rest(False, own(False, w_2), *spread_shared(w_2, share_2))
     r, z, rows = call(
         third_sums_kernel,
         "sums",

time: 76.4 us -> 73.3 us (0.959)
  starting transfers between devices: 22.3 us -> 15 us
  waiting for transfers between devices: 18.3 us -> 21.4 us
  blocking collectives: 17.8 us -> 19.6 us
    ppermute x6 -> x7, starting transfers between devices: 17.6 us -> 11.3 us  [the longest x6 9.55 us: shift(): return lax.ppermute(block, ring, pairs)]
    ppermute x6 -> x7, waiting for transfers between devices: 6.44 us -> 8.64 us  [the longest x6 7.65 us: shift(): return lax.ppermute(block, ring, pairs)]
    all_to_all x2, blocking collectives: 17.8 us -> 19.6 us  [exchange(): return lax.all_to_all(rows, ring, 0, 0, tiled=True)]
    ppermute x3, starting transfers between devices: 4.64 us -> 3.7 us  [gather_parts(): return [t, lax.ppermute(t, 'mpo', [(0, 1), (1, 0)])]]
    ppermute x3, waiting for transfers between devices: 11.9 us -> 12.8 us  [gather_parts(): return [t, lax.ppermute(t, 'mpo', [(0, 1), (1, 0)])]]
  transfers between devices with their start and end apart: 9 -> 10, of which waited for: 5 -> 6; matrix products, arithmetic and copies ran while one was open for 0% -> 0% of each run, Pallas kernels for 4% -> 4%
where the time goes in v5:
time: 73.3 us; the launch traced here: 73.4 us
  waiting for transfers between devices  21.4 us (29%)
  blocking collectives  19.6 us (27%)
  starting transfers between devices  15 us (20%)
  Pallas kernels  11.3 us (15%)
  local copies, waits for them, and re-layouts  5.34 us (7%)
    all_to_all x2, blocking collectives, exchange(): return lax.all_to_all(rows, ring, 0, 0, tiled=True)  19.6 us
    ppermute x3, waiting for transfers between devices, gather_parts(): return [t, lax.ppermute(t, 'mpo', [(0, 1), (1, 0)])]  12.8 us
    pallas_call x9, Pallas kernels, call(): pl.pallas_call(kernel, out_shape=outs, in_specs=[first] + [VMEM] * (len(a...  11.3 us
    ppermute x6, starting transfers between devices, shift(): return lax.ppermute(block, ring, pairs)  9.55 us
    ppermute x6, waiting for transfers between devices, shift(): return lax.ppermute(block, ring, pairs)  7.65 us
    unnamed x10, local copies, waits for them, and re-layouts  5.34 us
    ppermute x3, starting transfers between devices, gather_parts(): return [t, lax.ppermute(t, 'mpo', [(0, 1), (1, 0)])]  3.7 us
    ppermute x1, starting transfers between devices, spread_shared(): first = [piece, lax.ppermute(piece, 'mpo', [(0, 1), (1, 0)])]  1.74 us
  transfers between devices with their start and end apart: 10, of which 6 were waited for; matrix products, arithmetic and copies ran while one was open for 0% of the time, Pallas kernels for 4%

profile of v5, /device:TPU:0, one launch (start us, length us, event | category | flops | bytes accessed | tf_op | source)
XLA Modules:
  0.0 73.4 jit_solution(15496995555399065627)
XLA Ops:
  0.6 0.7 collective-permute-start.1
  1.3 5.5 %collective-permute-start = (bf16[256,256]{1,0:T(8,128)(2,1)}, bf16[256,256]{1,0:T(8,128)(2,1)S(1)}, u32[]{:S(2)}, u32[]{:S(2)}) collective-permute-start(bf16[256,256]{1,0:T(8,128)(2,1)} %bitcast.22), channel_id=1, source_target_pairs={{9,0},{8,1},{13,4},{12,5},{1,8},{0,9},{5,12},{4,13},{11,2},{10,3},... | collective-permute-start | bytes 393224 | tf_op jit(solution)/shard_map/ppermute | solution.py:408
  6.8 1.9 %copy-done = bf16[24,1,256,256]{3,2,1,0:T(8,128)(2,1)S(1)} copy-done((bf16[24,1,256,256]{3,2,1,0:T(8,128)(2,1)S(1)}, bf16[24,1,256,256]{3,2,1,0:T(8,128)(2,1)}, u32[]{:S(2)}) %copy-start) | copy-done | bytes 3145752
  8.7 1.9 %copy-done.1 = bf16[24,1,256,256]{3,2,1,0:T(8,128)(2,1)S(1)} copy-done((bf16[24,1,256,256]{3,2,1,0:T(8,128)(2,1)S(1)}, bf16[24,1,256,256]{3,2,1,0:T(8,128)(2,1)}, u32[]{:S(2)}) %copy-start.1) | copy-done | bytes 3145752
  10.6 0.9 %copy-done.2 = bf16[1,256,256]{2,1,0:T(8,128)(2,1)S(1)} copy-done((bf16[1,256,256]{2,1,0:T(8,128)(2,1)S(1)}, bf16[1,256,256]{2,1,0:T(8,128)(2,1)}, u32[]{:S(2)}) %copy-start.2) | copy-done | bytes 131096
  12.2 1.5 %own.2.refs_3_ = f32[256,256]{1,0:T(8,128)S(1)} custom-call(s32[24]{0:T(128)S(1)} %copy-done.4, bf16[24,256,256]{2,1,0:T(8,128)(2,1)S(1)} %bitcast.11, bf16[24,256,256]{2,1,0:T(8,128)(2,1)S(1)} %bitcast.16, bf16[256,256]{1,0:T(8,128)(2,1)S(1)} %bitcast.23), custom_call_target="tpu_custom_call" | custom-call | flops 322122560 | bytes 262144 | tf_op jit(solution)/shard_map/own/pallas_call | solution.py:371
  13.7 2.9 %collective-permute-done.refs_5_.refs_8_ = bf16[256,256]{1,0:T(8,128)(2,1)S(1)} collective-permute-done((bf16[256,256]{1,0:T(8,128)(2,1)}, bf16[256,256]{1,0:T(8,128)(2,1)S(1)}, u32[]{:S(2)}, u32[]{:S(2)}) %collective-permute-start) | collective-permute-done | bytes 131104 | tf_op jit(solution)/shard_map/ppermute | solution.py:408
  16.6 1.6 %rest.2 = (bf16[256,256]{1,0:T(8,128)(2,1)S(1)}, f32[8,128]{1,0:T(8,128)S(1)}) custom-call(s32[24]{0:T(128)S(1)} %copy-done.4, bf16[24,256,256]{2,1,0:T(8,128)(2,1)S(1)} %bitcast.12, bf16[24,256,256]{2,1,0:T(8,128)(2,1)S(1)} %bitcast.17, f32[256,256]{1,0:T(8,128)S(1)} %own.2.refs_3_, bf16[256,256]{1,0:T(8,128)(2,1)S(1)} %bitcast.24, ...), custom_call_target="tpu_custom_call" | custom-call | flops 644245120 | bytes 262144 | tf_op jit(solution)/shard_map/rest/pallas_call | solution.py:371
  18.2 1.1 %collective-permute-start.2 = (bf16[256,256]{1,0:T(8,128)(2,1)S(1)}, bf16[256,256]{1,0:T(8,128)(2,1)S(1)}, u32[]{:S(2)}, u32[]{:S(2)}) collective-permute-start(bf16[256,256]{1,0:T(8,128)(2,1)S(1)} %get-tuple-element.15.refs_0_), channel_id=1, source_target_pairs={{0,2},{2,0},{1,3},{3,1},{4,6},{6,4},{5,7},{7,5},{8,10},{10,8},{9,1... | collective-permute-start | bytes 393224 | tf_op jit(solution)/shard_map/ppermute | solution.py:423
  19.3 4.8 %collective-permute-done.2.refs_1_ = bf16[256,256]{1,0:T(8,128)(2,1)S(1)} collective-permute-done((bf16[256,256]{1,0:T(8,128)(2,1)S(1)}, bf16[256,256]{1,0:T(8,128)(2,1)S(1)}, u32[]{:S(2)}, u32[]{:S(2)}) %collective-permute-start.2) | collective-permute-done | bytes 131104 | tf_op jit(solution)/shard_map/ppermute | solution.py:423
  25.1 1.8 %collective-permute-start.3 = (bf16[256,256]{1,0:T(8,128)(2,1)S(1)}, bf16[256,256]{1,0:T(8,128)(2,1)S(1)}, u32[]{:S(2)}, u32[]{:S(2)}) collective-permute-start(bf16[256,256]{1,0:T(8,128)(2,1)S(1)} %get-tuple-element.18.refs_4_.refs_3_), channel_id=1, source_target_pairs={{9,0},{8,1},{13,4},{12,5},{1,8},{0,9},{5,12},{4,13},{11,2},{10,3},... | collective-permute-start | bytes 393224 | tf_op jit(solution)/shard_map/ppermute | solution.py:408
  26.9 10.8 %all_to_all.22 = f32[8,1,128]{2,1,0:T(1,128)S(1)} all-to-all(f32[8,1,128]{2,1,0:T(1,128)S(1)} %bitcast.30), channel_id=1, replica_groups=mesh['groups'=2,'blk'=4,'mpo'=2,'rep'=2] {'blk','rep'}, dimensions={0} | all-to-all | bytes 8192 | tf_op jit(solution)/shard_map/all_to_all | solution.py:428
  37.7 2.6 %second.1 = (bf16[256,256]{1,0:T(8,128)(2,1)S(1)}, bf16[256,256]{1,0:T(8,128)(2,1)S(1)}, f32[8,128]{1,0:T(8,128)S(1)}) custom-call(s32[24]{0:T(128)S(1)} %copy-done.4, bf16[24,256,256]{2,1,0:T(8,128)(2,1)S(1)} %bitcast.13, bf16[24,256,256]{2,1,0:T(8,128)(2,1)S(1)} %bitcast.18, f32[8,128]{1,0:T(8,128)S(1)} %bitcast.28, ...), custom_call_target="tpu_custom_call" | custom-call | flops 966367616 | bytes 262144 | tf_op jit(solution)/shard_map/second/pallas_call | solution.py:371
  40.4 1.3 %collective-permute-start.5 = (bf16[256,256]{1,0:T(8,128)(2,1)S(1)}, bf16[256,256]{1,0:T(8,128)(2,1)S(1)}, u32[]{:S(2)}, u32[]{:S(2)}) collective-permute-start(bf16[256,256]{1,0:T(8,128)(2,1)S(1)} %get-tuple-element.19.refs_0_), channel_id=1, source_target_pairs={{0,2},{2,0},{1,3},{3,1},{4,6},{6,4},{5,7},{7,5},{8,10},{10,8},{9,1... | collective-permute-start | bytes 393224 | tf_op jit(solution)/shard_map/ppermute | solution.py:423
  41.6 4.3 %collective-permute-done.5.refs_1_ = bf16[256,256]{1,0:T(8,128)(2,1)S(1)} collective-permute-done((bf16[256,256]{1,0:T(8,128)(2,1)S(1)}, bf16[256,256]{1,0:T(8,128)(2,1)S(1)}, u32[]{:S(2)}, u32[]{:S(2)}) %collective-permute-start.5) | collective-permute-done | bytes 131104 | tf_op jit(solution)/shard_map/ppermute | solution.py:423
  47.0 4.7 %collective-permute-done.6.refs_4_ = bf16[128,256]{1,0:T(8,128)(2,1)S(1)} collective-permute-done((bf16[128,256]{1,0:T(8,128)(2,1)S(1)}, bf16[128,256]{1,0:T(8,128)(2,1)S(1)}, u32[]{:S(2)}, u32[]{:S(2)}) %collective-permute-start.6) | collective-permute-done | bytes 65568 | tf_op jit(solution)/shard_map/ppermute | solution.py:408
  51.7 1.7 %collective-permute-start.7 = (bf16[128,256]{1,0:T(8,128)(2,1)S(1)}, bf16[128,256]{1,0:T(8,128)(2,1)S(1)}, u32[]{:S(2)}, u32[]{:S(2)}) collective-permute-start(bf16[128,256]{1,0:T(8,128)(2,1)S(1)} %collective-permute-done.6.refs_4_), channel_id=1, source_target_pairs={{0,2},{2,0},{1,3},{3,1},{4,6},{6,4},{5,7},{7,5},{8,10},{10,8},{9,1... | collective-permute-start | bytes 196616 | tf_op jit(solution)/shard_map/ppermute | solution.py:416
  53.4 1.5 %own.3.refs_3_ = f32[256,256]{1,0:T(8,128)S(1)} custom-call(s32[24]{0:T(128)S(1)} %copy-done.4, bf16[24,256,256]{2,1,0:T(8,128)(2,1)S(1)} %bitcast.14, bf16[24,256,256]{2,1,0:T(8,128)(2,1)S(1)} %bitcast.19, bf16[256,256]{1,0:T(8,128)(2,1)S(1)} %get-tuple-element.21.block_ref), custom_call_target="tpu_custom_call" | custom-call | flops 322122560 | bytes 262144 | tf_op jit(solution)/shard_map/own/pallas_call | solution.py:371
  55.0 1.0 %collective-permute-done.7.refs_5_ = bf16[128,256]{1,0:T(8,128)(2,1)S(1)} collective-permute-done((bf16[128,256]{1,0:T(8,128)(2,1)S(1)}, bf16[128,256]{1,0:T(8,128)(2,1)S(1)}, u32[]{:S(2)}, u32[]{:S(2)}) %collective-permute-start.7) | collective-permute-done | bytes 65568 | tf_op jit(solution)/shard_map/ppermute | solution.py:416
  56.0 1.6 %rest.3.refs_0_ = bf16[256,256]{1,0:T(8,128)(2,1)S(1)} custom-call(s32[24]{0:T(128)S(1)} %copy-done.4, bf16[24,256,256]{2,1,0:T(8,128)(2,1)S(1)} %bitcast.15, bf16[24,256,256]{2,1,0:T(8,128)(2,1)S(1)} %bitcast.20, f32[256,256]{1,0:T(8,128)S(1)} %own.3.refs_3_, bf16[128,256]{1,0:T(8,128)(2,1)S(1)} %collective-permute-done.6.refs_4_, ...), custom_call_target="tpu_custom_call" | custom-call | flops 644245120 | bytes 262144 | tf_op jit(solution)/shard_map/rest/pallas_call | solution.py:371
  57.5 1.3 %collective-permute-start.9 = (bf16[256,256]{1,0:T(8,128)(2,1)S(1)}, bf16[256,256]{1,0:T(8,128)(2,1)S(1)}, u32[]{:S(2)}, u32[]{:S(2)}) collective-permute-start(bf16[256,256]{1,0:T(8,128)(2,1)S(1)} %rest.3.refs_0_), channel_id=1, source_target_pairs={{0,2},{2,0},{1,3},{3,1},{4,6},{6,4},{5,7},{7,5},{8,10},{10,8},{9,1... | collective-permute-start | bytes 393224 | tf_op jit(solution)/shard_map/ppermute | solution.py:423
  58.9 3.8 %collective-permute-done.9.refs_1_ = bf16[256,256]{1,0:T(8,128)(2,1)S(1)} collective-permute-done((bf16[256,256]{1,0:T(8,128)(2,1)S(1)}, bf16[256,256]{1,0:T(8,128)(2,1)S(1)}, u32[]{:S(2)}, u32[]{:S(2)}) %collective-permute-start.9) | collective-permute-done | bytes 131104 | tf_op jit(solution)/shard_map/ppermute | solution.py:423
  63.2 8.8 %all_to_all.23 = f32[8,1,128]{2,1,0:T(1,128)S(1)} all-to-all(f32[8,1,128]{2,1,0:T(1,128)S(1)} %bitcast.31), channel_id=1, replica_groups=mesh['groups'=2,'blk'=4,'mpo'=2,'rep'=2] {'blk','rep'}, dimensions={0} | all-to-all | bytes 8192 | tf_op jit(solution)/shard_map/all_to_all | solution.py:428
  72.0 1.4 %final.1 = (bf16[3,1,128,256]{3,2,1,0:T(8,128)(2,1)}, f32[2,3]{1,0:T(2,128)}) custom-call(f32[8,128]{1,0:T(8,128)S(1)} %bitcast.29, f32[256,256]{1,0:T(8,128)S(1)} %get-tuple-element.26.r_ref, f32[256,256]{1,0:T(8,128)S(1)} %get-tuple-element.27.z_ref, f32[256,256]{1,0:T(8,128)S(1)} %get-tuple-element.24.refs_5_.w_ref, ...), custom_call_target="tpu_custom_call" | custom-call | bytes 262144 | tf_op jit(solution)/shard_map/final/pallas_call | solution.py:371
  (17 shorter events, 3.3 us)
Async XLA Ops:
  0.6 13.1 %collective-permute-start.1 = (bf16[256,256]{1,0:T(8,128)(2,1)}, bf16[256,256]{1,0:T(8,128)(2,1)S(1)}, u32[]{:S(2)}, u32[]{:S(2)}) collective-permute-start(bf16[256,256]{1,0:T(8,128)(2,1)} %bitcast.21), channel_id=1, source_target_pairs={{12,1},{9,4},{4,9},{1,12},{14,3},{11,6},{6,11},{3,14},{28,17},{25,... | collective-permute-start | bytes 393224 | tf_op jit(solution)/shard_map/ppermute | solution.py:408
  1.3 15.3 %collective-permute-start = (bf16[256,256]{1,0:T(8,128)(2,1)}, bf16[256,256]{1,0:T(8,128)(2,1)S(1)}, u32[]{:S(2)}, u32[]{:S(2)}) collective-permute-start(bf16[256,256]{1,0:T(8,128)(2,1)} %bitcast.22), channel_id=1, source_target_pairs={{9,0},{8,1},{13,4},{12,5},{1,8},{0,9},{5,12},{4,13},{11,2},{10,3},... | collective-permute-start | bytes 393224 | tf_op jit(solution)/shard_map/ppermute | solution.py:408
  6.8 1.9 %copy-start = (bf16[24,1,256,256]{3,2,1,0:T(8,128)(2,1)S(1)}, bf16[24,1,256,256]{3,2,1,0:T(8,128)(2,1)}, u32[]{:S(2)}) copy-start(bf16[24,1,256,256]{3,2,1,0:T(8,128)(2,1)} %param.5) | copy-start | bytes 9437188
  8.7 1.9 %copy-start.1 = (bf16[24,1,256,256]{3,2,1,0:T(8,128)(2,1)S(1)}, bf16[24,1,256,256]{3,2,1,0:T(8,128)(2,1)}, u32[]{:S(2)}) copy-start(bf16[24,1,256,256]{3,2,1,0:T(8,128)(2,1)} %param.6) | copy-start | bytes 9437188
  10.6 0.9 %copy-start.2 = (bf16[1,256,256]{2,1,0:T(8,128)(2,1)S(1)}, bf16[1,256,256]{2,1,0:T(8,128)(2,1)}, u32[]{:S(2)}) copy-start(bf16[1,256,256]{2,1,0:T(8,128)(2,1)} %param.4) | copy-start | bytes 393220
  11.5 0.7 copy-start.4
  18.2 5.8 %collective-permute-start.2 = (bf16[256,256]{1,0:T(8,128)(2,1)S(1)}, bf16[256,256]{1,0:T(8,128)(2,1)S(1)}, u32[]{:S(2)}, u32[]{:S(2)}) collective-permute-start(bf16[256,256]{1,0:T(8,128)(2,1)S(1)} %get-tuple-element.15.refs_0_), channel_id=1, source_target_pairs={{0,2},{2,0},{1,3},{3,1},{4,6},{6,4},{5,7},{7,5},{8,10},{10,8},{9,1... | collective-permute-start | bytes 393224 | tf_op jit(solution)/shard_map/ppermute | solution.py:423
  24.4 13.3 %collective-permute-start.4 = (bf16[256,256]{1,0:T(8,128)(2,1)S(1)}, bf16[256,256]{1,0:T(8,128)(2,1)S(1)}, u32[]{:S(2)}, u32[]{:S(2)}) collective-permute-start(bf16[256,256]{1,0:T(8,128)(2,1)S(1)} %get-tuple-element.18.refs_4_.refs_3_), channel_id=1, source_target_pairs={{12,1},{9,4},{4,9},{1,12},{14,3},{11,6},{6,11},{3,14},{28,17},{25,... | collective-permute-start | bytes 393224 | tf_op jit(solution)/shard_map/ppermute | solution.py:408
  25.1 12.6 %collective-permute-start.3 = (bf16[256,256]{1,0:T(8,128)(2,1)S(1)}, bf16[256,256]{1,0:T(8,128)(2,1)S(1)}, u32[]{:S(2)}, u32[]{:S(2)}) collective-permute-start(bf16[256,256]{1,0:T(8,128)(2,1)S(1)} %get-tuple-element.18.refs_4_.refs_3_), channel_id=1, source_target_pairs={{9,0},{8,1},{13,4},{12,5},{1,8},{0,9},{5,12},{4,13},{11,2},{10,3},... | collective-permute-start | bytes 393224 | tf_op jit(solution)/shard_map/ppermute | solution.py:408
  40.4 5.6 %collective-permute-start.5 = (bf16[256,256]{1,0:T(8,128)(2,1)S(1)}, bf16[256,256]{1,0:T(8,128)(2,1)S(1)}, u32[]{:S(2)}, u32[]{:S(2)}) collective-permute-start(bf16[256,256]{1,0:T(8,128)(2,1)S(1)} %get-tuple-element.19.refs_0_), channel_id=1, source_target_pairs={{0,2},{2,0},{1,3},{3,1},{4,6},{6,4},{5,7},{7,5},{8,10},{10,8},{9,1... | collective-permute-start | bytes 393224 | tf_op jit(solution)/shard_map/ppermute | solution.py:423
  46.1 5.6 %collective-permute-start.6 = (bf16[128,256]{1,0:T(8,128)(2,1)S(1)}, bf16[128,256]{1,0:T(8,128)(2,1)S(1)}, u32[]{:S(2)}, u32[]{:S(2)}) collective-permute-start(bf16[128,256]{1,0:T(8,128)(2,1)S(1)} %get-tuple-element.22), channel_id=1, source_target_pairs={{9,0},{8,1},{13,4},{12,5},{1,8},{0,9},{5,12},{4,13},{11,2},{10,3},... | collective-permute-start | bytes 196616 | tf_op jit(solution)/shard_map/ppermute | solution.py:408
  46.3 9.7 %collective-permute-start.8 = (bf16[256,256]{1,0:T(8,128)(2,1)S(1)}, bf16[256,256]{1,0:T(8,128)(2,1)S(1)}, u32[]{:S(2)}, u32[]{:S(2)}) collective-permute-start(bf16[256,256]{1,0:T(8,128)(2,1)S(1)} %get-tuple-element.21.block_ref), channel_id=1, source_target_pairs={{12,1},{9,4},{4,9},{1,12},{14,3},{11,6},{6,11},{3,14},{28,17},{25,... | collective-permute-start | bytes 393224 | tf_op jit(solution)/shard_map/ppermute | solution.py:408
  51.7 4.3 %collective-permute-start.7 = (bf16[128,256]{1,0:T(8,128)(2,1)S(1)}, bf16[128,256]{1,0:T(8,128)(2,1)S(1)}, u32[]{:S(2)}, u32[]{:S(2)}) collective-permute-start(bf16[128,256]{1,0:T(8,128)(2,1)S(1)} %collective-permute-done.6.refs_4_), channel_id=1, source_target_pairs={{0,2},{2,0},{1,3},{3,1},{4,6},{6,4},{5,7},{7,5},{8,10},{10,8},{9,1... | collective-permute-start | bytes 196616 | tf_op jit(solution)/shard_map/ppermute | solution.py:416
  55.0 7.7 %copy-start.3 = (bf16[1,256,256]{2,1,0:T(8,128)(2,1)S(1)}, bf16[1,256,256]{2,1,0:T(8,128)(2,1)}, u32[]{:S(2)}) copy-start(bf16[1,256,256]{2,1,0:T(8,128)(2,1)} %param.4) | copy-start | bytes 393220
  57.5 5.1 %collective-permute-start.9 = (bf16[256,256]{1,0:T(8,128)(2,1)S(1)}, bf16[256,256]{1,0:T(8,128)(2,1)S(1)}, u32[]{:S(2)}, u32[]{:S(2)}) collective-permute-start(bf16[256,256]{1,0:T(8,128)(2,1)S(1)} %rest.3.refs_0_), channel_id=1, source_target_pairs={{0,2},{2,0},{1,3},{3,1},{4,6},{6,4},{5,7},{7,5},{8,10},{10,8},{9,1... | collective-permute-start | bytes 393224 | tf_op jit(solution)/shard_map/ppermute | solution.py:423

commit v6 on v5

--- a/solution.py
+++ b/solution.py
@@ -189,47 +189,73 @@
     multiply_listed(count, left_ref, right_ref, source, acc, order, slot_of)
 
 
-def scaled_rest_kernel(slots, places, *refs):
+def rest_kernel(scaled, passes, shares, slots, places, *refs):
     kinds_ref, left_ref, right_ref, own_ref = refs[:4]
-    held, (t_ref, unit_ref, acc, source, order, slot_of) = refs[4 : 4 + slots], refs[4 + slots :]
+    refs = refs[4:]
+    if scaled:
+        block_ref, refs = refs[0], refs[1:]
+    first, refs = refs[:shares], refs[shares:]
+    others, refs = refs[: slots - 2], refs[slots - 2 :]
+    if passes:
+        rows_ref, refs = refs[0], refs[1:]
+    t_ref, refs = refs[0], refs[1:]
+    if scaled:
+        unit_ref, refs = refs[0], refs[1:]
+    if passes:
+        refs[0][...] = rows_ref[...]
+        refs = refs[1:]
+    acc, source, order, slot_of = refs
     count = list_channels("rest", places, kinds_ref, order, slot_of, slots)
-    peaks = [jnp.maximum(peak(wide_float(block)), SMALLEST) for block in held]
-    unit = functools.reduce(jnp.maximum, peaks)
-    unit_ref[...] = jnp.broadcast_to(unit, unit_ref.shape)
-    inverse = 1.0 / unit
-    for slot in range(1, slots):
-        source[slot] = (wide_float(held[slot]) * inverse).astype(jnp.bfloat16)
-    acc[...] = own_ref[...] * (peaks[0] * inverse)
+    if scaled:
+        mine = jnp.maximum(peak(wide_float(block_ref)), SMALLEST)
+        unit = mine
+        for block in (*first, *others):
+            unit = jnp.maximum(unit, peak(wide_float(block)))
+        unit_ref[...] = jnp.broadcast_to(unit, unit_ref.shape)
+        inverse = 1.0 / unit
+
+    def scale(block):
+        return (wide_float(block) * inverse).astype(jnp.bfloat16) if scaled else block[...]
+
+    share = source.shape[1] // shares
+    for step, block in enumerate(first):
+        at = 0 if shares == 1 else jnp.abs(step - lax.axis_index("mpo"))
+        source[1, pl.ds(pl.multiple_of(at * share, share), share), :] = scale(block)
+    for slot, block in enumerate(others, 2):
+        source[slot] = scale(block)
     source[slots] = jnp.zeros(source.shape[1:], jnp.bfloat16)
+    acc[...] = own_ref[...] * (mine * inverse) if scaled else own_ref[...]
     multiply_listed(count, left_ref, right_ref, source, acc, order, slot_of)
     t_ref[...] = acc[...].astype(jnp.bfloat16)
 
 
-def rest_kernel(slots, places, *refs):
-    kinds_ref, left_ref, right_ref, own_ref = refs[:4]
-    t_ref, acc, source, order, slot_of = refs[-5:]
-    shares, held = refs[4 : -5 - (slots - 2)], refs[-5 - (slots - 2) : -5]
-    count = list_channels("rest", places, kinds_ref, order, slot_of, slots)
-    share = source.shape[1] // lax.axis_size("mpo")
-    for step, block in enumerate(shares):
-        if len(shares) == 1:
-            source[1] = block[...]
-        else:
-            at = lax.axis_index("mpo") if step == 0 else 1 - lax.axis_index("mpo")
-            source[1, pl.ds(pl.multiple_of(at * share, share), share), :] = block[...]
-    for slot in range(2, slots):
-        source[slot] = held[slot - 2][...]
-    acc[...] = own_ref[...]
-    source[slots] = jnp.zeros(source.shape[1:], jnp.bfloat16)
-    multiply_listed(count, left_ref, right_ref, source, acc, order, slot_of)
-    t_ref[...] = acc[...].astype(jnp.bfloat16)
-
-
-def second_kernel(slots, places, origins, entries, *refs):
-    kinds_ref, left_ref, right_ref, rows_ref = refs[:4]
-    products, psis = refs[4 : 4 + slots], refs[4 + slots : 4 + 2 * slots]
-    t_ref, v_ref, scal_ref, acc, source, order, slot_of = refs[4 + 2 * slots :]
-    count = list_channels("all", places, kinds_ref, order, slot_of, slots)
+def my_rows(share):
+    return pl.ds(pl.multiple_of(lax.axis_index("mpo") * share, share), share)
+
+
+def first_sums_kernel(*refs):
+    parts, (psi_ref, unit_ref, w_ref, share_ref, rows_ref) = refs[:-5], refs[-5:]
+    w = sum_parts(parts)
+    unit = lane_of(first_row(unit_ref), 0)
+    w_ref[...] = (w * unit).astype(jnp.bfloat16)
+    share_ref[...] = w_ref[my_rows(share_ref.shape[0]), :]
+    v = wide_float(psi_ref) * (1.0 / unit)
+    a = total(v * w)
+    d = total(v * v)
+    local = a / jnp.maximum(d, SMALLEST)
+    r = w - local * v
+    sums = pack([a, d, local, total(r * v), total(r * r), unit], rows_ref.shape)
+    row = lax.broadcasted_iota(jnp.int32, rows_ref.shape, 0)
+    rows_ref[...] = jnp.where(row == here(), sums, 0.0)
+
+
+def shrink(scal):
+    return 1.0 / (jnp.abs(lane_of(scal, 0)) + lane_of(scal, 1))
+
+
+def second_sums_kernel(entries, *refs):
+    parts, refs = refs[:-9], refs[-9:]
+    rows_ref, psi_ref, first_ref, unit_ref, wide_ref, w_ref, share_ref, v_ref, scal_ref = refs
     rows = rows_ref[...]
     a, d, local, p, q, unit = (lane_of(rows, lane) for lane in range(6))
     beta_0 = jnp.sqrt(column_sum(unit * unit * d) / entries + EPSILON)
@@ -240,60 +266,28 @@
     square = column_sum(gain * (gain * (q + off * (2.0 * p + off * d))))
     beta = jnp.sqrt(jnp.maximum(square, 0.0) / entries + EPSILON)
     inverse = 1.0 / beta
-    sector = here()
-    row_of = lax.broadcasted_iota(jnp.int32, gain.shape, 0)
-    for slot in range(slots):
-        origin = sector if slot == 0 else look_up(origins[slot], sector, 0)
-        gain_here = column_sum(jnp.where(row_of == origin, gain, 0.0))
-        r = gain_here * wide_float(products[slot]) - (alpha * start_inverse) * wide_float(psis[slot])
-        source[slot] = (r * inverse).astype(jnp.bfloat16)
-        if slot == 0:
-            scal_ref[...] = pack([alpha, beta, start_inverse, gain_here], scal_ref.shape)
-            v_ref[...] = source[0]
-    source[slots] = jnp.zeros(source.shape[1:], jnp.bfloat16)
-    acc[...] = jnp.zeros_like(acc)
-    multiply_listed(count, left_ref, right_ref, source, acc, order, slot_of)
-    t_ref[...] = acc[...].astype(jnp.bfloat16)
-
-
-def first_sums_kernel(*refs):
-    parts, (psi_ref, unit_ref, w_ref, rows_ref) = refs[:-4], refs[-4:]
-    w = sum_parts(parts)
-    w_ref[...] = w.astype(jnp.bfloat16)
-    unit = lane_of(first_row(unit_ref), 0)
-    v = wide_float(psi_ref) * (1.0 / unit)
-    a = total(v * w)
-    d = total(v * v)
-    local = a / jnp.maximum(d, SMALLEST)
-    r = w - local * v
-    rows_ref[...] = pack([a, d, local, total(r * v), total(r * r), unit], rows_ref.shape)
-
-
-def shrink(scal):
-    return 1.0 / (jnp.abs(lane_of(scal, 0)) + lane_of(scal, 1))
-
-
-def second_sums_kernel(*refs):
-    parts, (scal_ref, wide_ref, w_ref, share_ref) = refs[:-4], refs[-4:]
-    w = sum_parts(parts) * shrink(first_row(scal_ref))
+    scal = pack([alpha, beta, start_inverse], scal_ref.shape)
+    scal_ref[...] = scal
+    image = wide_float(first_ref) * start_inverse
+    v_ref[...] = ((image - (alpha * start_inverse) * wide_float(psi_ref)) * inverse).astype(jnp.bfloat16)
+    lift = lane_of(first_row(unit_ref), 0) * start_inverse
+    w = (sum_parts(parts) * lift - alpha * image) * (inverse * shrink(first_row(scal)))
     wide_ref[...] = w
     w_ref[...] = w.astype(jnp.bfloat16)
-    share = share_ref.shape[0]
-    mine = pl.ds(pl.multiple_of(lax.axis_index("mpo") * share, share), share)
-    share_ref[...] = wide_ref[mine, :].astype(jnp.bfloat16)
+    share_ref[...] = w_ref[my_rows(share_ref.shape[0]), :]
 
 
 def third_sums_kernel(*refs):
     parts, refs = refs[:-8], refs[-8:]
     psi_ref, first_ref, v_ref, w_ref, scal_ref, r_ref, z_ref, rows_ref = refs
     scal = first_row(scal_ref)
-    beta, start_inverse, gain = (lane_of(scal, lane) for lane in range(1, 4))
     scale = shrink(scal)
+    push = scale * lane_of(scal, 1) * lane_of(scal, 2)
     v, w = wide_float(v_ref), w_ref[...]
     vv, vw = total(v * v), total(v * w)
     local = vw / jnp.maximum(vv, SMALLEST)
-    r = w - local * v - (scale * beta * start_inverse) * wide_float(psi_ref)
-    z = sum_parts(parts) - (local / scale) * w - (scale * beta * gain) * wide_float(first_ref)
+    r = w - local * v - push * wide_float(psi_ref)
+    z = sum_parts(parts) - (local / scale) * w - push * wide_float(first_ref)
     r_ref[...] = r
     z_ref[...] = z
     sums = [total(r * r), total(r * v), total(r * z), total(r * w)]
@@ -303,7 +297,7 @@
 
 def final_kernel(entries, rows_ref, r_ref, z_ref, w_ref, v_ref, scal_ref, basis_ref, coef_ref):
     share = basis_ref.shape[2]
-    mine = pl.ds(pl.multiple_of(lax.axis_index("mpo") * share, share), share)
+    mine = my_rows(share)
     vv, vw, local, rr, rv, rz, rw, zv, zw, zz, ww = (lane_of(rows_ref[...], i) for i in range(11))
     scal = first_row(scal_ref)
     scale = shrink(scal)
@@ -393,12 +387,15 @@
             16,
         )
 
-    def rest(scaled, mine, *held):
+    def rest(mine, first, others, block=None, rows=None):
+        scaled, passes = block is not None, rows is not None
+        outs = (narrow,) + (scalars,) * scaled + (rows_shape,) * passes
+        args = [channel_class, left, right, mine] + [block] * scaled + first + others + [rows] * passes
         return call(
-            functools.partial(scaled_rest_kernel if scaled else rest_kernel, slots, places),
+            functools.partial(rest_kernel, scaled, passes, len(first), slots, places),
             "rest",
-            (narrow, scalars) if scaled else narrow,
-            (channel_class, left, right, mine, *held),
+            outs,
+            args,
             [pltpu.VMEM((width, width), jnp.float32), sources(slots)] + lists,
             0.4,
             16,
@@ -407,16 +404,13 @@
     def shift(block, pairs):
         return lax.ppermute(block, ring, pairs)
 
-    def spread(block):
-        return [block] + [shift(block, pairs) for pairs in permutes]
-
-    def spread_shared(block, share):
+    def spread(block, share):
         piece = shift(share, permutes[0])
         if parts == 2:
             first = [piece, lax.ppermute(piece, "mpo", [(0, 1), (1, 0)])]
         else:
             first = [lax.all_gather(piece, "mpo", axis=0, tiled=True)]
-        return first + [shift(block, pairs) for pairs in permutes[1:]]
+        return first, [shift(block, pairs) for pairs in permutes[1:]]
 
     def gather_parts(t):
         if parts == 2:
@@ -427,24 +421,38 @@
     def exchange(rows):
         return lax.all_to_all(rows, ring, 0, 0, tiled=True)
 
-    psis = spread(psi)
-    t, unit = rest(True, own(True, psi), *psis)
-    w_1, rows = call(first_sums_kernel, "sums", (narrow, rows_shape), (*gather_parts(t), psi, unit))
-    products = spread(w_1)
-    t, v_2, scal = call(
-        functools.partial(second_kernel, slots, places, origins, entries),
-        "second",
-        (narrow, narrow, scalars),
-        (channel_class, left, right, exchange(rows), *products, *psis),
-        [pltpu.VMEM((width, width), jnp.float32), sources(slots)] + lists,
-        0.6,
-        16,
+    rounds = []
+    for axis in ("rep", "blk"):
+        size = lax.axis_size(axis)
+        bits = [1 << i for i in range(size.bit_length() - 1)]
+        if sum(bits) == size - 1:
+            rounds += [(axis, [(i, i ^ bit) for i in range(size)]) for bit in bits]
+        else:
+            rounds += [(axis, None)]
+
+    def add_round(rows, axis, pairs):
+        if pairs is None:
+            return lax.psum(rows, axis)
+        return rows + lax.ppermute(rows, axis, pairs)
+
+    share = jax.ShapeDtypeStruct((width // parts, width), jnp.bfloat16)
+    held = [shift(psi, pairs) for pairs in permutes]
+    t, unit = rest(own(True, psi), held[:1], held[1:], psi)
+    w_1, share_1, rows = call(
+        first_sums_kernel, "sums", (narrow, share, rows_shape), (*gather_parts(t), psi, unit)
     )
-    share = jax.ShapeDtypeStruct((width // parts, width), jnp.bfloat16)
-    w_wide, w_2, share_2 = call(
-        second_sums_kernel, "sums", (wide, narrow, share), (*gather_parts(t), scal)
+    held = spread(w_1, share_1)
+    for step in rounds[:-1]:
+        rows = add_round(rows, *step)
+    t, unit, rows = rest(own(True, w_1), *held, w_1, rows)
+    rows = add_round(rows, *rounds[-1])
+    w_wide, w_2, share_2, v_2, scal = call(
+        functools.partial(second_sums_kernel, entries),
+        "sums",
+        (wide, narrow, share, narrow, scalars),
+        (*gather_parts(t), rows, psi, w_1, unit),
     )
-    t = rest(False, own(False, w_2), *spread_shared(w_2, share_2))
+    (t,) = rest(own(False, w_2), *spread(w_2, share_2))
     r, z, rows = call(
         third_sums_kernel,
         "sums",

time: 73.3 us -> 75.3 us (1.027)
  blocking collectives: 19.6 us -> 9.19 us
  waiting for transfers between devices: 21.4 us -> 29.7 us
  starting transfers between devices: 15 us -> 19 us
    all_to_all x2 -> x1, blocking collectives: 19.6 us -> 9.19 us  [exchange(): return lax.all_to_all(rows, ring, 0, 0, tiled=True)]
    ppermute x1 -> x5, waiting for transfers between devices: 0.99 us -> 8.05 us  [the longest x3 6.32 us: add_round(): return rows + lax.ppermute(rows, axis, pairs)]
    ppermute x6, waiting for transfers between devices: 7.65 us -> 13.8 us  [shift(): return lax.ppermute(block, ring, pairs)]
    ppermute x3, waiting for transfers between devices: 12.8 us -> 7.89 us  [gather_parts(): return [t, lax.ppermute(t, 'mpo', [(0, 1), (1, 0)])]]
    ppermute x1 -> x5, starting transfers between devices: 1.74 us -> 3.73 us  [the longest x2 2.29 us: spread(): first = [piece, lax.ppermute(piece, 'mpo', [(0, 1), (1, 0)])]]
    ppermute x3, starting transfers between devices: 3.7 us -> 4.87 us  [gather_parts(): return [t, lax.ppermute(t, 'mpo', [(0, 1), (1, 0)])]]
    ppermute x6, starting transfers between devices: 9.55 us -> 10.4 us  [shift(): return lax.ppermute(block, ring, pairs)]
    pallas_call x9 -> x10, Pallas kernels: 11.3 us -> 11.2 us  [call(): pl.pallas_call(kernel, out_shape=outs, in_specs=[first] + [VMEM] * (len(a...]
  transfers between devices with their start and end apart: 10 -> 14, of which waited for: 6 -> 9; matrix products, arithmetic and copies ran while one was open for 0% -> 0% of each run, Pallas kernels for 4% -> 6%
where the time goes in v6:
time: 75.3 us; the launch traced here: 75.1 us
  waiting for transfers between devices  29.7 us (39%)
  starting transfers between devices  19 us (25%)
  Pallas kernels  11.2 us (15%)
  blocking collectives  9.19 us (12%)
  local copies, waits for them, and re-layouts  5.34 us (7%)
    ppermute x6, waiting for transfers between devices, shift(): return lax.ppermute(block, ring, pairs)  13.8 us
    pallas_call x10, Pallas kernels, call(): pl.pallas_call(kernel, out_shape=outs, in_specs=[first] + [VMEM] * (len(a...  11.2 us
    ppermute x6, starting transfers between devices, shift(): return lax.ppermute(block, ring, pairs)  10.4 us
    all_to_all x1, blocking collectives, exchange(): return lax.all_to_all(rows, ring, 0, 0, tiled=True)  9.19 us
    ppermute x3, waiting for transfers between devices, gather_parts(): return [t, lax.ppermute(t, 'mpo', [(0, 1), (1, 0)])]  7.89 us
    ppermute x3, waiting for transfers between devices, add_round(): return rows + lax.ppermute(rows, axis, pairs)  6.32 us
    unnamed x10, local copies, waits for them, and re-layouts  5.34 us
    ppermute x3, starting transfers between devices, gather_parts(): return [t, lax.ppermute(t, 'mpo', [(0, 1), (1, 0)])]  4.87 us
  transfers between devices with their start and end apart: 14, of which 9 were waited for; matrix products, arithmetic and copies ran while one was open for 0% of the time, Pallas kernels for 6%

profile of v6, /device:TPU:0, one launch (start us, length us, event | category | flops | bytes accessed | tf_op | source)
XLA Modules:
  0.0 75.1 jit_solution(1906463048032521239)
XLA Ops:
  1.3 5.5 %collective-permute-start = (bf16[256,256]{1,0:T(8,128)(2,1)}, bf16[256,256]{1,0:T(8,128)(2,1)S(1)}, u32[]{:S(2)}, u32[]{:S(2)}) collective-permute-start(bf16[256,256]{1,0:T(8,128)(2,1)} %bitcast.20), channel_id=1, source_target_pairs={{9,0},{8,1},{13,4},{12,5},{1,8},{0,9},{5,12},{4,13},{11,2},{10,3},... | collective-permute-start | bytes 393224 | tf_op jit(solution)/shard_map/ppermute | solution.py:405
  6.8 1.9 %copy-done = bf16[24,1,256,256]{3,2,1,0:T(8,128)(2,1)S(1)} copy-done((bf16[24,1,256,256]{3,2,1,0:T(8,128)(2,1)S(1)}, bf16[24,1,256,256]{3,2,1,0:T(8,128)(2,1)}, u32[]{:S(2)}) %copy-start) | copy-done | bytes 3145752
  8.7 1.9 %copy-done.1 = bf16[24,1,256,256]{3,2,1,0:T(8,128)(2,1)S(1)} copy-done((bf16[24,1,256,256]{3,2,1,0:T(8,128)(2,1)S(1)}, bf16[24,1,256,256]{3,2,1,0:T(8,128)(2,1)}, u32[]{:S(2)}) %copy-start.1) | copy-done | bytes 3145752
  12.2 1.5 %own.3.refs_3_ = f32[256,256]{1,0:T(8,128)S(1)} custom-call(s32[24]{0:T(128)S(1)} %copy-done.4, bf16[24,256,256]{2,1,0:T(8,128)(2,1)S(1)} %bitcast.7, bf16[24,256,256]{2,1,0:T(8,128)(2,1)S(1)} %bitcast.13, bf16[256,256]{1,0:T(8,128)(2,1)S(1)} %bitcast.21), custom_call_target="tpu_custom_call" | custom-call | flops 322122560 | bytes 262144 | tf_op jit(solution)/shard_map/own/pallas_call | solution.py:365
  13.7 2.9 %collective-permute-done.refs_5_ = bf16[256,256]{1,0:T(8,128)(2,1)S(1)} collective-permute-done((bf16[256,256]{1,0:T(8,128)(2,1)}, bf16[256,256]{1,0:T(8,128)(2,1)S(1)}, u32[]{:S(2)}, u32[]{:S(2)}) %collective-permute-start) | collective-permute-done | bytes 131104 | tf_op jit(solution)/shard_map/ppermute | solution.py:405
  16.6 1.1 %rest.3 = (bf16[256,256]{1,0:T(8,128)(2,1)S(1)}, f32[8,128]{1,0:T(8,128)S(1)}) custom-call(s32[24]{0:T(128)S(1)} %copy-done.4, bf16[24,256,256]{2,1,0:T(8,128)(2,1)S(1)} %bitcast.8, bf16[24,256,256]{2,1,0:T(8,128)(2,1)S(1)} %bitcast.14, f32[256,256]{1,0:T(8,128)S(1)} %own.3.refs_3_, bf16[256,256]{1,0:T(8,128)(2,1)S(1)} %bitcast.22, ...), custom_call_target="tpu_custom_call" | custom-call | flops 644245120 | bytes 262144 | tf_op jit(solution)/shard_map/rest/pallas_call | solution.py:365
  17.7 2.0 %collective-permute-start.2 = (bf16[256,256]{1,0:T(8,128)(2,1)S(1)}, bf16[256,256]{1,0:T(8,128)(2,1)S(1)}, u32[]{:S(2)}, u32[]{:S(2)}) collective-permute-start(bf16[256,256]{1,0:T(8,128)(2,1)S(1)} %get-tuple-element.18.refs_0_), channel_id=1, source_target_pairs={{0,2},{2,0},{1,3},{3,1},{4,6},{6,4},{5,7},{7,5},{8,10},{10,8},{9,1... | collective-permute-start | bytes 393224 | tf_op jit(solution)/shard_map/ppermute | solution.py:417
  19.8 3.9 %collective-permute-done.2.refs_1_ = bf16[256,256]{1,0:T(8,128)(2,1)S(1)} collective-permute-done((bf16[256,256]{1,0:T(8,128)(2,1)S(1)}, bf16[256,256]{1,0:T(8,128)(2,1)S(1)}, u32[]{:S(2)}, u32[]{:S(2)}) %collective-permute-start.2) | collective-permute-done | bytes 131104 | tf_op jit(solution)/shard_map/ppermute | solution.py:417
  24.7 2.1 %collective-permute-start.3 = (bf16[128,256]{1,0:T(8,128)(2,1)S(1)}, bf16[128,256]{1,0:T(8,128)(2,1)S(1)}, u32[]{:S(2)}, u32[]{:S(2)}) collective-permute-start(bf16[128,256]{1,0:T(8,128)(2,1)S(1)} %get-tuple-element.21), channel_id=1, source_target_pairs={{9,0},{8,1},{13,4},{12,5},{1,8},{0,9},{5,12},{4,13},{11,2},{10,3},... | collective-permute-start | bytes 196616 | tf_op jit(solution)/shard_map/ppermute | solution.py:405
  26.8 6.1 %collective-permute-done.3.refs_5_ = bf16[128,256]{1,0:T(8,128)(2,1)S(1)} collective-permute-done((bf16[128,256]{1,0:T(8,128)(2,1)S(1)}, bf16[128,256]{1,0:T(8,128)(2,1)S(1)}, u32[]{:S(2)}, u32[]{:S(2)}) %collective-permute-start.3) | collective-permute-done | bytes 65568 | tf_op jit(solution)/shard_map/ppermute | solution.py:405
  32.9 1.3 %collective-permute-start.4 = (bf16[128,256]{1,0:T(8,128)(2,1)S(1)}, bf16[128,256]{1,0:T(8,128)(2,1)S(1)}, u32[]{:S(2)}, u32[]{:S(2)}) collective-permute-start(bf16[128,256]{1,0:T(8,128)(2,1)S(1)} %collective-permute-done.3.refs_5_), channel_id=1, source_target_pairs={{0,2},{2,0},{1,3},{3,1},{4,6},{6,4},{5,7},{7,5},{8,10},{10,8},{9,1... | collective-permute-start | bytes 196616 | tf_op jit(solution)/shard_map/ppermute | solution.py:410
  35.3 1.5 %own.4.refs_3_ = f32[256,256]{1,0:T(8,128)S(1)} custom-call(s32[24]{0:T(128)S(1)} %copy-done.4, bf16[24,256,256]{2,1,0:T(8,128)(2,1)S(1)} %bitcast.9, bf16[24,256,256]{2,1,0:T(8,128)(2,1)S(1)} %bitcast.15, bf16[256,256]{1,0:T(8,128)(2,1)S(1)} %get-tuple-element.20.block_ref.refs_4_.refs_3_), custom_call_target="tpu_custom_call" | custom-call | flops 322122560 | bytes 262144 | tf_op jit(solution)/shard_map/own/pallas_call | solution.py:365
  36.8 2.1 %collective-permute-done.7 = f32[8,128]{1,0:T(8,128)S(1)} collective-permute-done((f32[8,128]{1,0:T(8,128)S(1)}, f32[8,128]{1,0:T(8,128)S(1)}, u32[]{:S(2)}, u32[]{:S(2)}) %collective-permute-start.7) | collective-permute-done | bytes 4128 | tf_op jit(solution)/shard_map/ppermute | solution.py:436
  38.9 1.2 %rest.4 = (bf16[256,256]{1,0:T(8,128)(2,1)S(1)}, f32[8,128]{1,0:T(8,128)S(1)}, f32[8,128]{1,0:T(8,128)S(1)}) custom-call(s32[24]{0:T(128)S(1)} %copy-done.4, bf16[24,256,256]{2,1,0:T(8,128)(2,1)S(1)} %bitcast.10, bf16[24,256,256]{2,1,0:T(8,128)(2,1)S(1)} %bitcast.16, f32[256,256]{1,0:T(8,128)S(1)} %own.4.refs_3_, ...), custom_call_target="tpu_custom_call" | custom-call | flops 644245120 | bytes 262144 | tf_op jit(solution)/shard_map/rest/pallas_call | solution.py:365
  40.1 1.3 %collective-permute-start.8 = (bf16[256,256]{1,0:T(8,128)(2,1)S(1)}, bf16[256,256]{1,0:T(8,128)(2,1)S(1)}, u32[]{:S(2)}, u32[]{:S(2)}) collective-permute-start(bf16[256,256]{1,0:T(8,128)(2,1)S(1)} %get-tuple-element.23.refs_0_), channel_id=1, source_target_pairs={{0,2},{2,0},{1,3},{3,1},{4,6},{6,4},{5,7},{7,5},{8,10},{10,8},{9,1... | collective-permute-start | bytes 393224 | tf_op jit(solution)/shard_map/ppermute | solution.py:417
  41.4 1.2 %collective-permute-start.9 = (f32[8,128]{1,0:T(8,128)S(1)}, f32[8,128]{1,0:T(8,128)S(1)}, u32[]{:S(2)}, u32[]{:S(2)}) collective-permute-start(f32[8,128]{1,0:T(8,128)S(1)} %get-tuple-element.24), channel_id=1, source_target_pairs={{0,8},{4,12},{8,0},{12,4},{1,9},{5,13},{9,1},{13,5},{2,10},{6,14},... | collective-permute-start | bytes 12296 | tf_op jit(solution)/shard_map/ppermute | solution.py:436
  42.6 3.3 %collective-permute-done.9 = f32[8,128]{1,0:T(8,128)S(1)} collective-permute-done((f32[8,128]{1,0:T(8,128)S(1)}, f32[8,128]{1,0:T(8,128)S(1)}, u32[]{:S(2)}, u32[]{:S(2)}) %collective-permute-start.9) | collective-permute-done | bytes 4128 | tf_op jit(solution)/shard_map/ppermute | solution.py:436
  48.2 4.8 %collective-permute-done.10.refs_4_ = bf16[128,256]{1,0:T(8,128)(2,1)S(1)} collective-permute-done((bf16[128,256]{1,0:T(8,128)(2,1)S(1)}, bf16[128,256]{1,0:T(8,128)(2,1)S(1)}, u32[]{:S(2)}, u32[]{:S(2)}) %collective-permute-start.10) | collective-permute-done | bytes 65568 | tf_op jit(solution)/shard_map/ppermute | solution.py:405
  54.0 1.5 %own.5.refs_3_ = f32[256,256]{1,0:T(8,128)S(1)} custom-call(s32[24]{0:T(128)S(1)} %copy-done.4, bf16[24,256,256]{2,1,0:T(8,128)(2,1)S(1)} %bitcast.11, bf16[24,256,256]{2,1,0:T(8,128)(2,1)S(1)} %bitcast.17, bf16[256,256]{1,0:T(8,128)(2,1)S(1)} %get-tuple-element.26.block_ref), custom_call_target="tpu_custom_call" | custom-call | flops 322122560 | bytes 262144 | tf_op jit(solution)/shard_map/own/pallas_call | solution.py:365
  55.6 1.7 %collective-permute-done.11.refs_5_ = bf16[128,256]{1,0:T(8,128)(2,1)S(1)} collective-permute-done((bf16[128,256]{1,0:T(8,128)(2,1)S(1)}, bf16[128,256]{1,0:T(8,128)(2,1)S(1)}, u32[]{:S(2)}, u32[]{:S(2)}) %collective-permute-start.11) | collective-permute-done | bytes 65568 | tf_op jit(solution)/shard_map/ppermute | solution.py:410
  58.4 1.5 %collective-permute-start.13 = (bf16[256,256]{1,0:T(8,128)(2,1)S(1)}, bf16[256,256]{1,0:T(8,128)(2,1)S(1)}, u32[]{:S(2)}, u32[]{:S(2)}) collective-permute-start(bf16[256,256]{1,0:T(8,128)(2,1)S(1)} %rest.5.refs_0_), channel_id=1, source_target_pairs={{0,2},{2,0},{1,3},{3,1},{4,6},{6,4},{5,7},{7,5},{8,10},{10,8},{9,1... | collective-permute-start | bytes 393224 | tf_op jit(solution)/shard_map/ppermute | solution.py:417
  60.0 4.0 %collective-permute-done.13.refs_1_ = bf16[256,256]{1,0:T(8,128)(2,1)S(1)} collective-permute-done((bf16[256,256]{1,0:T(8,128)(2,1)S(1)}, bf16[256,256]{1,0:T(8,128)(2,1)S(1)}, u32[]{:S(2)}, u32[]{:S(2)}) %collective-permute-start.13) | collective-permute-done | bytes 131104 | tf_op jit(solution)/shard_map/ppermute | solution.py:417
  64.6 9.2 %all_to_all.11 = f32[8,1,128]{2,1,0:T(1,128)S(1)} all-to-all(f32[8,1,128]{2,1,0:T(1,128)S(1)} %bitcast.27), channel_id=1, replica_groups=mesh['groups'=2,'blk'=4,'mpo'=2,'rep'=2] {'blk','rep'}, dimensions={0} | all-to-all | bytes 8192 | tf_op jit(solution)/shard_map/all_to_all | solution.py:422
  73.7 1.4 %final.1 = (bf16[3,1,128,256]{3,2,1,0:T(8,128)(2,1)}, f32[2,3]{1,0:T(2,128)}) custom-call(f32[8,128]{1,0:T(8,128)S(1)} %bitcast.26, f32[256,256]{1,0:T(8,128)S(1)} %get-tuple-element.32.r_ref, f32[256,256]{1,0:T(8,128)S(1)} %get-tuple-element.33.z_ref, f32[256,256]{1,0:T(8,128)S(1)} %get-tuple-element.29.refs_5_.w_ref, ...), custom_call_target="tpu_custom_call" | custom-call | bytes 262144 | tf_op jit(solution)/shard_map/final/pallas_call | solution.py:365
  (28 shorter events, 9.5 us)
Async XLA Ops:
  0.6 13.1 %collective-permute-start.1 = (bf16[256,256]{1,0:T(8,128)(2,1)}, bf16[256,256]{1,0:T(8,128)(2,1)S(1)}, u32[]{:S(2)}, u32[]{:S(2)}) collective-permute-start(bf16[256,256]{1,0:T(8,128)(2,1)} %bitcast.19), channel_id=1, source_target_pairs={{12,1},{9,4},{4,9},{1,12},{14,3},{11,6},{6,11},{3,14},{28,17},{25,... | collective-permute-start | bytes 393224 | tf_op jit(solution)/shard_map/ppermute | solution.py:405
  1.3 15.3 %collective-permute-start = (bf16[256,256]{1,0:T(8,128)(2,1)}, bf16[256,256]{1,0:T(8,128)(2,1)S(1)}, u32[]{:S(2)}, u32[]{:S(2)}) collective-permute-start(bf16[256,256]{1,0:T(8,128)(2,1)} %bitcast.20), channel_id=1, source_target_pairs={{9,0},{8,1},{13,4},{12,5},{1,8},{0,9},{5,12},{4,13},{11,2},{10,3},... | collective-permute-start | bytes 393224 | tf_op jit(solution)/shard_map/ppermute | solution.py:405
  6.8 1.9 %copy-start = (bf16[24,1,256,256]{3,2,1,0:T(8,128)(2,1)S(1)}, bf16[24,1,256,256]{3,2,1,0:T(8,128)(2,1)}, u32[]{:S(2)}) copy-start(bf16[24,1,256,256]{3,2,1,0:T(8,128)(2,1)} %param.5) | copy-start | bytes 9437188
  8.7 1.9 %copy-start.1 = (bf16[24,1,256,256]{3,2,1,0:T(8,128)(2,1)S(1)}, bf16[24,1,256,256]{3,2,1,0:T(8,128)(2,1)}, u32[]{:S(2)}) copy-start(bf16[24,1,256,256]{3,2,1,0:T(8,128)(2,1)} %param.6) | copy-start | bytes 9437188
  10.6 0.9 %copy-start.2 = (bf16[1,256,256]{2,1,0:T(8,128)(2,1)S(1)}, bf16[1,256,256]{2,1,0:T(8,128)(2,1)}, u32[]{:S(2)}) copy-start(bf16[1,256,256]{2,1,0:T(8,128)(2,1)} %param.4) | copy-start | bytes 393220
  11.5 0.7 copy-start.4
  17.7 6.0 %collective-permute-start.2 = (bf16[256,256]{1,0:T(8,128)(2,1)S(1)}, bf16[256,256]{1,0:T(8,128)(2,1)S(1)}, u32[]{:S(2)}, u32[]{:S(2)}) collective-permute-start(bf16[256,256]{1,0:T(8,128)(2,1)S(1)} %get-tuple-element.18.refs_0_), channel_id=1, source_target_pairs={{0,2},{2,0},{1,3},{3,1},{4,6},{6,4},{5,7},{7,5},{8,10},{10,8},{9,1... | collective-permute-start | bytes 393224 | tf_op jit(solution)/shard_map/ppermute | solution.py:417
  24.1 14.9 %collective-permute-start.5 = (bf16[256,256]{1,0:T(8,128)(2,1)S(1)}, bf16[256,256]{1,0:T(8,128)(2,1)S(1)}, u32[]{:S(2)}, u32[]{:S(2)}) collective-permute-start(bf16[256,256]{1,0:T(8,128)(2,1)S(1)} %get-tuple-element.20.block_ref.refs_4_.refs_3_), channel_id=1, source_target_pairs={{12,1},{9,4},{4,9},{1,12},{14,3},{11,6},{6,11},{3,14},{28,17},{25,... | collective-permute-start | bytes 393224 | tf_op jit(solution)/shard_map/ppermute | solution.py:405
  24.7 8.1 %collective-permute-start.3 = (bf16[128,256]{1,0:T(8,128)(2,1)S(1)}, bf16[128,256]{1,0:T(8,128)(2,1)S(1)}, u32[]{:S(2)}, u32[]{:S(2)}) collective-permute-start(bf16[128,256]{1,0:T(8,128)(2,1)S(1)} %get-tuple-element.21), channel_id=1, source_target_pairs={{9,0},{8,1},{13,4},{12,5},{1,8},{0,9},{5,12},{4,13},{11,2},{10,3},... | collective-permute-start | bytes 196616 | tf_op jit(solution)/shard_map/ppermute | solution.py:405
  32.9 6.1 %collective-permute-start.4 = (bf16[128,256]{1,0:T(8,128)(2,1)S(1)}, bf16[128,256]{1,0:T(8,128)(2,1)S(1)}, u32[]{:S(2)}, u32[]{:S(2)}) collective-permute-start(bf16[128,256]{1,0:T(8,128)(2,1)S(1)} %collective-permute-done.3.refs_5_), channel_id=1, source_target_pairs={{0,2},{2,0},{1,3},{3,1},{4,6},{6,4},{5,7},{7,5},{8,10},{10,8},{9,1... | collective-permute-start | bytes 196616 | tf_op jit(solution)/shard_map/ppermute | solution.py:410
  34.1 1.2 %collective-permute-start.6 = (f32[8,128]{1,0:T(8,128)S(1)}, f32[8,128]{1,0:T(8,128)S(1)}, u32[]{:S(2)}, u32[]{:S(2)}) collective-permute-start(f32[8,128]{1,0:T(8,128)S(1)} %get-tuple-element.22), channel_id=1, source_target_pairs={{0,1},{1,0},{2,3},{3,2},{4,5},{5,4},{6,7},{7,6},{8,9},{9,8},{10,11... | collective-permute-start | bytes 12296 | tf_op jit(solution)/shard_map/ppermute | solution.py:436
  35.3 3.6 %collective-permute-start.7 = (f32[8,128]{1,0:T(8,128)S(1)}, f32[8,128]{1,0:T(8,128)S(1)}, u32[]{:S(2)}, u32[]{:S(2)}) collective-permute-start(f32[8,128]{1,0:T(8,128)S(1)} %add.9), channel_id=1, source_target_pairs={{0,4},{4,0},{8,12},{12,8},{1,5},{5,1},{9,13},{13,9},{2,6},{6,2},{1... | collective-permute-start | bytes 12296 | tf_op jit(solution)/shard_map/ppermute | solution.py:436
  38.9 7.0 %copy-start.3 = (bf16[1,256,256]{2,1,0:T(8,128)(2,1)S(1)}, bf16[1,256,256]{2,1,0:T(8,128)(2,1)}, u32[]{:S(2)}) copy-start(bf16[1,256,256]{2,1,0:T(8,128)(2,1)} %param.4) | copy-start | bytes 393220
  40.1 5.8 %collective-permute-start.8 = (bf16[256,256]{1,0:T(8,128)(2,1)S(1)}, bf16[256,256]{1,0:T(8,128)(2,1)S(1)}, u32[]{:S(2)}, u32[]{:S(2)}) collective-permute-start(bf16[256,256]{1,0:T(8,128)(2,1)S(1)} %get-tuple-element.23.refs_0_), channel_id=1, source_target_pairs={{0,2},{2,0},{1,3},{3,1},{4,6},{6,4},{5,7},{7,5},{8,10},{10,8},{9,1... | collective-permute-start | bytes 393224 | tf_op jit(solution)/shard_map/ppermute | solution.py:417
  41.4 4.5 %collective-permute-start.9 = (f32[8,128]{1,0:T(8,128)S(1)}, f32[8,128]{1,0:T(8,128)S(1)}, u32[]{:S(2)}, u32[]{:S(2)}) collective-permute-start(f32[8,128]{1,0:T(8,128)S(1)} %get-tuple-element.24), channel_id=1, source_target_pairs={{0,8},{4,12},{8,0},{12,4},{1,9},{5,13},{9,1},{13,5},{2,10},{6,14},... | collective-permute-start | bytes 12296 | tf_op jit(solution)/shard_map/ppermute | solution.py:436
  46.8 6.3 %collective-permute-start.10 = (bf16[128,256]{1,0:T(8,128)(2,1)S(1)}, bf16[128,256]{1,0:T(8,128)(2,1)S(1)}, u32[]{:S(2)}, u32[]{:S(2)}) collective-permute-start(bf16[128,256]{1,0:T(8,128)(2,1)S(1)} %get-tuple-element.27), channel_id=1, source_target_pairs={{9,0},{8,1},{13,4},{12,5},{1,8},{0,9},{5,12},{4,13},{11,2},{10,3},... | collective-permute-start | bytes 196616 | tf_op jit(solution)/shard_map/ppermute | solution.py:405
  47.6 9.7 %collective-permute-start.12 = (bf16[256,256]{1,0:T(8,128)(2,1)S(1)}, bf16[256,256]{1,0:T(8,128)(2,1)S(1)}, u32[]{:S(2)}, u32[]{:S(2)}) collective-permute-start(bf16[256,256]{1,0:T(8,128)(2,1)S(1)} %get-tuple-element.26.block_ref), channel_id=1, source_target_pairs={{12,1},{9,4},{4,9},{1,12},{14,3},{11,6},{6,11},{3,14},{28,17},{25,... | collective-permute-start | bytes 393224 | tf_op jit(solution)/shard_map/ppermute | solution.py:405
  53.0 4.3 %collective-permute-start.11 = (bf16[128,256]{1,0:T(8,128)(2,1)S(1)}, bf16[128,256]{1,0:T(8,128)(2,1)S(1)}, u32[]{:S(2)}, u32[]{:S(2)}) collective-permute-start(bf16[128,256]{1,0:T(8,128)(2,1)S(1)} %collective-permute-done.10.refs_4_), channel_id=1, source_target_pairs={{0,2},{2,0},{1,3},{3,1},{4,6},{6,4},{5,7},{7,5},{8,10},{10,8},{9,1... | collective-permute-start | bytes 196616 | tf_op jit(solution)/shard_map/ppermute | solution.py:410
  58.4 5.5 %collective-permute-start.13 = (bf16[256,256]{1,0:T(8,128)(2,1)S(1)}, bf16[256,256]{1,0:T(8,128)(2,1)S(1)}, u32[]{:S(2)}, u32[]{:S(2)}) collective-permute-start(bf16[256,256]{1,0:T(8,128)(2,1)S(1)} %rest.5.refs_0_), channel_id=1, source_target_pairs={{0,2},{2,0},{1,3},{3,1},{4,6},{6,4},{5,7},{7,5},{8,10},{10,8},{9,1... | collective-permute-start | bytes 393224 | tf_op jit(solution)/shard_map/ppermute | solution.py:417

commit v7 on v6

--- a/solution.py
+++ b/solution.py
@@ -229,6 +229,10 @@
     t_ref[...] = acc[...].astype(jnp.bfloat16)
 
 
+def pass_kernel(block_ref, rows_ref, out_ref):
+    out_ref[...] = block_ref[...]
+
+
 def my_rows(share):
     return pl.ds(pl.multiple_of(lax.axis_index("mpo") * share, share), share)
 
@@ -355,6 +359,7 @@
     scalars = jax.ShapeDtypeStruct((8, 128), jnp.float32)
     wide = jax.ShapeDtypeStruct((width, width), jnp.float32)
     narrow = jax.ShapeDtypeStruct((width, width), jnp.bfloat16)
+    share_shape = jax.ShapeDtypeStruct((width // parts, width), jnp.bfloat16)
     lists = [pltpu.SMEM((channels + WIDE,), jnp.int32)] * 2
 
     def call(kernel, name, outs, args, scratch=(), share=0, limit=4):
@@ -404,23 +409,6 @@
     def shift(block, pairs):
         return lax.ppermute(block, ring, pairs)
 
-    def spread(block, share):
-        piece = shift(share, permutes[0])
-        if parts == 2:
-            first = [piece, lax.ppermute(piece, "mpo", [(0, 1), (1, 0)])]
-        else:
-            first = [lax.all_gather(piece, "mpo", axis=0, tiled=True)]
-        return first, [shift(block, pairs) for pairs in permutes[1:]]
-
-    def gather_parts(t):
-        if parts == 2:
-            return [t, lax.ppermute(t, "mpo", [(0, 1), (1, 0)])]
-        held = lax.all_gather(t, "mpo")
-        return [held[i] for i in range(parts)]
-
-    def exchange(rows):
-        return lax.all_to_all(rows, ring, 0, 0, tiled=True)
-
     rounds = []
     for axis in ("rep", "blk"):
         size = lax.axis_size(axis)
@@ -435,24 +423,43 @@
             return lax.psum(rows, axis)
         return rows + lax.ppermute(rows, axis, pairs)
 
-    share = jax.ShapeDtypeStruct((width // parts, width), jnp.bfloat16)
+    def spread(block, share, rows=None):
+        piece = shift(share, permutes[0])
+        if rows is not None:
+            for step in rounds[:-1]:
+                rows = add_round(rows, *step)
+            piece = call(pass_kernel, "hold", share_shape, (piece, rows))
+        if parts == 2:
+            first = [piece, lax.ppermute(piece, "mpo", [(0, 1), (1, 0)])]
+        else:
+            first = [lax.all_gather(piece, "mpo", axis=0, tiled=True)]
+        return first, [shift(block, pairs) for pairs in permutes[1:]], rows
+
+    def gather_parts(t):
+        if parts == 2:
+            return [t, lax.ppermute(t, "mpo", [(0, 1), (1, 0)])]
+        held = lax.all_gather(t, "mpo")
+        return [held[i] for i in range(parts)]
+
+    def exchange(rows):
+        return lax.all_to_all(rows, ring, 0, 0, tiled=True)
+
     held = [shift(psi, pairs) for pairs in permutes]
     t, unit = rest(own(True, psi), held[:1], held[1:], psi)
     w_1, share_1, rows = call(
-        first_sums_kernel, "sums", (narrow, share, rows_shape), (*gather_parts(t), psi, unit)
+        first_sums_kernel, "sums", (narrow, share_shape, rows_shape), (*gather_parts(t), psi, unit)
     )
-    held = spread(w_1, share_1)
-    for step in rounds[:-1]:
-        rows = add_round(rows, *step)
-    t, unit, rows = rest(own(True, w_1), *held, w_1, rows)
+    first, others, rows = spread(w_1, share_1, rows)
+    t, unit, rows = rest(own(True, w_1), first, others, w_1, rows)
     rows = add_round(rows, *rounds[-1])
     w_wide, w_2, share_2, v_2, scal = call(
         functools.partial(second_sums_kernel, entries),
         "sums",
-        (wide, narrow, share, narrow, scalars),
+        (wide, narrow, share_shape, narrow, scalars),
         (*gather_parts(t), rows, psi, w_1, unit),
     )
-    (t,) = rest(own(False, w_2), *spread(w_2, share_2))
+    first, others, _ = spread(w_2, share_2)
+    (t,) = rest(own(False, w_2), first, others)
     r, z, rows = call(
         third_sums_kernel,
         "sums",

time: 75.3 us -> 73.9 us (0.981)
  waiting for transfers between devices: 29.7 us -> 25 us
  starting transfers between devices: 19 us -> 21.5 us
    ppermute x6, waiting for transfers between devices: 13.8 us -> 6.72 us  [shift(): return lax.ppermute(block, ring, pairs)]
    ppermute x3, starting transfers between devices: 1.44 us -> 6.02 us  [add_round(): return rows + lax.ppermute(rows, axis, pairs)]
    ppermute x6, starting transfers between devices: 10.4 us -> 7.59 us  [shift(): return lax.ppermute(block, ring, pairs)]
    ppermute x3, waiting for transfers between devices: 7.89 us -> 9.3 us  [gather_parts(): return [t, lax.ppermute(t, 'mpo', [(0, 1), (1, 0)])]]
    ppermute x3, starting transfers between devices: 4.87 us -> 5.97 us  [gather_parts(): return [t, lax.ppermute(t, 'mpo', [(0, 1), (1, 0)])]]
    ppermute x2, waiting for transfers between devices: 1.73 us -> 2.56 us  [spread(): first = [piece, lax.ppermute(piece, 'mpo', [(0, 1), (1, 0)])]]
    pallas_call x10 -> x11, Pallas kernels: 11.2 us -> 11.7 us  [call(): pl.pallas_call(kernel, out_shape=outs, in_specs=[first] + [VMEM] * (len(a...]
  transfers between devices with their start and end apart: 14 -> 14, of which waited for: 9 -> 9; matrix products, arithmetic and copies ran while one was open for 0% -> 0% of each run, Pallas kernels for 6% -> 8%
where the time goes in v7:
time: 73.9 us; the launch traced here: 73.6 us
  waiting for transfers between devices  25 us (34%)
  starting transfers between devices  21.5 us (29%)
  Pallas kernels  11.7 us (16%)
  blocking collectives  9.22 us (12%)
  local copies, waits for them, and re-layouts  5.34 us (7%)
  between operations  0.77 us (1%)
    pallas_call x11, Pallas kernels, call(): pl.pallas_call(kernel, out_shape=outs, in_specs=[first] + [VMEM] * (len(a...  11.7 us
    ppermute x3, waiting for transfers between devices, gather_parts(): return [t, lax.ppermute(t, 'mpo', [(0, 1), (1, 0)])]  9.3 us
    all_to_all x1, blocking collectives, exchange(): return lax.all_to_all(rows, ring, 0, 0, tiled=True)  9.22 us
    ppermute x6, starting transfers between devices, shift(): return lax.ppermute(block, ring, pairs)  7.59 us
    ppermute x6, waiting for transfers between devices, shift(): return lax.ppermute(block, ring, pairs)  6.72 us
    ppermute x3, waiting for transfers between devices, add_round(): return rows + lax.ppermute(rows, axis, pairs)  6.45 us
    ppermute x3, starting transfers between devices, add_round(): return rows + lax.ppermute(rows, axis, pairs)  6.02 us
    ppermute x3, starting transfers between devices, gather_parts(): return [t, lax.ppermute(t, 'mpo', [(0, 1), (1, 0)])]  5.97 us
  transfers between devices with their start and end apart: 14, of which 9 were waited for; matrix products, arithmetic and copies ran while one was open for 0% of the time, Pallas kernels for 8%

profile of v7, /device:TPU:0, one launch (start us, length us, event | category | flops | bytes accessed | tf_op | source)
XLA Modules:
  0.0 73.6 jit_solution(7118608517526652907)
XLA Ops:
  1.3 5.5 %collective-permute-start = (bf16[256,256]{1,0:T(8,128)(2,1)}, bf16[256,256]{1,0:T(8,128)(2,1)S(1)}, u32[]{:S(2)}, u32[]{:S(2)}) collective-permute-start(bf16[256,256]{1,0:T(8,128)(2,1)} %bitcast.20), channel_id=1, source_target_pairs={{9,0},{8,1},{13,4},{12,5},{1,8},{0,9},{5,12},{4,13},{11,2},{10,3},... | collective-permute-start | bytes 393224 | tf_op jit(solution)/shard_map/ppermute | solution.py:410
  6.8 1.9 %copy-done = bf16[24,1,256,256]{3,2,1,0:T(8,128)(2,1)S(1)} copy-done((bf16[24,1,256,256]{3,2,1,0:T(8,128)(2,1)S(1)}, bf16[24,1,256,256]{3,2,1,0:T(8,128)(2,1)}, u32[]{:S(2)}) %copy-start) | copy-done | bytes 3145752
  8.7 1.9 %copy-done.1 = bf16[24,1,256,256]{3,2,1,0:T(8,128)(2,1)S(1)} copy-done((bf16[24,1,256,256]{3,2,1,0:T(8,128)(2,1)S(1)}, bf16[24,1,256,256]{3,2,1,0:T(8,128)(2,1)}, u32[]{:S(2)}) %copy-start.1) | copy-done | bytes 3145752
  10.6 0.9 %copy-done.2 = bf16[1,256,256]{2,1,0:T(8,128)(2,1)S(1)} copy-done((bf16[1,256,256]{2,1,0:T(8,128)(2,1)S(1)}, bf16[1,256,256]{2,1,0:T(8,128)(2,1)}, u32[]{:S(2)}) %copy-start.2) | copy-done | bytes 131096
  12.2 2.1 %own.3.refs_3_ = f32[256,256]{1,0:T(8,128)S(1)} custom-call(s32[24]{0:T(128)S(1)} %copy-done.4, bf16[24,256,256]{2,1,0:T(8,128)(2,1)S(1)} %bitcast.7, bf16[24,256,256]{2,1,0:T(8,128)(2,1)S(1)} %bitcast.13, bf16[256,256]{1,0:T(8,128)(2,1)S(1)} %bitcast.21), custom_call_target="tpu_custom_call" | custom-call | flops 322122560 | bytes 262144 | tf_op jit(solution)/shard_map/own/pallas_call | solution.py:370
  14.2 2.4 %collective-permute-done.refs_5_ = bf16[256,256]{1,0:T(8,128)(2,1)S(1)} collective-permute-done((bf16[256,256]{1,0:T(8,128)(2,1)}, bf16[256,256]{1,0:T(8,128)(2,1)S(1)}, u32[]{:S(2)}, u32[]{:S(2)}) %collective-permute-start) | collective-permute-done | bytes 131104 | tf_op jit(solution)/shard_map/ppermute | solution.py:410
  17.4 2.4 %collective-permute-start.2 = (bf16[256,256]{1,0:T(8,128)(2,1)S(1)}, bf16[256,256]{1,0:T(8,128)(2,1)S(1)}, u32[]{:S(2)}, u32[]{:S(2)}) collective-permute-start(bf16[256,256]{1,0:T(8,128)(2,1)S(1)} %get-tuple-element.18.refs_0_), channel_id=1, source_target_pairs={{0,2},{2,0},{1,3},{3,1},{4,6},{6,4},{5,7},{7,5},{8,10},{10,8},{9,1... | collective-permute-start | bytes 393224 | tf_op jit(solution)/shard_map/ppermute | solution.py:440
  19.8 4.2 %collective-permute-done.2.refs_1_ = bf16[256,256]{1,0:T(8,128)(2,1)S(1)} collective-permute-done((bf16[256,256]{1,0:T(8,128)(2,1)S(1)}, bf16[256,256]{1,0:T(8,128)(2,1)S(1)}, u32[]{:S(2)}, u32[]{:S(2)}) %collective-permute-start.2) | collective-permute-done | bytes 131104 | tf_op jit(solution)/shard_map/ppermute | solution.py:440
  25.0 3.4 %collective-permute-start.4 = (f32[8,128]{1,0:T(8,128)S(1)}, f32[8,128]{1,0:T(8,128)S(1)}, u32[]{:S(2)}, u32[]{:S(2)}) collective-permute-start(f32[8,128]{1,0:T(8,128)S(1)} %get-tuple-element.22), channel_id=1, source_target_pairs={{0,1},{1,0},{2,3},{3,2},{4,5},{5,4},{6,7},{7,6},{8,9},{9,8},{10,11... | collective-permute-start | bytes 12296 | tf_op jit(solution)/shard_map/ppermute | solution.py:424
  29.3 1.4 %collective-permute-start.5 = (f32[8,128]{1,0:T(8,128)S(1)}, f32[8,128]{1,0:T(8,128)S(1)}, u32[]{:S(2)}, u32[]{:S(2)}) collective-permute-start(f32[8,128]{1,0:T(8,128)S(1)} %add.9), channel_id=1, source_target_pairs={{0,4},{4,0},{8,12},{12,8},{1,5},{5,1},{9,13},{13,9},{2,6},{6,2},{1... | collective-permute-start | bytes 12296 | tf_op jit(solution)/shard_map/ppermute | solution.py:424
  30.7 2.3 %collective-permute-done.5 = f32[8,128]{1,0:T(8,128)S(1)} collective-permute-done((f32[8,128]{1,0:T(8,128)S(1)}, f32[8,128]{1,0:T(8,128)S(1)}, u32[]{:S(2)}, u32[]{:S(2)}) %collective-permute-start.5) | collective-permute-done | bytes 4128 | tf_op jit(solution)/shard_map/ppermute | solution.py:424
  33.0 1.4 %collective-permute-start.6 = (bf16[128,256]{1,0:T(8,128)(2,1)S(1)}, bf16[128,256]{1,0:T(8,128)(2,1)S(1)}, u32[]{:S(2)}, u32[]{:S(2)}) collective-permute-start(bf16[128,256]{1,0:T(8,128)(2,1)S(1)} %hold.1.refs_5_), channel_id=1, source_target_pairs={{0,2},{2,0},{1,3},{3,1},{4,6},{6,4},{5,7},{7,5},{8,10},{10,8},{9,1... | collective-permute-start | bytes 196616 | tf_op jit(solution)/shard_map/ppermute | solution.py:433
  34.5 2.1 %own.4.refs_3_ = f32[256,256]{1,0:T(8,128)S(1)} custom-call(s32[24]{0:T(128)S(1)} %copy-done.4, bf16[24,256,256]{2,1,0:T(8,128)(2,1)S(1)} %bitcast.9, bf16[24,256,256]{2,1,0:T(8,128)(2,1)S(1)} %bitcast.15, bf16[256,256]{1,0:T(8,128)(2,1)S(1)} %get-tuple-element.20.block_ref.refs_4_.refs_3_), custom_call_target="tpu_custom_call" | custom-call | flops 322122560 | bytes 262144 | tf_op jit(solution)/shard_map/own/pallas_call | solution.py:370
  38.2 2.3 %collective-permute-start.8 = (bf16[256,256]{1,0:T(8,128)(2,1)S(1)}, bf16[256,256]{1,0:T(8,128)(2,1)S(1)}, u32[]{:S(2)}, u32[]{:S(2)}) collective-permute-start(bf16[256,256]{1,0:T(8,128)(2,1)S(1)} %get-tuple-element.23.refs_0_), channel_id=1, source_target_pairs={{0,2},{2,0},{1,3},{3,1},{4,6},{6,4},{5,7},{7,5},{8,10},{10,8},{9,1... | collective-permute-start | bytes 393224 | tf_op jit(solution)/shard_map/ppermute | solution.py:440
  40.4 1.2 %collective-permute-start.9 = (f32[8,128]{1,0:T(8,128)S(1)}, f32[8,128]{1,0:T(8,128)S(1)}, u32[]{:S(2)}, u32[]{:S(2)}) collective-permute-start(f32[8,128]{1,0:T(8,128)S(1)} %get-tuple-element.24), channel_id=1, source_target_pairs={{0,8},{4,12},{8,0},{12,4},{1,9},{5,13},{9,1},{13,5},{2,10},{6,14},... | collective-permute-start | bytes 12296 | tf_op jit(solution)/shard_map/ppermute | solution.py:424
  41.6 3.3 %collective-permute-done.9 = f32[8,128]{1,0:T(8,128)S(1)} collective-permute-done((f32[8,128]{1,0:T(8,128)S(1)}, f32[8,128]{1,0:T(8,128)S(1)}, u32[]{:S(2)}, u32[]{:S(2)}) %collective-permute-start.9) | collective-permute-done | bytes 4128 | tf_op jit(solution)/shard_map/ppermute | solution.py:424
  44.9 0.9 %sums.4 = (f32[256,256]{1,0:T(8,128)S(1)}, bf16[256,256]{1,0:T(8,128)(2,1)S(1)}, bf16[128,256]{1,0:T(8,128)(2,1)S(1)}, bf16[256,256]{1,0:T(8,128)(2,1)S(1)}, f32[8,128]{1,0:T(8,128)S(1)}) custom-call(bf16[256,256]{1,0:T(8,128)(2,1)S(1)} %get-tuple-element.23.refs_0_, bf16[256,256]{1,0:T(8,128)(2,1)S(1)} %collective-permute-done.8.refs_1_, ...), custom_call_target="tpu_custom_call" | custom-call | bytes 262144 | tf_op jit(solution)/shard_map/sums/pallas_call | solution.py:370
  46.6 4.3 %collective-permute-done.10.refs_4_ = bf16[128,256]{1,0:T(8,128)(2,1)S(1)} collective-permute-done((bf16[128,256]{1,0:T(8,128)(2,1)S(1)}, bf16[128,256]{1,0:T(8,128)(2,1)S(1)}, u32[]{:S(2)}, u32[]{:S(2)}) %collective-permute-start.10) | collective-permute-done | bytes 65568 | tf_op jit(solution)/shard_map/ppermute | solution.py:410
  51.3 2.1 %own.5.refs_3_ = f32[256,256]{1,0:T(8,128)S(1)} custom-call(s32[24]{0:T(128)S(1)} %copy-done.4, bf16[24,256,256]{2,1,0:T(8,128)(2,1)S(1)} %bitcast.11, bf16[24,256,256]{2,1,0:T(8,128)(2,1)S(1)} %bitcast.17, bf16[256,256]{1,0:T(8,128)(2,1)S(1)} %get-tuple-element.26.block_ref), custom_call_target="tpu_custom_call" | custom-call | flops 322122560 | bytes 262144 | tf_op jit(solution)/shard_map/own/pallas_call | solution.py:370
  53.4 1.8 %collective-permute-done.11.refs_5_ = bf16[128,256]{1,0:T(8,128)(2,1)S(1)} collective-permute-done((bf16[128,256]{1,0:T(8,128)(2,1)S(1)}, bf16[128,256]{1,0:T(8,128)(2,1)S(1)}, u32[]{:S(2)}, u32[]{:S(2)}) %collective-permute-start.11) | collective-permute-done | bytes 65568 | tf_op jit(solution)/shard_map/ppermute | solution.py:433
  55.9 1.3 %collective-permute-start.13 = (bf16[256,256]{1,0:T(8,128)(2,1)S(1)}, bf16[256,256]{1,0:T(8,128)(2,1)S(1)}, u32[]{:S(2)}, u32[]{:S(2)}) collective-permute-start(bf16[256,256]{1,0:T(8,128)(2,1)S(1)} %rest.5.refs_0_), channel_id=1, source_target_pairs={{0,2},{2,0},{1,3},{3,1},{4,6},{6,4},{5,7},{7,5},{8,10},{10,8},{9,1... | collective-permute-start | bytes 393224 | tf_op jit(solution)/shard_map/ppermute | solution.py:440
  57.3 5.1 %collective-permute-done.13.refs_1_ = bf16[256,256]{1,0:T(8,128)(2,1)S(1)} collective-permute-done((bf16[256,256]{1,0:T(8,128)(2,1)S(1)}, bf16[256,256]{1,0:T(8,128)(2,1)S(1)}, u32[]{:S(2)}, u32[]{:S(2)}) %collective-permute-start.13) | collective-permute-done | bytes 131104 | tf_op jit(solution)/shard_map/ppermute | solution.py:440
  63.0 9.2 %all_to_all.11 = f32[8,1,128]{2,1,0:T(1,128)S(1)} all-to-all(f32[8,1,128]{2,1,0:T(1,128)S(1)} %bitcast.27), channel_id=1, replica_groups=mesh['groups'=2,'blk'=4,'mpo'=2,'rep'=2] {'blk','rep'}, dimensions={0} | all-to-all | bytes 8192 | tf_op jit(solution)/shard_map/all_to_all | solution.py:445
  72.2 1.4 %final.1 = (bf16[3,1,128,256]{3,2,1,0:T(8,128)(2,1)}, f32[2,3]{1,0:T(2,128)}) custom-call(f32[8,128]{1,0:T(8,128)S(1)} %bitcast.26, f32[256,256]{1,0:T(8,128)S(1)} %get-tuple-element.32.r_ref, f32[256,256]{1,0:T(8,128)S(1)} %get-tuple-element.33.z_ref, f32[256,256]{1,0:T(8,128)S(1)} %get-tuple-element.29.refs_5_.w_ref, ...), custom_call_target="tpu_custom_call" | custom-call | bytes 262144 | tf_op jit(solution)/shard_map/final/pallas_call | solution.py:370
  (29 shorter events, 8.1 us)
Async XLA Ops:
  0.6 13.6 %collective-permute-start.1 = (bf16[256,256]{1,0:T(8,128)(2,1)}, bf16[256,256]{1,0:T(8,128)(2,1)S(1)}, u32[]{:S(2)}, u32[]{:S(2)}) collective-permute-start(bf16[256,256]{1,0:T(8,128)(2,1)} %bitcast.19), channel_id=1, source_target_pairs={{12,1},{9,4},{4,9},{1,12},{14,3},{11,6},{6,11},{3,14},{28,17},{25,... | collective-permute-start | bytes 393224 | tf_op jit(solution)/shard_map/ppermute | solution.py:410
  1.3 15.3 %collective-permute-start = (bf16[256,256]{1,0:T(8,128)(2,1)}, bf16[256,256]{1,0:T(8,128)(2,1)S(1)}, u32[]{:S(2)}, u32[]{:S(2)}) collective-permute-start(bf16[256,256]{1,0:T(8,128)(2,1)} %bitcast.20), channel_id=1, source_target_pairs={{9,0},{8,1},{13,4},{12,5},{1,8},{0,9},{5,12},{4,13},{11,2},{10,3},... | collective-permute-start | bytes 393224 | tf_op jit(solution)/shard_map/ppermute | solution.py:410
  6.8 1.9 %copy-start = (bf16[24,1,256,256]{3,2,1,0:T(8,128)(2,1)S(1)}, bf16[24,1,256,256]{3,2,1,0:T(8,128)(2,1)}, u32[]{:S(2)}) copy-start(bf16[24,1,256,256]{3,2,1,0:T(8,128)(2,1)} %param.5) | copy-start | bytes 9437188
  8.7 1.9 %copy-start.1 = (bf16[24,1,256,256]{3,2,1,0:T(8,128)(2,1)S(1)}, bf16[24,1,256,256]{3,2,1,0:T(8,128)(2,1)}, u32[]{:S(2)}) copy-start(bf16[24,1,256,256]{3,2,1,0:T(8,128)(2,1)} %param.6) | copy-start | bytes 9437188
  10.6 0.9 %copy-start.2 = (bf16[1,256,256]{2,1,0:T(8,128)(2,1)S(1)}, bf16[1,256,256]{2,1,0:T(8,128)(2,1)}, u32[]{:S(2)}) copy-start(bf16[1,256,256]{2,1,0:T(8,128)(2,1)} %param.4) | copy-start | bytes 393220
  11.5 0.7 copy-start.4
  17.4 6.6 %collective-permute-start.2 = (bf16[256,256]{1,0:T(8,128)(2,1)S(1)}, bf16[256,256]{1,0:T(8,128)(2,1)S(1)}, u32[]{:S(2)}, u32[]{:S(2)}) collective-permute-start(bf16[256,256]{1,0:T(8,128)(2,1)S(1)} %get-tuple-element.18.refs_0_), channel_id=1, source_target_pairs={{0,2},{2,0},{1,3},{3,1},{4,6},{6,4},{5,7},{7,5},{8,10},{10,8},{9,1... | collective-permute-start | bytes 393224 | tf_op jit(solution)/shard_map/ppermute | solution.py:440
  24.4 8.7 %collective-permute-start.3 = (bf16[128,256]{1,0:T(8,128)(2,1)S(1)}, bf16[128,256]{1,0:T(8,128)(2,1)S(1)}, u32[]{:S(2)}, u32[]{:S(2)}) collective-permute-start(bf16[128,256]{1,0:T(8,128)(2,1)S(1)} %get-tuple-element.21), channel_id=1, source_target_pairs={{9,0},{8,1},{13,4},{12,5},{1,8},{0,9},{5,12},{4,13},{11,2},{10,3},... | collective-permute-start | bytes 196616 | tf_op jit(solution)/shard_map/ppermute | solution.py:410
  24.4 12.2 %collective-permute-start.7 = (bf16[256,256]{1,0:T(8,128)(2,1)S(1)}, bf16[256,256]{1,0:T(8,128)(2,1)S(1)}, u32[]{:S(2)}, u32[]{:S(2)}) collective-permute-start(bf16[256,256]{1,0:T(8,128)(2,1)S(1)} %get-tuple-element.20.block_ref.refs_4_.refs_3_), channel_id=1, source_target_pairs={{12,1},{9,4},{4,9},{1,12},{14,3},{11,6},{6,11},{3,14},{28,17},{25,... | collective-permute-start | bytes 393224 | tf_op jit(solution)/shard_map/ppermute | solution.py:410
  25.0 4.2 %collective-permute-start.4 = (f32[8,128]{1,0:T(8,128)S(1)}, f32[8,128]{1,0:T(8,128)S(1)}, u32[]{:S(2)}, u32[]{:S(2)}) collective-permute-start(f32[8,128]{1,0:T(8,128)S(1)} %get-tuple-element.22), channel_id=1, source_target_pairs={{0,1},{1,0},{2,3},{3,2},{4,5},{5,4},{6,7},{7,6},{8,9},{9,8},{10,11... | collective-permute-start | bytes 12296 | tf_op jit(solution)/shard_map/ppermute | solution.py:424
  29.3 3.7 %collective-permute-start.5 = (f32[8,128]{1,0:T(8,128)S(1)}, f32[8,128]{1,0:T(8,128)S(1)}, u32[]{:S(2)}, u32[]{:S(2)}) collective-permute-start(f32[8,128]{1,0:T(8,128)S(1)} %add.9), channel_id=1, source_target_pairs={{0,4},{4,0},{8,12},{12,8},{1,5},{5,1},{9,13},{13,9},{2,6},{6,2},{1... | collective-permute-start | bytes 12296 | tf_op jit(solution)/shard_map/ppermute | solution.py:424
  33.0 4.3 %collective-permute-start.6 = (bf16[128,256]{1,0:T(8,128)(2,1)S(1)}, bf16[128,256]{1,0:T(8,128)(2,1)S(1)}, u32[]{:S(2)}, u32[]{:S(2)}) collective-permute-start(bf16[128,256]{1,0:T(8,128)(2,1)S(1)} %hold.1.refs_5_), channel_id=1, source_target_pairs={{0,2},{2,0},{1,3},{3,1},{4,6},{6,4},{5,7},{7,5},{8,10},{10,8},{9,1... | collective-permute-start | bytes 196616 | tf_op jit(solution)/shard_map/ppermute | solution.py:433
  36.5 8.4 %copy-start.3 = (bf16[1,256,256]{2,1,0:T(8,128)(2,1)S(1)}, bf16[1,256,256]{2,1,0:T(8,128)(2,1)}, u32[]{:S(2)}) copy-start(bf16[1,256,256]{2,1,0:T(8,128)(2,1)} %param.4) | copy-start | bytes 393220
  38.2 6.8 %collective-permute-start.8 = (bf16[256,256]{1,0:T(8,128)(2,1)S(1)}, bf16[256,256]{1,0:T(8,128)(2,1)S(1)}, u32[]{:S(2)}, u32[]{:S(2)}) collective-permute-start(bf16[256,256]{1,0:T(8,128)(2,1)S(1)} %get-tuple-element.23.refs_0_), channel_id=1, source_target_pairs={{0,2},{2,0},{1,3},{3,1},{4,6},{6,4},{5,7},{7,5},{8,10},{10,8},{9,1... | collective-permute-start | bytes 393224 | tf_op jit(solution)/shard_map/ppermute | solution.py:440
  40.4 4.5 %collective-permute-start.9 = (f32[8,128]{1,0:T(8,128)S(1)}, f32[8,128]{1,0:T(8,128)S(1)}, u32[]{:S(2)}, u32[]{:S(2)}) collective-permute-start(f32[8,128]{1,0:T(8,128)S(1)} %get-tuple-element.24), channel_id=1, source_target_pairs={{0,8},{4,12},{8,0},{12,4},{1,9},{5,13},{9,1},{13,5},{2,10},{6,14},... | collective-permute-start | bytes 12296 | tf_op jit(solution)/shard_map/ppermute | solution.py:424
  45.8 5.1 %collective-permute-start.10 = (bf16[128,256]{1,0:T(8,128)(2,1)S(1)}, bf16[128,256]{1,0:T(8,128)(2,1)S(1)}, u32[]{:S(2)}, u32[]{:S(2)}) collective-permute-start(bf16[128,256]{1,0:T(8,128)(2,1)S(1)} %get-tuple-element.27), channel_id=1, source_target_pairs={{9,0},{8,1},{13,4},{12,5},{1,8},{0,9},{5,12},{4,13},{11,2},{10,3},... | collective-permute-start | bytes 196616 | tf_op jit(solution)/shard_map/ppermute | solution.py:410
  45.9 9.3 %collective-permute-start.12 = (bf16[256,256]{1,0:T(8,128)(2,1)S(1)}, bf16[256,256]{1,0:T(8,128)(2,1)S(1)}, u32[]{:S(2)}, u32[]{:S(2)}) collective-permute-start(bf16[256,256]{1,0:T(8,128)(2,1)S(1)} %get-tuple-element.26.block_ref), channel_id=1, source_target_pairs={{12,1},{9,4},{4,9},{1,12},{14,3},{11,6},{6,11},{3,14},{28,17},{25,... | collective-permute-start | bytes 393224 | tf_op jit(solution)/shard_map/ppermute | solution.py:410
  50.9 4.3 %collective-permute-start.11 = (bf16[128,256]{1,0:T(8,128)(2,1)S(1)}, bf16[128,256]{1,0:T(8,128)(2,1)S(1)}, u32[]{:S(2)}, u32[]{:S(2)}) collective-permute-start(bf16[128,256]{1,0:T(8,128)(2,1)S(1)} %collective-permute-done.10.refs_4_), channel_id=1, source_target_pairs={{0,2},{2,0},{1,3},{3,1},{4,6},{6,4},{5,7},{7,5},{8,10},{10,8},{9,1... | collective-permute-start | bytes 196616 | tf_op jit(solution)/shard_map/ppermute | solution.py:433
  55.9 6.4 %collective-permute-start.13 = (bf16[256,256]{1,0:T(8,128)(2,1)S(1)}, bf16[256,256]{1,0:T(8,128)(2,1)S(1)}, u32[]{:S(2)}, u32[]{:S(2)}) collective-permute-start(bf16[256,256]{1,0:T(8,128)(2,1)S(1)} %rest.5.refs_0_), channel_id=1, source_target_pairs={{0,2},{2,0},{1,3},{3,1},{4,6},{6,4},{5,7},{7,5},{8,10},{10,8},{9,1... | collective-permute-start | bytes 393224 | tf_op jit(solution)/shard_map/ppermute | solution.py:440

commit v8 on v7

--- a/solution.py
+++ b/solution.py
@@ -13,6 +13,7 @@
 EPSILON = 1e-06
 WIDE = 8
 SMALLEST = 1e-30
+TILE = 16
 MIB = 1024 * 1024
 VMEM = pl.BlockSpec(memory_space=pltpu.VMEM)
 SMEM = pl.BlockSpec(memory_space=pltpu.SMEM)
@@ -74,6 +75,29 @@
                     place[k] = slot
         places.append(place)
     return places, origins
+
+
+def carried_rounds(permutes, blocks):
+    if len(permutes) < 2 or blocks % 2:
+        return None
+    last = dict(permutes[1])
+    for k in range(blocks):
+        if k not in last:
+            last[k] = blocks - 1 - k
+    rounds = [dict(permutes[0]), {k: k ^ 1 for k in range(blocks)}, last]
+    held = [{k} for k in range(blocks)]
+    for pairs in rounds:
+        if sorted(pairs.values()) != list(range(blocks)):
+            return None
+        if any(held[source] & held[k] for source, k in pairs.items()):
+            return None
+        grown = list(held)
+        for source, k in pairs.items():
+            grown[k] = held[k] | held[source]
+        held = grown
+    if any(len(rows) < blocks for rows in held):
+        return None
+    return [sorted(pairs.items()) for pairs in rounds[1:]]
 
 
 def look_up(table, sector, default):
@@ -233,22 +257,47 @@
     out_ref[...] = block_ref[...]
 
 
+def unpack_kernel(origin, block_ref, rows_ref, out_ref, sums_ref):
+    share = out_ref.shape[0]
+    out_ref[...] = block_ref[0:share, :]
+    terms = block_ref[share : share + 2 * TILE, :].astype(jnp.float32)
+    sums = terms[0:TILE, 0:128] + terms[0:TILE, 128:256] + terms[TILE : 2 * TILE, 0:128]
+    row = lax.broadcasted_iota(jnp.int32, rows_ref.shape, 0)
+    source = look_up(origin, here(), 0)
+    sums_ref[...] = jnp.where(row == source, first_row(sums), rows_ref[...])
+
+
 def my_rows(share):
     return pl.ds(pl.multiple_of(lax.axis_index("mpo") * share, share), share)
 
 
-def first_sums_kernel(*refs):
+def first_sums_kernel(share, *refs):
     parts, (psi_ref, unit_ref, w_ref, share_ref, rows_ref) = refs[:-5], refs[-5:]
     w = sum_parts(parts)
     unit = lane_of(first_row(unit_ref), 0)
     w_ref[...] = (w * unit).astype(jnp.bfloat16)
-    share_ref[...] = w_ref[my_rows(share_ref.shape[0]), :]
+    share_ref[0:share, :] = w_ref[my_rows(share), :]
     v = wide_float(psi_ref) * (1.0 / unit)
     a = total(v * w)
     d = total(v * v)
     local = a / jnp.maximum(d, SMALLEST)
     r = w - local * v
-    sums = pack([a, d, local, total(r * v), total(r * r), unit], rows_ref.shape)
+    values = [a, d, local, total(r * v), total(r * r), unit]
+    if share_ref.shape[0] > share:
+        sums = pack(values, (TILE, 128))
+        high = sums.astype(jnp.bfloat16)
+        rest = sums - high.astype(jnp.float32)
+        middle = rest.astype(jnp.bfloat16)
+        low = (rest - middle.astype(jnp.float32)).astype(jnp.bfloat16)
+        blank = jnp.zeros((2 * TILE, share_ref.shape[1]), jnp.bfloat16)
+        share_ref[share : share + 2 * TILE, :] = blank
+        share_ref[share : share + TILE, 0:128] = high
+        share_ref[share : share + TILE, 128:256] = middle
+        share_ref[share + TILE : share + 2 * TILE, 0:128] = low
+        sums = high.astype(jnp.float32) + middle.astype(jnp.float32) + low.astype(jnp.float32)
+        sums = jnp.broadcast_to(first_row(sums), rows_ref.shape)
+    else:
+        sums = pack(values, rows_ref.shape)
     row = lax.broadcasted_iota(jnp.int32, rows_ref.shape, 0)
     rows_ref[...] = jnp.where(row == here(), sums, 0.0)
 
@@ -409,8 +458,9 @@
     def shift(block, pairs):
         return lax.ppermute(block, ring, pairs)
 
-    rounds = []
-    for axis in ("rep", "blk"):
+    carried = carried_rounds(permutes, blocks)
+    rounds = [(ring, pairs) for pairs in carried or []]
+    for axis in () if carried else ("rep", "blk"):
         size = lax.axis_size(axis)
         bits = [1 << i for i in range(size.bit_length() - 1)]
         if sum(bits) == size - 1:
@@ -425,7 +475,15 @@
 
     def spread(block, share, rows=None):
         piece = shift(share, permutes[0])
-        if rows is not None:
+        if rows is not None and carried:
+            piece, rows = call(
+                functools.partial(unpack_kernel, origins[1]),
+                "unpack",
+                (share_shape, rows_shape),
+                (piece, rows),
+            )
+            rows = add_round(rows, *rounds[0])
+        elif rows is not None:
             for step in rounds[:-1]:
                 rows = add_round(rows, *step)
             piece = call(pass_kernel, "hold", share_shape, (piece, rows))
@@ -446,8 +504,12 @@
 
     held = [shift(psi, pairs) for pairs in permutes]
     t, unit = rest(own(True, psi), held[:1], held[1:], psi)
+    rows_in_share = width // parts + (2 * TILE if carried else 0)
     w_1, share_1, rows = call(
-        first_sums_kernel, "sums", (narrow, share_shape, rows_shape), (*gather_parts(t), psi, unit)
+        functools.partial(first_sums_kernel, width // parts),
+        "sums",
+        (narrow, jax.ShapeDtypeStruct((rows_in_share, width), jnp.bfloat16), rows_shape),
+        (*gather_parts(t), psi, unit),
     )
     first, others, rows = spread(w_1, share_1, rows)
     t, unit, rows = rest(own(True, w_1), first, others, w_1, rows)

time: 73.9 us -> 71.4 us (0.966)
  starting transfers between devices: 21.5 us -> 14.5 us
  waiting for transfers between devices: 25 us -> 30.6 us
  Pallas kernels: 11.7 us -> 10.9 us
    ppermute x6, waiting for transfers between devices: 6.72 us -> 13.4 us  [shift(): return lax.ppermute(block, ring, pairs)]
    ppermute x3 -> x2, starting transfers between devices: 6.02 us -> 0.07 us  [add_round(): return rows + lax.ppermute(rows, axis, pairs)]
    ppermute x3 -> x2, waiting for transfers between devices: 6.45 us -> 4.77 us  [add_round(): return rows + lax.ppermute(rows, axis, pairs)]
    ppermute x3, starting transfers between devices: 5.97 us -> 4.63 us  [gather_parts(): return [t, lax.ppermute(t, 'mpo', [(0, 1), (1, 0)])]]
    ppermute x2, waiting for transfers between devices: 2.56 us -> 3.89 us  [spread(): first = [piece, lax.ppermute(piece, 'mpo', [(0, 1), (1, 0)])]]
    pallas_call x11, Pallas kernels: 11.7 us -> 10.9 us  [call(): pl.pallas_call(kernel, out_shape=outs, in_specs=[first] + [VMEM] * (len(a...]
    ppermute x3, waiting for transfers between devices: 9.3 us -> 8.56 us  [gather_parts(): return [t, lax.ppermute(t, 'mpo', [(0, 1), (1, 0)])]]
  transfers between devices with their start and end apart: 14 -> 13, of which waited for: 9 -> 8; matrix products, arithmetic and copies ran while one was open for 0% -> 0% of each run, Pallas kernels for 8% -> 5%
where the time goes in v8:
time: 71.4 us; the launch traced here: 71 us
  waiting for transfers between devices  30.6 us (43%)
  starting transfers between devices  14.5 us (20%)
  Pallas kernels  10.9 us (15%)
  blocking collectives  8.81 us (12%)
  local copies, waits for them, and re-layouts  5.34 us (7%)
  between operations  0.79 us (1%)
    ppermute x6, waiting for transfers between devices, shift(): return lax.ppermute(block, ring, pairs)  13.4 us
    pallas_call x11, Pallas kernels, call(): pl.pallas_call(kernel, out_shape=outs, in_specs=[first] + [VMEM] * (len(a...  10.9 us
    all_to_all x1, blocking collectives, exchange(): return lax.all_to_all(rows, ring, 0, 0, tiled=True)  8.81 us
    ppermute x3, waiting for transfers between devices, gather_parts(): return [t, lax.ppermute(t, 'mpo', [(0, 1), (1, 0)])]  8.56 us
    ppermute x6, starting transfers between devices, shift(): return lax.ppermute(block, ring, pairs)  7.62 us
    unnamed x10, local copies, waits for them, and re-layouts  5.34 us
    ppermute x2, waiting for transfers between devices, add_round(): return rows + lax.ppermute(rows, axis, pairs)  4.77 us
    ppermute x3, starting transfers between devices, gather_parts(): return [t, lax.ppermute(t, 'mpo', [(0, 1), (1, 0)])]  4.63 us
  transfers between devices with their start and end apart: 13, of which 8 were waited for; matrix products, arithmetic and copies ran while one was open for 0% of the time, Pallas kernels for 5%

profile of v8, /device:TPU:0, one launch (start us, length us, event | category | flops | bytes accessed | tf_op | source)
XLA Modules:
  0.0 71.0 jit_solution(7723431318080523769)
XLA Ops:
  1.3 5.5 %collective-permute-start = (bf16[256,256]{1,0:T(8,128)(2,1)}, bf16[256,256]{1,0:T(8,128)(2,1)S(1)}, u32[]{:S(2)}, u32[]{:S(2)}) collective-permute-start(bf16[256,256]{1,0:T(8,128)(2,1)} %bitcast.20), channel_id=1, source_target_pairs={{9,0},{8,1},{13,4},{12,5},{1,8},{0,9},{5,12},{4,13},{11,2},{10,3},... | collective-permute-start | bytes 393224 | tf_op jit(solution)/shard_map/ppermute | solution.py:459
  6.8 1.9 %copy-done = bf16[24,1,256,256]{3,2,1,0:T(8,128)(2,1)S(1)} copy-done((bf16[24,1,256,256]{3,2,1,0:T(8,128)(2,1)S(1)}, bf16[24,1,256,256]{3,2,1,0:T(8,128)(2,1)}, u32[]{:S(2)}) %copy-start) | copy-done | bytes 3145752
  8.7 1.9 %copy-done.1 = bf16[24,1,256,256]{3,2,1,0:T(8,128)(2,1)S(1)} copy-done((bf16[24,1,256,256]{3,2,1,0:T(8,128)(2,1)S(1)}, bf16[24,1,256,256]{3,2,1,0:T(8,128)(2,1)}, u32[]{:S(2)}) %copy-start.1) | copy-done | bytes 3145752
  10.6 0.9 %copy-done.2 = bf16[1,256,256]{2,1,0:T(8,128)(2,1)S(1)} copy-done((bf16[1,256,256]{2,1,0:T(8,128)(2,1)S(1)}, bf16[1,256,256]{2,1,0:T(8,128)(2,1)}, u32[]{:S(2)}) %copy-start.2) | copy-done | bytes 131096
  12.2 1.2 %own.3.refs_3_ = f32[256,256]{1,0:T(8,128)S(1)} custom-call(s32[24]{0:T(128)S(1)} %copy-done.4, bf16[24,256,256]{2,1,0:T(8,128)(2,1)S(1)} %bitcast.7, bf16[24,256,256]{2,1,0:T(8,128)(2,1)S(1)} %bitcast.13, bf16[256,256]{1,0:T(8,128)(2,1)S(1)} %bitcast.21), custom_call_target="tpu_custom_call" | custom-call | flops 322122560 | bytes 262144 | tf_op jit(solution)/shard_map/own/pallas_call | solution.py:419
  13.4 3.2 %collective-permute-done.refs_5_ = bf16[256,256]{1,0:T(8,128)(2,1)S(1)} collective-permute-done((bf16[256,256]{1,0:T(8,128)(2,1)}, bf16[256,256]{1,0:T(8,128)(2,1)S(1)}, u32[]{:S(2)}, u32[]{:S(2)}) %collective-permute-start) | collective-permute-done | bytes 131104 | tf_op jit(solution)/shard_map/ppermute | solution.py:459
  16.6 1.3 %rest.3 = (bf16[256,256]{1,0:T(8,128)(2,1)S(1)}, f32[8,128]{1,0:T(8,128)S(1)}) custom-call(s32[24]{0:T(128)S(1)} %copy-done.4, bf16[24,256,256]{2,1,0:T(8,128)(2,1)S(1)} %bitcast.8, bf16[24,256,256]{2,1,0:T(8,128)(2,1)S(1)} %bitcast.14, f32[256,256]{1,0:T(8,128)S(1)} %own.3.refs_3_, bf16[256,256]{1,0:T(8,128)(2,1)S(1)} %bitcast.22, ...), custom_call_target="tpu_custom_call" | custom-call | flops 644245120 | bytes 262144 | tf_op jit(solution)/shard_map/rest/pallas_call | solution.py:419
  17.9 1.8 %collective-permute-start.2 = (bf16[256,256]{1,0:T(8,128)(2,1)S(1)}, bf16[256,256]{1,0:T(8,128)(2,1)S(1)}, u32[]{:S(2)}, u32[]{:S(2)}) collective-permute-start(bf16[256,256]{1,0:T(8,128)(2,1)S(1)} %get-tuple-element.20.refs_0_), channel_id=1, source_target_pairs={{0,2},{2,0},{1,3},{3,1},{4,6},{6,4},{5,7},{7,5},{8,10},{10,8},{9,1... | collective-permute-start | bytes 393224 | tf_op jit(solution)/shard_map/ppermute | solution.py:498
  19.8 4.3 %collective-permute-done.2.refs_1_ = bf16[256,256]{1,0:T(8,128)(2,1)S(1)} collective-permute-done((bf16[256,256]{1,0:T(8,128)(2,1)S(1)}, bf16[256,256]{1,0:T(8,128)(2,1)S(1)}, u32[]{:S(2)}, u32[]{:S(2)}) %collective-permute-start.2) | collective-permute-done | bytes 131104 | tf_op jit(solution)/shard_map/ppermute | solution.py:498
  25.1 5.5 %collective-permute-done.3.block_ref = bf16[160,256]{1,0:T(8,128)(2,1)S(1)} collective-permute-done((bf16[160,256]{1,0:T(8,128)(2,1)S(1)}, bf16[160,256]{1,0:T(8,128)(2,1)S(1)}, u32[]{:S(2)}, u32[]{:S(2)}) %collective-permute-start.3) | collective-permute-done | bytes 81952 | tf_op jit(solution)/shard_map/ppermute | solution.py:459
  30.6 1.7 %collective-permute-start.4 = (bf16[128,256]{1,0:T(8,128)(2,1)S(1)}, bf16[128,256]{1,0:T(8,128)(2,1)S(1)}, u32[]{:S(2)}, u32[]{:S(2)}) collective-permute-start(bf16[128,256]{1,0:T(8,128)(2,1)S(1)} %get-tuple-element.25.refs_5_), channel_id=1, source_target_pairs={{0,2},{2,0},{1,3},{3,1},{4,6},{6,4},{5,7},{7,5},{8,10},{10,8},{9,1... | collective-permute-start | bytes 196616 | tf_op jit(solution)/shard_map/ppermute | solution.py:491
  32.4 1.2 %own.4.refs_3_ = f32[256,256]{1,0:T(8,128)S(1)} custom-call(s32[24]{0:T(128)S(1)} %copy-done.4, bf16[24,256,256]{2,1,0:T(8,128)(2,1)S(1)} %bitcast.9, bf16[24,256,256]{2,1,0:T(8,128)(2,1)S(1)} %bitcast.15, bf16[256,256]{1,0:T(8,128)(2,1)S(1)} %get-tuple-element.22.block_ref.refs_4_.refs_3_), custom_call_target="tpu_custom_call" | custom-call | flops 322122560 | bytes 262144 | tf_op jit(solution)/shard_map/own/pallas_call | solution.py:419
  33.7 1.3 %collective-permute-done.4.refs_6_ = bf16[128,256]{1,0:T(8,128)(2,1)S(1)} collective-permute-done((bf16[128,256]{1,0:T(8,128)(2,1)S(1)}, bf16[128,256]{1,0:T(8,128)(2,1)S(1)}, u32[]{:S(2)}, u32[]{:S(2)}) %collective-permute-start.4) | collective-permute-done | bytes 65568 | tf_op jit(solution)/shard_map/ppermute | solution.py:491
  35.0 1.3 %rest.4 = (bf16[256,256]{1,0:T(8,128)(2,1)S(1)}, f32[8,128]{1,0:T(8,128)S(1)}, f32[8,128]{1,0:T(8,128)S(1)}) custom-call(s32[24]{0:T(128)S(1)} %copy-done.4, bf16[24,256,256]{2,1,0:T(8,128)(2,1)S(1)} %bitcast.10, bf16[24,256,256]{2,1,0:T(8,128)(2,1)S(1)} %bitcast.16, f32[256,256]{1,0:T(8,128)S(1)} %own.4.refs_3_, ...), custom_call_target="tpu_custom_call" | custom-call | flops 644245120 | bytes 262144 | tf_op jit(solution)/shard_map/rest/pallas_call | solution.py:419
  36.3 2.0 %collective-permute-start.7 = (bf16[256,256]{1,0:T(8,128)(2,1)S(1)}, bf16[256,256]{1,0:T(8,128)(2,1)S(1)}, u32[]{:S(2)}, u32[]{:S(2)}) collective-permute-start(bf16[256,256]{1,0:T(8,128)(2,1)S(1)} %get-tuple-element.27.refs_0_), channel_id=1, source_target_pairs={{0,2},{2,0},{1,3},{3,1},{4,6},{6,4},{5,7},{7,5},{8,10},{10,8},{9,1... | collective-permute-start | bytes 393224 | tf_op jit(solution)/shard_map/ppermute | solution.py:498
  38.4 4.8 %collective-permute-done.8 = f32[8,128]{1,0:T(8,128)S(1)} collective-permute-done((f32[8,128]{1,0:T(8,128)S(1)}, f32[8,128]{1,0:T(8,128)S(1)}, u32[]{:S(2)}, u32[]{:S(2)}) %collective-permute-start.8) | collective-permute-done | bytes 4128 | tf_op jit(solution)/shard_map/ppermute | solution.py:474
  43.2 0.9 %sums.4 = (f32[256,256]{1,0:T(8,128)S(1)}, bf16[256,256]{1,0:T(8,128)(2,1)S(1)}, bf16[128,256]{1,0:T(8,128)(2,1)S(1)}, bf16[256,256]{1,0:T(8,128)(2,1)S(1)}, f32[8,128]{1,0:T(8,128)S(1)}) custom-call(bf16[256,256]{1,0:T(8,128)(2,1)S(1)} %get-tuple-element.27.refs_0_, bf16[256,256]{1,0:T(8,128)(2,1)S(1)} %collective-permute-done.7.refs_1_, ...), custom_call_target="tpu_custom_call" | custom-call | bytes 262144 | tf_op jit(solution)/shard_map/sums/pallas_call | solution.py:419
  44.8 4.7 %collective-permute-done.9.refs_4_ = bf16[128,256]{1,0:T(8,128)(2,1)S(1)} collective-permute-done((bf16[128,256]{1,0:T(8,128)(2,1)S(1)}, bf16[128,256]{1,0:T(8,128)(2,1)S(1)}, u32[]{:S(2)}, u32[]{:S(2)}) %collective-permute-start.9) | collective-permute-done | bytes 65568 | tf_op jit(solution)/shard_map/ppermute | solution.py:459
  49.9 1.2 %own.5.refs_3_ = f32[256,256]{1,0:T(8,128)S(1)} custom-call(s32[24]{0:T(128)S(1)} %copy-done.4, bf16[24,256,256]{2,1,0:T(8,128)(2,1)S(1)} %bitcast.11, bf16[24,256,256]{2,1,0:T(8,128)(2,1)S(1)} %bitcast.17, bf16[256,256]{1,0:T(8,128)(2,1)S(1)} %get-tuple-element.30.block_ref), custom_call_target="tpu_custom_call" | custom-call | flops 322122560 | bytes 262144 | tf_op jit(solution)/shard_map/own/pallas_call | solution.py:419
  51.2 2.6 %collective-permute-done.10.refs_5_ = bf16[128,256]{1,0:T(8,128)(2,1)S(1)} collective-permute-done((bf16[128,256]{1,0:T(8,128)(2,1)S(1)}, bf16[128,256]{1,0:T(8,128)(2,1)S(1)}, u32[]{:S(2)}, u32[]{:S(2)}) %collective-permute-start.10) | collective-permute-done | bytes 65568 | tf_op jit(solution)/shard_map/ppermute | solution.py:491
  53.8 1.3 %rest.5.refs_0_ = bf16[256,256]{1,0:T(8,128)(2,1)S(1)} custom-call(s32[24]{0:T(128)S(1)} %copy-done.4, bf16[24,256,256]{2,1,0:T(8,128)(2,1)S(1)} %bitcast.12, bf16[24,256,256]{2,1,0:T(8,128)(2,1)S(1)} %bitcast.18, f32[256,256]{1,0:T(8,128)S(1)} %own.5.refs_3_, bf16[128,256]{1,0:T(8,128)(2,1)S(1)} %collective-permute-done.9.refs_4_, ...), custom_call_target="tpu_custom_call" | custom-call | flops 644245120 | bytes 262144 | tf_op jit(solution)/shard_map/rest/pallas_call | solution.py:419
  55.9 4.3 %collective-permute-done.12.refs_1_ = bf16[256,256]{1,0:T(8,128)(2,1)S(1)} collective-permute-done((bf16[256,256]{1,0:T(8,128)(2,1)S(1)}, bf16[256,256]{1,0:T(8,128)(2,1)S(1)}, u32[]{:S(2)}, u32[]{:S(2)}) %collective-permute-start.12) | collective-permute-done | bytes 131104 | tf_op jit(solution)/shard_map/ppermute | solution.py:498
  60.8 8.8 %all_to_all.11 = f32[8,1,128]{2,1,0:T(1,128)S(1)} all-to-all(f32[8,1,128]{2,1,0:T(1,128)S(1)} %bitcast.27), channel_id=1, replica_groups=mesh['groups'=2,'blk'=4,'mpo'=2,'rep'=2] {'blk','rep'}, dimensions={0} | all-to-all | bytes 8192 | tf_op jit(solution)/shard_map/all_to_all | solution.py:503
  69.6 1.4 %final.1 = (bf16[3,1,128,256]{3,2,1,0:T(8,128)(2,1)}, f32[2,3]{1,0:T(2,128)}) custom-call(f32[8,128]{1,0:T(8,128)S(1)} %bitcast.26, f32[256,256]{1,0:T(8,128)S(1)} %get-tuple-element.36.r_ref, f32[256,256]{1,0:T(8,128)S(1)} %get-tuple-element.37.z_ref, f32[256,256]{1,0:T(8,128)S(1)} %get-tuple-element.33.refs_5_.w_ref, ...), custom_call_target="tpu_custom_call" | custom-call | bytes 262144 | tf_op jit(solution)/shard_map/final/pallas_call | solution.py:419
  (26 shorter events, 5.1 us)
Async XLA Ops:
  0.6 12.8 %collective-permute-start.1 = (bf16[256,256]{1,0:T(8,128)(2,1)}, bf16[256,256]{1,0:T(8,128)(2,1)S(1)}, u32[]{:S(2)}, u32[]{:S(2)}) collective-permute-start(bf16[256,256]{1,0:T(8,128)(2,1)} %bitcast.19), channel_id=1, source_target_pairs={{12,1},{9,4},{4,9},{1,12},{14,3},{11,6},{6,11},{3,14},{28,17},{25,... | collective-permute-start | bytes 393224 | tf_op jit(solution)/shard_map/ppermute | solution.py:459
  1.3 15.3 %collective-permute-start = (bf16[256,256]{1,0:T(8,128)(2,1)}, bf16[256,256]{1,0:T(8,128)(2,1)S(1)}, u32[]{:S(2)}, u32[]{:S(2)}) collective-permute-start(bf16[256,256]{1,0:T(8,128)(2,1)} %bitcast.20), channel_id=1, source_target_pairs={{9,0},{8,1},{13,4},{12,5},{1,8},{0,9},{5,12},{4,13},{11,2},{10,3},... | collective-permute-start | bytes 393224 | tf_op jit(solution)/shard_map/ppermute | solution.py:459
  6.8 1.9 %copy-start = (bf16[24,1,256,256]{3,2,1,0:T(8,128)(2,1)S(1)}, bf16[24,1,256,256]{3,2,1,0:T(8,128)(2,1)}, u32[]{:S(2)}) copy-start(bf16[24,1,256,256]{3,2,1,0:T(8,128)(2,1)} %param.5) | copy-start | bytes 9437188
  8.7 1.9 %copy-start.1 = (bf16[24,1,256,256]{3,2,1,0:T(8,128)(2,1)S(1)}, bf16[24,1,256,256]{3,2,1,0:T(8,128)(2,1)}, u32[]{:S(2)}) copy-start(bf16[24,1,256,256]{3,2,1,0:T(8,128)(2,1)} %param.6) | copy-start | bytes 9437188
  10.6 0.9 %copy-start.2 = (bf16[1,256,256]{2,1,0:T(8,128)(2,1)S(1)}, bf16[1,256,256]{2,1,0:T(8,128)(2,1)}, u32[]{:S(2)}) copy-start(bf16[1,256,256]{2,1,0:T(8,128)(2,1)} %param.4) | copy-start | bytes 393220
  11.5 0.7 copy-start.4
  17.9 6.1 %collective-permute-start.2 = (bf16[256,256]{1,0:T(8,128)(2,1)S(1)}, bf16[256,256]{1,0:T(8,128)(2,1)S(1)}, u32[]{:S(2)}, u32[]{:S(2)}) collective-permute-start(bf16[256,256]{1,0:T(8,128)(2,1)S(1)} %get-tuple-element.20.refs_0_), channel_id=1, source_target_pairs={{0,2},{2,0},{1,3},{3,1},{4,6},{6,4},{5,7},{7,5},{8,10},{10,8},{9,1... | collective-permute-start | bytes 393224 | tf_op jit(solution)/shard_map/ppermute | solution.py:498
  24.4 6.2 %collective-permute-start.3 = (bf16[160,256]{1,0:T(8,128)(2,1)S(1)}, bf16[160,256]{1,0:T(8,128)(2,1)S(1)}, u32[]{:S(2)}, u32[]{:S(2)}) collective-permute-start(bf16[160,256]{1,0:T(8,128)(2,1)S(1)} %get-tuple-element.23), channel_id=1, source_target_pairs={{9,0},{8,1},{13,4},{12,5},{1,8},{0,9},{5,12},{4,13},{11,2},{10,3},... | collective-permute-start | bytes 245768 | tf_op jit(solution)/shard_map/ppermute | solution.py:459
  24.5 9.2 %collective-permute-start.5 = (bf16[256,256]{1,0:T(8,128)(2,1)S(1)}, bf16[256,256]{1,0:T(8,128)(2,1)S(1)}, u32[]{:S(2)}, u32[]{:S(2)}) collective-permute-start(bf16[256,256]{1,0:T(8,128)(2,1)S(1)} %get-tuple-element.22.block_ref.refs_4_.refs_3_), channel_id=1, source_target_pairs={{12,1},{9,4},{4,9},{1,12},{14,3},{11,6},{6,11},{3,14},{28,17},{25,... | collective-permute-start | bytes 393224 | tf_op jit(solution)/shard_map/ppermute | solution.py:459
  30.6 4.3 %collective-permute-start.4 = (bf16[128,256]{1,0:T(8,128)(2,1)S(1)}, bf16[128,256]{1,0:T(8,128)(2,1)S(1)}, u32[]{:S(2)}, u32[]{:S(2)}) collective-permute-start(bf16[128,256]{1,0:T(8,128)(2,1)S(1)} %get-tuple-element.25.refs_5_), channel_id=1, source_target_pairs={{0,2},{2,0},{1,3},{3,1},{4,6},{6,4},{5,7},{7,5},{8,10},{10,8},{9,1... | collective-permute-start | bytes 196616 | tf_op jit(solution)/shard_map/ppermute | solution.py:491
  32.4 1.3 %collective-permute-start.6 = (f32[8,128]{1,0:T(8,128)S(1)}, f32[8,128]{1,0:T(8,128)S(1)}, u32[]{:S(2)}, u32[]{:S(2)}) collective-permute-start(f32[8,128]{1,0:T(8,128)S(1)} %get-tuple-element.26), channel_id=1, source_target_pairs={{0,1},{1,0},{4,5},{5,4},{8,9},{9,8},{12,13},{13,12},{2,3},{3,2},{6... | collective-permute-start | bytes 12296 | tf_op jit(solution)/shard_map/ppermute | solution.py:474
  33.6 9.5 %copy-start.3 = (bf16[1,256,256]{2,1,0:T(8,128)(2,1)S(1)}, bf16[1,256,256]{2,1,0:T(8,128)(2,1)}, u32[]{:S(2)}) copy-start(bf16[1,256,256]{2,1,0:T(8,128)(2,1)} %param.4) | copy-start | bytes 393220
  36.3 6.9 %collective-permute-start.7 = (bf16[256,256]{1,0:T(8,128)(2,1)S(1)}, bf16[256,256]{1,0:T(8,128)(2,1)S(1)}, u32[]{:S(2)}, u32[]{:S(2)}) collective-permute-start(bf16[256,256]{1,0:T(8,128)(2,1)S(1)} %get-tuple-element.27.refs_0_), channel_id=1, source_target_pairs={{0,2},{2,0},{1,3},{3,1},{4,6},{6,4},{5,7},{7,5},{8,10},{10,8},{9,1... | collective-permute-start | bytes 393224 | tf_op jit(solution)/shard_map/ppermute | solution.py:498
  38.3 4.8 %collective-permute-start.8 = (f32[8,128]{1,0:T(8,128)S(1)}, f32[8,128]{1,0:T(8,128)S(1)}, u32[]{:S(2)}, u32[]{:S(2)}) collective-permute-start(f32[8,128]{1,0:T(8,128)S(1)} %get-tuple-element.28), channel_id=1, source_target_pairs={{0,13},{1,12},{4,9},{5,8},{8,5},{9,4},{12,1},{13,0},{2,15},{3,14},... | collective-permute-start | bytes 12296 | tf_op jit(solution)/shard_map/ppermute | solution.py:474
  44.0 5.5 %collective-permute-start.9 = (bf16[128,256]{1,0:T(8,128)(2,1)S(1)}, bf16[128,256]{1,0:T(8,128)(2,1)S(1)}, u32[]{:S(2)}, u32[]{:S(2)}) collective-permute-start(bf16[128,256]{1,0:T(8,128)(2,1)S(1)} %get-tuple-element.31), channel_id=1, source_target_pairs={{9,0},{8,1},{13,4},{12,5},{1,8},{0,9},{5,12},{4,13},{11,2},{10,3},... | collective-permute-start | bytes 196616 | tf_op jit(solution)/shard_map/ppermute | solution.py:459
  44.1 9.7 %collective-permute-start.11 = (bf16[256,256]{1,0:T(8,128)(2,1)S(1)}, bf16[256,256]{1,0:T(8,128)(2,1)S(1)}, u32[]{:S(2)}, u32[]{:S(2)}) collective-permute-start(bf16[256,256]{1,0:T(8,128)(2,1)S(1)} %get-tuple-element.30.block_ref), channel_id=1, source_target_pairs={{12,1},{9,4},{4,9},{1,12},{14,3},{11,6},{6,11},{3,14},{28,17},{25,... | collective-permute-start | bytes 393224 | tf_op jit(solution)/shard_map/ppermute | solution.py:459
  49.5 4.3 %collective-permute-start.10 = (bf16[128,256]{1,0:T(8,128)(2,1)S(1)}, bf16[128,256]{1,0:T(8,128)(2,1)S(1)}, u32[]{:S(2)}, u32[]{:S(2)}) collective-permute-start(bf16[128,256]{1,0:T(8,128)(2,1)S(1)} %collective-permute-done.9.refs_4_), channel_id=1, source_target_pairs={{0,2},{2,0},{1,3},{3,1},{4,6},{6,4},{5,7},{7,5},{8,10},{10,8},{9,1... | collective-permute-start | bytes 196616 | tf_op jit(solution)/shard_map/ppermute | solution.py:491
  55.1 5.0 %collective-permute-start.12 = (bf16[256,256]{1,0:T(8,128)(2,1)S(1)}, bf16[256,256]{1,0:T(8,128)(2,1)S(1)}, u32[]{:S(2)}, u32[]{:S(2)}) collective-permute-start(bf16[256,256]{1,0:T(8,128)(2,1)S(1)} %rest.5.refs_0_), channel_id=1, source_target_pairs={{0,2},{2,0},{1,3},{3,1},{4,6},{6,4},{5,7},{7,5},{8,10},{10,8},{9,1... | collective-permute-start | bytes 393224 | tf_op jit(solution)/shard_map/ppermute | solution.py:498

commit v9 on v8

--- a/solution.py
+++ b/solution.py
@@ -11,7 +11,7 @@
 STEPS = 3
 OFFSETS = (0, NS + 1, NS - 1, -(NS + 1), -(NS - 1))
 EPSILON = 1e-06
-WIDE = 8
+PAD = 12
 SMALLEST = 1e-30
 TILE = 16
 MIB = 1024 * 1024
@@ -151,33 +151,37 @@
     return ref[0:1, :]
 
 
-def list_channels(which, places, kinds_ref, order, slot_of, idle):
+def list_kernel(places, idle, kinds_ref, lists_ref):
+    channels = kinds_ref.shape[0]
     sector = here()
-    slots = [jnp.int32(-1 if which == "rest" else 0)]
-    slots += [look_up(places[c], sector, -1) if which != "own" else jnp.int32(-1) for c in range(1, 5)]
-    count = jnp.int32(0)
-    for b in range(kinds_ref.shape[0]):
+    slots = [jnp.int32(0)] + [look_up(places[c], sector, -1) for c in range(1, 5)]
+    counts = [jnp.int32(0), jnp.int32(0)]
+    for b in range(channels):
         kind = kinds_ref[b]
         slot = slots[0]
         for c in range(1, 5):
             slot = jnp.where(kind == c, slots[c], slot)
-        order[count] = jnp.int32(b)
-        slot_of[count] = slot
-        count += jnp.where(slot >= 0, 1, 0)
-    for extra in range(WIDE):
-        order[count + extra] = jnp.int32(0)
-        slot_of[count + extra] = jnp.int32(idle)
-    return count
-
-
-def multiply_listed(count, left_ref, right_ref, source, acc, order, slot_of):
-    def multiply(start, wide):
-        held = [order[start + inner] for inner in range(wide)]
+        for which in range(2):
+            lists_ref[2 * which, counts[which]] = jnp.int32(b)
+            lists_ref[2 * which + 1, counts[which]] = slot
+        counts[0] += jnp.where(kind == 0, 1, 0)
+        counts[1] += jnp.where((kind != 0) & (slot >= 0), 1, 0)
+    for which, spare in enumerate((1, idle)):
+        for extra in range(PAD):
+            lists_ref[2 * which, counts[which] + extra] = jnp.int32(0)
+            lists_ref[2 * which + 1, counts[which] + extra] = jnp.int32(spare)
+        lists_ref[2 * which, channels + PAD] = counts[which]
+
+
+def multiply_listed(which, wide, lists_ref, left_ref, right_ref, source, acc):
+    count = lists_ref[2 * which, lists_ref.shape[1] - 1]
+
+    def multiply(start, size):
+        held = [lists_ref[2 * which, start + inner] for inner in range(size)]
+        slots = [lists_ref[2 * which + 1, start + inner] for inner in range(size)]
         pieces = [
-            jnp.dot(
-                left_ref[b], source[slot_of[start + inner]], preferred_element_type=jnp.float32
-            ).astype(jnp.bfloat16)
-            for inner, b in enumerate(held)
+            jnp.dot(left_ref[b], source[slot], preferred_element_type=jnp.float32).astype(jnp.bfloat16)
+            for b, slot in zip(held, slots)
         ]
         acc[...] += lax.dot_general(
             jnp.concatenate(pieces, axis=1),
@@ -187,21 +191,21 @@
         )
 
     def full(group, carry):
-        multiply(group * WIDE, WIDE)
+        multiply(group * wide, wide)
         return carry
 
-    groups = (count + WIDE // 2 - 1) // WIDE
+    smaller = [4, 8] if wide > 8 else [2, 4]
+    groups = (count + wide - 1 - smaller[-1]) // wide
     lax.fori_loop(0, groups, full, 0)
-    rest = count - groups * WIDE
-    for low, wide in ((0, 2), (2, 4)):
-
-        @pl.when((rest > low) & (rest <= wide))
+    rest = count - groups * wide
+    for low, size in zip([0] + smaller, smaller):
+
+        @pl.when((rest > low) & (rest <= size))
         def _():
-            multiply(groups * WIDE, wide)
-
-
-def own_kernel(scaled, places, kinds_ref, left_ref, right_ref, block_ref, acc, source, order, slot_of):
-    count = list_channels("own", places, kinds_ref, order, slot_of, 1)
+            multiply(groups * wide, size)
+
+
+def own_kernel(scaled, lists_ref, left_ref, right_ref, block_ref, acc, source):
     if scaled:
         block = wide_float(block_ref)
         inverse = 1.0 / jnp.maximum(peak(block), SMALLEST)
@@ -210,11 +214,11 @@
         source[0] = block_ref[...]
     source[1] = jnp.zeros(source.shape[1:], jnp.bfloat16)
     acc[...] = jnp.zeros_like(acc)
-    multiply_listed(count, left_ref, right_ref, source, acc, order, slot_of)
-
-
-def rest_kernel(scaled, passes, shares, slots, places, *refs):
-    kinds_ref, left_ref, right_ref, own_ref = refs[:4]
+    multiply_listed(0, 8, lists_ref, left_ref, right_ref, source, acc)
+
+
+def rest_kernel(scaled, passes, shares, slots, *refs):
+    lists_ref, left_ref, right_ref, own_ref = refs[:4]
     refs = refs[4:]
     if scaled:
         block_ref, refs = refs[0], refs[1:]
@@ -228,8 +232,7 @@
     if passes:
         refs[0][...] = rows_ref[...]
         refs = refs[1:]
-    acc, source, order, slot_of = refs
-    count = list_channels("rest", places, kinds_ref, order, slot_of, slots)
+    acc, source = refs
     if scaled:
         mine = jnp.maximum(peak(wide_float(block_ref)), SMALLEST)
         unit = mine
@@ -249,7 +252,7 @@
         source[slot] = scale(block)
     source[slots] = jnp.zeros(source.shape[1:], jnp.bfloat16)
     acc[...] = own_ref[...] * (mine * inverse) if scaled else own_ref[...]
-    multiply_listed(count, left_ref, right_ref, source, acc, order, slot_of)
+    multiply_listed(1, PAD, lists_ref, left_ref, right_ref, source, acc)
     t_ref[...] = acc[...].astype(jnp.bfloat16)
 
 
@@ -409,7 +412,14 @@
     wide = jax.ShapeDtypeStruct((width, width), jnp.float32)
     narrow = jax.ShapeDtypeStruct((width, width), jnp.bfloat16)
     share_shape = jax.ShapeDtypeStruct((width // parts, width), jnp.bfloat16)
-    lists = [pltpu.SMEM((channels + WIDE,), jnp.int32)] * 2
+    lists = pl.pallas_call(
+        functools.partial(list_kernel, places, slots),
+        out_shape=jax.ShapeDtypeStruct((4, channels + PAD + 1), jnp.int32),
+        in_specs=[SMEM],
+        out_specs=SMEM,
+        compiler_params=pltpu.CompilerParams(vmem_limit_bytes=4 * MIB),
+        name="list",
+    )(channel_class)
 
     def call(kernel, name, outs, args, scratch=(), share=0, limit=4):
         flops = int(4 * channels * share * width**3)
@@ -432,11 +442,11 @@
 
     def own(scaled, block):
         return call(
-            functools.partial(own_kernel, scaled, places),
+            functools.partial(own_kernel, scaled),
             "own",
             wide,
-            (channel_class, left, right, block),
-            [sources(1)] + lists,
+            (lists, left, right, block),
+            [sources(1)],
             0.2,
             16,
         )
@@ -444,13 +454,13 @@
     def rest(mine, first, others, block=None, rows=None):
         scaled, passes = block is not None, rows is not None
         outs = (narrow,) + (scalars,) * scaled + (rows_shape,) * passes
-        args = [channel_class, left, right, mine] + [block] * scaled + first + others + [rows] * passes
+        args = [lists, left, right, mine] + [block] * scaled + first + others + [rows] * passes
         return call(
-            functools.partial(rest_kernel, scaled, passes, len(first), slots, places),
+            functools.partial(rest_kernel, scaled, passes, len(first), slots),
             "rest",
             outs,
             args,
-            [pltpu.VMEM((width, width), jnp.float32), sources(slots)] + lists,
+            [pltpu.VMEM((width, width), jnp.float32), sources(slots)],
             0.4,
             16,
         )

time: 71.4 us -> 70.8 us (level)
  Pallas kernels: 10.9 us -> 13.1 us
  waiting for transfers between devices: 30.6 us -> 29.2 us
  starting transfers between devices: 14.5 us -> 13.7 us
    pallas_call x0 -> x1, Pallas kernels: none -> 1.5 us  [shards(): pl.pallas_call(functools.partial(list_kernel, places, slots), out_shape=j...]
    ppermute x6, waiting for transfers between devices: 13.4 us -> 12.1 us  [shift(): return lax.ppermute(block, ring, pairs)]
    ppermute x3, starting transfers between devices: 4.63 us -> 3.83 us  [gather_parts(): return [t, lax.ppermute(t, 'mpo', [(0, 1), (1, 0)])]]
  transfers between devices with their start and end apart: 13 -> 13, of which waited for: 8 -> 8; matrix products, arithmetic and copies ran while one was open for 0% -> 0% of each run, Pallas kernels for 5% -> 9%
where the time goes in v9:
time: 70.8 us; the launch traced here: 70.5 us
  waiting for transfers between devices  29.2 us (41%)
  starting transfers between devices  13.7 us (19%)
  Pallas kernels  13.1 us (19%)
  blocking collectives  8.38 us (12%)
  local copies, waits for them, and re-layouts  5.34 us (8%)
  between operations  0.8 us (1%)
    ppermute x6, waiting for transfers between devices, shift(): return lax.ppermute(block, ring, pairs)  12.1 us
    pallas_call x11, Pallas kernels, call(): pl.pallas_call(kernel, out_shape=outs, in_specs=[first] + [VMEM] * (len(a...  11.6 us
    ppermute x3, waiting for transfers between devices, gather_parts(): return [t, lax.ppermute(t, 'mpo', [(0, 1), (1, 0)])]  8.93 us
    all_to_all x1, blocking collectives, exchange(): return lax.all_to_all(rows, ring, 0, 0, tiled=True)  8.38 us
    ppermute x6, starting transfers between devices, shift(): return lax.ppermute(block, ring, pairs)  7.62 us
    unnamed x10, local copies, waits for them, and re-layouts  5.34 us
    ppermute x2, waiting for transfers between devices, add_round(): return rows + lax.ppermute(rows, axis, pairs)  4.83 us
    ppermute x3, starting transfers between devices, gather_parts(): return [t, lax.ppermute(t, 'mpo', [(0, 1), (1, 0)])]  3.83 us
  transfers between devices with their start and end apart: 13, of which 8 were waited for; matrix products, arithmetic and copies ran while one was open for 0% of the time, Pallas kernels for 9%

profile of v9, /device:TPU:0, one launch (start us, length us, event | category | flops | bytes accessed | tf_op | source)
XLA Modules:
  0.0 70.5 jit_solution(10548243127712089334)
XLA Ops:
  1.3 5.5 %collective-permute-start = (bf16[256,256]{1,0:T(8,128)(2,1)}, bf16[256,256]{1,0:T(8,128)(2,1)S(1)}, u32[]{:S(2)}, u32[]{:S(2)}) collective-permute-start(bf16[256,256]{1,0:T(8,128)(2,1)} %bitcast.20), channel_id=1, source_target_pairs={{9,0},{8,1},{13,4},{12,5},{1,8},{0,9},{5,12},{4,13},{11,2},{10,3},... | collective-permute-start | bytes 393224 | tf_op jit(solution)/shard_map/ppermute | solution.py:469
  7.5 1.5 %list.1.lists_ref.refs_0_ = s32[4,37]{1,0:T(4,128)S(1)} custom-call(s32[24]{0:T(128)S(1)} %copy-done.4), custom_call_target="tpu_custom_call" | custom-call | tf_op jit(solution)/shard_map/list/pallas_call | solution.py:415
  9.0 1.9 %copy-done = bf16[24,1,256,256]{3,2,1,0:T(8,128)(2,1)S(1)} copy-done((bf16[24,1,256,256]{3,2,1,0:T(8,128)(2,1)S(1)}, bf16[24,1,256,256]{3,2,1,0:T(8,128)(2,1)}, u32[]{:S(2)}) %copy-start) | copy-done | bytes 3145752
  10.9 1.9 %copy-done.1 = bf16[24,1,256,256]{3,2,1,0:T(8,128)(2,1)S(1)} copy-done((bf16[24,1,256,256]{3,2,1,0:T(8,128)(2,1)S(1)}, bf16[24,1,256,256]{3,2,1,0:T(8,128)(2,1)}, u32[]{:S(2)}) %copy-start.1) | copy-done | bytes 3145752
  12.8 0.9 %copy-done.2 = bf16[1,256,256]{2,1,0:T(8,128)(2,1)S(1)} copy-done((bf16[1,256,256]{2,1,0:T(8,128)(2,1)S(1)}, bf16[1,256,256]{2,1,0:T(8,128)(2,1)}, u32[]{:S(2)}) %copy-start.2) | copy-done | bytes 131096
  13.7 1.5 %own.3.refs_3_ = f32[256,256]{1,0:T(8,128)S(1)} custom-call(s32[4,37]{1,0:T(4,128)S(1)} %list.1.lists_ref.refs_0_, bf16[24,256,256]{2,1,0:T(8,128)(2,1)S(1)} %bitcast.7, bf16[24,256,256]{2,1,0:T(8,128)(2,1)S(1)} %bitcast.13, bf16[256,256]{1,0:T(8,128)(2,1)S(1)} %bitcast.21), custom_call_target="tpu_custom_call" | custom-call | flops 322122560 | bytes 262144 | tf_op jit(solution)/shard_map/own/pallas_call | solution.py:429
  15.2 1.4 %collective-permute-done.refs_5_ = bf16[256,256]{1,0:T(8,128)(2,1)S(1)} collective-permute-done((bf16[256,256]{1,0:T(8,128)(2,1)}, bf16[256,256]{1,0:T(8,128)(2,1)S(1)}, u32[]{:S(2)}, u32[]{:S(2)}) %collective-permute-start) | collective-permute-done | bytes 131104 | tf_op jit(solution)/shard_map/ppermute | solution.py:469
  16.6 1.3 %rest.3 = (bf16[256,256]{1,0:T(8,128)(2,1)S(1)}, f32[8,128]{1,0:T(8,128)S(1)}) custom-call(s32[4,37]{1,0:T(4,128)S(1)} %list.1.lists_ref.refs_0_, bf16[24,256,256]{2,1,0:T(8,128)(2,1)S(1)} %bitcast.8, bf16[24,256,256]{2,1,0:T(8,128)(2,1)S(1)} %bitcast.14, f32[256,256]{1,0:T(8,128)S(1)} %own.3.refs_3_, bf16[256,256]{1,0:T(8,128)(2,1)S(1)} %bitcast.22, ...), custom_call_target="tpu_custom_call" | custom-call | flops 644245120 | bytes 262144 | tf_op jit(solution)/shard_map/rest/pallas_call | solution.py:429
  18.0 1.6 %collective-permute-start.2 = (bf16[256,256]{1,0:T(8,128)(2,1)S(1)}, bf16[256,256]{1,0:T(8,128)(2,1)S(1)}, u32[]{:S(2)}, u32[]{:S(2)}) collective-permute-start(bf16[256,256]{1,0:T(8,128)(2,1)S(1)} %get-tuple-element.20.refs_0_), channel_id=1, source_target_pairs={{0,2},{2,0},{1,3},{3,1},{4,6},{6,4},{5,7},{7,5},{8,10},{10,8},{9,1... | collective-permute-start | bytes 393224 | tf_op jit(solution)/shard_map/ppermute | solution.py:508
  19.5 4.5 %collective-permute-done.2.refs_1_ = bf16[256,256]{1,0:T(8,128)(2,1)S(1)} collective-permute-done((bf16[256,256]{1,0:T(8,128)(2,1)S(1)}, bf16[256,256]{1,0:T(8,128)(2,1)S(1)}, u32[]{:S(2)}, u32[]{:S(2)}) %collective-permute-start.2) | collective-permute-done | bytes 131104 | tf_op jit(solution)/shard_map/ppermute | solution.py:508
  25.1 6.1 %collective-permute-done.3.block_ref = bf16[160,256]{1,0:T(8,128)(2,1)S(1)} collective-permute-done((bf16[160,256]{1,0:T(8,128)(2,1)S(1)}, bf16[160,256]{1,0:T(8,128)(2,1)S(1)}, u32[]{:S(2)}, u32[]{:S(2)}) %collective-permute-start.3) | collective-permute-done | bytes 81952 | tf_op jit(solution)/shard_map/ppermute | solution.py:469
  31.2 1.7 %collective-permute-start.4 = (bf16[128,256]{1,0:T(8,128)(2,1)S(1)}, bf16[128,256]{1,0:T(8,128)(2,1)S(1)}, u32[]{:S(2)}, u32[]{:S(2)}) collective-permute-start(bf16[128,256]{1,0:T(8,128)(2,1)S(1)} %get-tuple-element.25.refs_5_), channel_id=1, source_target_pairs={{0,2},{2,0},{1,3},{3,1},{4,6},{6,4},{5,7},{7,5},{8,10},{10,8},{9,1... | collective-permute-start | bytes 196616 | tf_op jit(solution)/shard_map/ppermute | solution.py:501
  32.9 1.5 %own.4.refs_3_ = f32[256,256]{1,0:T(8,128)S(1)} custom-call(s32[4,37]{1,0:T(4,128)S(1)} %list.1.lists_ref.refs_0_, bf16[24,256,256]{2,1,0:T(8,128)(2,1)S(1)} %bitcast.9, bf16[24,256,256]{2,1,0:T(8,128)(2,1)S(1)} %bitcast.15, bf16[256,256]{1,0:T(8,128)(2,1)S(1)} %get-tuple-element.22.block_ref.refs_4_.refs_3_), custom_call_target="tpu_custom_call" | custom-call | flops 322122560 | bytes 262144 | tf_op jit(solution)/shard_map/own/pallas_call | solution.py:429
  34.5 1.1 %collective-permute-done.4.refs_6_ = bf16[128,256]{1,0:T(8,128)(2,1)S(1)} collective-permute-done((bf16[128,256]{1,0:T(8,128)(2,1)S(1)}, bf16[128,256]{1,0:T(8,128)(2,1)S(1)}, u32[]{:S(2)}, u32[]{:S(2)}) %collective-permute-start.4) | collective-permute-done | bytes 65568 | tf_op jit(solution)/shard_map/ppermute | solution.py:501
  35.5 1.3 %rest.4 = (bf16[256,256]{1,0:T(8,128)(2,1)S(1)}, f32[8,128]{1,0:T(8,128)S(1)}, f32[8,128]{1,0:T(8,128)S(1)}) custom-call(s32[4,37]{1,0:T(4,128)S(1)} %list.1.lists_ref.refs_0_, bf16[24,256,256]{2,1,0:T(8,128)(2,1)S(1)} %bitcast.10, bf16[24,256,256]{2,1,0:T(8,128)(2,1)S(1)} %bitcast.16, f32[256,256]{1,0:T(8,128)S(1)} %own.4.refs_3_, ...), custom_call_target="tpu_custom_call" | custom-call | flops 644245120 | bytes 262144 | tf_op jit(solution)/shard_map/rest/pallas_call | solution.py:429
  36.9 1.7 %collective-permute-start.7 = (bf16[256,256]{1,0:T(8,128)(2,1)S(1)}, bf16[256,256]{1,0:T(8,128)(2,1)S(1)}, u32[]{:S(2)}, u32[]{:S(2)}) collective-permute-start(bf16[256,256]{1,0:T(8,128)(2,1)S(1)} %get-tuple-element.27.refs_0_), channel_id=1, source_target_pairs={{0,2},{2,0},{1,3},{3,1},{4,6},{6,4},{5,7},{7,5},{8,10},{10,8},{9,1... | collective-permute-start | bytes 393224 | tf_op jit(solution)/shard_map/ppermute | solution.py:508
  38.6 4.8 %collective-permute-done.8 = f32[8,128]{1,0:T(8,128)S(1)} collective-permute-done((f32[8,128]{1,0:T(8,128)S(1)}, f32[8,128]{1,0:T(8,128)S(1)}, u32[]{:S(2)}, u32[]{:S(2)}) %collective-permute-start.8) | collective-permute-done | bytes 4128 | tf_op jit(solution)/shard_map/ppermute | solution.py:484
  45.0 4.6 %collective-permute-done.9.refs_4_ = bf16[128,256]{1,0:T(8,128)(2,1)S(1)} collective-permute-done((bf16[128,256]{1,0:T(8,128)(2,1)S(1)}, bf16[128,256]{1,0:T(8,128)(2,1)S(1)}, u32[]{:S(2)}, u32[]{:S(2)}) %collective-permute-start.9) | collective-permute-done | bytes 65568 | tf_op jit(solution)/shard_map/ppermute | solution.py:469
  50.2 1.4 %own.5.refs_3_ = f32[256,256]{1,0:T(8,128)S(1)} custom-call(s32[4,37]{1,0:T(4,128)S(1)} %list.1.lists_ref.refs_0_, bf16[24,256,256]{2,1,0:T(8,128)(2,1)S(1)} %bitcast.11, bf16[24,256,256]{2,1,0:T(8,128)(2,1)S(1)} %bitcast.17, bf16[256,256]{1,0:T(8,128)(2,1)S(1)} %get-tuple-element.30.block_ref), custom_call_target="tpu_custom_call" | custom-call | flops 322122560 | bytes 262144 | tf_op jit(solution)/shard_map/own/pallas_call | solution.py:429
  51.6 2.3 %collective-permute-done.10.refs_5_ = bf16[128,256]{1,0:T(8,128)(2,1)S(1)} collective-permute-done((bf16[128,256]{1,0:T(8,128)(2,1)S(1)}, bf16[128,256]{1,0:T(8,128)(2,1)S(1)}, u32[]{:S(2)}, u32[]{:S(2)}) %collective-permute-start.10) | collective-permute-done | bytes 65568 | tf_op jit(solution)/shard_map/ppermute | solution.py:501
  53.9 1.2 %rest.5.refs_0_ = bf16[256,256]{1,0:T(8,128)(2,1)S(1)} custom-call(s32[4,37]{1,0:T(4,128)S(1)} %list.1.lists_ref.refs_0_, bf16[24,256,256]{2,1,0:T(8,128)(2,1)S(1)} %bitcast.12, bf16[24,256,256]{2,1,0:T(8,128)(2,1)S(1)} %bitcast.18, f32[256,256]{1,0:T(8,128)S(1)} %own.5.refs_3_, bf16[128,256]{1,0:T(8,128)(2,1)S(1)} %collective-permute-done.9.refs_4_, ...), custom_call_target="tpu_custom_call" | custom-call | flops 644245120 | bytes 262144 | tf_op jit(solution)/shard_map/rest/pallas_call | solution.py:429
  55.7 4.4 %collective-permute-done.12.refs_1_ = bf16[256,256]{1,0:T(8,128)(2,1)S(1)} collective-permute-done((bf16[256,256]{1,0:T(8,128)(2,1)S(1)}, bf16[256,256]{1,0:T(8,128)(2,1)S(1)}, u32[]{:S(2)}, u32[]{:S(2)}) %collective-permute-start.12) | collective-permute-done | bytes 131104 | tf_op jit(solution)/shard_map/ppermute | solution.py:508
  60.8 8.4 %all_to_all.11 = f32[8,1,128]{2,1,0:T(1,128)S(1)} all-to-all(f32[8,1,128]{2,1,0:T(1,128)S(1)} %bitcast.27), channel_id=1, replica_groups=mesh['groups'=2,'blk'=4,'mpo'=2,'rep'=2] {'blk','rep'}, dimensions={0} | all-to-all | bytes 8192 | tf_op jit(solution)/shard_map/all_to_all | solution.py:513
  69.1 1.4 %final.1 = (bf16[3,1,128,256]{3,2,1,0:T(8,128)(2,1)}, f32[2,3]{1,0:T(2,128)}) custom-call(f32[8,128]{1,0:T(8,128)S(1)} %bitcast.26, f32[256,256]{1,0:T(8,128)S(1)} %get-tuple-element.36.r_ref, f32[256,256]{1,0:T(8,128)S(1)} %get-tuple-element.37.z_ref, f32[256,256]{1,0:T(8,128)S(1)} %get-tuple-element.33.refs_5_.w_ref, ...), custom_call_target="tpu_custom_call" | custom-call | bytes 262144 | tf_op jit(solution)/shard_map/final/pallas_call | solution.py:429
  (27 shorter events, 5.8 us)
Async XLA Ops:
  0.6 14.6 %collective-permute-start.1 = (bf16[256,256]{1,0:T(8,128)(2,1)}, bf16[256,256]{1,0:T(8,128)(2,1)S(1)}, u32[]{:S(2)}, u32[]{:S(2)}) collective-permute-start(bf16[256,256]{1,0:T(8,128)(2,1)} %bitcast.19), channel_id=1, source_target_pairs={{12,1},{9,4},{4,9},{1,12},{14,3},{11,6},{6,11},{3,14},{28,17},{25,... | collective-permute-start | bytes 393224 | tf_op jit(solution)/shard_map/ppermute | solution.py:469
  1.3 15.3 %collective-permute-start = (bf16[256,256]{1,0:T(8,128)(2,1)}, bf16[256,256]{1,0:T(8,128)(2,1)S(1)}, u32[]{:S(2)}, u32[]{:S(2)}) collective-permute-start(bf16[256,256]{1,0:T(8,128)(2,1)} %bitcast.20), channel_id=1, source_target_pairs={{9,0},{8,1},{13,4},{12,5},{1,8},{0,9},{5,12},{4,13},{11,2},{10,3},... | collective-permute-start | bytes 393224 | tf_op jit(solution)/shard_map/ppermute | solution.py:469
  6.8 0.7 copy-start.4
  9.0 1.9 %copy-start = (bf16[24,1,256,256]{3,2,1,0:T(8,128)(2,1)S(1)}, bf16[24,1,256,256]{3,2,1,0:T(8,128)(2,1)}, u32[]{:S(2)}) copy-start(bf16[24,1,256,256]{3,2,1,0:T(8,128)(2,1)} %param.5) | copy-start | bytes 9437188
  10.9 1.9 %copy-start.1 = (bf16[24,1,256,256]{3,2,1,0:T(8,128)(2,1)S(1)}, bf16[24,1,256,256]{3,2,1,0:T(8,128)(2,1)}, u32[]{:S(2)}) copy-start(bf16[24,1,256,256]{3,2,1,0:T(8,128)(2,1)} %param.6) | copy-start | bytes 9437188
  12.8 0.9 %copy-start.2 = (bf16[1,256,256]{2,1,0:T(8,128)(2,1)S(1)}, bf16[1,256,256]{2,1,0:T(8,128)(2,1)}, u32[]{:S(2)}) copy-start(bf16[1,256,256]{2,1,0:T(8,128)(2,1)} %param.4) | copy-start | bytes 393220
  18.0 6.0 %collective-permute-start.2 = (bf16[256,256]{1,0:T(8,128)(2,1)S(1)}, bf16[256,256]{1,0:T(8,128)(2,1)S(1)}, u32[]{:S(2)}, u32[]{:S(2)}) collective-permute-start(bf16[256,256]{1,0:T(8,128)(2,1)S(1)} %get-tuple-element.20.refs_0_), channel_id=1, source_target_pairs={{0,2},{2,0},{1,3},{3,1},{4,6},{6,4},{5,7},{7,5},{8,10},{10,8},{9,1... | collective-permute-start | bytes 393224 | tf_op jit(solution)/shard_map/ppermute | solution.py:508
  24.4 6.8 %collective-permute-start.3 = (bf16[160,256]{1,0:T(8,128)(2,1)S(1)}, bf16[160,256]{1,0:T(8,128)(2,1)S(1)}, u32[]{:S(2)}, u32[]{:S(2)}) collective-permute-start(bf16[160,256]{1,0:T(8,128)(2,1)S(1)} %get-tuple-element.23), channel_id=1, source_target_pairs={{9,0},{8,1},{13,4},{12,5},{1,8},{0,9},{5,12},{4,13},{11,2},{10,3},... | collective-permute-start | bytes 245768 | tf_op jit(solution)/shard_map/ppermute | solution.py:469
  24.4 10.1 %collective-permute-start.5 = (bf16[256,256]{1,0:T(8,128)(2,1)S(1)}, bf16[256,256]{1,0:T(8,128)(2,1)S(1)}, u32[]{:S(2)}, u32[]{:S(2)}) collective-permute-start(bf16[256,256]{1,0:T(8,128)(2,1)S(1)} %get-tuple-element.22.block_ref.refs_4_.refs_3_), channel_id=1, source_target_pairs={{12,1},{9,4},{4,9},{1,12},{14,3},{11,6},{6,11},{3,14},{28,17},{25,... | collective-permute-start | bytes 393224 | tf_op jit(solution)/shard_map/ppermute | solution.py:469
  31.2 4.3 %collective-permute-start.4 = (bf16[128,256]{1,0:T(8,128)(2,1)S(1)}, bf16[128,256]{1,0:T(8,128)(2,1)S(1)}, u32[]{:S(2)}, u32[]{:S(2)}) collective-permute-start(bf16[128,256]{1,0:T(8,128)(2,1)S(1)} %get-tuple-element.25.refs_5_), channel_id=1, source_target_pairs={{0,2},{2,0},{1,3},{3,1},{4,6},{6,4},{5,7},{7,5},{8,10},{10,8},{9,1... | collective-permute-start | bytes 196616 | tf_op jit(solution)/shard_map/ppermute | solution.py:501
  32.9 1.5 %collective-permute-start.6 = (f32[8,128]{1,0:T(8,128)S(1)}, f32[8,128]{1,0:T(8,128)S(1)}, u32[]{:S(2)}, u32[]{:S(2)}) collective-permute-start(f32[8,128]{1,0:T(8,128)S(1)} %get-tuple-element.26), channel_id=1, source_target_pairs={{0,1},{1,0},{4,5},{5,4},{8,9},{9,8},{12,13},{13,12},{2,3},{3,2},{6... | collective-permute-start | bytes 12296 | tf_op jit(solution)/shard_map/ppermute | solution.py:484
  34.5 8.9 %copy-start.3 = (bf16[1,256,256]{2,1,0:T(8,128)(2,1)S(1)}, bf16[1,256,256]{2,1,0:T(8,128)(2,1)}, u32[]{:S(2)}) copy-start(bf16[1,256,256]{2,1,0:T(8,128)(2,1)} %param.4) | copy-start | bytes 393220
  36.9 6.5 %collective-permute-start.7 = (bf16[256,256]{1,0:T(8,128)(2,1)S(1)}, bf16[256,256]{1,0:T(8,128)(2,1)S(1)}, u32[]{:S(2)}, u32[]{:S(2)}) collective-permute-start(bf16[256,256]{1,0:T(8,128)(2,1)S(1)} %get-tuple-element.27.refs_0_), channel_id=1, source_target_pairs={{0,2},{2,0},{1,3},{3,1},{4,6},{6,4},{5,7},{7,5},{8,10},{10,8},{9,1... | collective-permute-start | bytes 393224 | tf_op jit(solution)/shard_map/ppermute | solution.py:508
  38.6 4.8 %collective-permute-start.8 = (f32[8,128]{1,0:T(8,128)S(1)}, f32[8,128]{1,0:T(8,128)S(1)}, u32[]{:S(2)}, u32[]{:S(2)}) collective-permute-start(f32[8,128]{1,0:T(8,128)S(1)} %get-tuple-element.28), channel_id=1, source_target_pairs={{0,13},{1,12},{4,9},{5,8},{8,5},{9,4},{12,1},{13,0},{2,15},{3,14},... | collective-permute-start | bytes 12296 | tf_op jit(solution)/shard_map/ppermute | solution.py:484
  44.3 5.4 %collective-permute-start.9 = (bf16[128,256]{1,0:T(8,128)(2,1)S(1)}, bf16[128,256]{1,0:T(8,128)(2,1)S(1)}, u32[]{:S(2)}, u32[]{:S(2)}) collective-permute-start(bf16[128,256]{1,0:T(8,128)(2,1)S(1)} %get-tuple-element.31), channel_id=1, source_target_pairs={{9,0},{8,1},{13,4},{12,5},{1,8},{0,9},{5,12},{4,13},{11,2},{10,3},... | collective-permute-start | bytes 196616 | tf_op jit(solution)/shard_map/ppermute | solution.py:469
  44.3 9.6 %collective-permute-start.11 = (bf16[256,256]{1,0:T(8,128)(2,1)S(1)}, bf16[256,256]{1,0:T(8,128)(2,1)S(1)}, u32[]{:S(2)}, u32[]{:S(2)}) collective-permute-start(bf16[256,256]{1,0:T(8,128)(2,1)S(1)} %get-tuple-element.30.block_ref), channel_id=1, source_target_pairs={{12,1},{9,4},{4,9},{1,12},{14,3},{11,6},{6,11},{3,14},{28,17},{25,... | collective-permute-start | bytes 393224 | tf_op jit(solution)/shard_map/ppermute | solution.py:469
  49.6 4.3 %collective-permute-start.10 = (bf16[128,256]{1,0:T(8,128)(2,1)S(1)}, bf16[128,256]{1,0:T(8,128)(2,1)S(1)}, u32[]{:S(2)}, u32[]{:S(2)}) collective-permute-start(bf16[128,256]{1,0:T(8,128)(2,1)S(1)} %collective-permute-done.9.refs_4_), channel_id=1, source_target_pairs={{0,2},{2,0},{1,3},{3,1},{4,6},{6,4},{5,7},{7,5},{8,10},{10,8},{9,1... | collective-permute-start | bytes 196616 | tf_op jit(solution)/shard_map/ppermute | solution.py:501
  55.1 5.0 %collective-permute-start.12 = (bf16[256,256]{1,0:T(8,128)(2,1)S(1)}, bf16[256,256]{1,0:T(8,128)(2,1)S(1)}, u32[]{:S(2)}, u32[]{:S(2)}) collective-permute-start(bf16[256,256]{1,0:T(8,128)(2,1)S(1)} %rest.5.refs_0_), channel_id=1, source_target_pairs={{0,2},{2,0},{1,3},{3,1},{4,6},{6,4},{5,7},{7,5},{8,10},{10,8},{9,1... | collective-permute-start | bytes 393224 | tf_op jit(solution)/shard_map/ppermute | solution.py:508

commit v10 on v8

--- a/solution.py
+++ b/solution.py
@@ -78,13 +78,9 @@
 
 
 def carried_rounds(permutes, blocks):
-    if len(permutes) < 2 or blocks % 2:
+    if not permutes or blocks % 4:
         return None
-    last = dict(permutes[1])
-    for k in range(blocks):
-        if k not in last:
-            last[k] = blocks - 1 - k
-    rounds = [dict(permutes[0]), {k: k ^ 1 for k in range(blocks)}, last]
+    rounds = [dict(permutes[0])] + [{k: k ^ bit for k in range(blocks)} for bit in (1, 2)]
     held = [{k} for k in range(blocks)]
     for pairs in rounds:
         if sorted(pairs.values()) != list(range(blocks)):

time: 71.4 us -> 70.5 us (0.987)
  blocking collectives: 8.81 us -> 7.91 us
  starting transfers between devices: 14.5 us -> 13.7 us
    ppermute x2, waiting for transfers between devices: 4.77 us -> 3.61 us  [add_round(): return rows + lax.ppermute(rows, axis, pairs)]
    all_to_all x1, blocking collectives: 8.81 us -> 7.91 us  [exchange(): return lax.all_to_all(rows, ring, 0, 0, tiled=True)]
    ppermute x3, waiting for transfers between devices: 8.56 us -> 9.4 us  [gather_parts(): return [t, lax.ppermute(t, 'mpo', [(0, 1), (1, 0)])]]
  transfers between devices with their start and end apart: 13 -> 13, of which waited for: 8 -> 9; matrix products, arithmetic and copies ran while one was open for 0% -> 0% of each run, Pallas kernels for 5% -> 5%
where the time goes in v10:
time: 70.5 us; the launch traced here: 69.9 us
  waiting for transfers between devices  31.2 us (44%)
  starting transfers between devices  13.7 us (19%)
  Pallas kernels  10.9 us (15%)
  blocking collectives  7.91 us (11%)
  local copies, waits for them, and re-layouts  5.34 us (8%)
  between operations  0.79 us (1%)
    ppermute x6, waiting for transfers between devices, shift(): return lax.ppermute(block, ring, pairs)  14 us
    pallas_call x11, Pallas kernels, call(): pl.pallas_call(kernel, out_shape=outs, in_specs=[first] + [VMEM] * (len(a...  10.9 us
    ppermute x3, waiting for transfers between devices, gather_parts(): return [t, lax.ppermute(t, 'mpo', [(0, 1), (1, 0)])]  9.4 us
    all_to_all x1, blocking collectives, exchange(): return lax.all_to_all(rows, ring, 0, 0, tiled=True)  7.91 us
    ppermute x6, starting transfers between devices, shift(): return lax.ppermute(block, ring, pairs)  7.62 us
    unnamed x10, local copies, waits for them, and re-layouts  5.34 us
    ppermute x3, starting transfers between devices, gather_parts(): return [t, lax.ppermute(t, 'mpo', [(0, 1), (1, 0)])]  4.29 us
    ppermute x2, waiting for transfers between devices, spread(): first = [piece, lax.ppermute(piece, 'mpo', [(0, 1), (1, 0)])]  4.22 us
  transfers between devices with their start and end apart: 13, of which 9 were waited for; matrix products, arithmetic and copies ran while one was open for 0% of the time, Pallas kernels for 5%

profile of v10, /device:TPU:0, one launch (start us, length us, event | category | flops | bytes accessed | tf_op | source)
XLA Modules:
  0.0 69.9 jit_solution(11818923469501407411)
XLA Ops:
  1.3 5.5 %collective-permute-start = (bf16[256,256]{1,0:T(8,128)(2,1)}, bf16[256,256]{1,0:T(8,128)(2,1)S(1)}, u32[]{:S(2)}, u32[]{:S(2)}) collective-permute-start(bf16[256,256]{1,0:T(8,128)(2,1)} %bitcast.20), channel_id=1, source_target_pairs={{9,0},{8,1},{13,4},{12,5},{1,8},{0,9},{5,12},{4,13},{11,2},{10,3},... | collective-permute-start | bytes 393224 | tf_op jit(solution)/shard_map/ppermute | solution.py:455
  6.8 1.9 %copy-done = bf16[24,1,256,256]{3,2,1,0:T(8,128)(2,1)S(1)} copy-done((bf16[24,1,256,256]{3,2,1,0:T(8,128)(2,1)S(1)}, bf16[24,1,256,256]{3,2,1,0:T(8,128)(2,1)}, u32[]{:S(2)}) %copy-start) | copy-done | bytes 3145752
  8.7 1.9 %copy-done.1 = bf16[24,1,256,256]{3,2,1,0:T(8,128)(2,1)S(1)} copy-done((bf16[24,1,256,256]{3,2,1,0:T(8,128)(2,1)S(1)}, bf16[24,1,256,256]{3,2,1,0:T(8,128)(2,1)}, u32[]{:S(2)}) %copy-start.1) | copy-done | bytes 3145752
  10.6 0.9 %copy-done.2 = bf16[1,256,256]{2,1,0:T(8,128)(2,1)S(1)} copy-done((bf16[1,256,256]{2,1,0:T(8,128)(2,1)S(1)}, bf16[1,256,256]{2,1,0:T(8,128)(2,1)}, u32[]{:S(2)}) %copy-start.2) | copy-done | bytes 131096
  12.2 1.2 %own.3.refs_3_ = f32[256,256]{1,0:T(8,128)S(1)} custom-call(s32[24]{0:T(128)S(1)} %copy-done.4, bf16[24,256,256]{2,1,0:T(8,128)(2,1)S(1)} %bitcast.7, bf16[24,256,256]{2,1,0:T(8,128)(2,1)S(1)} %bitcast.13, bf16[256,256]{1,0:T(8,128)(2,1)S(1)} %bitcast.21), custom_call_target="tpu_custom_call" | custom-call | flops 322122560 | bytes 262144 | tf_op jit(solution)/shard_map/own/pallas_call | solution.py:415
  13.4 3.2 %collective-permute-done.refs_5_ = bf16[256,256]{1,0:T(8,128)(2,1)S(1)} collective-permute-done((bf16[256,256]{1,0:T(8,128)(2,1)}, bf16[256,256]{1,0:T(8,128)(2,1)S(1)}, u32[]{:S(2)}, u32[]{:S(2)}) %collective-permute-start) | collective-permute-done | bytes 131104 | tf_op jit(solution)/shard_map/ppermute | solution.py:455
  16.6 1.3 %rest.3 = (bf16[256,256]{1,0:T(8,128)(2,1)S(1)}, f32[8,128]{1,0:T(8,128)S(1)}) custom-call(s32[24]{0:T(128)S(1)} %copy-done.4, bf16[24,256,256]{2,1,0:T(8,128)(2,1)S(1)} %bitcast.8, bf16[24,256,256]{2,1,0:T(8,128)(2,1)S(1)} %bitcast.14, f32[256,256]{1,0:T(8,128)S(1)} %own.3.refs_3_, bf16[256,256]{1,0:T(8,128)(2,1)S(1)} %bitcast.22, ...), custom_call_target="tpu_custom_call" | custom-call | flops 644245120 | bytes 262144 | tf_op jit(solution)/shard_map/rest/pallas_call | solution.py:415
  17.9 1.8 %collective-permute-start.2 = (bf16[256,256]{1,0:T(8,128)(2,1)S(1)}, bf16[256,256]{1,0:T(8,128)(2,1)S(1)}, u32[]{:S(2)}, u32[]{:S(2)}) collective-permute-start(bf16[256,256]{1,0:T(8,128)(2,1)S(1)} %get-tuple-element.20.refs_0_), channel_id=1, source_target_pairs={{0,2},{2,0},{1,3},{3,1},{4,6},{6,4},{5,7},{7,5},{8,10},{10,8},{9,1... | collective-permute-start | bytes 393224 | tf_op jit(solution)/shard_map/ppermute | solution.py:494
  19.8 4.4 %collective-permute-done.2.refs_1_ = bf16[256,256]{1,0:T(8,128)(2,1)S(1)} collective-permute-done((bf16[256,256]{1,0:T(8,128)(2,1)S(1)}, bf16[256,256]{1,0:T(8,128)(2,1)S(1)}, u32[]{:S(2)}, u32[]{:S(2)}) %collective-permute-start.2) | collective-permute-done | bytes 131104 | tf_op jit(solution)/shard_map/ppermute | solution.py:494
  25.3 5.8 %collective-permute-done.3.block_ref = bf16[160,256]{1,0:T(8,128)(2,1)S(1)} collective-permute-done((bf16[160,256]{1,0:T(8,128)(2,1)S(1)}, bf16[160,256]{1,0:T(8,128)(2,1)S(1)}, u32[]{:S(2)}, u32[]{:S(2)}) %collective-permute-start.3) | collective-permute-done | bytes 81952 | tf_op jit(solution)/shard_map/ppermute | solution.py:455
  31.1 1.3 %collective-permute-start.4 = (bf16[128,256]{1,0:T(8,128)(2,1)S(1)}, bf16[128,256]{1,0:T(8,128)(2,1)S(1)}, u32[]{:S(2)}, u32[]{:S(2)}) collective-permute-start(bf16[128,256]{1,0:T(8,128)(2,1)S(1)} %get-tuple-element.25.refs_5_), channel_id=1, source_target_pairs={{0,2},{2,0},{1,3},{3,1},{4,6},{6,4},{5,7},{7,5},{8,10},{10,8},{9,1... | collective-permute-start | bytes 196616 | tf_op jit(solution)/shard_map/ppermute | solution.py:487
  32.4 1.2 %own.4.refs_3_ = f32[256,256]{1,0:T(8,128)S(1)} custom-call(s32[24]{0:T(128)S(1)} %copy-done.4, bf16[24,256,256]{2,1,0:T(8,128)(2,1)S(1)} %bitcast.9, bf16[24,256,256]{2,1,0:T(8,128)(2,1)S(1)} %bitcast.15, bf16[256,256]{1,0:T(8,128)(2,1)S(1)} %get-tuple-element.22.block_ref.refs_4_.refs_3_), custom_call_target="tpu_custom_call" | custom-call | flops 322122560 | bytes 262144 | tf_op jit(solution)/shard_map/own/pallas_call | solution.py:415
  33.7 1.7 %collective-permute-done.4.refs_6_ = bf16[128,256]{1,0:T(8,128)(2,1)S(1)} collective-permute-done((bf16[128,256]{1,0:T(8,128)(2,1)S(1)}, bf16[128,256]{1,0:T(8,128)(2,1)S(1)}, u32[]{:S(2)}, u32[]{:S(2)}) %collective-permute-start.4) | collective-permute-done | bytes 65568 | tf_op jit(solution)/shard_map/ppermute | solution.py:487
  35.4 1.3 %rest.4 = (bf16[256,256]{1,0:T(8,128)(2,1)S(1)}, f32[8,128]{1,0:T(8,128)S(1)}, f32[8,128]{1,0:T(8,128)S(1)}) custom-call(s32[24]{0:T(128)S(1)} %copy-done.4, bf16[24,256,256]{2,1,0:T(8,128)(2,1)S(1)} %bitcast.10, bf16[24,256,256]{2,1,0:T(8,128)(2,1)S(1)} %bitcast.16, f32[256,256]{1,0:T(8,128)S(1)} %own.4.refs_3_, ...), custom_call_target="tpu_custom_call" | custom-call | flops 644245120 | bytes 262144 | tf_op jit(solution)/shard_map/rest/pallas_call | solution.py:415
  36.7 1.6 %collective-permute-start.7 = (bf16[256,256]{1,0:T(8,128)(2,1)S(1)}, bf16[256,256]{1,0:T(8,128)(2,1)S(1)}, u32[]{:S(2)}, u32[]{:S(2)}) collective-permute-start(bf16[256,256]{1,0:T(8,128)(2,1)S(1)} %get-tuple-element.27.refs_0_), channel_id=1, source_target_pairs={{0,2},{2,0},{1,3},{3,1},{4,6},{6,4},{5,7},{7,5},{8,10},{10,8},{9,1... | collective-permute-start | bytes 393224 | tf_op jit(solution)/shard_map/ppermute | solution.py:494
  38.3 3.6 %collective-permute-done.8 = f32[8,128]{1,0:T(8,128)S(1)} collective-permute-done((f32[8,128]{1,0:T(8,128)S(1)}, f32[8,128]{1,0:T(8,128)S(1)}, u32[]{:S(2)}, u32[]{:S(2)}) %collective-permute-start.8) | collective-permute-done | bytes 4128 | tf_op jit(solution)/shard_map/ppermute | solution.py:470
  43.9 5.0 %collective-permute-done.9.refs_4_ = bf16[128,256]{1,0:T(8,128)(2,1)S(1)} collective-permute-done((bf16[128,256]{1,0:T(8,128)(2,1)S(1)}, bf16[128,256]{1,0:T(8,128)(2,1)S(1)}, u32[]{:S(2)}, u32[]{:S(2)}) %collective-permute-start.9) | collective-permute-done | bytes 65568 | tf_op jit(solution)/shard_map/ppermute | solution.py:455
  49.5 1.2 %own.5.refs_3_ = f32[256,256]{1,0:T(8,128)S(1)} custom-call(s32[24]{0:T(128)S(1)} %copy-done.4, bf16[24,256,256]{2,1,0:T(8,128)(2,1)S(1)} %bitcast.11, bf16[24,256,256]{2,1,0:T(8,128)(2,1)S(1)} %bitcast.17, bf16[256,256]{1,0:T(8,128)(2,1)S(1)} %get-tuple-element.30.block_ref), custom_call_target="tpu_custom_call" | custom-call | flops 322122560 | bytes 262144 | tf_op jit(solution)/shard_map/own/pallas_call | solution.py:415
  50.7 2.5 %collective-permute-done.10.refs_5_ = bf16[128,256]{1,0:T(8,128)(2,1)S(1)} collective-permute-done((bf16[128,256]{1,0:T(8,128)(2,1)S(1)}, bf16[128,256]{1,0:T(8,128)(2,1)S(1)}, u32[]{:S(2)}, u32[]{:S(2)}) %collective-permute-start.10) | collective-permute-done | bytes 65568 | tf_op jit(solution)/shard_map/ppermute | solution.py:487
  53.2 1.3 %rest.5.refs_0_ = bf16[256,256]{1,0:T(8,128)(2,1)S(1)} custom-call(s32[24]{0:T(128)S(1)} %copy-done.4, bf16[24,256,256]{2,1,0:T(8,128)(2,1)S(1)} %bitcast.12, bf16[24,256,256]{2,1,0:T(8,128)(2,1)S(1)} %bitcast.18, f32[256,256]{1,0:T(8,128)S(1)} %own.5.refs_3_, bf16[128,256]{1,0:T(8,128)(2,1)S(1)} %collective-permute-done.9.refs_4_, ...), custom_call_target="tpu_custom_call" | custom-call | flops 644245120 | bytes 262144 | tf_op jit(solution)/shard_map/rest/pallas_call | solution.py:415
  54.5 0.9 %collective-permute-start.12 = (bf16[256,256]{1,0:T(8,128)(2,1)S(1)}, bf16[256,256]{1,0:T(8,128)(2,1)S(1)}, u32[]{:S(2)}, u32[]{:S(2)}) collective-permute-start(bf16[256,256]{1,0:T(8,128)(2,1)S(1)} %rest.5.refs_0_), channel_id=1, source_target_pairs={{0,2},{2,0},{1,3},{3,1},{4,6},{6,4},{5,7},{7,5},{8,10},{10,8},{9,1... | collective-permute-start | bytes 393224 | tf_op jit(solution)/shard_map/ppermute | solution.py:494
  55.4 4.6 %collective-permute-done.12.refs_1_ = bf16[256,256]{1,0:T(8,128)(2,1)S(1)} collective-permute-done((bf16[256,256]{1,0:T(8,128)(2,1)S(1)}, bf16[256,256]{1,0:T(8,128)(2,1)S(1)}, u32[]{:S(2)}, u32[]{:S(2)}) %collective-permute-start.12) | collective-permute-done | bytes 131104 | tf_op jit(solution)/shard_map/ppermute | solution.py:494
  60.6 7.9 %all_to_all.11 = f32[8,1,128]{2,1,0:T(1,128)S(1)} all-to-all(f32[8,1,128]{2,1,0:T(1,128)S(1)} %bitcast.27), channel_id=1, replica_groups=mesh['groups'=2,'blk'=4,'mpo'=2,'rep'=2] {'blk','rep'}, dimensions={0} | all-to-all | bytes 8192 | tf_op jit(solution)/shard_map/all_to_all | solution.py:499
  68.6 1.4 %final.1 = (bf16[3,1,128,256]{3,2,1,0:T(8,128)(2,1)}, f32[2,3]{1,0:T(2,128)}) custom-call(f32[8,128]{1,0:T(8,128)S(1)} %bitcast.26, f32[256,256]{1,0:T(8,128)S(1)} %get-tuple-element.36.r_ref, f32[256,256]{1,0:T(8,128)S(1)} %get-tuple-element.37.z_ref, f32[256,256]{1,0:T(8,128)S(1)} %get-tuple-element.33.refs_5_.w_ref, ...), custom_call_target="tpu_custom_call" | custom-call | bytes 262144 | tf_op jit(solution)/shard_map/final/pallas_call | solution.py:415
  (26 shorter events, 5.5 us)
Async XLA Ops:
  0.6 12.8 %collective-permute-start.1 = (bf16[256,256]{1,0:T(8,128)(2,1)}, bf16[256,256]{1,0:T(8,128)(2,1)S(1)}, u32[]{:S(2)}, u32[]{:S(2)}) collective-permute-start(bf16[256,256]{1,0:T(8,128)(2,1)} %bitcast.19), channel_id=1, source_target_pairs={{12,1},{9,4},{4,9},{1,12},{14,3},{11,6},{6,11},{3,14},{28,17},{25,... | collective-permute-start | bytes 393224 | tf_op jit(solution)/shard_map/ppermute | solution.py:455
  1.3 15.3 %collective-permute-start = (bf16[256,256]{1,0:T(8,128)(2,1)}, bf16[256,256]{1,0:T(8,128)(2,1)S(1)}, u32[]{:S(2)}, u32[]{:S(2)}) collective-permute-start(bf16[256,256]{1,0:T(8,128)(2,1)} %bitcast.20), channel_id=1, source_target_pairs={{9,0},{8,1},{13,4},{12,5},{1,8},{0,9},{5,12},{4,13},{11,2},{10,3},... | collective-permute-start | bytes 393224 | tf_op jit(solution)/shard_map/ppermute | solution.py:455
  6.8 1.9 %copy-start = (bf16[24,1,256,256]{3,2,1,0:T(8,128)(2,1)S(1)}, bf16[24,1,256,256]{3,2,1,0:T(8,128)(2,1)}, u32[]{:S(2)}) copy-start(bf16[24,1,256,256]{3,2,1,0:T(8,128)(2,1)} %param.5) | copy-start | bytes 9437188
  8.7 1.9 %copy-start.1 = (bf16[24,1,256,256]{3,2,1,0:T(8,128)(2,1)S(1)}, bf16[24,1,256,256]{3,2,1,0:T(8,128)(2,1)}, u32[]{:S(2)}) copy-start(bf16[24,1,256,256]{3,2,1,0:T(8,128)(2,1)} %param.6) | copy-start | bytes 9437188
  10.6 0.9 %copy-start.2 = (bf16[1,256,256]{2,1,0:T(8,128)(2,1)S(1)}, bf16[1,256,256]{2,1,0:T(8,128)(2,1)}, u32[]{:S(2)}) copy-start(bf16[1,256,256]{2,1,0:T(8,128)(2,1)} %param.4) | copy-start | bytes 393220
  11.5 0.7 copy-start.4
  17.9 6.3 %collective-permute-start.2 = (bf16[256,256]{1,0:T(8,128)(2,1)S(1)}, bf16[256,256]{1,0:T(8,128)(2,1)S(1)}, u32[]{:S(2)}, u32[]{:S(2)}) collective-permute-start(bf16[256,256]{1,0:T(8,128)(2,1)S(1)} %get-tuple-element.20.refs_0_), channel_id=1, source_target_pairs={{0,2},{2,0},{1,3},{3,1},{4,6},{6,4},{5,7},{7,5},{8,10},{10,8},{9,1... | collective-permute-start | bytes 393224 | tf_op jit(solution)/shard_map/ppermute | solution.py:494
  24.6 6.5 %collective-permute-start.3 = (bf16[160,256]{1,0:T(8,128)(2,1)S(1)}, bf16[160,256]{1,0:T(8,128)(2,1)S(1)}, u32[]{:S(2)}, u32[]{:S(2)}) collective-permute-start(bf16[160,256]{1,0:T(8,128)(2,1)S(1)} %get-tuple-element.23), channel_id=1, source_target_pairs={{9,0},{8,1},{13,4},{12,5},{1,8},{0,9},{5,12},{4,13},{11,2},{10,3},... | collective-permute-start | bytes 245768 | tf_op jit(solution)/shard_map/ppermute | solution.py:455
  24.6 9.0 %collective-permute-start.5 = (bf16[256,256]{1,0:T(8,128)(2,1)S(1)}, bf16[256,256]{1,0:T(8,128)(2,1)S(1)}, u32[]{:S(2)}, u32[]{:S(2)}) collective-permute-start(bf16[256,256]{1,0:T(8,128)(2,1)S(1)} %get-tuple-element.22.block_ref.refs_4_.refs_3_), channel_id=1, source_target_pairs={{12,1},{9,4},{4,9},{1,12},{14,3},{11,6},{6,11},{3,14},{28,17},{25,... | collective-permute-start | bytes 393224 | tf_op jit(solution)/shard_map/ppermute | solution.py:455
  31.1 4.3 %collective-permute-start.4 = (bf16[128,256]{1,0:T(8,128)(2,1)S(1)}, bf16[128,256]{1,0:T(8,128)(2,1)S(1)}, u32[]{:S(2)}, u32[]{:S(2)}) collective-permute-start(bf16[128,256]{1,0:T(8,128)(2,1)S(1)} %get-tuple-element.25.refs_5_), channel_id=1, source_target_pairs={{0,2},{2,0},{1,3},{3,1},{4,6},{6,4},{5,7},{7,5},{8,10},{10,8},{9,1... | collective-permute-start | bytes 196616 | tf_op jit(solution)/shard_map/ppermute | solution.py:487
  32.4 1.3 %collective-permute-start.6 = (f32[8,128]{1,0:T(8,128)S(1)}, f32[8,128]{1,0:T(8,128)S(1)}, u32[]{:S(2)}, u32[]{:S(2)}) collective-permute-start(f32[8,128]{1,0:T(8,128)S(1)} %get-tuple-element.26), channel_id=1, source_target_pairs={{0,1},{1,0},{4,5},{5,4},{8,9},{9,8},{12,13},{13,12},{2,3},{3,2},{6... | collective-permute-start | bytes 12296 | tf_op jit(solution)/shard_map/ppermute | solution.py:470
  33.6 8.6 %copy-start.3 = (bf16[1,256,256]{2,1,0:T(8,128)(2,1)S(1)}, bf16[1,256,256]{2,1,0:T(8,128)(2,1)}, u32[]{:S(2)}) copy-start(bf16[1,256,256]{2,1,0:T(8,128)(2,1)} %param.4) | copy-start | bytes 393220
  36.7 5.5 %collective-permute-start.7 = (bf16[256,256]{1,0:T(8,128)(2,1)S(1)}, bf16[256,256]{1,0:T(8,128)(2,1)S(1)}, u32[]{:S(2)}, u32[]{:S(2)}) collective-permute-start(bf16[256,256]{1,0:T(8,128)(2,1)S(1)} %get-tuple-element.27.refs_0_), channel_id=1, source_target_pairs={{0,2},{2,0},{1,3},{3,1},{4,6},{6,4},{5,7},{7,5},{8,10},{10,8},{9,1... | collective-permute-start | bytes 393224 | tf_op jit(solution)/shard_map/ppermute | solution.py:494
  38.3 3.6 %collective-permute-start.8 = (f32[8,128]{1,0:T(8,128)S(1)}, f32[8,128]{1,0:T(8,128)S(1)}, u32[]{:S(2)}, u32[]{:S(2)}) collective-permute-start(f32[8,128]{1,0:T(8,128)S(1)} %get-tuple-element.28), channel_id=1, source_target_pairs={{0,4},{1,5},{4,0},{5,1},{8,12},{9,13},{12,8},{13,9},{2,6},{3,7},{6... | collective-permute-start | bytes 12296 | tf_op jit(solution)/shard_map/ppermute | solution.py:470
  43.1 5.8 %collective-permute-start.9 = (bf16[128,256]{1,0:T(8,128)(2,1)S(1)}, bf16[128,256]{1,0:T(8,128)(2,1)S(1)}, u32[]{:S(2)}, u32[]{:S(2)}) collective-permute-start(bf16[128,256]{1,0:T(8,128)(2,1)S(1)} %get-tuple-element.31), channel_id=1, source_target_pairs={{9,0},{8,1},{13,4},{12,5},{1,8},{0,9},{5,12},{4,13},{11,2},{10,3},... | collective-permute-start | bytes 196616 | tf_op jit(solution)/shard_map/ppermute | solution.py:455
  43.2 10.0 %collective-permute-start.11 = (bf16[256,256]{1,0:T(8,128)(2,1)S(1)}, bf16[256,256]{1,0:T(8,128)(2,1)S(1)}, u32[]{:S(2)}, u32[]{:S(2)}) collective-permute-start(bf16[256,256]{1,0:T(8,128)(2,1)S(1)} %get-tuple-element.30.block_ref), channel_id=1, source_target_pairs={{12,1},{9,4},{4,9},{1,12},{14,3},{11,6},{6,11},{3,14},{28,17},{25,... | collective-permute-start | bytes 393224 | tf_op jit(solution)/shard_map/ppermute | solution.py:455
  48.9 4.3 %collective-permute-start.10 = (bf16[128,256]{1,0:T(8,128)(2,1)S(1)}, bf16[128,256]{1,0:T(8,128)(2,1)S(1)}, u32[]{:S(2)}, u32[]{:S(2)}) collective-permute-start(bf16[128,256]{1,0:T(8,128)(2,1)S(1)} %collective-permute-done.9.refs_4_), channel_id=1, source_target_pairs={{0,2},{2,0},{1,3},{3,1},{4,6},{6,4},{5,7},{7,5},{8,10},{10,8},{9,1... | collective-permute-start | bytes 196616 | tf_op jit(solution)/shard_map/ppermute | solution.py:487
  54.5 5.5 %collective-permute-start.12 = (bf16[256,256]{1,0:T(8,128)(2,1)S(1)}, bf16[256,256]{1,0:T(8,128)(2,1)S(1)}, u32[]{:S(2)}, u32[]{:S(2)}) collective-permute-start(bf16[256,256]{1,0:T(8,128)(2,1)S(1)} %rest.5.refs_0_), channel_id=1, source_target_pairs={{0,2},{2,0},{1,3},{3,1},{4,6},{6,4},{5,7},{7,5},{8,10},{10,8},{9,1... | collective-permute-start | bytes 393224 | tf_op jit(solution)/shard_map/ppermute | solution.py:494

commit v11 on v10

--- a/solution.py
+++ b/solution.py
@@ -14,6 +14,7 @@
 WIDE = 8
 SMALLEST = 1e-30
 TILE = 16
+LOADS = 4
 MIB = 1024 * 1024
 VMEM = pl.BlockSpec(memory_space=pltpu.VMEM)
 SMEM = pl.BlockSpec(memory_space=pltpu.SMEM)
@@ -194,6 +195,20 @@
         @pl.when((rest > low) & (rest <= wide))
         def _():
             multiply(groups * WIDE, wide)
+
+
+def load_kernel(left_hbm, right_hbm, left_ref, right_ref, sems):
+    channels = left_ref.shape[0]
+    step = max(1, channels // LOADS)
+    copies = []
+    for side, (source, target) in enumerate(((left_hbm, left_ref), (right_hbm, right_ref))):
+        for at, low in enumerate(range(0, channels, step)):
+            part = pl.ds(low, min(step, channels - low))
+            copies.append(pltpu.make_async_copy(source.at[part], target.at[part], sems.at[side, at]))
+    for copy in copies:
+        copy.start()
+    for copy in copies:
+        copy.wait()
 
 
 def own_kernel(scaled, places, kinds_ref, left_ref, right_ref, block_ref, acc, source, order, slot_of):
@@ -261,6 +276,10 @@
     row = lax.broadcasted_iota(jnp.int32, rows_ref.shape, 0)
     source = look_up(origin, here(), 0)
     sums_ref[...] = jnp.where(row == source, first_row(sums), rows_ref[...])
+
+
+def take_kernel(block_ref, share_ref):
+    share_ref[...] = block_ref[my_rows(share_ref.shape[0]), :]
 
 
 def my_rows(share):
@@ -400,6 +419,15 @@
     slots = 1 + len(permutes)
     channels = channel_class.shape[0]
     psi, left, right = wavefunction[0], env_left[:, 0], env_right[:, 0]
+    left, right = pl.pallas_call(
+        load_kernel,
+        out_shape=(jax.ShapeDtypeStruct(left.shape, left.dtype),) * 2,
+        in_specs=[pl.BlockSpec(memory_space=pl.ANY)] * 2,
+        out_specs=(VMEM, VMEM),
+        scratch_shapes=[pltpu.SemaphoreType.DMA((2, channels))],
+        compiler_params=pltpu.CompilerParams(vmem_limit_bytes=46 * MIB),
+        name="load",
+    )(left, right)
     rows_shape = jax.ShapeDtypeStruct((blocks, 128), jnp.float32)
     scalars = jax.ShapeDtypeStruct((8, 128), jnp.float32)
     wide = jax.ShapeDtypeStruct((width, width), jnp.float32)
@@ -469,7 +497,7 @@
             return lax.psum(rows, axis)
         return rows + lax.ppermute(rows, axis, pairs)
 
-    def spread(block, share, rows=None):
+    def spread(block, share, rows=None, after=None):
         piece = shift(share, permutes[0])
         if rows is not None and carried:
             piece, rows = call(
@@ -483,6 +511,8 @@
             for step in rounds[:-1]:
                 rows = add_round(rows, *step)
             piece = call(pass_kernel, "hold", share_shape, (piece, rows))
+        elif after is not None:
+            piece = call(pass_kernel, "hold", share_shape, (piece, after))
         if parts == 2:
             first = [piece, lax.ppermute(piece, "mpo", [(0, 1), (1, 0)])]
         else:
@@ -498,8 +528,8 @@
     def exchange(rows):
         return lax.all_to_all(rows, ring, 0, 0, tiled=True)
 
-    held = [shift(psi, pairs) for pairs in permutes]
-    t, unit = rest(own(True, psi), held[:1], held[1:], psi)
+    first, others, _ = spread(psi, call(take_kernel, "take", share_shape, (psi,)), after=left)
+    t, unit = rest(own(True, psi), first, others, psi)
     rows_in_share = width // parts + (2 * TILE if carried else 0)
     w_1, share_1, rows = call(
         functools.partial(first_sums_kernel, width // parts),

time: 70.5 us -> 73 us (1.035)
  waiting for transfers between devices: 31.2 us -> 15.9 us
  starting transfers between devices: 13.7 us -> 23.8 us
  Pallas kernels: 10.9 us -> 19.4 us
  local copies, waits for them, and re-layouts: 5.34 us -> 0.01 us
  blocking collectives: 7.91 us -> 12 us
    ppermute x6, waiting for transfers between devices: 14 us -> 5.42 us  [shift(): return lax.ppermute(block, ring, pairs)]
    ppermute x2, starting transfers between devices: 0.01 us -> 5.97 us  [add_round(): return rows + lax.ppermute(rows, axis, pairs)]
    unnamed x10 -> x2, local copies, waits for them, and re-layouts: 5.34 us -> 0.01 us
    pallas_call x11 -> x13, Pallas kernels: 10.9 us -> 16.1 us  [call(): pl.pallas_call(kernel, out_shape=outs, in_specs=[first] + [VMEM] * (len(a...]
    all_to_all x1, blocking collectives: 7.91 us -> 12 us  [exchange(): return lax.all_to_all(rows, ring, 0, 0, tiled=True)]
    ppermute x2 -> x3, starting transfers between devices: 1.83 us -> 5.53 us  [spread(): first = [piece, lax.ppermute(piece, 'mpo', [(0, 1), (1, 0)])]]
    pallas_call x0 -> x1, Pallas kernels: none -> 3.22 us  [shards(): pl.pallas_call(load_kernel, out_shape=(jax.ShapeDtypeStruct(left.shape, l...]
    ppermute x2 -> x3, waiting for transfers between devices: 4.22 us -> 1.84 us  [spread(): first = [piece, lax.ppermute(piece, 'mpo', [(0, 1), (1, 0)])]]
  transfers between devices with their start and end apart: 13 -> 14, of which waited for: 9 -> 8; matrix products, arithmetic and copies ran while one was open for 0% -> 0% of each run, Pallas kernels for 5% -> 11%
where the time goes in v11:
time: 73 us; the launch traced here: 71.9 us
  starting transfers between devices  23.8 us (33%)
  Pallas kernels  19.4 us (27%)
  waiting for transfers between devices  15.9 us (22%)
  blocking collectives  12 us (16%)
  between operations  0.8 us (1%)
    pallas_call x13, Pallas kernels, call(): pl.pallas_call(kernel, out_shape=outs, in_specs=[first] + [VMEM] * (len(a...  16.1 us
    all_to_all x1, blocking collectives, exchange(): return lax.all_to_all(rows, ring, 0, 0, tiled=True)  12 us
    ppermute x6, starting transfers between devices, shift(): return lax.ppermute(block, ring, pairs)  8.34 us
    ppermute x3, waiting for transfers between devices, gather_parts(): return [t, lax.ppermute(t, 'mpo', [(0, 1), (1, 0)])]  7.08 us
    ppermute x2, starting transfers between devices, add_round(): return rows + lax.ppermute(rows, axis, pairs)  5.97 us
    ppermute x3, starting transfers between devices, spread(): first = [piece, lax.ppermute(piece, 'mpo', [(0, 1), (1, 0)])]  5.53 us
    ppermute x6, waiting for transfers between devices, shift(): return lax.ppermute(block, ring, pairs)  5.42 us
    ppermute x3, starting transfers between devices, gather_parts(): return [t, lax.ppermute(t, 'mpo', [(0, 1), (1, 0)])]  3.98 us
  transfers between devices with their start and end apart: 14, of which 8 were waited for; matrix products, arithmetic and copies ran while one was open for 0% of the time, Pallas kernels for 11%

profile of v11, /device:TPU:0, one launch (start us, length us, event | category | flops | bytes accessed | tf_op | source)
XLA Modules:
  0.0 71.9 jit_solution(7800764823659616086)
XLA Ops:
  1.5 3.5 %collective-permute-start = (bf16[128,256]{1,0:T(8,128)(2,1)S(1)}, bf16[128,256]{1,0:T(8,128)(2,1)S(1)}, u32[]{:S(2)}, u32[]{:S(2)}) collective-permute-start(bf16[128,256]{1,0:T(8,128)(2,1)S(1)} %take.1), channel_id=1, source_target_pairs={{9,0},{8,1},{13,4},{12,5},{1,8},{0,9},{5,12},{4,13},{11,2},{10,3},... | collective-permute-start | bytes 196616 | tf_op jit(solution)/shard_map/ppermute | solution.py:483
  5.7 3.2 %load.1 = (bf16[24,256,256]{2,1,0:T(8,128)(2,1)S(1)}, bf16[24,256,256]{2,1,0:T(8,128)(2,1)S(1)}) custom-call(bf16[24,256,256]{2,1,0:T(8,128)(2,1)} %bitcast.9, bf16[24,256,256]{2,1,0:T(8,128)(2,1)} %bitcast.10), custom_call_target="tpu_custom_call" | custom-call | tf_op jit(solution)/shard_map/load/pallas_call | solution.py:422
  8.9 2.0 %collective-permute-start.1 = (bf16[128,256]{1,0:T(8,128)(2,1)S(1)}, bf16[128,256]{1,0:T(8,128)(2,1)S(1)}, u32[]{:S(2)}, u32[]{:S(2)}) collective-permute-start(bf16[128,256]{1,0:T(8,128)(2,1)S(1)} %hold.1.refs_5_), channel_id=1, source_target_pairs={{0,2},{2,0},{1,3},{3,1},{4,6},{6,4},{5,7},{7,5},{8,10},{10,8},{9,1... | collective-permute-start | bytes 196616 | tf_op jit(solution)/shard_map/ppermute | solution.py:517
  10.9 1.9 %own.3.refs_3_ = f32[256,256]{1,0:T(8,128)S(1)} custom-call(s32[24]{0:T(128)S(1)} %copy-done, bf16[24,256,256]{2,1,0:T(8,128)(2,1)S(1)} %get-tuple-element.22.left_ref.rows_ref.refs_1_, bf16[24,256,256]{2,1,0:T(8,128)(2,1)S(1)} %get-tuple-element.23.right_ref.refs_2_, bf16[256,256]{1,0:T(8,128)(2,1)} %bitcast.2.block_ref.refs_4_.refs_2_.refs_3_), custom_call_target="tpu_custom_call" | custom-call | flops 322122560 | bytes 262144 | tf_op jit(solution)/shard_map/own/pallas_call | solution.py:443
  13.3 1.7 %rest.3 = (bf16[256,256]{1,0:T(8,128)(2,1)S(1)}, f32[8,128]{1,0:T(8,128)S(1)}) custom-call(s32[24]{0:T(128)S(1)} %copy-done, bf16[24,256,256]{2,1,0:T(8,128)(2,1)S(1)} %get-tuple-element.22.left_ref.rows_ref.refs_1_, bf16[24,256,256]{2,1,0:T(8,128)(2,1)S(1)} %get-tuple-element.23.right_ref.refs_2_, f32[256,256]{1,0:T(8,128)S(1)} %own.3.refs_3_, ...), custom_call_target="tpu_custom_call" | custom-call | flops 644245120 | bytes 262144 | tf_op jit(solution)/shard_map/rest/pallas_call | solution.py:443
  15.0 2.0 %collective-permute-start.3 = (bf16[256,256]{1,0:T(8,128)(2,1)S(1)}, bf16[256,256]{1,0:T(8,128)(2,1)S(1)}, u32[]{:S(2)}, u32[]{:S(2)}) collective-permute-start(bf16[256,256]{1,0:T(8,128)(2,1)S(1)} %get-tuple-element.24.refs_0_), channel_id=1, source_target_pairs={{0,2},{2,0},{1,3},{3,1},{4,6},{6,4},{5,7},{7,5},{8,10},{10,8},{9,1... | collective-permute-start | bytes 393224 | tf_op jit(solution)/shard_map/ppermute | solution.py:524
  17.0 3.0 %collective-permute-done.3.refs_1_ = bf16[256,256]{1,0:T(8,128)(2,1)S(1)} collective-permute-done((bf16[256,256]{1,0:T(8,128)(2,1)S(1)}, bf16[256,256]{1,0:T(8,128)(2,1)S(1)}, u32[]{:S(2)}, u32[]{:S(2)}) %collective-permute-start.3) | collective-permute-done | bytes 131104 | tf_op jit(solution)/shard_map/ppermute | solution.py:524
  21.3 2.8 %collective-permute-start.4 = (bf16[160,256]{1,0:T(8,128)(2,1)S(1)}, bf16[160,256]{1,0:T(8,128)(2,1)S(1)}, u32[]{:S(2)}, u32[]{:S(2)}) collective-permute-start(bf16[160,256]{1,0:T(8,128)(2,1)S(1)} %get-tuple-element.27), channel_id=1, source_target_pairs={{9,0},{8,1},{13,4},{12,5},{1,8},{0,9},{5,12},{4,13},{11,2},{10,3},... | collective-permute-start | bytes 245768 | tf_op jit(solution)/shard_map/ppermute | solution.py:483
  24.8 1.5 %collective-permute-done.4.block_ref = bf16[160,256]{1,0:T(8,128)(2,1)S(1)} collective-permute-done((bf16[160,256]{1,0:T(8,128)(2,1)S(1)}, bf16[160,256]{1,0:T(8,128)(2,1)S(1)}, u32[]{:S(2)}, u32[]{:S(2)}) %collective-permute-start.4) | collective-permute-done | bytes 81952 | tf_op jit(solution)/shard_map/ppermute | solution.py:483
  26.3 2.2 %collective-permute-start.5 = (bf16[128,256]{1,0:T(8,128)(2,1)S(1)}, bf16[128,256]{1,0:T(8,128)(2,1)S(1)}, u32[]{:S(2)}, u32[]{:S(2)}) collective-permute-start(bf16[128,256]{1,0:T(8,128)(2,1)S(1)} %get-tuple-element.29.refs_5_), channel_id=1, source_target_pairs={{0,2},{2,0},{1,3},{3,1},{4,6},{6,4},{5,7},{7,5},{8,10},{10,8},{9,1... | collective-permute-start | bytes 196616 | tf_op jit(solution)/shard_map/ppermute | solution.py:517
  28.5 2.2 %collective-permute-start.7 = (f32[8,128]{1,0:T(8,128)S(1)}, f32[8,128]{1,0:T(8,128)S(1)}, u32[]{:S(2)}, u32[]{:S(2)}) collective-permute-start(f32[8,128]{1,0:T(8,128)S(1)} %get-tuple-element.30), channel_id=1, source_target_pairs={{0,1},{1,0},{4,5},{5,4},{8,9},{9,8},{12,13},{13,12},{2,3},{3,2},{6... | collective-permute-start | bytes 12296 | tf_op jit(solution)/shard_map/ppermute | solution.py:498
  30.7 1.5 %own.4.refs_3_ = f32[256,256]{1,0:T(8,128)S(1)} custom-call(s32[24]{0:T(128)S(1)} %copy-done, bf16[24,256,256]{2,1,0:T(8,128)(2,1)S(1)} %get-tuple-element.22.left_ref.rows_ref.refs_1_, bf16[24,256,256]{2,1,0:T(8,128)(2,1)S(1)} %get-tuple-element.23.right_ref.refs_2_, bf16[256,256]{1,0:T(8,128)(2,1)S(1)} %get-tuple-element.26.block_ref.refs_4_.refs_3_), custom_call_target="tpu_custom_call" | custom-call | flops 322122560 | bytes 262144 | tf_op jit(solution)/shard_map/own/pallas_call | solution.py:443
  34.2 3.8 %collective-permute-start.9 = (f32[8,128]{1,0:T(8,128)S(1)}, f32[8,128]{1,0:T(8,128)S(1)}, u32[]{:S(2)}, u32[]{:S(2)}) collective-permute-start(f32[8,128]{1,0:T(8,128)S(1)} %get-tuple-element.32), channel_id=1, source_target_pairs={{0,4},{1,5},{4,0},{5,1},{8,12},{9,13},{12,8},{13,9},{2,6},{3,7},{6... | collective-permute-start | bytes 12296 | tf_op jit(solution)/shard_map/ppermute | solution.py:498
  38.0 1.6 %collective-permute-done.9 = f32[8,128]{1,0:T(8,128)S(1)} collective-permute-done((f32[8,128]{1,0:T(8,128)S(1)}, f32[8,128]{1,0:T(8,128)S(1)}, u32[]{:S(2)}, u32[]{:S(2)}) %collective-permute-start.9) | collective-permute-done | bytes 4128 | tf_op jit(solution)/shard_map/ppermute | solution.py:498
  40.0 1.8 %sums.4 = (f32[256,256]{1,0:T(8,128)S(1)}, bf16[256,256]{1,0:T(8,128)(2,1)S(1)}, bf16[128,256]{1,0:T(8,128)(2,1)S(1)}, bf16[256,256]{1,0:T(8,128)(2,1)S(1)}, f32[8,128]{1,0:T(8,128)S(1)}) custom-call(bf16[256,256]{1,0:T(8,128)(2,1)S(1)} %get-tuple-element.31.refs_0_, bf16[256,256]{1,0:T(8,128)(2,1)S(1)} %collective-permute-done.8.refs_1_, ...), custom_call_target="tpu_custom_call" | custom-call | bytes 262144 | tf_op jit(solution)/shard_map/sums/pallas_call | solution.py:443
  42.5 3.9 %collective-permute-done.10.refs_4_ = bf16[128,256]{1,0:T(8,128)(2,1)S(1)} collective-permute-done((bf16[128,256]{1,0:T(8,128)(2,1)S(1)}, bf16[128,256]{1,0:T(8,128)(2,1)S(1)}, u32[]{:S(2)}, u32[]{:S(2)}) %collective-permute-start.10) | collective-permute-done | bytes 65568 | tf_op jit(solution)/shard_map/ppermute | solution.py:483
  46.4 1.4 %collective-permute-start.11 = (bf16[128,256]{1,0:T(8,128)(2,1)S(1)}, bf16[128,256]{1,0:T(8,128)(2,1)S(1)}, u32[]{:S(2)}, u32[]{:S(2)}) collective-permute-start(bf16[128,256]{1,0:T(8,128)(2,1)S(1)} %collective-permute-done.10.refs_4_), channel_id=1, source_target_pairs={{0,2},{2,0},{1,3},{3,1},{4,6},{6,4},{5,7},{7,5},{8,10},{10,8},{9,1... | collective-permute-start | bytes 196616 | tf_op jit(solution)/shard_map/ppermute | solution.py:517
  47.7 1.5 %own.5.refs_3_ = f32[256,256]{1,0:T(8,128)S(1)} custom-call(s32[24]{0:T(128)S(1)} %copy-done, bf16[24,256,256]{2,1,0:T(8,128)(2,1)S(1)} %get-tuple-element.22.left_ref.rows_ref.refs_1_, bf16[24,256,256]{2,1,0:T(8,128)(2,1)S(1)} %get-tuple-element.23.right_ref.refs_2_, bf16[256,256]{1,0:T(8,128)(2,1)S(1)} %get-tuple-element.34.block_ref), custom_call_target="tpu_custom_call" | custom-call | flops 322122560 | bytes 262144 | tf_op jit(solution)/shard_map/own/pallas_call | solution.py:443
  49.3 1.4 %collective-permute-done.11.refs_5_ = bf16[128,256]{1,0:T(8,128)(2,1)S(1)} collective-permute-done((bf16[128,256]{1,0:T(8,128)(2,1)S(1)}, bf16[128,256]{1,0:T(8,128)(2,1)S(1)}, u32[]{:S(2)}, u32[]{:S(2)}) %collective-permute-start.11) | collective-permute-done | bytes 65568 | tf_op jit(solution)/shard_map/ppermute | solution.py:517
  52.0 1.4 %collective-permute-start.13 = (bf16[256,256]{1,0:T(8,128)(2,1)S(1)}, bf16[256,256]{1,0:T(8,128)(2,1)S(1)}, u32[]{:S(2)}, u32[]{:S(2)}) collective-permute-start(bf16[256,256]{1,0:T(8,128)(2,1)S(1)} %rest.5.refs_0_), channel_id=1, source_target_pairs={{0,2},{2,0},{1,3},{3,1},{4,6},{6,4},{5,7},{7,5},{8,10},{10,8},{9,1... | collective-permute-start | bytes 393224 | tf_op jit(solution)/shard_map/ppermute | solution.py:524
  53.4 3.6 %collective-permute-done.13.refs_1_ = bf16[256,256]{1,0:T(8,128)(2,1)S(1)} collective-permute-done((bf16[256,256]{1,0:T(8,128)(2,1)S(1)}, bf16[256,256]{1,0:T(8,128)(2,1)S(1)}, u32[]{:S(2)}, u32[]{:S(2)}) %collective-permute-start.13) | collective-permute-done | bytes 131104 | tf_op jit(solution)/shard_map/ppermute | solution.py:524
  57.0 1.5 %sums.5 = (f32[256,256]{1,0:T(8,128)S(1)}, f32[256,256]{1,0:T(8,128)S(1)}, f32[8,128]{1,0:T(8,128)S(1)}) custom-call(bf16[256,256]{1,0:T(8,128)(2,1)S(1)} %rest.5.refs_0_, bf16[256,256]{1,0:T(8,128)(2,1)S(1)} %collective-permute-done.13.refs_1_, bf16[256,256]{1,0:T(8,128)(2,1)} %bitcast.2.block_ref.refs_4_.refs_2_.refs_3_, ...), custom_call_target="tpu_custom_call" | custom-call | bytes 262144 | tf_op jit(solution)/shard_map/sums/pallas_call | solution.py:443
  58.5 12.0 %all_to_all.11 = f32[8,1,128]{2,1,0:T(1,128)S(1)} all-to-all(f32[8,1,128]{2,1,0:T(1,128)S(1)} %bitcast.8), channel_id=1, replica_groups=mesh['groups'=2,'blk'=4,'mpo'=2,'rep'=2] {'blk','rep'}, dimensions={0} | all-to-all | bytes 8192 | tf_op jit(solution)/shard_map/all_to_all | solution.py:529
  70.5 1.4 %final.1 = (bf16[3,1,128,256]{3,2,1,0:T(8,128)(2,1)}, f32[2,3]{1,0:T(2,128)}) custom-call(f32[8,128]{1,0:T(8,128)S(1)} %bitcast.7, f32[256,256]{1,0:T(8,128)S(1)} %get-tuple-element.40.r_ref, f32[256,256]{1,0:T(8,128)S(1)} %get-tuple-element.41.z_ref, f32[256,256]{1,0:T(8,128)S(1)} %get-tuple-element.37.refs_5_.w_ref, ...), custom_call_target="tpu_custom_call" | custom-call | bytes 262144 | tf_op jit(solution)/shard_map/final/pallas_call | solution.py:443
  (23 shorter events, 8.4 us)
Async XLA Ops:
  1.5 7.4 %collective-permute-start = (bf16[128,256]{1,0:T(8,128)(2,1)S(1)}, bf16[128,256]{1,0:T(8,128)(2,1)S(1)}, u32[]{:S(2)}, u32[]{:S(2)}) collective-permute-start(bf16[128,256]{1,0:T(8,128)(2,1)S(1)} %take.1), channel_id=1, source_target_pairs={{9,0},{8,1},{13,4},{12,5},{1,8},{0,9},{5,12},{4,13},{11,2},{10,3},... | collective-permute-start | bytes 196616 | tf_op jit(solution)/shard_map/ppermute | solution.py:483
  5.0 7.8 %collective-permute-start.2 = (bf16[256,256]{1,0:T(8,128)(2,1)}, bf16[256,256]{1,0:T(8,128)(2,1)S(1)}, u32[]{:S(2)}, u32[]{:S(2)}) collective-permute-start(bf16[256,256]{1,0:T(8,128)(2,1)} %bitcast.2.block_ref.refs_4_.refs_2_.refs_3_), channel_id=1, source_target_pairs={{12,1},{9,4},{4,9},{1,12},{14,3},{11,6},{6,11},{3,14},{28,17},{25,... | collective-permute-start | bytes 393224 | tf_op jit(solution)/shard_map/ppermute | solution.py:483
  8.9 2.0 %copy-start = (s32[24]{0:T(128)S(1)}, s32[24]{0:T(128)}, u32[]{:S(2)}) copy-start(s32[24]{0:T(128)} %refs_0_.5) | copy-start | bytes 292
  8.9 4.3 %collective-permute-start.1 = (bf16[128,256]{1,0:T(8,128)(2,1)S(1)}, bf16[128,256]{1,0:T(8,128)(2,1)S(1)}, u32[]{:S(2)}, u32[]{:S(2)}) collective-permute-start(bf16[128,256]{1,0:T(8,128)(2,1)S(1)} %hold.1.refs_5_), channel_id=1, source_target_pairs={{0,2},{2,0},{1,3},{3,1},{4,6},{6,4},{5,7},{7,5},{8,10},{10,8},{9,1... | collective-permute-start | bytes 196616 | tf_op jit(solution)/shard_map/ppermute | solution.py:517
  15.0 5.0 %collective-permute-start.3 = (bf16[256,256]{1,0:T(8,128)(2,1)S(1)}, bf16[256,256]{1,0:T(8,128)(2,1)S(1)}, u32[]{:S(2)}, u32[]{:S(2)}) collective-permute-start(bf16[256,256]{1,0:T(8,128)(2,1)S(1)} %get-tuple-element.24.refs_0_), channel_id=1, source_target_pairs={{0,2},{2,0},{1,3},{3,1},{4,6},{6,4},{5,7},{7,5},{8,10},{10,8},{9,1... | collective-permute-start | bytes 393224 | tf_op jit(solution)/shard_map/ppermute | solution.py:524
  21.3 5.0 %collective-permute-start.4 = (bf16[160,256]{1,0:T(8,128)(2,1)S(1)}, bf16[160,256]{1,0:T(8,128)(2,1)S(1)}, u32[]{:S(2)}, u32[]{:S(2)}) collective-permute-start(bf16[160,256]{1,0:T(8,128)(2,1)S(1)} %get-tuple-element.27), channel_id=1, source_target_pairs={{9,0},{8,1},{13,4},{12,5},{1,8},{0,9},{5,12},{4,13},{11,2},{10,3},... | collective-permute-start | bytes 245768 | tf_op jit(solution)/shard_map/ppermute | solution.py:483
  24.1 8.1 %collective-permute-start.6 = (bf16[256,256]{1,0:T(8,128)(2,1)S(1)}, bf16[256,256]{1,0:T(8,128)(2,1)S(1)}, u32[]{:S(2)}, u32[]{:S(2)}) collective-permute-start(bf16[256,256]{1,0:T(8,128)(2,1)S(1)} %get-tuple-element.26.block_ref.refs_4_.refs_3_), channel_id=1, source_target_pairs={{12,1},{9,4},{4,9},{1,12},{14,3},{11,6},{6,11},{3,14},{28,17},{25,... | collective-permute-start | bytes 393224 | tf_op jit(solution)/shard_map/ppermute | solution.py:483
  26.3 5.9 %collective-permute-start.5 = (bf16[128,256]{1,0:T(8,128)(2,1)S(1)}, bf16[128,256]{1,0:T(8,128)(2,1)S(1)}, u32[]{:S(2)}, u32[]{:S(2)}) collective-permute-start(bf16[128,256]{1,0:T(8,128)(2,1)S(1)} %get-tuple-element.29.refs_5_), channel_id=1, source_target_pairs={{0,2},{2,0},{1,3},{3,1},{4,6},{6,4},{5,7},{7,5},{8,10},{10,8},{9,1... | collective-permute-start | bytes 196616 | tf_op jit(solution)/shard_map/ppermute | solution.py:517
  28.5 3.7 %collective-permute-start.7 = (f32[8,128]{1,0:T(8,128)S(1)}, f32[8,128]{1,0:T(8,128)S(1)}, u32[]{:S(2)}, u32[]{:S(2)}) collective-permute-start(f32[8,128]{1,0:T(8,128)S(1)} %get-tuple-element.30), channel_id=1, source_target_pairs={{0,1},{1,0},{4,5},{5,4},{8,9},{9,8},{12,13},{13,12},{2,3},{3,2},{6... | collective-permute-start | bytes 12296 | tf_op jit(solution)/shard_map/ppermute | solution.py:498
  33.6 6.4 %collective-permute-start.8 = (bf16[256,256]{1,0:T(8,128)(2,1)S(1)}, bf16[256,256]{1,0:T(8,128)(2,1)S(1)}, u32[]{:S(2)}, u32[]{:S(2)}) collective-permute-start(bf16[256,256]{1,0:T(8,128)(2,1)S(1)} %get-tuple-element.31.refs_0_), channel_id=1, source_target_pairs={{0,2},{2,0},{1,3},{3,1},{4,6},{6,4},{5,7},{7,5},{8,10},{10,8},{9,1... | collective-permute-start | bytes 393224 | tf_op jit(solution)/shard_map/ppermute | solution.py:524
  34.2 5.4 %collective-permute-start.9 = (f32[8,128]{1,0:T(8,128)S(1)}, f32[8,128]{1,0:T(8,128)S(1)}, u32[]{:S(2)}, u32[]{:S(2)}) collective-permute-start(f32[8,128]{1,0:T(8,128)S(1)} %get-tuple-element.32), channel_id=1, source_target_pairs={{0,4},{1,5},{4,0},{5,1},{8,12},{9,13},{12,8},{13,9},{2,6},{3,7},{6... | collective-permute-start | bytes 12296 | tf_op jit(solution)/shard_map/ppermute | solution.py:498
  41.7 4.7 %collective-permute-start.10 = (bf16[128,256]{1,0:T(8,128)(2,1)S(1)}, bf16[128,256]{1,0:T(8,128)(2,1)S(1)}, u32[]{:S(2)}, u32[]{:S(2)}) collective-permute-start(bf16[128,256]{1,0:T(8,128)(2,1)S(1)} %get-tuple-element.35), channel_id=1, source_target_pairs={{9,0},{8,1},{13,4},{12,5},{1,8},{0,9},{5,12},{4,13},{11,2},{10,3},... | collective-permute-start | bytes 196616 | tf_op jit(solution)/shard_map/ppermute | solution.py:483
  41.8 8.8 %collective-permute-start.12 = (bf16[256,256]{1,0:T(8,128)(2,1)S(1)}, bf16[256,256]{1,0:T(8,128)(2,1)S(1)}, u32[]{:S(2)}, u32[]{:S(2)}) collective-permute-start(bf16[256,256]{1,0:T(8,128)(2,1)S(1)} %get-tuple-element.34.block_ref), channel_id=1, source_target_pairs={{12,1},{9,4},{4,9},{1,12},{14,3},{11,6},{6,11},{3,14},{28,17},{25,... | collective-permute-start | bytes 393224 | tf_op jit(solution)/shard_map/ppermute | solution.py:483
  46.4 4.3 %collective-permute-start.11 = (bf16[128,256]{1,0:T(8,128)(2,1)S(1)}, bf16[128,256]{1,0:T(8,128)(2,1)S(1)}, u32[]{:S(2)}, u32[]{:S(2)}) collective-permute-start(bf16[128,256]{1,0:T(8,128)(2,1)S(1)} %collective-permute-done.10.refs_4_), channel_id=1, source_target_pairs={{0,2},{2,0},{1,3},{3,1},{4,6},{6,4},{5,7},{7,5},{8,10},{10,8},{9,1... | collective-permute-start | bytes 196616 | tf_op jit(solution)/shard_map/ppermute | solution.py:517
  52.0 5.0 %collective-permute-start.13 = (bf16[256,256]{1,0:T(8,128)(2,1)S(1)}, bf16[256,256]{1,0:T(8,128)(2,1)S(1)}, u32[]{:S(2)}, u32[]{:S(2)}) collective-permute-start(bf16[256,256]{1,0:T(8,128)(2,1)S(1)} %rest.5.refs_0_), channel_id=1, source_target_pairs={{0,2},{2,0},{1,3},{3,1},{4,6},{6,4},{5,7},{7,5},{8,10},{10,8},{9,1... | collective-permute-start | bytes 393224 | tf_op jit(solution)/shard_map/ppermute | solution.py:524

commit v12 on v11

--- a/solution.py
+++ b/solution.py
@@ -278,7 +278,8 @@
     sums_ref[...] = jnp.where(row == source, first_row(sums), rows_ref[...])
 
 
-def take_kernel(block_ref, share_ref):
+def take_kernel(block_ref, copy_ref, share_ref):
+    copy_ref[...] = block_ref[...]
     share_ref[...] = block_ref[my_rows(share_ref.shape[0]), :]
 
 
@@ -528,7 +529,8 @@
     def exchange(rows):
         return lax.all_to_all(rows, ring, 0, 0, tiled=True)
 
-    first, others, _ = spread(psi, call(take_kernel, "take", share_shape, (psi,)), after=left)
+    psi, share_0 = call(take_kernel, "take", (narrow, share_shape), (psi,))
+    first, others, _ = spread(psi, share_0, after=left)
     t, unit = rest(own(True, psi), first, others, psi)
     rows_in_share = width // parts + (2 * TILE if carried else 0)
     w_1, share_1, rows = call(

time: 73 us -> 70.3 us (0.963); the launches traced: 71.9 us -> 70.4 us
  Pallas kernels: 19.4 us -> 15 us
  waiting for transfers between devices: 15.9 us -> 19.3 us
  starting transfers between devices: 23.8 us -> 20.8 us
  blocking collectives: 12 us -> 13.6 us
  local copies, waits for them, and re-layouts: 0.01 us -> 0.9 us
    pallas_call x13, Pallas kernels: 16.1 us -> 11.8 us  [call(): pl.pallas_call(kernel, out_shape=outs, in_specs=[first] + [VMEM] * (len(a...]
    ppermute x3, waiting for transfers between devices: 7.08 us -> 9.73 us  [gather_parts(): return [t, lax.ppermute(t, 'mpo', [(0, 1), (1, 0)])]]
    ppermute x3, starting transfers between devices: 3.98 us -> 1.94 us  [gather_parts(): return [t, lax.ppermute(t, 'mpo', [(0, 1), (1, 0)])]]
    ppermute x3, waiting for transfers between devices: 1.84 us -> 3.56 us  [spread(): first = [piece, lax.ppermute(piece, 'mpo', [(0, 1), (1, 0)])]]
    all_to_all x1, blocking collectives: 12 us -> 13.6 us  [exchange(): return lax.all_to_all(rows, ring, 0, 0, tiled=True)]
    ppermute x3, starting transfers between devices: 5.53 us -> 4.11 us  [spread(): first = [piece, lax.ppermute(piece, 'mpo', [(0, 1), (1, 0)])]]
    ppermute x6, waiting for transfers between devices: 5.42 us -> 4.42 us  [shift(): return lax.ppermute(block, ring, pairs)]
    unnamed x2 -> x4, local copies, waits for them, and re-layouts: 0.01 us -> 0.9 us
where the time goes in v12:
time: 70.3 us; the launch traced here: 70.4 us
  starting transfers between devices  20.8 us (30%)
  waiting for transfers between devices  19.3 us (27%)
  Pallas kernels  15 us (21%)
  blocking collectives  13.6 us (19%)
  local copies, waits for them, and re-layouts  0.9 us (1%)
  between operations  0.83 us (1%)
    all_to_all x1, blocking collectives, exchange(): return lax.all_to_all(rows, ring, 0, 0, tiled=True)  13.6 us
    pallas_call x13, Pallas kernels, call(): pl.pallas_call(kernel, out_shape=outs, in_specs=[first] + [VMEM] * (len(a...  11.8 us
    ppermute x3, waiting for transfers between devices, gather_parts(): return [t, lax.ppermute(t, 'mpo', [(0, 1), (1, 0)])]  9.73 us
    ppermute x6, starting transfers between devices, shift(): return lax.ppermute(block, ring, pairs)  9.22 us
    ppermute x2, starting transfers between devices, add_round(): return rows + lax.ppermute(rows, axis, pairs)  5.49 us
    ppermute x6, waiting for transfers between devices, shift(): return lax.ppermute(block, ring, pairs)  4.42 us
    ppermute x3, starting transfers between devices, spread(): first = [piece, lax.ppermute(piece, 'mpo', [(0, 1), (1, 0)])]  4.11 us
    ppermute x3, waiting for transfers between devices, spread(): first = [piece, lax.ppermute(piece, 'mpo', [(0, 1), (1, 0)])]  3.56 us
  transfers between devices with their start and end apart: 14, of which 8 were waited for; matrix products, arithmetic and copies ran while one was open for 0% of the time, Pallas kernels for 11%

profile of v12, /device:TPU:0, one launch (start us, length us, event | category | flops | bytes accessed | tf_op | source)
XLA Modules:
  0.0 70.4 jit_solution(3409015014243953541)
XLA Ops:
  1.6 3.5 %collective-permute-start = (bf16[128,256]{1,0:T(8,128)(2,1)S(1)}, bf16[128,256]{1,0:T(8,128)(2,1)S(1)}, u32[]{:S(2)}, u32[]{:S(2)}) collective-permute-start(bf16[128,256]{1,0:T(8,128)(2,1)S(1)} %get-tuple-element.27), channel_id=1, source_target_pairs={{9,0},{8,1},{13,4},{12,5},{1,8},{0,9},{5,12},{4,13},{11,2},{10,3},... | collective-permute-start | bytes 196616 | tf_op jit(solution)/shard_map/ppermute | solution.py:484
  5.8 3.2 %load.1 = (bf16[24,256,256]{2,1,0:T(8,128)(2,1)S(1)}, bf16[24,256,256]{2,1,0:T(8,128)(2,1)S(1)}) custom-call(bf16[24,256,256]{2,1,0:T(8,128)(2,1)} %bitcast.10, bf16[24,256,256]{2,1,0:T(8,128)(2,1)} %bitcast.11), custom_call_target="tpu_custom_call" | custom-call | tf_op jit(solution)/shard_map/load/pallas_call | solution.py:423
  9.0 2.0 %collective-permute-start.1 = (bf16[128,256]{1,0:T(8,128)(2,1)S(1)}, bf16[128,256]{1,0:T(8,128)(2,1)S(1)}, u32[]{:S(2)}, u32[]{:S(2)}) collective-permute-start(bf16[128,256]{1,0:T(8,128)(2,1)S(1)} %hold.1.refs_5_), channel_id=1, source_target_pairs={{0,2},{2,0},{1,3},{3,1},{4,6},{6,4},{5,7},{7,5},{8,10},{10,8},{9,1... | collective-permute-start | bytes 196616 | tf_op jit(solution)/shard_map/ppermute | solution.py:518
  11.0 1.5 %own.3.refs_3_ = f32[256,256]{1,0:T(8,128)S(1)} custom-call(s32[24]{0:T(128)S(1)} %copy-done.1, bf16[24,256,256]{2,1,0:T(8,128)(2,1)S(1)} %get-tuple-element.24.left_ref.rows_ref.refs_1_, bf16[24,256,256]{2,1,0:T(8,128)(2,1)S(1)} %get-tuple-element.25.right_ref.refs_2_, bf16[256,256]{1,0:T(8,128)(2,1)S(1)} %get-tuple-element.26.block_ref.refs_4_.refs_2_.refs_3_), custom_call_target="tpu_custom_call" | custom-call | flops 322122560 | bytes 262144 | tf_op jit(solution)/shard_map/own/pallas_call | solution.py:444
  13.4 1.3 %rest.3 = (bf16[256,256]{1,0:T(8,128)(2,1)S(1)}, f32[8,128]{1,0:T(8,128)S(1)}) custom-call(s32[24]{0:T(128)S(1)} %copy-done.1, bf16[24,256,256]{2,1,0:T(8,128)(2,1)S(1)} %get-tuple-element.24.left_ref.rows_ref.refs_1_, bf16[24,256,256]{2,1,0:T(8,128)(2,1)S(1)} %get-tuple-element.25.right_ref.refs_2_, f32[256,256]{1,0:T(8,128)S(1)} %own.3.refs_3_, ...), custom_call_target="tpu_custom_call" | custom-call | flops 644245120 | bytes 262144 | tf_op jit(solution)/shard_map/rest/pallas_call | solution.py:444
  14.7 1.8 %collective-permute-start.3 = (bf16[256,256]{1,0:T(8,128)(2,1)S(1)}, bf16[256,256]{1,0:T(8,128)(2,1)S(1)}, u32[]{:S(2)}, u32[]{:S(2)}) collective-permute-start(bf16[256,256]{1,0:T(8,128)(2,1)S(1)} %get-tuple-element.28.refs_0_), channel_id=1, source_target_pairs={{0,2},{2,0},{1,3},{3,1},{4,6},{6,4},{5,7},{7,5},{8,10},{10,8},{9,1... | collective-permute-start | bytes 393224 | tf_op jit(solution)/shard_map/ppermute | solution.py:525
  16.5 3.5 %collective-permute-done.3.refs_1_ = bf16[256,256]{1,0:T(8,128)(2,1)S(1)} collective-permute-done((bf16[256,256]{1,0:T(8,128)(2,1)S(1)}, bf16[256,256]{1,0:T(8,128)(2,1)S(1)}, u32[]{:S(2)}, u32[]{:S(2)}) %collective-permute-start.3) | collective-permute-done | bytes 131104 | tf_op jit(solution)/shard_map/ppermute | solution.py:525
  20.4 2.6 %collective-permute-start.4 = (bf16[160,256]{1,0:T(8,128)(2,1)S(1)}, bf16[160,256]{1,0:T(8,128)(2,1)S(1)}, u32[]{:S(2)}, u32[]{:S(2)}) collective-permute-start(bf16[160,256]{1,0:T(8,128)(2,1)S(1)} %get-tuple-element.31), channel_id=1, source_target_pairs={{9,0},{8,1},{13,4},{12,5},{1,8},{0,9},{5,12},{4,13},{11,2},{10,3},... | collective-permute-start | bytes 245768 | tf_op jit(solution)/shard_map/ppermute | solution.py:484
  23.7 1.5 %collective-permute-done.4.block_ref = bf16[160,256]{1,0:T(8,128)(2,1)S(1)} collective-permute-done((bf16[160,256]{1,0:T(8,128)(2,1)S(1)}, bf16[160,256]{1,0:T(8,128)(2,1)S(1)}, u32[]{:S(2)}, u32[]{:S(2)}) %collective-permute-start.4) | collective-permute-done | bytes 81952 | tf_op jit(solution)/shard_map/ppermute | solution.py:484
  25.2 2.1 %collective-permute-start.5 = (bf16[128,256]{1,0:T(8,128)(2,1)S(1)}, bf16[128,256]{1,0:T(8,128)(2,1)S(1)}, u32[]{:S(2)}, u32[]{:S(2)}) collective-permute-start(bf16[128,256]{1,0:T(8,128)(2,1)S(1)} %get-tuple-element.33.refs_5_), channel_id=1, source_target_pairs={{0,2},{2,0},{1,3},{3,1},{4,6},{6,4},{5,7},{7,5},{8,10},{10,8},{9,1... | collective-permute-start | bytes 196616 | tf_op jit(solution)/shard_map/ppermute | solution.py:518
  27.3 2.6 %collective-permute-start.7 = (f32[8,128]{1,0:T(8,128)S(1)}, f32[8,128]{1,0:T(8,128)S(1)}, u32[]{:S(2)}, u32[]{:S(2)}) collective-permute-start(f32[8,128]{1,0:T(8,128)S(1)} %get-tuple-element.34), channel_id=1, source_target_pairs={{0,1},{1,0},{4,5},{5,4},{8,9},{9,8},{12,13},{13,12},{2,3},{3,2},{6... | collective-permute-start | bytes 12296 | tf_op jit(solution)/shard_map/ppermute | solution.py:499
  29.9 1.5 %own.4.refs_3_ = f32[256,256]{1,0:T(8,128)S(1)} custom-call(s32[24]{0:T(128)S(1)} %copy-done.1, bf16[24,256,256]{2,1,0:T(8,128)(2,1)S(1)} %get-tuple-element.24.left_ref.rows_ref.refs_1_, bf16[24,256,256]{2,1,0:T(8,128)(2,1)S(1)} %get-tuple-element.25.right_ref.refs_2_, bf16[256,256]{1,0:T(8,128)(2,1)S(1)} %get-tuple-element.30.block_ref.refs_4_.refs_3_), custom_call_target="tpu_custom_call" | custom-call | flops 322122560 | bytes 262144 | tf_op jit(solution)/shard_map/own/pallas_call | solution.py:444
  31.5 1.3 %rest.4 = (bf16[256,256]{1,0:T(8,128)(2,1)S(1)}, f32[8,128]{1,0:T(8,128)S(1)}, f32[8,128]{1,0:T(8,128)S(1)}) custom-call(s32[24]{0:T(128)S(1)} %copy-done.1, bf16[24,256,256]{2,1,0:T(8,128)(2,1)S(1)} %get-tuple-element.24.left_ref.rows_ref.refs_1_, bf16[24,256,256]{2,1,0:T(8,128)(2,1)S(1)} %get-tuple-element.25.right_ref.refs_2_, ...), custom_call_target="tpu_custom_call" | custom-call | flops 644245120 | bytes 262144 | tf_op jit(solution)/shard_map/rest/pallas_call | solution.py:444
  32.9 2.9 %collective-permute-start.9 = (f32[8,128]{1,0:T(8,128)S(1)}, f32[8,128]{1,0:T(8,128)S(1)}, u32[]{:S(2)}, u32[]{:S(2)}) collective-permute-start(f32[8,128]{1,0:T(8,128)S(1)} %get-tuple-element.36), channel_id=1, source_target_pairs={{0,4},{1,5},{4,0},{5,1},{8,12},{9,13},{12,8},{13,9},{2,6},{3,7},{6... | collective-permute-start | bytes 12296 | tf_op jit(solution)/shard_map/ppermute | solution.py:499
  35.8 1.6 %collective-permute-done.9 = f32[8,128]{1,0:T(8,128)S(1)} collective-permute-done((f32[8,128]{1,0:T(8,128)S(1)}, f32[8,128]{1,0:T(8,128)S(1)}, u32[]{:S(2)}, u32[]{:S(2)}) %collective-permute-start.9) | collective-permute-done | bytes 4128 | tf_op jit(solution)/shard_map/ppermute | solution.py:499
  37.4 1.3 %collective-permute-done.8.refs_1_ = bf16[256,256]{1,0:T(8,128)(2,1)S(1)} collective-permute-done((bf16[256,256]{1,0:T(8,128)(2,1)S(1)}, bf16[256,256]{1,0:T(8,128)(2,1)S(1)}, u32[]{:S(2)}, u32[]{:S(2)}) %collective-permute-start.8) | collective-permute-done | bytes 131104 | tf_op jit(solution)/shard_map/ppermute | solution.py:525
  39.5 1.1 %collective-permute-start.10 = (bf16[128,256]{1,0:T(8,128)(2,1)S(1)}, bf16[128,256]{1,0:T(8,128)(2,1)S(1)}, u32[]{:S(2)}, u32[]{:S(2)}) collective-permute-start(bf16[128,256]{1,0:T(8,128)(2,1)S(1)} %get-tuple-element.39), channel_id=1, source_target_pairs={{9,0},{8,1},{13,4},{12,5},{1,8},{0,9},{5,12},{4,13},{11,2},{10,3},... | collective-permute-start | bytes 196616 | tf_op jit(solution)/shard_map/ppermute | solution.py:484
  41.3 2.9 %collective-permute-done.10.refs_4_ = bf16[128,256]{1,0:T(8,128)(2,1)S(1)} collective-permute-done((bf16[128,256]{1,0:T(8,128)(2,1)S(1)}, bf16[128,256]{1,0:T(8,128)(2,1)S(1)}, u32[]{:S(2)}, u32[]{:S(2)}) %collective-permute-start.10) | collective-permute-done | bytes 65568 | tf_op jit(solution)/shard_map/ppermute | solution.py:484
  44.2 1.5 %own.5.refs_3_ = f32[256,256]{1,0:T(8,128)S(1)} custom-call(s32[24]{0:T(128)S(1)} %copy-done.1, bf16[24,256,256]{2,1,0:T(8,128)(2,1)S(1)} %get-tuple-element.24.left_ref.rows_ref.refs_1_, bf16[24,256,256]{2,1,0:T(8,128)(2,1)S(1)} %get-tuple-element.25.right_ref.refs_2_, bf16[256,256]{1,0:T(8,128)(2,1)S(1)} %get-tuple-element.38.block_ref), custom_call_target="tpu_custom_call" | custom-call | flops 322122560 | bytes 262144 | tf_op jit(solution)/shard_map/own/pallas_call | solution.py:444
  45.7 2.7 %collective-permute-done.11.refs_5_ = bf16[128,256]{1,0:T(8,128)(2,1)S(1)} collective-permute-done((bf16[128,256]{1,0:T(8,128)(2,1)S(1)}, bf16[128,256]{1,0:T(8,128)(2,1)S(1)}, u32[]{:S(2)}, u32[]{:S(2)}) %collective-permute-start.11) | collective-permute-done | bytes 65568 | tf_op jit(solution)/shard_map/ppermute | solution.py:518
  48.5 1.3 %rest.5.refs_0_ = bf16[256,256]{1,0:T(8,128)(2,1)S(1)} custom-call(s32[24]{0:T(128)S(1)} %copy-done.1, bf16[24,256,256]{2,1,0:T(8,128)(2,1)S(1)} %get-tuple-element.24.left_ref.rows_ref.refs_1_, bf16[24,256,256]{2,1,0:T(8,128)(2,1)S(1)} %get-tuple-element.25.right_ref.refs_2_, f32[256,256]{1,0:T(8,128)S(1)} %own.5.refs_3_, ...), custom_call_target="tpu_custom_call" | custom-call | flops 644245120 | bytes 262144 | tf_op jit(solution)/shard_map/rest/pallas_call | solution.py:444
  49.9 5.0 %collective-permute-done.13.refs_1_ = bf16[256,256]{1,0:T(8,128)(2,1)S(1)} collective-permute-done((bf16[256,256]{1,0:T(8,128)(2,1)S(1)}, bf16[256,256]{1,0:T(8,128)(2,1)S(1)}, u32[]{:S(2)}, u32[]{:S(2)}) %collective-permute-start.13) | collective-permute-done | bytes 131104 | tf_op jit(solution)/shard_map/ppermute | solution.py:525
  55.4 13.6 %all_to_all.11 = f32[8,1,128]{2,1,0:T(1,128)S(1)} all-to-all(f32[8,1,128]{2,1,0:T(1,128)S(1)} %bitcast.9), channel_id=1, replica_groups=mesh['groups'=2,'blk'=4,'mpo'=2,'rep'=2] {'blk','rep'}, dimensions={0} | all-to-all | bytes 8192 | tf_op jit(solution)/shard_map/all_to_all | solution.py:530
  69.0 1.4 %final.1 = (bf16[3,1,128,256]{3,2,1,0:T(8,128)(2,1)}, f32[2,3]{1,0:T(2,128)}) custom-call(f32[8,128]{1,0:T(8,128)S(1)} %bitcast.8, f32[256,256]{1,0:T(8,128)S(1)} %get-tuple-element.44.r_ref, f32[256,256]{1,0:T(8,128)S(1)} %get-tuple-element.45.z_ref, f32[256,256]{1,0:T(8,128)S(1)} %get-tuple-element.41.refs_5_.w_ref, ...), custom_call_target="tpu_custom_call" | custom-call | bytes 262144 | tf_op jit(solution)/shard_map/final/pallas_call | solution.py:444
  (25 shorter events, 5.7 us)
Async XLA Ops:
  0.6 0.9 %copy-start = (bf16[1,256,256]{2,1,0:T(8,128)(2,1)S(1)}, bf16[1,256,256]{2,1,0:T(8,128)(2,1)}, u32[]{:S(2)}) copy-start(bf16[1,256,256]{2,1,0:T(8,128)(2,1)} %param.4) | copy-start | bytes 393220
  1.6 7.4 %collective-permute-start = (bf16[128,256]{1,0:T(8,128)(2,1)S(1)}, bf16[128,256]{1,0:T(8,128)(2,1)S(1)}, u32[]{:S(2)}, u32[]{:S(2)}) collective-permute-start(bf16[128,256]{1,0:T(8,128)(2,1)S(1)} %get-tuple-element.27), channel_id=1, source_target_pairs={{9,0},{8,1},{13,4},{12,5},{1,8},{0,9},{5,12},{4,13},{11,2},{10,3},... | collective-permute-start | bytes 196616 | tf_op jit(solution)/shard_map/ppermute | solution.py:484
  5.1 7.4 %collective-permute-start.2 = (bf16[256,256]{1,0:T(8,128)(2,1)S(1)}, bf16[256,256]{1,0:T(8,128)(2,1)S(1)}, u32[]{:S(2)}, u32[]{:S(2)}) collective-permute-start(bf16[256,256]{1,0:T(8,128)(2,1)S(1)} %get-tuple-element.26.block_ref.refs_4_.refs_2_.refs_3_), channel_id=1, source_target_pairs={{12,1},{9,4},{4,9},{1,12},{14,3},{11,6},{6,11},{3,14},{28,17},{25,... | collective-permute-start | bytes 393224 | tf_op jit(solution)/shard_map/ppermute | solution.py:484
  9.0 2.0 %copy-start.1 = (s32[24]{0:T(128)S(1)}, s32[24]{0:T(128)}, u32[]{:S(2)}) copy-start(s32[24]{0:T(128)} %refs_0_.5) | copy-start | bytes 292
  9.0 4.3 %collective-permute-start.1 = (bf16[128,256]{1,0:T(8,128)(2,1)S(1)}, bf16[128,256]{1,0:T(8,128)(2,1)S(1)}, u32[]{:S(2)}, u32[]{:S(2)}) collective-permute-start(bf16[128,256]{1,0:T(8,128)(2,1)S(1)} %hold.1.refs_5_), channel_id=1, source_target_pairs={{0,2},{2,0},{1,3},{3,1},{4,6},{6,4},{5,7},{7,5},{8,10},{10,8},{9,1... | collective-permute-start | bytes 196616 | tf_op jit(solution)/shard_map/ppermute | solution.py:518
  14.7 5.3 %collective-permute-start.3 = (bf16[256,256]{1,0:T(8,128)(2,1)S(1)}, bf16[256,256]{1,0:T(8,128)(2,1)S(1)}, u32[]{:S(2)}, u32[]{:S(2)}) collective-permute-start(bf16[256,256]{1,0:T(8,128)(2,1)S(1)} %get-tuple-element.28.refs_0_), channel_id=1, source_target_pairs={{0,2},{2,0},{1,3},{3,1},{4,6},{6,4},{5,7},{7,5},{8,10},{10,8},{9,1... | collective-permute-start | bytes 393224 | tf_op jit(solution)/shard_map/ppermute | solution.py:525
  20.4 4.8 %collective-permute-start.4 = (bf16[160,256]{1,0:T(8,128)(2,1)S(1)}, bf16[160,256]{1,0:T(8,128)(2,1)S(1)}, u32[]{:S(2)}, u32[]{:S(2)}) collective-permute-start(bf16[160,256]{1,0:T(8,128)(2,1)S(1)} %get-tuple-element.31), channel_id=1, source_target_pairs={{9,0},{8,1},{13,4},{12,5},{1,8},{0,9},{5,12},{4,13},{11,2},{10,3},... | collective-permute-start | bytes 245768 | tf_op jit(solution)/shard_map/ppermute | solution.py:484
  23.0 8.5 %collective-permute-start.6 = (bf16[256,256]{1,0:T(8,128)(2,1)S(1)}, bf16[256,256]{1,0:T(8,128)(2,1)S(1)}, u32[]{:S(2)}, u32[]{:S(2)}) collective-permute-start(bf16[256,256]{1,0:T(8,128)(2,1)S(1)} %get-tuple-element.30.block_ref.refs_4_.refs_3_), channel_id=1, source_target_pairs={{12,1},{9,4},{4,9},{1,12},{14,3},{11,6},{6,11},{3,14},{28,17},{25,... | collective-permute-start | bytes 393224 | tf_op jit(solution)/shard_map/ppermute | solution.py:484
  25.2 6.3 %collective-permute-start.5 = (bf16[128,256]{1,0:T(8,128)(2,1)S(1)}, bf16[128,256]{1,0:T(8,128)(2,1)S(1)}, u32[]{:S(2)}, u32[]{:S(2)}) collective-permute-start(bf16[128,256]{1,0:T(8,128)(2,1)S(1)} %get-tuple-element.33.refs_5_), channel_id=1, source_target_pairs={{0,2},{2,0},{1,3},{3,1},{4,6},{6,4},{5,7},{7,5},{8,10},{10,8},{9,1... | collective-permute-start | bytes 196616 | tf_op jit(solution)/shard_map/ppermute | solution.py:518
  27.3 4.1 %collective-permute-start.7 = (f32[8,128]{1,0:T(8,128)S(1)}, f32[8,128]{1,0:T(8,128)S(1)}, u32[]{:S(2)}, u32[]{:S(2)}) collective-permute-start(f32[8,128]{1,0:T(8,128)S(1)} %get-tuple-element.34), channel_id=1, source_target_pairs={{0,1},{1,0},{4,5},{5,4},{8,9},{9,8},{12,13},{13,12},{2,3},{3,2},{6... | collective-permute-start | bytes 12296 | tf_op jit(solution)/shard_map/ppermute | solution.py:499
  32.8 5.8 %collective-permute-start.8 = (bf16[256,256]{1,0:T(8,128)(2,1)S(1)}, bf16[256,256]{1,0:T(8,128)(2,1)S(1)}, u32[]{:S(2)}, u32[]{:S(2)}) collective-permute-start(bf16[256,256]{1,0:T(8,128)(2,1)S(1)} %get-tuple-element.35.refs_0_), channel_id=1, source_target_pairs={{0,2},{2,0},{1,3},{3,1},{4,6},{6,4},{5,7},{7,5},{8,10},{10,8},{9,1... | collective-permute-start | bytes 393224 | tf_op jit(solution)/shard_map/ppermute | solution.py:525
  32.9 4.5 %collective-permute-start.9 = (f32[8,128]{1,0:T(8,128)S(1)}, f32[8,128]{1,0:T(8,128)S(1)}, u32[]{:S(2)}, u32[]{:S(2)}) collective-permute-start(f32[8,128]{1,0:T(8,128)S(1)} %get-tuple-element.36), channel_id=1, source_target_pairs={{0,4},{1,5},{4,0},{5,1},{8,12},{9,13},{12,8},{13,9},{2,6},{3,7},{6... | collective-permute-start | bytes 12296 | tf_op jit(solution)/shard_map/ppermute | solution.py:499
  39.5 4.7 %collective-permute-start.10 = (bf16[128,256]{1,0:T(8,128)(2,1)S(1)}, bf16[128,256]{1,0:T(8,128)(2,1)S(1)}, u32[]{:S(2)}, u32[]{:S(2)}) collective-permute-start(bf16[128,256]{1,0:T(8,128)(2,1)S(1)} %get-tuple-element.39), channel_id=1, source_target_pairs={{9,0},{8,1},{13,4},{12,5},{1,8},{0,9},{5,12},{4,13},{11,2},{10,3},... | collective-permute-start | bytes 196616 | tf_op jit(solution)/shard_map/ppermute | solution.py:484
  40.6 7.8 %collective-permute-start.12 = (bf16[256,256]{1,0:T(8,128)(2,1)S(1)}, bf16[256,256]{1,0:T(8,128)(2,1)S(1)}, u32[]{:S(2)}, u32[]{:S(2)}) collective-permute-start(bf16[256,256]{1,0:T(8,128)(2,1)S(1)} %get-tuple-element.38.block_ref), channel_id=1, source_target_pairs={{12,1},{9,4},{4,9},{1,12},{14,3},{11,6},{6,11},{3,14},{28,17},{25,... | collective-permute-start | bytes 393224 | tf_op jit(solution)/shard_map/ppermute | solution.py:484
  44.2 4.3 %collective-permute-start.11 = (bf16[128,256]{1,0:T(8,128)(2,1)S(1)}, bf16[128,256]{1,0:T(8,128)(2,1)S(1)}, u32[]{:S(2)}, u32[]{:S(2)}) collective-permute-start(bf16[128,256]{1,0:T(8,128)(2,1)S(1)} %collective-permute-done.10.refs_4_), channel_id=1, source_target_pairs={{0,2},{2,0},{1,3},{3,1},{4,6},{6,4},{5,7},{7,5},{8,10},{10,8},{9,1... | collective-permute-start | bytes 196616 | tf_op jit(solution)/shard_map/ppermute | solution.py:518
  49.8 5.0 %collective-permute-start.13 = (bf16[256,256]{1,0:T(8,128)(2,1)S(1)}, bf16[256,256]{1,0:T(8,128)(2,1)S(1)}, u32[]{:S(2)}, u32[]{:S(2)}) collective-permute-start(bf16[256,256]{1,0:T(8,128)(2,1)S(1)} %rest.5.refs_0_), channel_id=1, source_target_pairs={{0,2},{2,0},{1,3},{3,1},{4,6},{6,4},{5,7},{7,5},{8,10},{10,8},{9,1... | collective-permute-start | bytes 393224 | tf_op jit(solution)/shard_map/ppermute | solution.py:525

commit v13 on v12

--- a/solution.py
+++ b/solution.py
@@ -150,8 +150,11 @@
 
 def list_channels(which, places, kinds_ref, order, slot_of, idle):
     sector = here()
-    slots = [jnp.int32(-1 if which == "rest" else 0)]
-    slots += [look_up(places[c], sector, -1) if which != "own" else jnp.int32(-1) for c in range(1, 5)]
+    low, high = {"own": (0, 0), "rest": (1, idle), "first": (1, 1), "others": (2, idle)}[which]
+    slots = []
+    for place in places:
+        kept = {k: slot for k, slot in place.items() if low <= slot <= high}
+        slots.append(look_up(kept, sector, -1))
     count = jnp.int32(0)
     for b in range(kinds_ref.shape[0]):
         kind = kinds_ref[b]
@@ -211,12 +214,15 @@
         copy.wait()
 
 
-def own_kernel(scaled, places, kinds_ref, left_ref, right_ref, block_ref, acc, source, order, slot_of):
+def own_kernel(scaled, places, *refs):
+    kinds_ref, left_ref, right_ref, block_ref, acc = refs[:5]
+    source, order, slot_of = refs[-3:]
     count = list_channels("own", places, kinds_ref, order, slot_of, 1)
     if scaled:
         block = wide_float(block_ref)
-        inverse = 1.0 / jnp.maximum(peak(block), SMALLEST)
-        source[0] = (block * inverse).astype(jnp.bfloat16)
+        unit = jnp.maximum(peak(block), SMALLEST)
+        refs[5][...] = jnp.broadcast_to(unit, refs[5].shape)
+        source[0] = (block * (1.0 / unit)).astype(jnp.bfloat16)
     else:
         source[0] = block_ref[...]
     source[1] = jnp.zeros(source.shape[1:], jnp.bfloat16)
@@ -224,13 +230,14 @@
     multiply_listed(count, left_ref, right_ref, source, acc, order, slot_of)
 
 
-def rest_kernel(scaled, passes, shares, slots, places, *refs):
+def rest_kernel(which, scaled, passes, shares, slots, places, *refs):
     kinds_ref, left_ref, right_ref, own_ref = refs[:4]
     refs = refs[4:]
     if scaled:
-        block_ref, refs = refs[0], refs[1:]
+        met_ref, refs = refs[0], refs[1:]
     first, refs = refs[:shares], refs[shares:]
-    others, refs = refs[: slots - 2], refs[slots - 2 :]
+    count_others = 0 if which == "first" else slots - 2
+    others, refs = refs[:count_others], refs[count_others:]
     if passes:
         rows_ref, refs = refs[0], refs[1:]
     t_ref, refs = refs[0], refs[1:]
@@ -240,10 +247,10 @@
         refs[0][...] = rows_ref[...]
         refs = refs[1:]
     acc, source, order, slot_of = refs
-    count = list_channels("rest", places, kinds_ref, order, slot_of, slots)
+    count = list_channels(which, places, kinds_ref, order, slot_of, slots)
     if scaled:
-        mine = jnp.maximum(peak(wide_float(block_ref)), SMALLEST)
-        unit = mine
+        met = lane_of(first_row(met_ref), 0)
+        unit = met
         for block in (*first, *others):
             unit = jnp.maximum(unit, peak(wide_float(block)))
         unit_ref[...] = jnp.broadcast_to(unit, unit_ref.shape)
@@ -252,16 +259,16 @@
     def scale(block):
         return (wide_float(block) * inverse).astype(jnp.bfloat16) if scaled else block[...]
 
-    share = source.shape[1] // shares
     for step, block in enumerate(first):
+        share = source.shape[1] // shares
         at = 0 if shares == 1 else jnp.abs(step - lax.axis_index("mpo"))
         source[1, pl.ds(pl.multiple_of(at * share, share), share), :] = scale(block)
     for slot, block in enumerate(others, 2):
         source[slot] = scale(block)
     source[slots] = jnp.zeros(source.shape[1:], jnp.bfloat16)
-    acc[...] = own_ref[...] * (mine * inverse) if scaled else own_ref[...]
+    acc[...] = own_ref[...] * (met * inverse) if scaled else own_ref[...]
     multiply_listed(count, left_ref, right_ref, source, acc, order, slot_of)
-    t_ref[...] = acc[...].astype(jnp.bfloat16)
+    t_ref[...] = acc[...].astype(t_ref.dtype)
 
 
 def pass_kernel(block_ref, rows_ref, out_ref):
@@ -436,8 +443,8 @@
     share_shape = jax.ShapeDtypeStruct((width // parts, width), jnp.bfloat16)
     lists = [pltpu.SMEM((channels + WIDE,), jnp.int32)] * 2
 
-    def call(kernel, name, outs, args, scratch=(), share=0, limit=4):
-        flops = int(4 * channels * share * width**3)
+    def call(kernel, name, outs, args, scratch=(), share=0, limit=4, weight=0):
+        flops = int(4 * channels * max(share, weight) * width**3)
         cost = pl.CostEstimate(flops=flops, bytes_accessed=4 * width * width, transcendentals=0)
         listed = outs if isinstance(outs, tuple) else (outs,)
         first = SMEM if share else VMEM
@@ -459,24 +466,24 @@
         return call(
             functools.partial(own_kernel, scaled, places),
             "own",
-            wide,
+            (wide,) + (scalars,) * scaled,
             (channel_class, left, right, block),
             [sources(1)] + lists,
             0.2,
             16,
         )
 
-    def rest(mine, first, others, block=None, rows=None):
-        scaled, passes = block is not None, rows is not None
-        outs = (narrow,) + (scalars,) * scaled + (rows_shape,) * passes
-        args = [channel_class, left, right, mine] + [block] * scaled + first + others + [rows] * passes
+    def rest(which, summed, first, others, rows=None):
+        scaled, passes = len(summed) > 1, rows is not None
+        outs = (wide if which == "others" else narrow,) + (scalars,) * scaled + (rows_shape,) * passes
+        args = [channel_class, left, right, *summed] + first + others + [rows] * passes
         return call(
-            functools.partial(rest_kernel, scaled, passes, len(first), slots, places),
+            functools.partial(rest_kernel, which, scaled, passes, len(first), slots, places),
             "rest",
             outs,
             args,
             [pltpu.VMEM((width, width), jnp.float32), sources(slots)] + lists,
-            0.4,
+            0.4 if which == "rest" else 0.2,
             16,
         )
 
@@ -513,7 +520,7 @@
                 rows = add_round(rows, *step)
             piece = call(pass_kernel, "hold", share_shape, (piece, rows))
         elif after is not None:
-            piece = call(pass_kernel, "hold", share_shape, (piece, after))
+            piece = call(pass_kernel, "hold", share_shape, (piece, after), weight=0.5)
         if parts == 2:
             first = [piece, lax.ppermute(piece, "mpo", [(0, 1), (1, 0)])]
         else:
@@ -531,7 +538,8 @@
 
     psi, share_0 = call(take_kernel, "take", (narrow, share_shape), (psi,))
     first, others, _ = spread(psi, share_0, after=left)
-    t, unit = rest(own(True, psi), first, others, psi)
+    summed = rest("others", own(True, psi), [], others)
+    t, unit = rest("first", summed, first, [])
     rows_in_share = width // parts + (2 * TILE if carried else 0)
     w_1, share_1, rows = call(
         functools.partial(first_sums_kernel, width // parts),
@@ -540,7 +548,7 @@
         (*gather_parts(t), psi, unit),
     )
     first, others, rows = spread(w_1, share_1, rows)
-    t, unit, rows = rest(own(True, w_1), first, others, w_1, rows)
+    t, unit, rows = rest("rest", own(True, w_1), first, others, rows)
     rows = add_round(rows, *rounds[-1])
     w_wide, w_2, share_2, v_2, scal = call(
         functools.partial(second_sums_kernel, entries),
@@ -548,8 +556,9 @@
         (wide, narrow, share_shape, narrow, scalars),
         (*gather_parts(t), rows, psi, w_1, unit),
     )
-    first, others, _ = spread(w_2, share_2)
-    (t,) = rest(own(False, w_2), first, others)
+    first, others, _ = spread(w_2, share_2, after=w_2)
+    summed = rest("others", own(False, w_2), [], others)
+    (t,) = rest("first", summed, first, [])
     r, z, rows = call(
         third_sums_kernel,
         "sums",

time: 70.3 us -> 69.2 us (0.984)
  blocking collectives: 13.6 us -> 8.58 us
  waiting for transfers between devices: 19.3 us -> 21.5 us
  Pallas kernels: 15 us -> 16.2 us
    all_to_all x1, blocking collectives: 13.6 us -> 8.58 us  [exchange(): return lax.all_to_all(rows, ring, 0, 0, tiled=True)]
    ppermute x6, waiting for transfers between devices: 4.42 us -> 7.18 us  [shift(): return lax.ppermute(block, ring, pairs)]
    ppermute x3, starting transfers between devices: 1.94 us -> 3.21 us  [gather_parts(): return [t, lax.ppermute(t, 'mpo', [(0, 1), (1, 0)])]]
    pallas_call x13 -> x16, Pallas kernels: 11.8 us -> 13 us  [call(): pl.pallas_call(kernel, out_shape=outs, in_specs=[first] + [VMEM] * (len(a...]
    ppermute x6, starting transfers between devices: 9.22 us -> 8.36 us  [shift(): return lax.ppermute(block, ring, pairs)]
  transfers between devices with their start and end apart: 14 -> 14, of which waited for: 8 -> 8; matrix products, arithmetic and copies ran while one was open for 0% -> 0% of each run, Pallas kernels for 11% -> 12%
where the time goes in v13:
time: 69.2 us; the launch traced here: 69.1 us
  waiting for transfers between devices  21.5 us (31%)
  starting transfers between devices  21 us (30%)
  Pallas kernels  16.2 us (23%)
  blocking collectives  8.58 us (12%)
  local copies, waits for them, and re-layouts  0.9 us (1%)
  between operations  0.85 us (1%)
    pallas_call x16, Pallas kernels, call(): pl.pallas_call(kernel, out_shape=outs, in_specs=[first] + [VMEM] * (len(a...  13 us
    ppermute x3, waiting for transfers between devices, gather_parts(): return [t, lax.ppermute(t, 'mpo', [(0, 1), (1, 0)])]  9.84 us
    all_to_all x1, blocking collectives, exchange(): return lax.all_to_all(rows, ring, 0, 0, tiled=True)  8.58 us
    ppermute x6, starting transfers between devices, shift(): return lax.ppermute(block, ring, pairs)  8.36 us
    ppermute x6, waiting for transfers between devices, shift(): return lax.ppermute(block, ring, pairs)  7.18 us
    ppermute x2, starting transfers between devices, add_round(): return rows + lax.ppermute(rows, axis, pairs)  5.18 us
    ppermute x3, starting transfers between devices, spread(): first = [piece, lax.ppermute(piece, 'mpo', [(0, 1), (1, 0)])]  4.27 us
    pallas_call x1, Pallas kernels, shards(): pl.pallas_call(load_kernel, out_shape=(jax.ShapeDtypeStruct(left.shape, l...  3.22 us
  transfers between devices with their start and end apart: 14, of which 8 were waited for; matrix products, arithmetic and copies ran while one was open for 0% of the time, Pallas kernels for 12%

profile of v13, /device:TPU:0, one launch (start us, length us, event | category | flops | bytes accessed | tf_op | source)
XLA Modules:
  0.0 69.1 jit_solution(14789320530983181638)
XLA Ops:
  1.6 3.5 %collective-permute-start.1 = (bf16[128,256]{1,0:T(8,128)(2,1)S(1)}, bf16[128,256]{1,0:T(8,128)(2,1)S(1)}, u32[]{:S(2)}, u32[]{:S(2)}) collective-permute-start(bf16[128,256]{1,0:T(8,128)(2,1)S(1)} %get-tuple-element.37), channel_id=1, source_target_pairs={{9,0},{8,1},{13,4},{12,5},{1,8},{0,9},{5,12},{4,13},{11,2},{10,3},... | collective-permute-start | bytes 196616 | tf_op jit(solution)/shard_map/ppermute | solution.py:491
  5.8 3.2 %load.1 = (bf16[24,256,256]{2,1,0:T(8,128)(2,1)S(1)}, bf16[24,256,256]{2,1,0:T(8,128)(2,1)S(1)}) custom-call(bf16[24,256,256]{2,1,0:T(8,128)(2,1)} %bitcast.10, bf16[24,256,256]{2,1,0:T(8,128)(2,1)} %bitcast.11), custom_call_target="tpu_custom_call" | custom-call | tf_op jit(solution)/shard_map/load/pallas_call | solution.py:430
  9.0 2.0 %collective-permute-start.2 = (bf16[128,256]{1,0:T(8,128)(2,1)S(1)}, bf16[128,256]{1,0:T(8,128)(2,1)S(1)}, u32[]{:S(2)}, u32[]{:S(2)}) collective-permute-start(bf16[128,256]{1,0:T(8,128)(2,1)S(1)} %hold.2.refs_5_), channel_id=1, source_target_pairs={{0,2},{2,0},{1,3},{3,1},{4,6},{6,4},{5,7},{7,5},{8,10},{10,8},{9,1... | collective-permute-start | bytes 196616 | tf_op jit(solution)/shard_map/ppermute | solution.py:525
  11.0 1.1 %own.3 = (f32[256,256]{1,0:T(8,128)S(1)}, f32[8,128]{1,0:T(8,128)S(1)}) custom-call(s32[24]{0:T(128)S(1)} %copy-done.1, bf16[24,256,256]{2,1,0:T(8,128)(2,1)S(1)} %get-tuple-element.30.refs_1_.rows_ref, bf16[24,256,256]{2,1,0:T(8,128)(2,1)S(1)} %get-tuple-element.31.refs_2_, bf16[256,256]{1,0:T(8,128)(2,1)S(1)} %get-tuple-element.32.refs_3_.refs_2_), custom_call_target="tpu_custom_call" | custom-call | flops 322122560 | bytes 262144 | tf_op jit(solution)/shard_map/own/pallas_call | solution.py:451
  13.4 1.6 %rest.6 = (bf16[256,256]{1,0:T(8,128)(2,1)S(1)}, f32[8,128]{1,0:T(8,128)S(1)}) custom-call(s32[24]{0:T(128)S(1)} %copy-done.1, bf16[24,256,256]{2,1,0:T(8,128)(2,1)S(1)} %get-tuple-element.30.refs_1_.rows_ref, bf16[24,256,256]{2,1,0:T(8,128)(2,1)S(1)} %get-tuple-element.31.refs_2_, f32[256,256]{1,0:T(8,128)S(1)} %get-tuple-element.35.refs_3_, ...), custom_call_target="tpu_custom_call" | custom-call | flops 322122560 | bytes 262144 | tf_op jit(solution)/shard_map/rest/pallas_call | solution.py:451
  15.0 2.0 %collective-permute-start.3 = (bf16[256,256]{1,0:T(8,128)(2,1)S(1)}, bf16[256,256]{1,0:T(8,128)(2,1)S(1)}, u32[]{:S(2)}, u32[]{:S(2)}) collective-permute-start(bf16[256,256]{1,0:T(8,128)(2,1)S(1)} %get-tuple-element.38.refs_0_), channel_id=1, source_target_pairs={{0,2},{2,0},{1,3},{3,1},{4,6},{6,4},{5,7},{7,5},{8,10},{10,8},{9,1... | collective-permute-start | bytes 393224 | tf_op jit(solution)/shard_map/ppermute | solution.py:532
  17.0 3.1 %collective-permute-done.3.refs_1_ = bf16[256,256]{1,0:T(8,128)(2,1)S(1)} collective-permute-done((bf16[256,256]{1,0:T(8,128)(2,1)S(1)}, bf16[256,256]{1,0:T(8,128)(2,1)S(1)}, u32[]{:S(2)}, u32[]{:S(2)}) %collective-permute-start.3) | collective-permute-done | bytes 131104 | tf_op jit(solution)/shard_map/ppermute | solution.py:532
  20.4 2.8 %collective-permute-start.4 = (bf16[160,256]{1,0:T(8,128)(2,1)S(1)}, bf16[160,256]{1,0:T(8,128)(2,1)S(1)}, u32[]{:S(2)}, u32[]{:S(2)}) collective-permute-start(bf16[160,256]{1,0:T(8,128)(2,1)S(1)} %get-tuple-element.43), channel_id=1, source_target_pairs={{9,0},{8,1},{13,4},{12,5},{1,8},{0,9},{5,12},{4,13},{11,2},{10,3},... | collective-permute-start | bytes 245768 | tf_op jit(solution)/shard_map/ppermute | solution.py:491
  23.8 1.5 %collective-permute-done.4.block_ref = bf16[160,256]{1,0:T(8,128)(2,1)S(1)} collective-permute-done((bf16[160,256]{1,0:T(8,128)(2,1)S(1)}, bf16[160,256]{1,0:T(8,128)(2,1)S(1)}, u32[]{:S(2)}, u32[]{:S(2)}) %collective-permute-start.4) | collective-permute-done | bytes 81952 | tf_op jit(solution)/shard_map/ppermute | solution.py:491
  25.3 2.3 %collective-permute-start.5 = (bf16[128,256]{1,0:T(8,128)(2,1)S(1)}, bf16[128,256]{1,0:T(8,128)(2,1)S(1)}, u32[]{:S(2)}, u32[]{:S(2)}) collective-permute-start(bf16[128,256]{1,0:T(8,128)(2,1)S(1)} %get-tuple-element.45.refs_5_), channel_id=1, source_target_pairs={{0,2},{2,0},{1,3},{3,1},{4,6},{6,4},{5,7},{7,5},{8,10},{10,8},{9,1... | collective-permute-start | bytes 196616 | tf_op jit(solution)/shard_map/ppermute | solution.py:525
  27.6 2.6 %collective-permute-start.7 = (f32[8,128]{1,0:T(8,128)S(1)}, f32[8,128]{1,0:T(8,128)S(1)}, u32[]{:S(2)}, u32[]{:S(2)}) collective-permute-start(f32[8,128]{1,0:T(8,128)S(1)} %get-tuple-element.46), channel_id=1, source_target_pairs={{0,1},{1,0},{4,5},{5,4},{8,9},{9,8},{12,13},{13,12},{2,3},{3,2},{6... | collective-permute-start | bytes 12296 | tf_op jit(solution)/shard_map/ppermute | solution.py:506
  30.2 1.1 %own.4 = (f32[256,256]{1,0:T(8,128)S(1)}, f32[8,128]{1,0:T(8,128)S(1)}) custom-call(s32[24]{0:T(128)S(1)} %copy-done.1, bf16[24,256,256]{2,1,0:T(8,128)(2,1)S(1)} %get-tuple-element.30.refs_1_.rows_ref, bf16[24,256,256]{2,1,0:T(8,128)(2,1)S(1)} %get-tuple-element.31.refs_2_, bf16[256,256]{1,0:T(8,128)(2,1)S(1)} %get-tuple-element.40.refs_3_.refs_4_), custom_call_target="tpu_custom_call" | custom-call | flops 322122560 | bytes 262144 | tf_op jit(solution)/shard_map/own/pallas_call | solution.py:451
  31.3 1.7 %rest.7 = (bf16[256,256]{1,0:T(8,128)(2,1)S(1)}, f32[8,128]{1,0:T(8,128)S(1)}, f32[8,128]{1,0:T(8,128)S(1)}) custom-call(s32[24]{0:T(128)S(1)} %copy-done.1, bf16[24,256,256]{2,1,0:T(8,128)(2,1)S(1)} %get-tuple-element.30.refs_1_.rows_ref, bf16[24,256,256]{2,1,0:T(8,128)(2,1)S(1)} %get-tuple-element.31.refs_2_, f32[256,256]{1,0:T(8,128)S(1)} %get-tuple-element.41.refs_3_, ...), custom_call_target="tpu_custom_call" | custom-call | flops 644245120 | bytes 262144 | tf_op jit(solution)/shard_map/rest/pallas_call | solution.py:451
  33.9 2.6 %collective-permute-start.9 = (f32[8,128]{1,0:T(8,128)S(1)}, f32[8,128]{1,0:T(8,128)S(1)}, u32[]{:S(2)}, u32[]{:S(2)}) collective-permute-start(f32[8,128]{1,0:T(8,128)S(1)} %get-tuple-element.48), channel_id=1, source_target_pairs={{0,4},{1,5},{4,0},{5,1},{8,12},{9,13},{12,8},{13,9},{2,6},{3,7},{6... | collective-permute-start | bytes 12296 | tf_op jit(solution)/shard_map/ppermute | solution.py:506
  36.5 1.6 %collective-permute-done.9 = f32[8,128]{1,0:T(8,128)S(1)} collective-permute-done((f32[8,128]{1,0:T(8,128)S(1)}, f32[8,128]{1,0:T(8,128)S(1)}, u32[]{:S(2)}, u32[]{:S(2)}) %collective-permute-start.9) | collective-permute-done | bytes 4128 | tf_op jit(solution)/shard_map/ppermute | solution.py:506
  38.1 1.2 %collective-permute-done.8.refs_1_ = bf16[256,256]{1,0:T(8,128)(2,1)S(1)} collective-permute-done((bf16[256,256]{1,0:T(8,128)(2,1)S(1)}, bf16[256,256]{1,0:T(8,128)(2,1)S(1)}, u32[]{:S(2)}, u32[]{:S(2)}) %collective-permute-start.8) | collective-permute-done | bytes 131104 | tf_op jit(solution)/shard_map/ppermute | solution.py:532
  40.9 5.7 %collective-permute-done.11.block_ref = bf16[128,256]{1,0:T(8,128)(2,1)S(1)} collective-permute-done((bf16[128,256]{1,0:T(8,128)(2,1)S(1)}, bf16[128,256]{1,0:T(8,128)(2,1)S(1)}, u32[]{:S(2)}, u32[]{:S(2)}) %collective-permute-start.11) | collective-permute-done | bytes 65568 | tf_op jit(solution)/shard_map/ppermute | solution.py:491
  46.6 1.1 %own.5.refs_3_ = f32[256,256]{1,0:T(8,128)S(1)} custom-call(s32[24]{0:T(128)S(1)} %copy-done.1, bf16[24,256,256]{2,1,0:T(8,128)(2,1)S(1)} %get-tuple-element.30.refs_1_.rows_ref, bf16[24,256,256]{2,1,0:T(8,128)(2,1)S(1)} %get-tuple-element.31.refs_2_, bf16[256,256]{1,0:T(8,128)(2,1)S(1)} %get-tuple-element.50.refs_3_.rows_ref), custom_call_target="tpu_custom_call" | custom-call | flops 322122560 | bytes 262144 | tf_op jit(solution)/shard_map/own/pallas_call | solution.py:451
  47.7 0.9 %rest.8.refs_3_ = f32[256,256]{1,0:T(8,128)S(1)} custom-call(s32[24]{0:T(128)S(1)} %copy-done.1, bf16[24,256,256]{2,1,0:T(8,128)(2,1)S(1)} %get-tuple-element.30.refs_1_.rows_ref, bf16[24,256,256]{2,1,0:T(8,128)(2,1)S(1)} %get-tuple-element.31.refs_2_, f32[256,256]{1,0:T(8,128)S(1)} %own.5.refs_3_, bf16[256,256]{1,0:T(8,128)(2,1)S(1)} %collective-permute-done.10.refs_4_), custom_call_target="tpu_custom_call" | custom-call | flops 322122560 | bytes 262144 | tf_op jit(solution)/shard_map/rest/pallas_call | solution.py:451
  48.6 2.4 %collective-permute-done.12.refs_5_ = bf16[128,256]{1,0:T(8,128)(2,1)S(1)} collective-permute-done((bf16[128,256]{1,0:T(8,128)(2,1)S(1)}, bf16[128,256]{1,0:T(8,128)(2,1)S(1)}, u32[]{:S(2)}, u32[]{:S(2)}) %collective-permute-start.12) | collective-permute-done | bytes 65568 | tf_op jit(solution)/shard_map/ppermute | solution.py:525
  51.0 1.6 %rest.9.refs_0_ = bf16[256,256]{1,0:T(8,128)(2,1)S(1)} custom-call(s32[24]{0:T(128)S(1)} %copy-done.1, bf16[24,256,256]{2,1,0:T(8,128)(2,1)S(1)} %get-tuple-element.30.refs_1_.rows_ref, bf16[24,256,256]{2,1,0:T(8,128)(2,1)S(1)} %get-tuple-element.31.refs_2_, f32[256,256]{1,0:T(8,128)S(1)} %rest.8.refs_3_, bf16[128,256]{1,0:T(8,128)(2,1)S(1)} %hold.3.refs_4_, ...), custom_call_target="tpu_custom_call" | custom-call | flops 322122560 | bytes 262144 | tf_op jit(solution)/shard_map/rest/pallas_call | solution.py:451
  52.9 5.6 %collective-permute-done.13.refs_1_ = bf16[256,256]{1,0:T(8,128)(2,1)S(1)} collective-permute-done((bf16[256,256]{1,0:T(8,128)(2,1)S(1)}, bf16[256,256]{1,0:T(8,128)(2,1)S(1)}, u32[]{:S(2)}, u32[]{:S(2)}) %collective-permute-start.13) | collective-permute-done | bytes 131104 | tf_op jit(solution)/shard_map/ppermute | solution.py:532
  59.1 8.6 %all_to_all.11 = f32[8,1,128]{2,1,0:T(1,128)S(1)} all-to-all(f32[8,1,128]{2,1,0:T(1,128)S(1)} %bitcast.9), channel_id=1, replica_groups=mesh['groups'=2,'blk'=4,'mpo'=2,'rep'=2] {'blk','rep'}, dimensions={0} | all-to-all | bytes 8192 | tf_op jit(solution)/shard_map/all_to_all | solution.py:537
  67.7 1.4 %final.1 = (bf16[3,1,128,256]{3,2,1,0:T(8,128)(2,1)}, f32[2,3]{1,0:T(2,128)}) custom-call(f32[8,128]{1,0:T(8,128)S(1)} %bitcast.8, f32[256,256]{1,0:T(8,128)S(1)} %get-tuple-element.56.r_ref, f32[256,256]{1,0:T(8,128)S(1)} %get-tuple-element.57.z_ref, f32[256,256]{1,0:T(8,128)S(1)} %get-tuple-element.53.refs_5_.w_ref, ...), custom_call_target="tpu_custom_call" | custom-call | bytes 262144 | tf_op jit(solution)/shard_map/final/pallas_call | solution.py:451
  (28 shorter events, 7.3 us)
Async XLA Ops:
  0.6 0.9 %copy-start = (bf16[1,256,256]{2,1,0:T(8,128)(2,1)S(1)}, bf16[1,256,256]{2,1,0:T(8,128)(2,1)}, u32[]{:S(2)}) copy-start(bf16[1,256,256]{2,1,0:T(8,128)(2,1)} %param.4) | copy-start | bytes 393220
  1.6 7.4 %collective-permute-start.1 = (bf16[128,256]{1,0:T(8,128)(2,1)S(1)}, bf16[128,256]{1,0:T(8,128)(2,1)S(1)}, u32[]{:S(2)}, u32[]{:S(2)}) collective-permute-start(bf16[128,256]{1,0:T(8,128)(2,1)S(1)} %get-tuple-element.37), channel_id=1, source_target_pairs={{9,0},{8,1},{13,4},{12,5},{1,8},{0,9},{5,12},{4,13},{11,2},{10,3},... | collective-permute-start | bytes 196616 | tf_op jit(solution)/shard_map/ppermute | solution.py:491
  5.1 7.0 %collective-permute-start = (bf16[256,256]{1,0:T(8,128)(2,1)S(1)}, bf16[256,256]{1,0:T(8,128)(2,1)S(1)}, u32[]{:S(2)}, u32[]{:S(2)}) collective-permute-start(bf16[256,256]{1,0:T(8,128)(2,1)S(1)} %get-tuple-element.32.refs_3_.refs_2_), channel_id=1, source_target_pairs={{12,1},{9,4},{4,9},{1,12},{14,3},{11,6},{6,11},{3,14},{28,17},{25,... | collective-permute-start | bytes 393224 | tf_op jit(solution)/shard_map/ppermute | solution.py:491
  9.0 2.0 %copy-start.1 = (s32[24]{0:T(128)S(1)}, s32[24]{0:T(128)}, u32[]{:S(2)}) copy-start(s32[24]{0:T(128)} %refs_0_.15) | copy-start | bytes 292
  9.0 4.3 %collective-permute-start.2 = (bf16[128,256]{1,0:T(8,128)(2,1)S(1)}, bf16[128,256]{1,0:T(8,128)(2,1)S(1)}, u32[]{:S(2)}, u32[]{:S(2)}) collective-permute-start(bf16[128,256]{1,0:T(8,128)(2,1)S(1)} %hold.2.refs_5_), channel_id=1, source_target_pairs={{0,2},{2,0},{1,3},{3,1},{4,6},{6,4},{5,7},{7,5},{8,10},{10,8},{9,1... | collective-permute-start | bytes 196616 | tf_op jit(solution)/shard_map/ppermute | solution.py:525
  15.0 5.1 %collective-permute-start.3 = (bf16[256,256]{1,0:T(8,128)(2,1)S(1)}, bf16[256,256]{1,0:T(8,128)(2,1)S(1)}, u32[]{:S(2)}, u32[]{:S(2)}) collective-permute-start(bf16[256,256]{1,0:T(8,128)(2,1)S(1)} %get-tuple-element.38.refs_0_), channel_id=1, source_target_pairs={{0,2},{2,0},{1,3},{3,1},{4,6},{6,4},{5,7},{7,5},{8,10},{10,8},{9,1... | collective-permute-start | bytes 393224 | tf_op jit(solution)/shard_map/ppermute | solution.py:532
  20.4 4.9 %collective-permute-start.4 = (bf16[160,256]{1,0:T(8,128)(2,1)S(1)}, bf16[160,256]{1,0:T(8,128)(2,1)S(1)}, u32[]{:S(2)}, u32[]{:S(2)}) collective-permute-start(bf16[160,256]{1,0:T(8,128)(2,1)S(1)} %get-tuple-element.43), channel_id=1, source_target_pairs={{9,0},{8,1},{13,4},{12,5},{1,8},{0,9},{5,12},{4,13},{11,2},{10,3},... | collective-permute-start | bytes 245768 | tf_op jit(solution)/shard_map/ppermute | solution.py:491
  23.2 8.1 %collective-permute-start.6 = (bf16[256,256]{1,0:T(8,128)(2,1)S(1)}, bf16[256,256]{1,0:T(8,128)(2,1)S(1)}, u32[]{:S(2)}, u32[]{:S(2)}) collective-permute-start(bf16[256,256]{1,0:T(8,128)(2,1)S(1)} %get-tuple-element.40.refs_3_.refs_4_), channel_id=1, source_target_pairs={{12,1},{9,4},{4,9},{1,12},{14,3},{11,6},{6,11},{3,14},{28,17},{25,... | collective-permute-start | bytes 393224 | tf_op jit(solution)/shard_map/ppermute | solution.py:491
  25.3 5.9 %collective-permute-start.5 = (bf16[128,256]{1,0:T(8,128)(2,1)S(1)}, bf16[128,256]{1,0:T(8,128)(2,1)S(1)}, u32[]{:S(2)}, u32[]{:S(2)}) collective-permute-start(bf16[128,256]{1,0:T(8,128)(2,1)S(1)} %get-tuple-element.45.refs_5_), channel_id=1, source_target_pairs={{0,2},{2,0},{1,3},{3,1},{4,6},{6,4},{5,7},{7,5},{8,10},{10,8},{9,1... | collective-permute-start | bytes 196616 | tf_op jit(solution)/shard_map/ppermute | solution.py:525
  27.6 3.6 %collective-permute-start.7 = (f32[8,128]{1,0:T(8,128)S(1)}, f32[8,128]{1,0:T(8,128)S(1)}, u32[]{:S(2)}, u32[]{:S(2)}) collective-permute-start(f32[8,128]{1,0:T(8,128)S(1)} %get-tuple-element.46), channel_id=1, source_target_pairs={{0,1},{1,0},{4,5},{5,4},{8,9},{9,8},{12,13},{13,12},{2,3},{3,2},{6... | collective-permute-start | bytes 12296 | tf_op jit(solution)/shard_map/ppermute | solution.py:506
  33.0 6.3 %collective-permute-start.8 = (bf16[256,256]{1,0:T(8,128)(2,1)S(1)}, bf16[256,256]{1,0:T(8,128)(2,1)S(1)}, u32[]{:S(2)}, u32[]{:S(2)}) collective-permute-start(bf16[256,256]{1,0:T(8,128)(2,1)S(1)} %get-tuple-element.47.refs_0_), channel_id=1, source_target_pairs={{0,2},{2,0},{1,3},{3,1},{4,6},{6,4},{5,7},{7,5},{8,10},{10,8},{9,1... | collective-permute-start | bytes 393224 | tf_op jit(solution)/shard_map/ppermute | solution.py:532
  33.9 4.2 %collective-permute-start.9 = (f32[8,128]{1,0:T(8,128)S(1)}, f32[8,128]{1,0:T(8,128)S(1)}, u32[]{:S(2)}, u32[]{:S(2)}) collective-permute-start(f32[8,128]{1,0:T(8,128)S(1)} %get-tuple-element.48), channel_id=1, source_target_pairs={{0,4},{1,5},{4,0},{5,1},{8,12},{9,13},{12,8},{13,9},{2,6},{3,7},{6... | collective-permute-start | bytes 12296 | tf_op jit(solution)/shard_map/ppermute | solution.py:506
  40.1 6.5 %collective-permute-start.11 = (bf16[128,256]{1,0:T(8,128)(2,1)S(1)}, bf16[128,256]{1,0:T(8,128)(2,1)S(1)}, u32[]{:S(2)}, u32[]{:S(2)}) collective-permute-start(bf16[128,256]{1,0:T(8,128)(2,1)S(1)} %get-tuple-element.51), channel_id=1, source_target_pairs={{9,0},{8,1},{13,4},{12,5},{1,8},{0,9},{5,12},{4,13},{11,2},{10,3},... | collective-permute-start | bytes 196616 | tf_op jit(solution)/shard_map/ppermute | solution.py:491
  40.2 7.5 %collective-permute-start.10 = (bf16[256,256]{1,0:T(8,128)(2,1)S(1)}, bf16[256,256]{1,0:T(8,128)(2,1)S(1)}, u32[]{:S(2)}, u32[]{:S(2)}) collective-permute-start(bf16[256,256]{1,0:T(8,128)(2,1)S(1)} %get-tuple-element.50.refs_3_.rows_ref), channel_id=1, source_target_pairs={{12,1},{9,4},{4,9},{1,12},{14,3},{11,6},{6,11},{3,14},{28,17},{25,... | collective-permute-start | bytes 393224 | tf_op jit(solution)/shard_map/ppermute | solution.py:491
  46.6 4.4 %collective-permute-start.12 = (bf16[128,256]{1,0:T(8,128)(2,1)S(1)}, bf16[128,256]{1,0:T(8,128)(2,1)S(1)}, u32[]{:S(2)}, u32[]{:S(2)}) collective-permute-start(bf16[128,256]{1,0:T(8,128)(2,1)S(1)} %hold.3.refs_4_), channel_id=1, source_target_pairs={{0,2},{2,0},{1,3},{3,1},{4,6},{6,4},{5,7},{7,5},{8,10},{10,8},{9,1... | collective-permute-start | bytes 196616 | tf_op jit(solution)/shard_map/ppermute | solution.py:525
  52.6 5.9 %collective-permute-start.13 = (bf16[256,256]{1,0:T(8,128)(2,1)S(1)}, bf16[256,256]{1,0:T(8,128)(2,1)S(1)}, u32[]{:S(2)}, u32[]{:S(2)}) collective-permute-start(bf16[256,256]{1,0:T(8,128)(2,1)S(1)} %rest.9.refs_0_), channel_id=1, source_target_pairs={{0,2},{2,0},{1,3},{3,1},{4,6},{6,4},{5,7},{7,5},{8,10},{10,8},{9,1... | collective-permute-start | bytes 393224 | tf_op jit(solution)/shard_map/ppermute | solution.py:532

commit v14 on v13

--- a/solution.py
+++ b/solution.py
@@ -14,7 +14,6 @@
 WIDE = 8
 SMALLEST = 1e-30
 TILE = 16
-LOADS = 4
 MIB = 1024 * 1024
 VMEM = pl.BlockSpec(memory_space=pltpu.VMEM)
 SMEM = pl.BlockSpec(memory_space=pltpu.SMEM)
@@ -200,18 +199,24 @@
             multiply(groups * WIDE, wide)
 
 
-def load_kernel(left_hbm, right_hbm, left_ref, right_ref, sems):
-    channels = left_ref.shape[0]
-    step = max(1, channels // LOADS)
-    copies = []
-    for side, (source, target) in enumerate(((left_hbm, left_ref), (right_hbm, right_ref))):
-        for at, low in enumerate(range(0, channels, step)):
-            part = pl.ds(low, min(step, channels - low))
-            copies.append(pltpu.make_async_copy(source.at[part], target.at[part], sems.at[side, at]))
-    for copy in copies:
-        copy.start()
-    for copy in copies:
-        copy.wait()
+def load_kernel(places, kinds_ref, left_hbm, right_hbm, left_ref, right_ref, sems):
+    sector = here()
+    slots = [look_up(place, sector, -1) for place in places]
+
+    def each(act):
+        for b in range(left_ref.shape[0]):
+            kind = kinds_ref[b]
+            slot = slots[0]
+            for c in range(1, 5):
+                slot = jnp.where(kind == c, slots[c], slot)
+
+            @pl.when((slot >= 0) | (b == 0))
+            def _():
+                act(pltpu.make_async_copy(left_hbm.at[b], left_ref.at[b], sems.at[0, b]))
+                act(pltpu.make_async_copy(right_hbm.at[b], right_ref.at[b], sems.at[1, b]))
+
+    each(lambda copy: copy.start())
+    each(lambda copy: copy.wait())
 
 
 def own_kernel(scaled, places, *refs):
@@ -428,14 +433,14 @@
     channels = channel_class.shape[0]
     psi, left, right = wavefunction[0], env_left[:, 0], env_right[:, 0]
     left, right = pl.pallas_call(
-        load_kernel,
+        functools.partial(load_kernel, places),
         out_shape=(jax.ShapeDtypeStruct(left.shape, left.dtype),) * 2,
-        in_specs=[pl.BlockSpec(memory_space=pl.ANY)] * 2,
+        in_specs=[SMEM] + [pl.BlockSpec(memory_space=pl.ANY)] * 2,
         out_specs=(VMEM, VMEM),
         scratch_shapes=[pltpu.SemaphoreType.DMA((2, channels))],
         compiler_params=pltpu.CompilerParams(vmem_limit_bytes=46 * MIB),
         name="load",
-    )(left, right)
+    )(channel_class, left, right)
     rows_shape = jax.ShapeDtypeStruct((blocks, 128), jnp.float32)
     scalars = jax.ShapeDtypeStruct((8, 128), jnp.float32)
     wide = jax.ShapeDtypeStruct((width, width), jnp.float32)

time: 69.2 us -> 69.2 us (level)
  waiting for transfers between devices: 21.5 us -> 14.4 us
  starting transfers between devices: 21 us -> 25.7 us
  blocking collectives: 8.58 us -> 10.7 us
    ppermute x3, waiting for transfers between devices: 2.92 us -> 0.22 us  [spread(): first = [piece, lax.ppermute(piece, 'mpo', [(0, 1), (1, 0)])]]
    ppermute x6, waiting for transfers between devices: 7.18 us -> 4.84 us  [shift(): return lax.ppermute(block, ring, pairs)]
    ppermute x3, waiting for transfers between devices: 9.84 us -> 7.53 us  [gather_parts(): return [t, lax.ppermute(t, 'mpo', [(0, 1), (1, 0)])]]
    ppermute x3, starting transfers between devices: 3.21 us -> 5.39 us  [gather_parts(): return [t, lax.ppermute(t, 'mpo', [(0, 1), (1, 0)])]]
    all_to_all x1, blocking collectives: 8.58 us -> 10.7 us  [exchange(): return lax.all_to_all(rows, ring, 0, 0, tiled=True)]
    ppermute x3, starting transfers between devices: 4.27 us -> 5.75 us  [spread(): first = [piece, lax.ppermute(piece, 'mpo', [(0, 1), (1, 0)])]]
    ppermute x6, starting transfers between devices: 8.36 us -> 9.72 us  [shift(): return lax.ppermute(block, ring, pairs)]
  transfers between devices with their start and end apart: 14 -> 14, of which waited for: 8 -> 7; matrix products, arithmetic and copies ran while one was open for 0% -> 0% of each run, Pallas kernels for 12% -> 13%
where the time goes in v14:
time: 69.2 us; the launch traced here: 69.5 us
  starting transfers between devices  25.7 us (37%)
  Pallas kernels  16.3 us (24%)
  waiting for transfers between devices  14.4 us (21%)
  blocking collectives  10.7 us (15%)
  local copies, waits for them, and re-layouts  1.55 us (2%)
  between operations  0.84 us (1%)
    pallas_call x16, Pallas kernels, call(): pl.pallas_call(kernel, out_shape=outs, in_specs=[first] + [VMEM] * (len(a...  13.6 us
    all_to_all x1, blocking collectives, exchange(): return lax.all_to_all(rows, ring, 0, 0, tiled=True)  10.7 us
    ppermute x6, starting transfers between devices, shift(): return lax.ppermute(block, ring, pairs)  9.72 us
    ppermute x3, waiting for transfers between devices, gather_parts(): return [t, lax.ppermute(t, 'mpo', [(0, 1), (1, 0)])]  7.53 us
    ppermute x3, starting transfers between devices, spread(): first = [piece, lax.ppermute(piece, 'mpo', [(0, 1), (1, 0)])]  5.75 us
    ppermute x3, starting transfers between devices, gather_parts(): return [t, lax.ppermute(t, 'mpo', [(0, 1), (1, 0)])]  5.39 us
    ppermute x6, waiting for transfers between devices, shift(): return lax.ppermute(block, ring, pairs)  4.84 us
    ppermute x2, starting transfers between devices, add_round(): return rows + lax.ppermute(rows, axis, pairs)  4.8 us
  transfers between devices with their start and end apart: 14, of which 7 were waited for; matrix products, arithmetic and copies ran while one was open for 0% of the time, Pallas kernels for 13%

profile of v14, /device:TPU:0, one launch (start us, length us, event | category | flops | bytes accessed | tf_op | source)
XLA Modules:
  0.0 69.5 jit_solution(12646591858619616052)
XLA Ops:
  1.6 3.5 %collective-permute-start.1 = (bf16[128,256]{1,0:T(8,128)(2,1)S(1)}, bf16[128,256]{1,0:T(8,128)(2,1)S(1)}, u32[]{:S(2)}, u32[]{:S(2)}) collective-permute-start(bf16[128,256]{1,0:T(8,128)(2,1)S(1)} %get-tuple-element.37), channel_id=1, source_target_pairs={{9,0},{8,1},{13,4},{12,5},{1,8},{0,9},{5,12},{4,13},{11,2},{10,3},... | collective-permute-start | bytes 196616 | tf_op jit(solution)/shard_map/ppermute | solution.py:496
  6.4 2.7 %load.1 = (bf16[24,256,256]{2,1,0:T(8,128)(2,1)S(1)}, bf16[24,256,256]{2,1,0:T(8,128)(2,1)S(1)}) custom-call(s32[24]{0:T(128)S(1)} %copy-done.1, bf16[24,256,256]{2,1,0:T(8,128)(2,1)} %bitcast.10, bf16[24,256,256]{2,1,0:T(8,128)(2,1)} %bitcast.11), custom_call_target="tpu_custom_call" | custom-call | tf_op jit(solution)/shard_map/load/pallas_call | solution.py:435
  9.2 1.8 %collective-permute-start.2 = (bf16[128,256]{1,0:T(8,128)(2,1)S(1)}, bf16[128,256]{1,0:T(8,128)(2,1)S(1)}, u32[]{:S(2)}, u32[]{:S(2)}) collective-permute-start(bf16[128,256]{1,0:T(8,128)(2,1)S(1)} %hold.2.refs_5_), channel_id=1, source_target_pairs={{0,2},{2,0},{1,3},{3,1},{4,6},{6,4},{5,7},{7,5},{8,10},{10,8},{9,1... | collective-permute-start | bytes 196616 | tf_op jit(solution)/shard_map/ppermute | solution.py:530
  11.0 1.5 %own.3 = (f32[256,256]{1,0:T(8,128)S(1)}, f32[8,128]{1,0:T(8,128)S(1)}) custom-call(s32[24]{0:T(128)S(1)} %copy-done.1, bf16[24,256,256]{2,1,0:T(8,128)(2,1)S(1)} %get-tuple-element.30.refs_1_.rows_ref, bf16[24,256,256]{2,1,0:T(8,128)(2,1)S(1)} %get-tuple-element.31.refs_2_, bf16[256,256]{1,0:T(8,128)(2,1)S(1)} %get-tuple-element.32.refs_3_.refs_2_), custom_call_target="tpu_custom_call" | custom-call | flops 322122560 | bytes 262144 | tf_op jit(solution)/shard_map/own/pallas_call | solution.py:456
  13.5 1.3 %rest.6 = (bf16[256,256]{1,0:T(8,128)(2,1)S(1)}, f32[8,128]{1,0:T(8,128)S(1)}) custom-call(s32[24]{0:T(128)S(1)} %copy-done.1, bf16[24,256,256]{2,1,0:T(8,128)(2,1)S(1)} %get-tuple-element.30.refs_1_.rows_ref, bf16[24,256,256]{2,1,0:T(8,128)(2,1)S(1)} %get-tuple-element.31.refs_2_, f32[256,256]{1,0:T(8,128)S(1)} %get-tuple-element.35.refs_3_, ...), custom_call_target="tpu_custom_call" | custom-call | flops 322122560 | bytes 262144 | tf_op jit(solution)/shard_map/rest/pallas_call | solution.py:456
  14.9 1.6 %collective-permute-start.3 = (bf16[256,256]{1,0:T(8,128)(2,1)S(1)}, bf16[256,256]{1,0:T(8,128)(2,1)S(1)}, u32[]{:S(2)}, u32[]{:S(2)}) collective-permute-start(bf16[256,256]{1,0:T(8,128)(2,1)S(1)} %get-tuple-element.38.refs_0_), channel_id=1, source_target_pairs={{0,2},{2,0},{1,3},{3,1},{4,6},{6,4},{5,7},{7,5},{8,10},{10,8},{9,1... | collective-permute-start | bytes 393224 | tf_op jit(solution)/shard_map/ppermute | solution.py:537
  16.5 3.4 %collective-permute-done.3.refs_1_ = bf16[256,256]{1,0:T(8,128)(2,1)S(1)} collective-permute-done((bf16[256,256]{1,0:T(8,128)(2,1)S(1)}, bf16[256,256]{1,0:T(8,128)(2,1)S(1)}, u32[]{:S(2)}, u32[]{:S(2)}) %collective-permute-start.3) | collective-permute-done | bytes 131104 | tf_op jit(solution)/shard_map/ppermute | solution.py:537
  20.3 3.6 %collective-permute-start.4 = (bf16[160,256]{1,0:T(8,128)(2,1)S(1)}, bf16[160,256]{1,0:T(8,128)(2,1)S(1)}, u32[]{:S(2)}, u32[]{:S(2)}) collective-permute-start(bf16[160,256]{1,0:T(8,128)(2,1)S(1)} %get-tuple-element.43), channel_id=1, source_target_pairs={{9,0},{8,1},{13,4},{12,5},{1,8},{0,9},{5,12},{4,13},{11,2},{10,3},... | collective-permute-start | bytes 245768 | tf_op jit(solution)/shard_map/ppermute | solution.py:496
  24.5 1.5 %collective-permute-done.4.block_ref = bf16[160,256]{1,0:T(8,128)(2,1)S(1)} collective-permute-done((bf16[160,256]{1,0:T(8,128)(2,1)S(1)}, bf16[160,256]{1,0:T(8,128)(2,1)S(1)}, u32[]{:S(2)}, u32[]{:S(2)}) %collective-permute-start.4) | collective-permute-done | bytes 81952 | tf_op jit(solution)/shard_map/ppermute | solution.py:496
  26.9 3.0 %collective-permute-start.7 = (f32[8,128]{1,0:T(8,128)S(1)}, f32[8,128]{1,0:T(8,128)S(1)}, u32[]{:S(2)}, u32[]{:S(2)}) collective-permute-start(f32[8,128]{1,0:T(8,128)S(1)} %get-tuple-element.46), channel_id=1, source_target_pairs={{0,1},{1,0},{4,5},{5,4},{8,9},{9,8},{12,13},{13,12},{2,3},{3,2},{6... | collective-permute-start | bytes 12296 | tf_op jit(solution)/shard_map/ppermute | solution.py:511
  29.9 1.5 %own.4 = (f32[256,256]{1,0:T(8,128)S(1)}, f32[8,128]{1,0:T(8,128)S(1)}) custom-call(s32[24]{0:T(128)S(1)} %copy-done.1, bf16[24,256,256]{2,1,0:T(8,128)(2,1)S(1)} %get-tuple-element.30.refs_1_.rows_ref, bf16[24,256,256]{2,1,0:T(8,128)(2,1)S(1)} %get-tuple-element.31.refs_2_, bf16[256,256]{1,0:T(8,128)(2,1)S(1)} %get-tuple-element.40.refs_3_.refs_4_), custom_call_target="tpu_custom_call" | custom-call | flops 322122560 | bytes 262144 | tf_op jit(solution)/shard_map/own/pallas_call | solution.py:456
  31.5 1.4 %rest.7 = (bf16[256,256]{1,0:T(8,128)(2,1)S(1)}, f32[8,128]{1,0:T(8,128)S(1)}, f32[8,128]{1,0:T(8,128)S(1)}) custom-call(s32[24]{0:T(128)S(1)} %copy-done.1, bf16[24,256,256]{2,1,0:T(8,128)(2,1)S(1)} %get-tuple-element.30.refs_1_.rows_ref, bf16[24,256,256]{2,1,0:T(8,128)(2,1)S(1)} %get-tuple-element.31.refs_2_, f32[256,256]{1,0:T(8,128)S(1)} %get-tuple-element.41.refs_3_, ...), custom_call_target="tpu_custom_call" | custom-call | flops 644245120 | bytes 262144 | tf_op jit(solution)/shard_map/rest/pallas_call | solution.py:456
  32.9 1.5 %collective-permute-start.8 = (bf16[256,256]{1,0:T(8,128)(2,1)S(1)}, bf16[256,256]{1,0:T(8,128)(2,1)S(1)}, u32[]{:S(2)}, u32[]{:S(2)}) collective-permute-start(bf16[256,256]{1,0:T(8,128)(2,1)S(1)} %get-tuple-element.47.refs_0_), channel_id=1, source_target_pairs={{0,2},{2,0},{1,3},{3,1},{4,6},{6,4},{5,7},{7,5},{8,10},{10,8},{9,1... | collective-permute-start | bytes 393224 | tf_op jit(solution)/shard_map/ppermute | solution.py:537
  34.4 1.8 %collective-permute-start.9 = (f32[8,128]{1,0:T(8,128)S(1)}, f32[8,128]{1,0:T(8,128)S(1)}, u32[]{:S(2)}, u32[]{:S(2)}) collective-permute-start(f32[8,128]{1,0:T(8,128)S(1)} %get-tuple-element.48), channel_id=1, source_target_pairs={{0,4},{1,5},{4,0},{5,1},{8,12},{9,13},{12,8},{13,9},{2,6},{3,7},{6... | collective-permute-start | bytes 12296 | tf_op jit(solution)/shard_map/ppermute | solution.py:511
  36.2 1.8 %collective-permute-done.9 = f32[8,128]{1,0:T(8,128)S(1)} collective-permute-done((f32[8,128]{1,0:T(8,128)S(1)}, f32[8,128]{1,0:T(8,128)S(1)}, u32[]{:S(2)}, u32[]{:S(2)}) %collective-permute-start.9) | collective-permute-done | bytes 4128 | tf_op jit(solution)/shard_map/ppermute | solution.py:511
  40.8 3.4 %collective-permute-done.11.block_ref = bf16[128,256]{1,0:T(8,128)(2,1)S(1)} collective-permute-done((bf16[128,256]{1,0:T(8,128)(2,1)S(1)}, bf16[128,256]{1,0:T(8,128)(2,1)S(1)}, u32[]{:S(2)}, u32[]{:S(2)}) %collective-permute-start.11) | collective-permute-done | bytes 65568 | tf_op jit(solution)/shard_map/ppermute | solution.py:496
  44.2 3.1 %collective-permute-start.12 = (bf16[128,256]{1,0:T(8,128)(2,1)S(1)}, bf16[128,256]{1,0:T(8,128)(2,1)S(1)}, u32[]{:S(2)}, u32[]{:S(2)}) collective-permute-start(bf16[128,256]{1,0:T(8,128)(2,1)S(1)} %hold.3.refs_4_), channel_id=1, source_target_pairs={{0,2},{2,0},{1,3},{3,1},{4,6},{6,4},{5,7},{7,5},{8,10},{10,8},{9,1... | collective-permute-start | bytes 196616 | tf_op jit(solution)/shard_map/ppermute | solution.py:530
  47.3 1.5 %own.5.refs_3_ = f32[256,256]{1,0:T(8,128)S(1)} custom-call(s32[24]{0:T(128)S(1)} %copy-done.1, bf16[24,256,256]{2,1,0:T(8,128)(2,1)S(1)} %get-tuple-element.30.refs_1_.rows_ref, bf16[24,256,256]{2,1,0:T(8,128)(2,1)S(1)} %get-tuple-element.31.refs_2_, bf16[256,256]{1,0:T(8,128)(2,1)S(1)} %get-tuple-element.50.refs_3_.rows_ref), custom_call_target="tpu_custom_call" | custom-call | flops 322122560 | bytes 262144 | tf_op jit(solution)/shard_map/own/pallas_call | solution.py:456
  48.8 0.9 %rest.8.refs_3_ = f32[256,256]{1,0:T(8,128)S(1)} custom-call(s32[24]{0:T(128)S(1)} %copy-done.1, bf16[24,256,256]{2,1,0:T(8,128)(2,1)S(1)} %get-tuple-element.30.refs_1_.rows_ref, bf16[24,256,256]{2,1,0:T(8,128)(2,1)S(1)} %get-tuple-element.31.refs_2_, f32[256,256]{1,0:T(8,128)S(1)} %own.5.refs_3_, bf16[256,256]{1,0:T(8,128)(2,1)S(1)} %collective-permute-done.10.refs_4_), custom_call_target="tpu_custom_call" | custom-call | flops 322122560 | bytes 262144 | tf_op jit(solution)/shard_map/rest/pallas_call | solution.py:456
  49.7 1.3 %rest.9.refs_0_ = bf16[256,256]{1,0:T(8,128)(2,1)S(1)} custom-call(s32[24]{0:T(128)S(1)} %copy-done.1, bf16[24,256,256]{2,1,0:T(8,128)(2,1)S(1)} %get-tuple-element.30.refs_1_.rows_ref, bf16[24,256,256]{2,1,0:T(8,128)(2,1)S(1)} %get-tuple-element.31.refs_2_, f32[256,256]{1,0:T(8,128)S(1)} %rest.8.refs_3_, bf16[128,256]{1,0:T(8,128)(2,1)S(1)} %hold.3.refs_4_, ...), custom_call_target="tpu_custom_call" | custom-call | flops 322122560 | bytes 262144 | tf_op jit(solution)/shard_map/rest/pallas_call | solution.py:456
  51.0 2.3 %collective-permute-start.13 = (bf16[256,256]{1,0:T(8,128)(2,1)S(1)}, bf16[256,256]{1,0:T(8,128)(2,1)S(1)}, u32[]{:S(2)}, u32[]{:S(2)}) collective-permute-start(bf16[256,256]{1,0:T(8,128)(2,1)S(1)} %rest.9.refs_0_), channel_id=1, source_target_pairs={{0,2},{2,0},{1,3},{3,1},{4,6},{6,4},{5,7},{7,5},{8,10},{10,8},{9,1... | collective-permute-start | bytes 393224 | tf_op jit(solution)/shard_map/ppermute | solution.py:537
  53.3 3.4 %collective-permute-done.13.refs_1_ = bf16[256,256]{1,0:T(8,128)(2,1)S(1)} collective-permute-done((bf16[256,256]{1,0:T(8,128)(2,1)S(1)}, bf16[256,256]{1,0:T(8,128)(2,1)S(1)}, u32[]{:S(2)}, u32[]{:S(2)}) %collective-permute-start.13) | collective-permute-done | bytes 131104 | tf_op jit(solution)/shard_map/ppermute | solution.py:537
  57.4 10.7 %all_to_all.11 = f32[8,1,128]{2,1,0:T(1,128)S(1)} all-to-all(f32[8,1,128]{2,1,0:T(1,128)S(1)} %bitcast.9), channel_id=1, replica_groups=mesh['groups'=2,'blk'=4,'mpo'=2,'rep'=2] {'blk','rep'}, dimensions={0} | all-to-all | bytes 8192 | tf_op jit(solution)/shard_map/all_to_all | solution.py:542
  68.1 1.4 %final.1 = (bf16[3,1,128,256]{3,2,1,0:T(8,128)(2,1)}, f32[2,3]{1,0:T(2,128)}) custom-call(f32[8,128]{1,0:T(8,128)S(1)} %bitcast.8, f32[256,256]{1,0:T(8,128)S(1)} %get-tuple-element.56.r_ref, f32[256,256]{1,0:T(8,128)S(1)} %get-tuple-element.57.z_ref, f32[256,256]{1,0:T(8,128)S(1)} %get-tuple-element.53.refs_5_.w_ref, ...), custom_call_target="tpu_custom_call" | custom-call | bytes 262144 | tf_op jit(solution)/shard_map/final/pallas_call | solution.py:456
  (28 shorter events, 8.6 us)
Async XLA Ops:
  0.6 0.9 %copy-start = (bf16[1,256,256]{2,1,0:T(8,128)(2,1)S(1)}, bf16[1,256,256]{2,1,0:T(8,128)(2,1)}, u32[]{:S(2)}) copy-start(bf16[1,256,256]{2,1,0:T(8,128)(2,1)} %param.4) | copy-start | bytes 393220
  1.6 7.6 %collective-permute-start.1 = (bf16[128,256]{1,0:T(8,128)(2,1)S(1)}, bf16[128,256]{1,0:T(8,128)(2,1)S(1)}, u32[]{:S(2)}, u32[]{:S(2)}) collective-permute-start(bf16[128,256]{1,0:T(8,128)(2,1)S(1)} %get-tuple-element.37), channel_id=1, source_target_pairs={{9,0},{8,1},{13,4},{12,5},{1,8},{0,9},{5,12},{4,13},{11,2},{10,3},... | collective-permute-start | bytes 196616 | tf_op jit(solution)/shard_map/ppermute | solution.py:496
  5.1 7.5 %collective-permute-start = (bf16[256,256]{1,0:T(8,128)(2,1)S(1)}, bf16[256,256]{1,0:T(8,128)(2,1)S(1)}, u32[]{:S(2)}, u32[]{:S(2)}) collective-permute-start(bf16[256,256]{1,0:T(8,128)(2,1)S(1)} %get-tuple-element.32.refs_3_.refs_2_), channel_id=1, source_target_pairs={{12,1},{9,4},{4,9},{1,12},{14,3},{11,6},{6,11},{3,14},{28,17},{25,... | collective-permute-start | bytes 393224 | tf_op jit(solution)/shard_map/ppermute | solution.py:496
  5.8 0.7 copy-start.1
  9.2 4.3 %collective-permute-start.2 = (bf16[128,256]{1,0:T(8,128)(2,1)S(1)}, bf16[128,256]{1,0:T(8,128)(2,1)S(1)}, u32[]{:S(2)}, u32[]{:S(2)}) collective-permute-start(bf16[128,256]{1,0:T(8,128)(2,1)S(1)} %hold.2.refs_5_), channel_id=1, source_target_pairs={{0,2},{2,0},{1,3},{3,1},{4,6},{6,4},{5,7},{7,5},{8,10},{10,8},{9,1... | collective-permute-start | bytes 196616 | tf_op jit(solution)/shard_map/ppermute | solution.py:530
  14.9 5.0 %collective-permute-start.3 = (bf16[256,256]{1,0:T(8,128)(2,1)S(1)}, bf16[256,256]{1,0:T(8,128)(2,1)S(1)}, u32[]{:S(2)}, u32[]{:S(2)}) collective-permute-start(bf16[256,256]{1,0:T(8,128)(2,1)S(1)} %get-tuple-element.38.refs_0_), channel_id=1, source_target_pairs={{0,2},{2,0},{1,3},{3,1},{4,6},{6,4},{5,7},{7,5},{8,10},{10,8},{9,1... | collective-permute-start | bytes 393224 | tf_op jit(solution)/shard_map/ppermute | solution.py:537
  20.3 5.7 %collective-permute-start.4 = (bf16[160,256]{1,0:T(8,128)(2,1)S(1)}, bf16[160,256]{1,0:T(8,128)(2,1)S(1)}, u32[]{:S(2)}, u32[]{:S(2)}) collective-permute-start(bf16[160,256]{1,0:T(8,128)(2,1)S(1)} %get-tuple-element.43), channel_id=1, source_target_pairs={{9,0},{8,1},{13,4},{12,5},{1,8},{0,9},{5,12},{4,13},{11,2},{10,3},... | collective-permute-start | bytes 245768 | tf_op jit(solution)/shard_map/ppermute | solution.py:496
  23.9 7.6 %collective-permute-start.6 = (bf16[256,256]{1,0:T(8,128)(2,1)S(1)}, bf16[256,256]{1,0:T(8,128)(2,1)S(1)}, u32[]{:S(2)}, u32[]{:S(2)}) collective-permute-start(bf16[256,256]{1,0:T(8,128)(2,1)S(1)} %get-tuple-element.40.refs_3_.refs_4_), channel_id=1, source_target_pairs={{12,1},{9,4},{4,9},{1,12},{14,3},{11,6},{6,11},{3,14},{28,17},{25,... | collective-permute-start | bytes 393224 | tf_op jit(solution)/shard_map/ppermute | solution.py:496
  26.0 5.5 %collective-permute-start.5 = (bf16[128,256]{1,0:T(8,128)(2,1)S(1)}, bf16[128,256]{1,0:T(8,128)(2,1)S(1)}, u32[]{:S(2)}, u32[]{:S(2)}) collective-permute-start(bf16[128,256]{1,0:T(8,128)(2,1)S(1)} %get-tuple-element.45.refs_5_), channel_id=1, source_target_pairs={{0,2},{2,0},{1,3},{3,1},{4,6},{6,4},{5,7},{7,5},{8,10},{10,8},{9,1... | collective-permute-start | bytes 196616 | tf_op jit(solution)/shard_map/ppermute | solution.py:530
  26.9 4.6 %collective-permute-start.7 = (f32[8,128]{1,0:T(8,128)S(1)}, f32[8,128]{1,0:T(8,128)S(1)}, u32[]{:S(2)}, u32[]{:S(2)}) collective-permute-start(f32[8,128]{1,0:T(8,128)S(1)} %get-tuple-element.46), channel_id=1, source_target_pairs={{0,1},{1,0},{4,5},{5,4},{8,9},{9,8},{12,13},{13,12},{2,3},{3,2},{6... | collective-permute-start | bytes 12296 | tf_op jit(solution)/shard_map/ppermute | solution.py:511
  32.9 5.8 %collective-permute-start.8 = (bf16[256,256]{1,0:T(8,128)(2,1)S(1)}, bf16[256,256]{1,0:T(8,128)(2,1)S(1)}, u32[]{:S(2)}, u32[]{:S(2)}) collective-permute-start(bf16[256,256]{1,0:T(8,128)(2,1)S(1)} %get-tuple-element.47.refs_0_), channel_id=1, source_target_pairs={{0,2},{2,0},{1,3},{3,1},{4,6},{6,4},{5,7},{7,5},{8,10},{10,8},{9,1... | collective-permute-start | bytes 393224 | tf_op jit(solution)/shard_map/ppermute | solution.py:537
  34.4 3.6 %collective-permute-start.9 = (f32[8,128]{1,0:T(8,128)S(1)}, f32[8,128]{1,0:T(8,128)S(1)}, u32[]{:S(2)}, u32[]{:S(2)}) collective-permute-start(f32[8,128]{1,0:T(8,128)S(1)} %get-tuple-element.48), channel_id=1, source_target_pairs={{0,4},{1,5},{4,0},{5,1},{8,12},{9,13},{12,8},{13,9},{2,6},{3,7},{6... | collective-permute-start | bytes 12296 | tf_op jit(solution)/shard_map/ppermute | solution.py:511
  39.5 4.7 %collective-permute-start.11 = (bf16[128,256]{1,0:T(8,128)(2,1)S(1)}, bf16[128,256]{1,0:T(8,128)(2,1)S(1)}, u32[]{:S(2)}, u32[]{:S(2)}) collective-permute-start(bf16[128,256]{1,0:T(8,128)(2,1)S(1)} %get-tuple-element.51), channel_id=1, source_target_pairs={{9,0},{8,1},{13,4},{12,5},{1,8},{0,9},{5,12},{4,13},{11,2},{10,3},... | collective-permute-start | bytes 196616 | tf_op jit(solution)/shard_map/ppermute | solution.py:496
  40.1 8.6 %collective-permute-start.10 = (bf16[256,256]{1,0:T(8,128)(2,1)S(1)}, bf16[256,256]{1,0:T(8,128)(2,1)S(1)}, u32[]{:S(2)}, u32[]{:S(2)}) collective-permute-start(bf16[256,256]{1,0:T(8,128)(2,1)S(1)} %get-tuple-element.50.refs_3_.rows_ref), channel_id=1, source_target_pairs={{12,1},{9,4},{4,9},{1,12},{14,3},{11,6},{6,11},{3,14},{28,17},{25,... | collective-permute-start | bytes 393224 | tf_op jit(solution)/shard_map/ppermute | solution.py:496
  44.2 5.5 %collective-permute-start.12 = (bf16[128,256]{1,0:T(8,128)(2,1)S(1)}, bf16[128,256]{1,0:T(8,128)(2,1)S(1)}, u32[]{:S(2)}, u32[]{:S(2)}) collective-permute-start(bf16[128,256]{1,0:T(8,128)(2,1)S(1)} %hold.3.refs_4_), channel_id=1, source_target_pairs={{0,2},{2,0},{1,3},{3,1},{4,6},{6,4},{5,7},{7,5},{8,10},{10,8},{9,1... | collective-permute-start | bytes 196616 | tf_op jit(solution)/shard_map/ppermute | solution.py:530
  51.0 5.7 %collective-permute-start.13 = (bf16[256,256]{1,0:T(8,128)(2,1)S(1)}, bf16[256,256]{1,0:T(8,128)(2,1)S(1)}, u32[]{:S(2)}, u32[]{:S(2)}) collective-permute-start(bf16[256,256]{1,0:T(8,128)(2,1)S(1)} %rest.9.refs_0_), channel_id=1, source_target_pairs={{0,2},{2,0},{1,3},{3,1},{4,6},{6,4},{5,7},{7,5},{8,10},{10,8},{9,1... | collective-permute-start | bytes 393224 | tf_op jit(solution)/shard_map/ppermute | solution.py:537

commit v15 on v13

--- a/solution.py
+++ b/solution.py
@@ -14,7 +14,6 @@
 WIDE = 8
 SMALLEST = 1e-30
 TILE = 16
-LOADS = 4
 MIB = 1024 * 1024
 VMEM = pl.BlockSpec(memory_space=pltpu.VMEM)
 SMEM = pl.BlockSpec(memory_space=pltpu.SMEM)
@@ -198,20 +197,6 @@
         @pl.when((rest > low) & (rest <= wide))
         def _():
             multiply(groups * WIDE, wide)
-
-
-def load_kernel(left_hbm, right_hbm, left_ref, right_ref, sems):
-    channels = left_ref.shape[0]
-    step = max(1, channels // LOADS)
-    copies = []
-    for side, (source, target) in enumerate(((left_hbm, left_ref), (right_hbm, right_ref))):
-        for at, low in enumerate(range(0, channels, step)):
-            part = pl.ds(low, min(step, channels - low))
-            copies.append(pltpu.make_async_copy(source.at[part], target.at[part], sems.at[side, at]))
-    for copy in copies:
-        copy.start()
-    for copy in copies:
-        copy.wait()
 
 
 def own_kernel(scaled, places, *refs):
@@ -427,15 +412,6 @@
     slots = 1 + len(permutes)
     channels = channel_class.shape[0]
     psi, left, right = wavefunction[0], env_left[:, 0], env_right[:, 0]
-    left, right = pl.pallas_call(
-        load_kernel,
-        out_shape=(jax.ShapeDtypeStruct(left.shape, left.dtype),) * 2,
-        in_specs=[pl.BlockSpec(memory_space=pl.ANY)] * 2,
-        out_specs=(VMEM, VMEM),
-        scratch_shapes=[pltpu.SemaphoreType.DMA((2, channels))],
-        compiler_params=pltpu.CompilerParams(vmem_limit_bytes=46 * MIB),
-        name="load",
-    )(left, right)
     rows_shape = jax.ShapeDtypeStruct((blocks, 128), jnp.float32)
     scalars = jax.ShapeDtypeStruct((8, 128), jnp.float32)
     wide = jax.ShapeDtypeStruct((width, width), jnp.float32)
@@ -536,8 +512,8 @@
     def exchange(rows):
         return lax.all_to_all(rows, ring, 0, 0, tiled=True)
 
-    psi, share_0 = call(take_kernel, "take", (narrow, share_shape), (psi,))
-    first, others, _ = spread(psi, share_0, after=left)
+    psi, share_0 = call(take_kernel, "take", (narrow, share_shape), (psi,), weight=2)
+    first, others, _ = spread(psi, share_0, after=psi)
     summed = rest("others", own(True, psi), [], others)
     t, unit = rest("first", summed, first, [])
     rows_in_share = width // parts + (2 * TILE if carried else 0)

time: 69.2 us -> 70.3 us (1.016)
  Pallas kernels: 16.2 us -> 13.6 us
  blocking collectives: 8.58 us -> 10.8 us
  waiting for transfers between devices: 21.5 us -> 22.8 us
    ppermute x2, starting transfers between devices: 5.18 us -> 0.01 us  [add_round(): return rows + lax.ppermute(rows, axis, pairs)]
    pallas_call x1 -> x0, Pallas kernels: 3.22 us -> none  [shards(): pl.pallas_call(load_kernel, out_shape=(jax.ShapeDtypeStruct(left.shape, l...]
    ppermute x6, waiting for transfers between devices: 7.18 us -> 10.2 us  [shift(): return lax.ppermute(block, ring, pairs)]
    ppermute x3, starting transfers between devices: 4.27 us -> 7.26 us  [spread(): first = [piece, lax.ppermute(piece, 'mpo', [(0, 1), (1, 0)])]]
    ppermute x3, waiting for transfers between devices: 9.84 us -> 6.96 us  [gather_parts(): return [t, lax.ppermute(t, 'mpo', [(0, 1), (1, 0)])]]
    ppermute x3, starting transfers between devices: 3.21 us -> 6.04 us  [gather_parts(): return [t, lax.ppermute(t, 'mpo', [(0, 1), (1, 0)])]]
    all_to_all x1, blocking collectives: 8.58 us -> 10.8 us  [exchange(): return lax.all_to_all(rows, ring, 0, 0, tiled=True)]
    ppermute x2, waiting for transfers between devices: 1.6 us -> 3.61 us  [add_round(): return rows + lax.ppermute(rows, axis, pairs)]
  transfers between devices with their start and end apart: 14 -> 14, of which waited for: 8 -> 9; matrix products, arithmetic and copies ran while one was open for 0% -> 0% of each run, Pallas kernels for 12% -> 9%
where the time goes in v15:
time: 70.3 us; the launch traced here: 70.2 us
  waiting for transfers between devices  22.8 us (32%)
  starting transfers between devices  21.4 us (30%)
  Pallas kernels  13.6 us (19%)
  blocking collectives  10.8 us (15%)
  local copies, waits for them, and re-layouts  0.91 us (1%)
  between operations  0.81 us (1%)
    pallas_call x16, Pallas kernels, call(): pl.pallas_call(kernel, out_shape=outs, in_specs=[first] + [VMEM] * (len(a...  13.6 us
    all_to_all x1, blocking collectives, exchange(): return lax.all_to_all(rows, ring, 0, 0, tiled=True)  10.8 us
    ppermute x6, waiting for transfers between devices, shift(): return lax.ppermute(block, ring, pairs)  10.2 us
    ppermute x6, starting transfers between devices, shift(): return lax.ppermute(block, ring, pairs)  8.05 us
    ppermute x3, starting transfers between devices, spread(): first = [piece, lax.ppermute(piece, 'mpo', [(0, 1), (1, 0)])]  7.26 us
    ppermute x3, waiting for transfers between devices, gather_parts(): return [t, lax.ppermute(t, 'mpo', [(0, 1), (1, 0)])]  6.96 us
    ppermute x3, starting transfers between devices, gather_parts(): return [t, lax.ppermute(t, 'mpo', [(0, 1), (1, 0)])]  6.04 us
    ppermute x2, waiting for transfers between devices, add_round(): return rows + lax.ppermute(rows, axis, pairs)  3.61 us
  transfers between devices with their start and end apart: 14, of which 9 were waited for; matrix products, arithmetic and copies ran while one was open for 0% of the time, Pallas kernels for 9%

profile of v15, /device:TPU:0, one launch (start us, length us, event | category | flops | bytes accessed | tf_op | source)
XLA Modules:
  0.0 70.2 jit_solution(1733753925449748049)
XLA Ops:
  1.6 3.5 %collective-permute-start.1 = (bf16[128,256]{1,0:T(8,128)(2,1)S(1)}, bf16[128,256]{1,0:T(8,128)(2,1)S(1)}, u32[]{:S(2)}, u32[]{:S(2)}) collective-permute-start(bf16[128,256]{1,0:T(8,128)(2,1)S(1)} %get-tuple-element.33), channel_id=1, source_target_pairs={{9,0},{8,1},{13,4},{12,5},{1,8},{0,9},{5,12},{4,13},{11,2},{10,3},... | collective-permute-start | bytes 196616 | tf_op jit(solution)/shard_map/ppermute | solution.py:467
  5.8 1.8 %collective-permute-done.1.block_ref = bf16[128,256]{1,0:T(8,128)(2,1)S(1)} collective-permute-done((bf16[128,256]{1,0:T(8,128)(2,1)S(1)}, bf16[128,256]{1,0:T(8,128)(2,1)S(1)}, u32[]{:S(2)}, u32[]{:S(2)}) %collective-permute-start.1) | collective-permute-done | bytes 65568 | tf_op jit(solution)/shard_map/ppermute | solution.py:467
  7.6 3.4 %collective-permute-start.2 = (bf16[128,256]{1,0:T(8,128)(2,1)S(1)}, bf16[128,256]{1,0:T(8,128)(2,1)S(1)}, u32[]{:S(2)}, u32[]{:S(2)}) collective-permute-start(bf16[128,256]{1,0:T(8,128)(2,1)S(1)} %hold.2.refs_5_), channel_id=1, source_target_pairs={{0,2},{2,0},{1,3},{3,1},{4,6},{6,4},{5,7},{7,5},{8,10},{10,8},{9,1... | collective-permute-start | bytes 196616 | tf_op jit(solution)/shard_map/ppermute | solution.py:501
  11.0 1.5 %own.3 = (f32[256,256]{1,0:T(8,128)S(1)}, f32[8,128]{1,0:T(8,128)S(1)}) custom-call(s32[24]{0:T(128)S(1)} %copy-done.2, bf16[24,256,256]{2,1,0:T(8,128)(2,1)S(1)} %bitcast.7, bf16[24,256,256]{2,1,0:T(8,128)(2,1)S(1)} %bitcast.15, bf16[256,256]{1,0:T(8,128)(2,1)S(1)} %get-tuple-element.28.refs_3_.rows_ref.refs_2_), custom_call_target="tpu_custom_call" | custom-call | flops 322122560 | bytes 262144 | tf_op jit(solution)/shard_map/own/pallas_call | solution.py:427
  13.4 1.3 %rest.6 = (bf16[256,256]{1,0:T(8,128)(2,1)S(1)}, f32[8,128]{1,0:T(8,128)S(1)}) custom-call(s32[24]{0:T(128)S(1)} %copy-done.2, bf16[24,256,256]{2,1,0:T(8,128)(2,1)S(1)} %bitcast.9, bf16[24,256,256]{2,1,0:T(8,128)(2,1)S(1)} %bitcast.17, f32[256,256]{1,0:T(8,128)S(1)} %get-tuple-element.31.refs_3_, f32[8,128]{1,0:T(8,128)S(1)} %get-tuple-element.32.refs_4_, ...), custom_call_target="tpu_custom_call" | custom-call | flops 322122560 | bytes 262144 | tf_op jit(solution)/shard_map/rest/pallas_call | solution.py:427
  14.7 2.2 %collective-permute-start.3 = (bf16[256,256]{1,0:T(8,128)(2,1)S(1)}, bf16[256,256]{1,0:T(8,128)(2,1)S(1)}, u32[]{:S(2)}, u32[]{:S(2)}) collective-permute-start(bf16[256,256]{1,0:T(8,128)(2,1)S(1)} %get-tuple-element.34.refs_0_), channel_id=1, source_target_pairs={{0,2},{2,0},{1,3},{3,1},{4,6},{6,4},{5,7},{7,5},{8,10},{10,8},{9,1... | collective-permute-start | bytes 393224 | tf_op jit(solution)/shard_map/ppermute | solution.py:508
  17.0 3.4 %collective-permute-done.3.refs_1_ = bf16[256,256]{1,0:T(8,128)(2,1)S(1)} collective-permute-done((bf16[256,256]{1,0:T(8,128)(2,1)S(1)}, bf16[256,256]{1,0:T(8,128)(2,1)S(1)}, u32[]{:S(2)}, u32[]{:S(2)}) %collective-permute-start.3) | collective-permute-done | bytes 131104 | tf_op jit(solution)/shard_map/ppermute | solution.py:508
  20.7 2.5 %collective-permute-start.4 = (bf16[160,256]{1,0:T(8,128)(2,1)S(1)}, bf16[160,256]{1,0:T(8,128)(2,1)S(1)}, u32[]{:S(2)}, u32[]{:S(2)}) collective-permute-start(bf16[160,256]{1,0:T(8,128)(2,1)S(1)} %get-tuple-element.39), channel_id=1, source_target_pairs={{9,0},{8,1},{13,4},{12,5},{1,8},{0,9},{5,12},{4,13},{11,2},{10,3},... | collective-permute-start | bytes 245768 | tf_op jit(solution)/shard_map/ppermute | solution.py:467
  23.9 3.7 %collective-permute-done.4.block_ref = bf16[160,256]{1,0:T(8,128)(2,1)S(1)} collective-permute-done((bf16[160,256]{1,0:T(8,128)(2,1)S(1)}, bf16[160,256]{1,0:T(8,128)(2,1)S(1)}, u32[]{:S(2)}, u32[]{:S(2)}) %collective-permute-start.4) | collective-permute-done | bytes 81952 | tf_op jit(solution)/shard_map/ppermute | solution.py:467
  27.5 2.7 %collective-permute-start.5 = (bf16[128,256]{1,0:T(8,128)(2,1)S(1)}, bf16[128,256]{1,0:T(8,128)(2,1)S(1)}, u32[]{:S(2)}, u32[]{:S(2)}) collective-permute-start(bf16[128,256]{1,0:T(8,128)(2,1)S(1)} %get-tuple-element.41.refs_5_), channel_id=1, source_target_pairs={{0,2},{2,0},{1,3},{3,1},{4,6},{6,4},{5,7},{7,5},{8,10},{10,8},{9,1... | collective-permute-start | bytes 196616 | tf_op jit(solution)/shard_map/ppermute | solution.py:501
  30.3 1.5 %own.4 = (f32[256,256]{1,0:T(8,128)S(1)}, f32[8,128]{1,0:T(8,128)S(1)}) custom-call(s32[24]{0:T(128)S(1)} %copy-done.2, bf16[24,256,256]{2,1,0:T(8,128)(2,1)S(1)} %bitcast.10, bf16[24,256,256]{2,1,0:T(8,128)(2,1)S(1)} %bitcast.18, bf16[256,256]{1,0:T(8,128)(2,1)S(1)} %get-tuple-element.36.refs_3_.refs_4_), custom_call_target="tpu_custom_call" | custom-call | flops 322122560 | bytes 262144 | tf_op jit(solution)/shard_map/own/pallas_call | solution.py:427
  32.7 1.4 %rest.7 = (bf16[256,256]{1,0:T(8,128)(2,1)S(1)}, f32[8,128]{1,0:T(8,128)S(1)}, f32[8,128]{1,0:T(8,128)S(1)}) custom-call(s32[24]{0:T(128)S(1)} %copy-done.2, bf16[24,256,256]{2,1,0:T(8,128)(2,1)S(1)} %bitcast.11, bf16[24,256,256]{2,1,0:T(8,128)(2,1)S(1)} %bitcast.19, f32[256,256]{1,0:T(8,128)S(1)} %get-tuple-element.37.refs_3_, ...), custom_call_target="tpu_custom_call" | custom-call | flops 644245120 | bytes 262144 | tf_op jit(solution)/shard_map/rest/pallas_call | solution.py:427
  34.1 2.2 %collective-permute-start.8 = (bf16[256,256]{1,0:T(8,128)(2,1)S(1)}, bf16[256,256]{1,0:T(8,128)(2,1)S(1)}, u32[]{:S(2)}, u32[]{:S(2)}) collective-permute-start(bf16[256,256]{1,0:T(8,128)(2,1)S(1)} %get-tuple-element.43.refs_0_), channel_id=1, source_target_pairs={{0,2},{2,0},{1,3},{3,1},{4,6},{6,4},{5,7},{7,5},{8,10},{10,8},{9,1... | collective-permute-start | bytes 393224 | tf_op jit(solution)/shard_map/ppermute | solution.py:508
  36.3 3.6 %collective-permute-done.9 = f32[8,128]{1,0:T(8,128)S(1)} collective-permute-done((f32[8,128]{1,0:T(8,128)S(1)}, f32[8,128]{1,0:T(8,128)S(1)}, u32[]{:S(2)}, u32[]{:S(2)}) %collective-permute-start.9) | collective-permute-done | bytes 4128 | tf_op jit(solution)/shard_map/ppermute | solution.py:482
  41.5 4.7 %collective-permute-done.11.block_ref = bf16[128,256]{1,0:T(8,128)(2,1)S(1)} collective-permute-done((bf16[128,256]{1,0:T(8,128)(2,1)S(1)}, bf16[128,256]{1,0:T(8,128)(2,1)S(1)}, u32[]{:S(2)}, u32[]{:S(2)}) %collective-permute-start.11) | collective-permute-done | bytes 65568 | tf_op jit(solution)/shard_map/ppermute | solution.py:467
  46.3 1.1 %collective-permute-start.12 = (bf16[128,256]{1,0:T(8,128)(2,1)S(1)}, bf16[128,256]{1,0:T(8,128)(2,1)S(1)}, u32[]{:S(2)}, u32[]{:S(2)}) collective-permute-start(bf16[128,256]{1,0:T(8,128)(2,1)S(1)} %hold.3.refs_4_), channel_id=1, source_target_pairs={{0,2},{2,0},{1,3},{3,1},{4,6},{6,4},{5,7},{7,5},{8,10},{10,8},{9,1... | collective-permute-start | bytes 196616 | tf_op jit(solution)/shard_map/ppermute | solution.py:501
  47.4 1.5 %own.5.refs_3_ = f32[256,256]{1,0:T(8,128)S(1)} custom-call(s32[24]{0:T(128)S(1)} %copy-done.2, bf16[24,256,256]{2,1,0:T(8,128)(2,1)S(1)} %bitcast.12, bf16[24,256,256]{2,1,0:T(8,128)(2,1)S(1)} %bitcast.20, bf16[256,256]{1,0:T(8,128)(2,1)S(1)} %get-tuple-element.46.refs_3_.rows_ref), custom_call_target="tpu_custom_call" | custom-call | flops 322122560 | bytes 262144 | tf_op jit(solution)/shard_map/own/pallas_call | solution.py:427
  48.9 0.9 %rest.8.refs_3_ = f32[256,256]{1,0:T(8,128)S(1)} custom-call(s32[24]{0:T(128)S(1)} %copy-done.2, bf16[24,256,256]{2,1,0:T(8,128)(2,1)S(1)} %bitcast.13, bf16[24,256,256]{2,1,0:T(8,128)(2,1)S(1)} %bitcast.21, f32[256,256]{1,0:T(8,128)S(1)} %own.5.refs_3_, bf16[256,256]{1,0:T(8,128)(2,1)S(1)} %collective-permute-done.10.refs_4_), custom_call_target="tpu_custom_call" | custom-call | flops 322122560 | bytes 262144 | tf_op jit(solution)/shard_map/rest/pallas_call | solution.py:427
  49.8 1.1 %collective-permute-done.12.refs_5_ = bf16[128,256]{1,0:T(8,128)(2,1)S(1)} collective-permute-done((bf16[128,256]{1,0:T(8,128)(2,1)S(1)}, bf16[128,256]{1,0:T(8,128)(2,1)S(1)}, u32[]{:S(2)}, u32[]{:S(2)}) %collective-permute-start.12) | collective-permute-done | bytes 65568 | tf_op jit(solution)/shard_map/ppermute | solution.py:501
  50.9 1.3 %rest.9.refs_0_ = bf16[256,256]{1,0:T(8,128)(2,1)S(1)} custom-call(s32[24]{0:T(128)S(1)} %copy-done.2, bf16[24,256,256]{2,1,0:T(8,128)(2,1)S(1)} %bitcast.14, bf16[24,256,256]{2,1,0:T(8,128)(2,1)S(1)} %bitcast.22, f32[256,256]{1,0:T(8,128)S(1)} %rest.8.refs_3_, bf16[128,256]{1,0:T(8,128)(2,1)S(1)} %hold.3.refs_4_, ...), custom_call_target="tpu_custom_call" | custom-call | flops 322122560 | bytes 262144 | tf_op jit(solution)/shard_map/rest/pallas_call | solution.py:427
  52.2 1.6 %collective-permute-start.13 = (bf16[256,256]{1,0:T(8,128)(2,1)S(1)}, bf16[256,256]{1,0:T(8,128)(2,1)S(1)}, u32[]{:S(2)}, u32[]{:S(2)}) collective-permute-start(bf16[256,256]{1,0:T(8,128)(2,1)S(1)} %rest.9.refs_0_), channel_id=1, source_target_pairs={{0,2},{2,0},{1,3},{3,1},{4,6},{6,4},{5,7},{7,5},{8,10},{10,8},{9,1... | collective-permute-start | bytes 393224 | tf_op jit(solution)/shard_map/ppermute | solution.py:508
  53.9 3.6 %collective-permute-done.13.refs_1_ = bf16[256,256]{1,0:T(8,128)(2,1)S(1)} collective-permute-done((bf16[256,256]{1,0:T(8,128)(2,1)S(1)}, bf16[256,256]{1,0:T(8,128)(2,1)S(1)}, u32[]{:S(2)}, u32[]{:S(2)}) %collective-permute-start.13) | collective-permute-done | bytes 131104 | tf_op jit(solution)/shard_map/ppermute | solution.py:508
  58.0 10.8 %all_to_all.11 = f32[8,1,128]{2,1,0:T(1,128)S(1)} all-to-all(f32[8,1,128]{2,1,0:T(1,128)S(1)} %bitcast.24), channel_id=1, replica_groups=mesh['groups'=2,'blk'=4,'mpo'=2,'rep'=2] {'blk','rep'}, dimensions={0} | all-to-all | bytes 8192 | tf_op jit(solution)/shard_map/all_to_all | solution.py:513
  68.8 1.4 %final.1 = (bf16[3,1,128,256]{3,2,1,0:T(8,128)(2,1)}, f32[2,3]{1,0:T(2,128)}) custom-call(f32[8,128]{1,0:T(8,128)S(1)} %bitcast.23, f32[256,256]{1,0:T(8,128)S(1)} %get-tuple-element.52.r_ref, f32[256,256]{1,0:T(8,128)S(1)} %get-tuple-element.53.z_ref, f32[256,256]{1,0:T(8,128)S(1)} %get-tuple-element.49.refs_5_.w_ref, ...), custom_call_target="tpu_custom_call" | custom-call | bytes 262144 | tf_op jit(solution)/shard_map/final/pallas_call | solution.py:427
  (31 shorter events, 6.6 us)
Async XLA Ops:
  0.6 0.9 %copy-start.3 = (bf16[1,256,256]{2,1,0:T(8,128)(2,1)S(1)}, bf16[1,256,256]{2,1,0:T(8,128)(2,1)}, u32[]{:S(2)}) copy-start(bf16[1,256,256]{2,1,0:T(8,128)(2,1)} %param.4) | copy-start | bytes 393220
  1.5 9.5 %copy-start = (bf16[24,1,256,256]{3,2,1,0:T(8,128)(2,1)S(1)}, bf16[24,1,256,256]{3,2,1,0:T(8,128)(2,1)}, u32[]{:S(2)}) copy-start(bf16[24,1,256,256]{3,2,1,0:T(8,128)(2,1)} %param.5) | copy-start | bytes 9437188
  1.5 9.5 %copy-start.1 = (bf16[24,1,256,256]{3,2,1,0:T(8,128)(2,1)S(1)}, bf16[24,1,256,256]{3,2,1,0:T(8,128)(2,1)}, u32[]{:S(2)}) copy-start(bf16[24,1,256,256]{3,2,1,0:T(8,128)(2,1)} %param.6) | copy-start | bytes 9437188
  1.5 9.5 %copy-start.2 = (s32[24]{0:T(128)S(1)}, s32[24]{0:T(128)}, u32[]{:S(2)}) copy-start(s32[24]{0:T(128)} %refs_0_.15) | copy-start | bytes 292
  1.6 6.0 %collective-permute-start.1 = (bf16[128,256]{1,0:T(8,128)(2,1)S(1)}, bf16[128,256]{1,0:T(8,128)(2,1)S(1)}, u32[]{:S(2)}, u32[]{:S(2)}) collective-permute-start(bf16[128,256]{1,0:T(8,128)(2,1)S(1)} %get-tuple-element.33), channel_id=1, source_target_pairs={{9,0},{8,1},{13,4},{12,5},{1,8},{0,9},{5,12},{4,13},{11,2},{10,3},... | collective-permute-start | bytes 196616 | tf_op jit(solution)/shard_map/ppermute | solution.py:467
  5.1 7.5 %collective-permute-start = (bf16[256,256]{1,0:T(8,128)(2,1)S(1)}, bf16[256,256]{1,0:T(8,128)(2,1)S(1)}, u32[]{:S(2)}, u32[]{:S(2)}) collective-permute-start(bf16[256,256]{1,0:T(8,128)(2,1)S(1)} %get-tuple-element.28.refs_3_.rows_ref.refs_2_), channel_id=1, source_target_pairs={{12,1},{9,4},{4,9},{1,12},{14,3},{11,6},{6,11},{3,14},{28,17},{25,... | collective-permute-start | bytes 393224 | tf_op jit(solution)/shard_map/ppermute | solution.py:467
  7.6 5.8 %collective-permute-start.2 = (bf16[128,256]{1,0:T(8,128)(2,1)S(1)}, bf16[128,256]{1,0:T(8,128)(2,1)S(1)}, u32[]{:S(2)}, u32[]{:S(2)}) collective-permute-start(bf16[128,256]{1,0:T(8,128)(2,1)S(1)} %hold.2.refs_5_), channel_id=1, source_target_pairs={{0,2},{2,0},{1,3},{3,1},{4,6},{6,4},{5,7},{7,5},{8,10},{10,8},{9,1... | collective-permute-start | bytes 196616 | tf_op jit(solution)/shard_map/ppermute | solution.py:501
  14.7 5.6 %collective-permute-start.3 = (bf16[256,256]{1,0:T(8,128)(2,1)S(1)}, bf16[256,256]{1,0:T(8,128)(2,1)S(1)}, u32[]{:S(2)}, u32[]{:S(2)}) collective-permute-start(bf16[256,256]{1,0:T(8,128)(2,1)S(1)} %get-tuple-element.34.refs_0_), channel_id=1, source_target_pairs={{0,2},{2,0},{1,3},{3,1},{4,6},{6,4},{5,7},{7,5},{8,10},{10,8},{9,1... | collective-permute-start | bytes 393224 | tf_op jit(solution)/shard_map/ppermute | solution.py:508
  20.7 6.8 %collective-permute-start.4 = (bf16[160,256]{1,0:T(8,128)(2,1)S(1)}, bf16[160,256]{1,0:T(8,128)(2,1)S(1)}, u32[]{:S(2)}, u32[]{:S(2)}) collective-permute-start(bf16[160,256]{1,0:T(8,128)(2,1)S(1)} %get-tuple-element.39), channel_id=1, source_target_pairs={{9,0},{8,1},{13,4},{12,5},{1,8},{0,9},{5,12},{4,13},{11,2},{10,3},... | collective-permute-start | bytes 245768 | tf_op jit(solution)/shard_map/ppermute | solution.py:467
  23.2 8.6 %collective-permute-start.6 = (bf16[256,256]{1,0:T(8,128)(2,1)S(1)}, bf16[256,256]{1,0:T(8,128)(2,1)S(1)}, u32[]{:S(2)}, u32[]{:S(2)}) collective-permute-start(bf16[256,256]{1,0:T(8,128)(2,1)S(1)} %get-tuple-element.36.refs_3_.refs_4_), channel_id=1, source_target_pairs={{12,1},{9,4},{4,9},{1,12},{14,3},{11,6},{6,11},{3,14},{28,17},{25,... | collective-permute-start | bytes 393224 | tf_op jit(solution)/shard_map/ppermute | solution.py:467
  27.5 5.2 %collective-permute-start.5 = (bf16[128,256]{1,0:T(8,128)(2,1)S(1)}, bf16[128,256]{1,0:T(8,128)(2,1)S(1)}, u32[]{:S(2)}, u32[]{:S(2)}) collective-permute-start(bf16[128,256]{1,0:T(8,128)(2,1)S(1)} %get-tuple-element.41.refs_5_), channel_id=1, source_target_pairs={{0,2},{2,0},{1,3},{3,1},{4,6},{6,4},{5,7},{7,5},{8,10},{10,8},{9,1... | collective-permute-start | bytes 196616 | tf_op jit(solution)/shard_map/ppermute | solution.py:501
  30.3 1.5 %collective-permute-start.7 = (f32[8,128]{1,0:T(8,128)S(1)}, f32[8,128]{1,0:T(8,128)S(1)}, u32[]{:S(2)}, u32[]{:S(2)}) collective-permute-start(f32[8,128]{1,0:T(8,128)S(1)} %get-tuple-element.42), channel_id=1, source_target_pairs={{0,1},{1,0},{4,5},{5,4},{8,9},{9,8},{12,13},{13,12},{2,3},{3,2},{6... | collective-permute-start | bytes 12296 | tf_op jit(solution)/shard_map/ppermute | solution.py:482
  34.1 5.8 %collective-permute-start.8 = (bf16[256,256]{1,0:T(8,128)(2,1)S(1)}, bf16[256,256]{1,0:T(8,128)(2,1)S(1)}, u32[]{:S(2)}, u32[]{:S(2)}) collective-permute-start(bf16[256,256]{1,0:T(8,128)(2,1)S(1)} %get-tuple-element.43.refs_0_), channel_id=1, source_target_pairs={{0,2},{2,0},{1,3},{3,1},{4,6},{6,4},{5,7},{7,5},{8,10},{10,8},{9,1... | collective-permute-start | bytes 393224 | tf_op jit(solution)/shard_map/ppermute | solution.py:508
  36.3 3.6 %collective-permute-start.9 = (f32[8,128]{1,0:T(8,128)S(1)}, f32[8,128]{1,0:T(8,128)S(1)}, u32[]{:S(2)}, u32[]{:S(2)}) collective-permute-start(f32[8,128]{1,0:T(8,128)S(1)} %get-tuple-element.44), channel_id=1, source_target_pairs={{0,4},{1,5},{4,0},{5,1},{8,12},{9,13},{12,8},{13,9},{2,6},{3,7},{6... | collective-permute-start | bytes 12296 | tf_op jit(solution)/shard_map/ppermute | solution.py:482
  40.7 5.5 %collective-permute-start.11 = (bf16[128,256]{1,0:T(8,128)(2,1)S(1)}, bf16[128,256]{1,0:T(8,128)(2,1)S(1)}, u32[]{:S(2)}, u32[]{:S(2)}) collective-permute-start(bf16[128,256]{1,0:T(8,128)(2,1)S(1)} %get-tuple-element.47), channel_id=1, source_target_pairs={{9,0},{8,1},{13,4},{12,5},{1,8},{0,9},{5,12},{4,13},{11,2},{10,3},... | collective-permute-start | bytes 196616 | tf_op jit(solution)/shard_map/ppermute | solution.py:467
  40.8 8.1 %collective-permute-start.10 = (bf16[256,256]{1,0:T(8,128)(2,1)S(1)}, bf16[256,256]{1,0:T(8,128)(2,1)S(1)}, u32[]{:S(2)}, u32[]{:S(2)}) collective-permute-start(bf16[256,256]{1,0:T(8,128)(2,1)S(1)} %get-tuple-element.46.refs_3_.rows_ref), channel_id=1, source_target_pairs={{12,1},{9,4},{4,9},{1,12},{14,3},{11,6},{6,11},{3,14},{28,17},{25,... | collective-permute-start | bytes 393224 | tf_op jit(solution)/shard_map/ppermute | solution.py:467
  46.3 4.7 %collective-permute-start.12 = (bf16[128,256]{1,0:T(8,128)(2,1)S(1)}, bf16[128,256]{1,0:T(8,128)(2,1)S(1)}, u32[]{:S(2)}, u32[]{:S(2)}) collective-permute-start(bf16[128,256]{1,0:T(8,128)(2,1)S(1)} %hold.3.refs_4_), channel_id=1, source_target_pairs={{0,2},{2,0},{1,3},{3,1},{4,6},{6,4},{5,7},{7,5},{8,10},{10,8},{9,1... | collective-permute-start | bytes 196616 | tf_op jit(solution)/shard_map/ppermute | solution.py:501
  52.2 5.2 %collective-permute-start.13 = (bf16[256,256]{1,0:T(8,128)(2,1)S(1)}, bf16[256,256]{1,0:T(8,128)(2,1)S(1)}, u32[]{:S(2)}, u32[]{:S(2)}) collective-permute-start(bf16[256,256]{1,0:T(8,128)(2,1)S(1)} %rest.9.refs_0_), channel_id=1, source_target_pairs={{0,2},{2,0},{1,3},{3,1},{4,6},{6,4},{5,7},{7,5},{8,10},{10,8},{9,1... | collective-permute-start | bytes 393224 | tf_op jit(solution)/shard_map/ppermute | solution.py:508

commit v16 on v15

--- a/solution.py
+++ b/solution.py
@@ -532,9 +532,8 @@
         (wide, narrow, share_shape, narrow, scalars),
         (*gather_parts(t), rows, psi, w_1, unit),
     )
-    first, others, _ = spread(w_2, share_2, after=w_2)
-    summed = rest("others", own(False, w_2), [], others)
-    (t,) = rest("first", summed, first, [])
+    first, others, _ = spread(w_2, share_2)
+    (t,) = rest("rest", own(False, w_2), first, others)
     r, z, rows = call(
         third_sums_kernel,
         "sums",

time: 70.3 us -> 69.7 us (level); the launches traced: 70.2 us -> 68.4 us
  waiting for transfers between devices: 22.8 us -> 24.5 us
  starting transfers between devices: 21.4 us -> 20 us
  blocking collectives: 10.8 us -> 9.58 us
  Pallas kernels: 13.6 us -> 12.6 us
    all_to_all x1, blocking collectives: 10.8 us -> 9.58 us  [exchange(): return lax.all_to_all(rows, ring, 0, 0, tiled=True)]
    pallas_call x16 -> x14, Pallas kernels: 13.6 us -> 12.6 us  [call(): pl.pallas_call(kernel, out_shape=outs, in_specs=[first] + [VMEM] * (len(a...]
    ppermute x3, starting transfers between devices: 7.26 us -> 6.4 us  [spread(): first = [piece, lax.ppermute(piece, 'mpo', [(0, 1), (1, 0)])]]
    ppermute x6, waiting for transfers between devices: 10.2 us -> 11.1 us  [shift(): return lax.ppermute(block, ring, pairs)]
  transfers between devices with their start and end apart: 14 -> 14, of which waited for: 9 -> 9; matrix products, arithmetic and copies ran while one was open for 0% -> 0% of each run, Pallas kernels for 9% -> 8%
where the time goes in v16:
time: 69.7 us; the launch traced here: 68.4 us
  waiting for transfers between devices  24.5 us (35%)
  starting transfers between devices  20 us (29%)
  Pallas kernels  12.6 us (18%)
  blocking collectives  9.58 us (14%)
  local copies, waits for them, and re-layouts  0.91 us (1%)
  between operations  0.79 us (1%)
    pallas_call x14, Pallas kernels, call(): pl.pallas_call(kernel, out_shape=outs, in_specs=[first] + [VMEM] * (len(a...  12.6 us
    ppermute x6, waiting for transfers between devices, shift(): return lax.ppermute(block, ring, pairs)  11.1 us
    all_to_all x1, blocking collectives, exchange(): return lax.all_to_all(rows, ring, 0, 0, tiled=True)  9.58 us
    ppermute x6, starting transfers between devices, shift(): return lax.ppermute(block, ring, pairs)  7.73 us
    ppermute x3, waiting for transfers between devices, gather_parts(): return [t, lax.ppermute(t, 'mpo', [(0, 1), (1, 0)])]  7.28 us
    ppermute x3, starting transfers between devices, spread(): first = [piece, lax.ppermute(piece, 'mpo', [(0, 1), (1, 0)])]  6.4 us
    ppermute x3, starting transfers between devices, gather_parts(): return [t, lax.ppermute(t, 'mpo', [(0, 1), (1, 0)])]  5.84 us
    ppermute x2, waiting for transfers between devices, add_round(): return rows + lax.ppermute(rows, axis, pairs)  3.61 us
  transfers between devices with their start and end apart: 14, of which 9 were waited for; matrix products, arithmetic and copies ran while one was open for 0% of the time, Pallas kernels for 8%

profile of v16, /device:TPU:0, one launch (start us, length us, event | category | flops | bytes accessed | tf_op | source)
XLA Modules:
  0.0 68.4 jit_solution(3966742778178546555)
XLA Ops:
  1.6 3.5 %collective-permute-start.1 = (bf16[128,256]{1,0:T(8,128)(2,1)S(1)}, bf16[128,256]{1,0:T(8,128)(2,1)S(1)}, u32[]{:S(2)}, u32[]{:S(2)}) collective-permute-start(bf16[128,256]{1,0:T(8,128)(2,1)S(1)} %get-tuple-element.33), channel_id=1, source_target_pairs={{9,0},{8,1},{13,4},{12,5},{1,8},{0,9},{5,12},{4,13},{11,2},{10,3},... | collective-permute-start | bytes 196616 | tf_op jit(solution)/shard_map/ppermute | solution.py:467
  5.8 1.8 %collective-permute-done.1.block_ref = bf16[128,256]{1,0:T(8,128)(2,1)S(1)} collective-permute-done((bf16[128,256]{1,0:T(8,128)(2,1)S(1)}, bf16[128,256]{1,0:T(8,128)(2,1)S(1)}, u32[]{:S(2)}, u32[]{:S(2)}) %collective-permute-start.1) | collective-permute-done | bytes 65568 | tf_op jit(solution)/shard_map/ppermute | solution.py:467
  7.6 3.4 %collective-permute-start.2 = (bf16[128,256]{1,0:T(8,128)(2,1)S(1)}, bf16[128,256]{1,0:T(8,128)(2,1)S(1)}, u32[]{:S(2)}, u32[]{:S(2)}) collective-permute-start(bf16[128,256]{1,0:T(8,128)(2,1)S(1)} %hold.1.refs_5_), channel_id=1, source_target_pairs={{0,2},{2,0},{1,3},{3,1},{4,6},{6,4},{5,7},{7,5},{8,10},{10,8},{9,1... | collective-permute-start | bytes 196616 | tf_op jit(solution)/shard_map/ppermute | solution.py:501
  11.0 1.5 %own.3 = (f32[256,256]{1,0:T(8,128)S(1)}, f32[8,128]{1,0:T(8,128)S(1)}) custom-call(s32[24]{0:T(128)S(1)} %copy-done.2, bf16[24,256,256]{2,1,0:T(8,128)(2,1)S(1)} %bitcast.7, bf16[24,256,256]{2,1,0:T(8,128)(2,1)S(1)} %bitcast.14, bf16[256,256]{1,0:T(8,128)(2,1)S(1)} %get-tuple-element.28.refs_3_.rows_ref.refs_2_), custom_call_target="tpu_custom_call" | custom-call | flops 322122560 | bytes 262144 | tf_op jit(solution)/shard_map/own/pallas_call | solution.py:427
  13.4 1.3 %rest.5 = (bf16[256,256]{1,0:T(8,128)(2,1)S(1)}, f32[8,128]{1,0:T(8,128)S(1)}) custom-call(s32[24]{0:T(128)S(1)} %copy-done.2, bf16[24,256,256]{2,1,0:T(8,128)(2,1)S(1)} %bitcast.9, bf16[24,256,256]{2,1,0:T(8,128)(2,1)S(1)} %bitcast.16, f32[256,256]{1,0:T(8,128)S(1)} %get-tuple-element.31.refs_3_, f32[8,128]{1,0:T(8,128)S(1)} %get-tuple-element.32.refs_4_, ...), custom_call_target="tpu_custom_call" | custom-call | flops 322122560 | bytes 262144 | tf_op jit(solution)/shard_map/rest/pallas_call | solution.py:427
  14.7 2.2 %collective-permute-start.3 = (bf16[256,256]{1,0:T(8,128)(2,1)S(1)}, bf16[256,256]{1,0:T(8,128)(2,1)S(1)}, u32[]{:S(2)}, u32[]{:S(2)}) collective-permute-start(bf16[256,256]{1,0:T(8,128)(2,1)S(1)} %get-tuple-element.34.refs_0_), channel_id=1, source_target_pairs={{0,2},{2,0},{1,3},{3,1},{4,6},{6,4},{5,7},{7,5},{8,10},{10,8},{9,1... | collective-permute-start | bytes 393224 | tf_op jit(solution)/shard_map/ppermute | solution.py:508
  17.0 3.7 %collective-permute-done.3.refs_1_ = bf16[256,256]{1,0:T(8,128)(2,1)S(1)} collective-permute-done((bf16[256,256]{1,0:T(8,128)(2,1)S(1)}, bf16[256,256]{1,0:T(8,128)(2,1)S(1)}, u32[]{:S(2)}, u32[]{:S(2)}) %collective-permute-start.3) | collective-permute-done | bytes 131104 | tf_op jit(solution)/shard_map/ppermute | solution.py:508
  21.1 2.1 %collective-permute-start.4 = (bf16[160,256]{1,0:T(8,128)(2,1)S(1)}, bf16[160,256]{1,0:T(8,128)(2,1)S(1)}, u32[]{:S(2)}, u32[]{:S(2)}) collective-permute-start(bf16[160,256]{1,0:T(8,128)(2,1)S(1)} %get-tuple-element.39), channel_id=1, source_target_pairs={{9,0},{8,1},{13,4},{12,5},{1,8},{0,9},{5,12},{4,13},{11,2},{10,3},... | collective-permute-start | bytes 245768 | tf_op jit(solution)/shard_map/ppermute | solution.py:467
  23.9 4.5 %collective-permute-done.4.block_ref = bf16[160,256]{1,0:T(8,128)(2,1)S(1)} collective-permute-done((bf16[160,256]{1,0:T(8,128)(2,1)S(1)}, bf16[160,256]{1,0:T(8,128)(2,1)S(1)}, u32[]{:S(2)}, u32[]{:S(2)}) %collective-permute-start.4) | collective-permute-done | bytes 81952 | tf_op jit(solution)/shard_map/ppermute | solution.py:467
  28.4 1.8 %collective-permute-start.5 = (bf16[128,256]{1,0:T(8,128)(2,1)S(1)}, bf16[128,256]{1,0:T(8,128)(2,1)S(1)}, u32[]{:S(2)}, u32[]{:S(2)}) collective-permute-start(bf16[128,256]{1,0:T(8,128)(2,1)S(1)} %get-tuple-element.41.refs_5_), channel_id=1, source_target_pairs={{0,2},{2,0},{1,3},{3,1},{4,6},{6,4},{5,7},{7,5},{8,10},{10,8},{9,1... | collective-permute-start | bytes 196616 | tf_op jit(solution)/shard_map/ppermute | solution.py:501
  30.2 1.5 %own.4 = (f32[256,256]{1,0:T(8,128)S(1)}, f32[8,128]{1,0:T(8,128)S(1)}) custom-call(s32[24]{0:T(128)S(1)} %copy-done.2, bf16[24,256,256]{2,1,0:T(8,128)(2,1)S(1)} %bitcast.10, bf16[24,256,256]{2,1,0:T(8,128)(2,1)S(1)} %bitcast.17, bf16[256,256]{1,0:T(8,128)(2,1)S(1)} %get-tuple-element.36.refs_3_.refs_4_), custom_call_target="tpu_custom_call" | custom-call | flops 322122560 | bytes 262144 | tf_op jit(solution)/shard_map/own/pallas_call | solution.py:427
  31.7 1.0 %collective-permute-done.5.refs_6_ = bf16[128,256]{1,0:T(8,128)(2,1)S(1)} collective-permute-done((bf16[128,256]{1,0:T(8,128)(2,1)S(1)}, bf16[128,256]{1,0:T(8,128)(2,1)S(1)}, u32[]{:S(2)}, u32[]{:S(2)}) %collective-permute-start.5) | collective-permute-done | bytes 65568 | tf_op jit(solution)/shard_map/ppermute | solution.py:501
  32.7 1.4 %rest.6 = (bf16[256,256]{1,0:T(8,128)(2,1)S(1)}, f32[8,128]{1,0:T(8,128)S(1)}, f32[8,128]{1,0:T(8,128)S(1)}) custom-call(s32[24]{0:T(128)S(1)} %copy-done.2, bf16[24,256,256]{2,1,0:T(8,128)(2,1)S(1)} %bitcast.11, bf16[24,256,256]{2,1,0:T(8,128)(2,1)S(1)} %bitcast.18, f32[256,256]{1,0:T(8,128)S(1)} %get-tuple-element.37.refs_3_, ...), custom_call_target="tpu_custom_call" | custom-call | flops 644245120 | bytes 262144 | tf_op jit(solution)/shard_map/rest/pallas_call | solution.py:427
  34.1 2.0 %collective-permute-start.8 = (bf16[256,256]{1,0:T(8,128)(2,1)S(1)}, bf16[256,256]{1,0:T(8,128)(2,1)S(1)}, u32[]{:S(2)}, u32[]{:S(2)}) collective-permute-start(bf16[256,256]{1,0:T(8,128)(2,1)S(1)} %get-tuple-element.43.refs_0_), channel_id=1, source_target_pairs={{0,2},{2,0},{1,3},{3,1},{4,6},{6,4},{5,7},{7,5},{8,10},{10,8},{9,1... | collective-permute-start | bytes 393224 | tf_op jit(solution)/shard_map/ppermute | solution.py:508
  36.2 3.6 %collective-permute-done.9 = f32[8,128]{1,0:T(8,128)S(1)} collective-permute-done((f32[8,128]{1,0:T(8,128)S(1)}, f32[8,128]{1,0:T(8,128)S(1)}, u32[]{:S(2)}, u32[]{:S(2)}) %collective-permute-start.9) | collective-permute-done | bytes 4128 | tf_op jit(solution)/shard_map/ppermute | solution.py:482
  41.4 4.7 %collective-permute-done.10.refs_4_ = bf16[128,256]{1,0:T(8,128)(2,1)S(1)} collective-permute-done((bf16[128,256]{1,0:T(8,128)(2,1)S(1)}, bf16[128,256]{1,0:T(8,128)(2,1)S(1)}, u32[]{:S(2)}, u32[]{:S(2)}) %collective-permute-start.10) | collective-permute-done | bytes 65568 | tf_op jit(solution)/shard_map/ppermute | solution.py:467
  46.1 1.2 %collective-permute-start.11 = (bf16[128,256]{1,0:T(8,128)(2,1)S(1)}, bf16[128,256]{1,0:T(8,128)(2,1)S(1)}, u32[]{:S(2)}, u32[]{:S(2)}) collective-permute-start(bf16[128,256]{1,0:T(8,128)(2,1)S(1)} %collective-permute-done.10.refs_4_), channel_id=1, source_target_pairs={{0,2},{2,0},{1,3},{3,1},{4,6},{6,4},{5,7},{7,5},{8,10},{10,8},{9,1... | collective-permute-start | bytes 196616 | tf_op jit(solution)/shard_map/ppermute | solution.py:501
  47.3 1.5 %own.5.refs_3_ = f32[256,256]{1,0:T(8,128)S(1)} custom-call(s32[24]{0:T(128)S(1)} %copy-done.2, bf16[24,256,256]{2,1,0:T(8,128)(2,1)S(1)} %bitcast.12, bf16[24,256,256]{2,1,0:T(8,128)(2,1)S(1)} %bitcast.19, bf16[256,256]{1,0:T(8,128)(2,1)S(1)} %get-tuple-element.46.refs_3_), custom_call_target="tpu_custom_call" | custom-call | flops 322122560 | bytes 262144 | tf_op jit(solution)/shard_map/own/pallas_call | solution.py:427
  48.9 1.5 %collective-permute-done.11.refs_5_ = bf16[128,256]{1,0:T(8,128)(2,1)S(1)} collective-permute-done((bf16[128,256]{1,0:T(8,128)(2,1)S(1)}, bf16[128,256]{1,0:T(8,128)(2,1)S(1)}, u32[]{:S(2)}, u32[]{:S(2)}) %collective-permute-start.11) | collective-permute-done | bytes 65568 | tf_op jit(solution)/shard_map/ppermute | solution.py:501
  50.4 1.3 %rest.7.refs_0_ = bf16[256,256]{1,0:T(8,128)(2,1)S(1)} custom-call(s32[24]{0:T(128)S(1)} %copy-done.2, bf16[24,256,256]{2,1,0:T(8,128)(2,1)S(1)} %bitcast.13, bf16[24,256,256]{2,1,0:T(8,128)(2,1)S(1)} %bitcast.20, f32[256,256]{1,0:T(8,128)S(1)} %own.5.refs_3_, bf16[128,256]{1,0:T(8,128)(2,1)S(1)} %collective-permute-done.10.refs_4_, ...), custom_call_target="tpu_custom_call" | custom-call | flops 644245120 | bytes 262144 | tf_op jit(solution)/shard_map/rest/pallas_call | solution.py:427
  51.7 1.6 %collective-permute-start.13 = (bf16[256,256]{1,0:T(8,128)(2,1)S(1)}, bf16[256,256]{1,0:T(8,128)(2,1)S(1)}, u32[]{:S(2)}, u32[]{:S(2)}) collective-permute-start(bf16[256,256]{1,0:T(8,128)(2,1)S(1)} %rest.7.refs_0_), channel_id=1, source_target_pairs={{0,2},{2,0},{1,3},{3,1},{4,6},{6,4},{5,7},{7,5},{8,10},{10,8},{9,1... | collective-permute-start | bytes 393224 | tf_op jit(solution)/shard_map/ppermute | solution.py:508
  53.3 3.6 %collective-permute-done.13.refs_1_ = bf16[256,256]{1,0:T(8,128)(2,1)S(1)} collective-permute-done((bf16[256,256]{1,0:T(8,128)(2,1)S(1)}, bf16[256,256]{1,0:T(8,128)(2,1)S(1)}, u32[]{:S(2)}, u32[]{:S(2)}) %collective-permute-start.13) | collective-permute-done | bytes 131104 | tf_op jit(solution)/shard_map/ppermute | solution.py:508
  57.5 9.6 %all_to_all.11 = f32[8,1,128]{2,1,0:T(1,128)S(1)} all-to-all(f32[8,1,128]{2,1,0:T(1,128)S(1)} %bitcast.22), channel_id=1, replica_groups=mesh['groups'=2,'blk'=4,'mpo'=2,'rep'=2] {'blk','rep'}, dimensions={0} | all-to-all | bytes 8192 | tf_op jit(solution)/shard_map/all_to_all | solution.py:513
  67.1 1.4 %final.1 = (bf16[3,1,128,256]{3,2,1,0:T(8,128)(2,1)}, f32[2,3]{1,0:T(2,128)}) custom-call(f32[8,128]{1,0:T(8,128)S(1)} %bitcast.21, f32[256,256]{1,0:T(8,128)S(1)} %get-tuple-element.52.r_ref, f32[256,256]{1,0:T(8,128)S(1)} %get-tuple-element.53.z_ref, f32[256,256]{1,0:T(8,128)S(1)} %get-tuple-element.49.refs_5_.w_ref, ...), custom_call_target="tpu_custom_call" | custom-call | bytes 262144 | tf_op jit(solution)/shard_map/final/pallas_call | solution.py:427
  (29 shorter events, 5.7 us)
Async XLA Ops:
  0.6 0.9 %copy-start.3 = (bf16[1,256,256]{2,1,0:T(8,128)(2,1)S(1)}, bf16[1,256,256]{2,1,0:T(8,128)(2,1)}, u32[]{:S(2)}) copy-start(bf16[1,256,256]{2,1,0:T(8,128)(2,1)} %param.4) | copy-start | bytes 393220
  1.5 9.5 %copy-start = (bf16[24,1,256,256]{3,2,1,0:T(8,128)(2,1)S(1)}, bf16[24,1,256,256]{3,2,1,0:T(8,128)(2,1)}, u32[]{:S(2)}) copy-start(bf16[24,1,256,256]{3,2,1,0:T(8,128)(2,1)} %param.5) | copy-start | bytes 9437188
  1.5 9.5 %copy-start.1 = (bf16[24,1,256,256]{3,2,1,0:T(8,128)(2,1)S(1)}, bf16[24,1,256,256]{3,2,1,0:T(8,128)(2,1)}, u32[]{:S(2)}) copy-start(bf16[24,1,256,256]{3,2,1,0:T(8,128)(2,1)} %param.6) | copy-start | bytes 9437188
  1.5 9.5 %copy-start.2 = (s32[24]{0:T(128)S(1)}, s32[24]{0:T(128)}, u32[]{:S(2)}) copy-start(s32[24]{0:T(128)} %refs_0_.13) | copy-start | bytes 292
  1.6 6.0 %collective-permute-start.1 = (bf16[128,256]{1,0:T(8,128)(2,1)S(1)}, bf16[128,256]{1,0:T(8,128)(2,1)S(1)}, u32[]{:S(2)}, u32[]{:S(2)}) collective-permute-start(bf16[128,256]{1,0:T(8,128)(2,1)S(1)} %get-tuple-element.33), channel_id=1, source_target_pairs={{9,0},{8,1},{13,4},{12,5},{1,8},{0,9},{5,12},{4,13},{11,2},{10,3},... | collective-permute-start | bytes 196616 | tf_op jit(solution)/shard_map/ppermute | solution.py:467
  5.1 7.5 %collective-permute-start = (bf16[256,256]{1,0:T(8,128)(2,1)S(1)}, bf16[256,256]{1,0:T(8,128)(2,1)S(1)}, u32[]{:S(2)}, u32[]{:S(2)}) collective-permute-start(bf16[256,256]{1,0:T(8,128)(2,1)S(1)} %get-tuple-element.28.refs_3_.rows_ref.refs_2_), channel_id=1, source_target_pairs={{12,1},{9,4},{4,9},{1,12},{14,3},{11,6},{6,11},{3,14},{28,17},{25,... | collective-permute-start | bytes 393224 | tf_op jit(solution)/shard_map/ppermute | solution.py:467
  7.6 5.8 %collective-permute-start.2 = (bf16[128,256]{1,0:T(8,128)(2,1)S(1)}, bf16[128,256]{1,0:T(8,128)(2,1)S(1)}, u32[]{:S(2)}, u32[]{:S(2)}) collective-permute-start(bf16[128,256]{1,0:T(8,128)(2,1)S(1)} %hold.1.refs_5_), channel_id=1, source_target_pairs={{0,2},{2,0},{1,3},{3,1},{4,6},{6,4},{5,7},{7,5},{8,10},{10,8},{9,1... | collective-permute-start | bytes 196616 | tf_op jit(solution)/shard_map/ppermute | solution.py:501
  14.7 5.9 %collective-permute-start.3 = (bf16[256,256]{1,0:T(8,128)(2,1)S(1)}, bf16[256,256]{1,0:T(8,128)(2,1)S(1)}, u32[]{:S(2)}, u32[]{:S(2)}) collective-permute-start(bf16[256,256]{1,0:T(8,128)(2,1)S(1)} %get-tuple-element.34.refs_0_), channel_id=1, source_target_pairs={{0,2},{2,0},{1,3},{3,1},{4,6},{6,4},{5,7},{7,5},{8,10},{10,8},{9,1... | collective-permute-start | bytes 393224 | tf_op jit(solution)/shard_map/ppermute | solution.py:508
  21.1 7.3 %collective-permute-start.4 = (bf16[160,256]{1,0:T(8,128)(2,1)S(1)}, bf16[160,256]{1,0:T(8,128)(2,1)S(1)}, u32[]{:S(2)}, u32[]{:S(2)}) collective-permute-start(bf16[160,256]{1,0:T(8,128)(2,1)S(1)} %get-tuple-element.39), channel_id=1, source_target_pairs={{9,0},{8,1},{13,4},{12,5},{1,8},{0,9},{5,12},{4,13},{11,2},{10,3},... | collective-permute-start | bytes 245768 | tf_op jit(solution)/shard_map/ppermute | solution.py:467
  23.2 8.5 %collective-permute-start.6 = (bf16[256,256]{1,0:T(8,128)(2,1)S(1)}, bf16[256,256]{1,0:T(8,128)(2,1)S(1)}, u32[]{:S(2)}, u32[]{:S(2)}) collective-permute-start(bf16[256,256]{1,0:T(8,128)(2,1)S(1)} %get-tuple-element.36.refs_3_.refs_4_), channel_id=1, source_target_pairs={{12,1},{9,4},{4,9},{1,12},{14,3},{11,6},{6,11},{3,14},{28,17},{25,... | collective-permute-start | bytes 393224 | tf_op jit(solution)/shard_map/ppermute | solution.py:467
  28.4 4.3 %collective-permute-start.5 = (bf16[128,256]{1,0:T(8,128)(2,1)S(1)}, bf16[128,256]{1,0:T(8,128)(2,1)S(1)}, u32[]{:S(2)}, u32[]{:S(2)}) collective-permute-start(bf16[128,256]{1,0:T(8,128)(2,1)S(1)} %get-tuple-element.41.refs_5_), channel_id=1, source_target_pairs={{0,2},{2,0},{1,3},{3,1},{4,6},{6,4},{5,7},{7,5},{8,10},{10,8},{9,1... | collective-permute-start | bytes 196616 | tf_op jit(solution)/shard_map/ppermute | solution.py:501
  30.1 1.5 %collective-permute-start.7 = (f32[8,128]{1,0:T(8,128)S(1)}, f32[8,128]{1,0:T(8,128)S(1)}, u32[]{:S(2)}, u32[]{:S(2)}) collective-permute-start(f32[8,128]{1,0:T(8,128)S(1)} %get-tuple-element.42), channel_id=1, source_target_pairs={{0,1},{1,0},{4,5},{5,4},{8,9},{9,8},{12,13},{13,12},{2,3},{3,2},{6... | collective-permute-start | bytes 12296 | tf_op jit(solution)/shard_map/ppermute | solution.py:482
  34.1 5.7 %collective-permute-start.8 = (bf16[256,256]{1,0:T(8,128)(2,1)S(1)}, bf16[256,256]{1,0:T(8,128)(2,1)S(1)}, u32[]{:S(2)}, u32[]{:S(2)}) collective-permute-start(bf16[256,256]{1,0:T(8,128)(2,1)S(1)} %get-tuple-element.43.refs_0_), channel_id=1, source_target_pairs={{0,2},{2,0},{1,3},{3,1},{4,6},{6,4},{5,7},{7,5},{8,10},{10,8},{9,1... | collective-permute-start | bytes 393224 | tf_op jit(solution)/shard_map/ppermute | solution.py:508
  36.2 3.6 %collective-permute-start.9 = (f32[8,128]{1,0:T(8,128)S(1)}, f32[8,128]{1,0:T(8,128)S(1)}, u32[]{:S(2)}, u32[]{:S(2)}) collective-permute-start(f32[8,128]{1,0:T(8,128)S(1)} %get-tuple-element.44), channel_id=1, source_target_pairs={{0,4},{1,5},{4,0},{5,1},{8,12},{9,13},{12,8},{13,9},{2,6},{3,7},{6... | collective-permute-start | bytes 12296 | tf_op jit(solution)/shard_map/ppermute | solution.py:482
  40.6 5.5 %collective-permute-start.10 = (bf16[128,256]{1,0:T(8,128)(2,1)S(1)}, bf16[128,256]{1,0:T(8,128)(2,1)S(1)}, u32[]{:S(2)}, u32[]{:S(2)}) collective-permute-start(bf16[128,256]{1,0:T(8,128)(2,1)S(1)} %get-tuple-element.47), channel_id=1, source_target_pairs={{9,0},{8,1},{13,4},{12,5},{1,8},{0,9},{5,12},{4,13},{11,2},{10,3},... | collective-permute-start | bytes 196616 | tf_op jit(solution)/shard_map/ppermute | solution.py:467
  40.7 9.7 %collective-permute-start.12 = (bf16[256,256]{1,0:T(8,128)(2,1)S(1)}, bf16[256,256]{1,0:T(8,128)(2,1)S(1)}, u32[]{:S(2)}, u32[]{:S(2)}) collective-permute-start(bf16[256,256]{1,0:T(8,128)(2,1)S(1)} %get-tuple-element.46.refs_3_), channel_id=1, source_target_pairs={{12,1},{9,4},{4,9},{1,12},{14,3},{11,6},{6,11},{3,14},{28,17},{25,... | collective-permute-start | bytes 393224 | tf_op jit(solution)/shard_map/ppermute | solution.py:467
  46.1 4.3 %collective-permute-start.11 = (bf16[128,256]{1,0:T(8,128)(2,1)S(1)}, bf16[128,256]{1,0:T(8,128)(2,1)S(1)}, u32[]{:S(2)}, u32[]{:S(2)}) collective-permute-start(bf16[128,256]{1,0:T(8,128)(2,1)S(1)} %collective-permute-done.10.refs_4_), channel_id=1, source_target_pairs={{0,2},{2,0},{1,3},{3,1},{4,6},{6,4},{5,7},{7,5},{8,10},{10,8},{9,1... | collective-permute-start | bytes 196616 | tf_op jit(solution)/shard_map/ppermute | solution.py:501
  51.7 5.1 %collective-permute-start.13 = (bf16[256,256]{1,0:T(8,128)(2,1)S(1)}, bf16[256,256]{1,0:T(8,128)(2,1)S(1)}, u32[]{:S(2)}, u32[]{:S(2)}) collective-permute-start(bf16[256,256]{1,0:T(8,128)(2,1)S(1)} %rest.7.refs_0_), channel_id=1, source_target_pairs={{0,2},{2,0},{1,3},{3,1},{4,6},{6,4},{5,7},{7,5},{8,10},{10,8},{9,1... | collective-permute-start | bytes 393224 | tf_op jit(solution)/shard_map/ppermute | solution.py:508

commit v17 on v16

--- a/solution.py
+++ b/solution.py
@@ -11,7 +11,7 @@
 STEPS = 3
 OFFSETS = (0, NS + 1, NS - 1, -(NS + 1), -(NS - 1))
 EPSILON = 1e-06
-WIDE = 8
+WIDE, WIDEST = 8, 12
 SMALLEST = 1e-30
 TILE = 16
 MIB = 1024 * 1024
@@ -163,13 +163,13 @@
         order[count] = jnp.int32(b)
         slot_of[count] = slot
         count += jnp.where(slot >= 0, 1, 0)
-    for extra in range(WIDE):
+    for extra in range(WIDEST):
         order[count + extra] = jnp.int32(0)
         slot_of[count + extra] = jnp.int32(idle)
     return count
 
 
-def multiply_listed(count, left_ref, right_ref, source, acc, order, slot_of):
+def multiply_listed(count, size, left_ref, right_ref, source, acc, order, slot_of):
     def multiply(start, wide):
         held = [order[start + inner] for inner in range(wide)]
         pieces = [
@@ -186,17 +186,18 @@
         )
 
     def full(group, carry):
-        multiply(group * WIDE, WIDE)
+        multiply(group * size, size)
         return carry
 
-    groups = (count + WIDE // 2 - 1) // WIDE
+    smaller = [wide for wide in (2, 4, WIDE) if wide < size]
+    groups = (count + size - 1 - smaller[-1]) // size
     lax.fori_loop(0, groups, full, 0)
-    rest = count - groups * WIDE
-    for low, wide in ((0, 2), (2, 4)):
+    rest = count - groups * size
+    for low, wide in zip([0] + smaller, smaller):
 
         @pl.when((rest > low) & (rest <= wide))
         def _():
-            multiply(groups * WIDE, wide)
+            multiply(groups * size, wide)
 
 
 def own_kernel(scaled, places, *refs):
@@ -212,7 +213,7 @@
         source[0] = block_ref[...]
     source[1] = jnp.zeros(source.shape[1:], jnp.bfloat16)
     acc[...] = jnp.zeros_like(acc)
-    multiply_listed(count, left_ref, right_ref, source, acc, order, slot_of)
+    multiply_listed(count, WIDE, left_ref, right_ref, source, acc, order, slot_of)
 
 
 def rest_kernel(which, scaled, passes, shares, slots, places, *refs):
@@ -252,7 +253,7 @@
         source[slot] = scale(block)
     source[slots] = jnp.zeros(source.shape[1:], jnp.bfloat16)
     acc[...] = own_ref[...] * (met * inverse) if scaled else own_ref[...]
-    multiply_listed(count, left_ref, right_ref, source, acc, order, slot_of)
+    multiply_listed(count, WIDEST if which == "rest" else WIDE, left_ref, right_ref, source, acc, order, slot_of)
     t_ref[...] = acc[...].astype(t_ref.dtype)
 
 
@@ -417,7 +418,7 @@
     wide = jax.ShapeDtypeStruct((width, width), jnp.float32)
     narrow = jax.ShapeDtypeStruct((width, width), jnp.bfloat16)
     share_shape = jax.ShapeDtypeStruct((width // parts, width), jnp.bfloat16)
-    lists = [pltpu.SMEM((channels + WIDE,), jnp.int32)] * 2
+    lists = [pltpu.SMEM((channels + WIDEST,), jnp.int32)] * 2
 
     def call(kernel, name, outs, args, scratch=(), share=0, limit=4, weight=0):
         flops = int(4 * channels * max(share, weight) * width**3)

time: 69.7 us -> 69.8 us (level)
  waiting for transfers between devices: 24.5 us -> 27.9 us
  starting transfers between devices: 20 us -> 16.9 us
  Pallas kernels: 12.6 us -> 13.7 us
  blocking collectives: 9.58 us -> 8.71 us
    ppermute x3, starting transfers between devices: 5.84 us -> 3.45 us  [gather_parts(): return [t, lax.ppermute(t, 'mpo', [(0, 1), (1, 0)])]]
    ppermute x3, waiting for transfers between devices: 7.28 us -> 9.39 us  [gather_parts(): return [t, lax.ppermute(t, 'mpo', [(0, 1), (1, 0)])]]
    ppermute x3, waiting for transfers between devices: 2.58 us -> 3.96 us  [spread(): first = [piece, lax.ppermute(piece, 'mpo', [(0, 1), (1, 0)])]]
    pallas_call x14, Pallas kernels: 12.6 us -> 13.7 us  [call(): pl.pallas_call(kernel, out_shape=outs, in_specs=[first] + [VMEM] * (len(a...]
    all_to_all x1, blocking collectives: 9.58 us -> 8.71 us  [exchange(): return lax.all_to_all(rows, ring, 0, 0, tiled=True)]
  transfers between devices with their start and end apart: 14 -> 14, of which waited for: 9 -> 10; matrix products, arithmetic and copies ran while one was open for 0% -> 0% of each run, Pallas kernels for 8% -> 8%
where the time goes in v17:
time: 69.8 us; the launch traced here: 68.9 us
  waiting for transfers between devices  27.9 us (40%)
  starting transfers between devices  16.9 us (24%)
  Pallas kernels  13.7 us (20%)
  blocking collectives  8.71 us (12%)
  local copies, waits for them, and re-layouts  0.91 us (1%)
  between operations  0.79 us (1%)
    pallas_call x14, Pallas kernels, call(): pl.pallas_call(kernel, out_shape=outs, in_specs=[first] + [VMEM] * (len(a...  13.7 us
    ppermute x6, waiting for transfers between devices, shift(): return lax.ppermute(block, ring, pairs)  10.9 us
    ppermute x3, waiting for transfers between devices, gather_parts(): return [t, lax.ppermute(t, 'mpo', [(0, 1), (1, 0)])]  9.39 us
    all_to_all x1, blocking collectives, exchange(): return lax.all_to_all(rows, ring, 0, 0, tiled=True)  8.71 us
    ppermute x6, starting transfers between devices, shift(): return lax.ppermute(block, ring, pairs)  7.63 us
    ppermute x3, starting transfers between devices, spread(): first = [piece, lax.ppermute(piece, 'mpo', [(0, 1), (1, 0)])]  5.84 us
    ppermute x3, waiting for transfers between devices, spread(): first = [piece, lax.ppermute(piece, 'mpo', [(0, 1), (1, 0)])]  3.96 us
    ppermute x2, waiting for transfers between devices, add_round(): return rows + lax.ppermute(rows, axis, pairs)  3.61 us
  transfers between devices with their start and end apart: 14, of which 10 were waited for; matrix products, arithmetic and copies ran while one was open for 0% of the time, Pallas kernels for 8%

profile of v17, /device:TPU:0, one launch (start us, length us, event | category | flops | bytes accessed | tf_op | source)
XLA Modules:
  0.0 68.9 jit_solution(993164504201310392)
XLA Ops:
  0.6 0.9 %copy-done.3 = bf16[1,256,256]{2,1,0:T(8,128)(2,1)S(1)} copy-done((bf16[1,256,256]{2,1,0:T(8,128)(2,1)S(1)}, bf16[1,256,256]{2,1,0:T(8,128)(2,1)}, u32[]{:S(2)}) %copy-start.3) | copy-done | bytes 131096
  1.6 3.5 %collective-permute-start.1 = (bf16[128,256]{1,0:T(8,128)(2,1)S(1)}, bf16[128,256]{1,0:T(8,128)(2,1)S(1)}, u32[]{:S(2)}, u32[]{:S(2)}) collective-permute-start(bf16[128,256]{1,0:T(8,128)(2,1)S(1)} %get-tuple-element.33), channel_id=1, source_target_pairs={{9,0},{8,1},{13,4},{12,5},{1,8},{0,9},{5,12},{4,13},{11,2},{10,3},... | collective-permute-start | bytes 196616 | tf_op jit(solution)/shard_map/ppermute | solution.py:468
  5.8 1.8 %collective-permute-done.1.block_ref = bf16[128,256]{1,0:T(8,128)(2,1)S(1)} collective-permute-done((bf16[128,256]{1,0:T(8,128)(2,1)S(1)}, bf16[128,256]{1,0:T(8,128)(2,1)S(1)}, u32[]{:S(2)}, u32[]{:S(2)}) %collective-permute-start.1) | collective-permute-done | bytes 65568 | tf_op jit(solution)/shard_map/ppermute | solution.py:468
  7.6 3.4 %collective-permute-start.2 = (bf16[128,256]{1,0:T(8,128)(2,1)S(1)}, bf16[128,256]{1,0:T(8,128)(2,1)S(1)}, u32[]{:S(2)}, u32[]{:S(2)}) collective-permute-start(bf16[128,256]{1,0:T(8,128)(2,1)S(1)} %hold.1.refs_5_), channel_id=1, source_target_pairs={{0,2},{2,0},{1,3},{3,1},{4,6},{6,4},{5,7},{7,5},{8,10},{10,8},{9,1... | collective-permute-start | bytes 196616 | tf_op jit(solution)/shard_map/ppermute | solution.py:502
  11.0 1.5 %own.3 = (f32[256,256]{1,0:T(8,128)S(1)}, f32[8,128]{1,0:T(8,128)S(1)}) custom-call(s32[24]{0:T(128)S(1)} %copy-done.2, bf16[24,256,256]{2,1,0:T(8,128)(2,1)S(1)} %bitcast.7, bf16[24,256,256]{2,1,0:T(8,128)(2,1)S(1)} %bitcast.14, bf16[256,256]{1,0:T(8,128)(2,1)S(1)} %get-tuple-element.28.refs_3_.rows_ref.refs_2_), custom_call_target="tpu_custom_call" | custom-call | flops 322122560 | bytes 262144 | tf_op jit(solution)/shard_map/own/pallas_call | solution.py:428
  13.4 1.6 %rest.5 = (bf16[256,256]{1,0:T(8,128)(2,1)S(1)}, f32[8,128]{1,0:T(8,128)S(1)}) custom-call(s32[24]{0:T(128)S(1)} %copy-done.2, bf16[24,256,256]{2,1,0:T(8,128)(2,1)S(1)} %bitcast.9, bf16[24,256,256]{2,1,0:T(8,128)(2,1)S(1)} %bitcast.16, f32[256,256]{1,0:T(8,128)S(1)} %get-tuple-element.31.refs_3_, f32[8,128]{1,0:T(8,128)S(1)} %get-tuple-element.32.refs_4_, ...), custom_call_target="tpu_custom_call" | custom-call | flops 322122560 | bytes 262144 | tf_op jit(solution)/shard_map/rest/pallas_call | solution.py:428
  15.0 2.0 %collective-permute-start.3 = (bf16[256,256]{1,0:T(8,128)(2,1)S(1)}, bf16[256,256]{1,0:T(8,128)(2,1)S(1)}, u32[]{:S(2)}, u32[]{:S(2)}) collective-permute-start(bf16[256,256]{1,0:T(8,128)(2,1)S(1)} %get-tuple-element.34.refs_0_), channel_id=1, source_target_pairs={{0,2},{2,0},{1,3},{3,1},{4,6},{6,4},{5,7},{7,5},{8,10},{10,8},{9,1... | collective-permute-start | bytes 393224 | tf_op jit(solution)/shard_map/ppermute | solution.py:509
  17.0 3.6 %collective-permute-done.3.refs_1_ = bf16[256,256]{1,0:T(8,128)(2,1)S(1)} collective-permute-done((bf16[256,256]{1,0:T(8,128)(2,1)S(1)}, bf16[256,256]{1,0:T(8,128)(2,1)S(1)}, u32[]{:S(2)}, u32[]{:S(2)}) %collective-permute-start.3) | collective-permute-done | bytes 131104 | tf_op jit(solution)/shard_map/ppermute | solution.py:509
  20.9 2.0 %collective-permute-start.4 = (bf16[160,256]{1,0:T(8,128)(2,1)S(1)}, bf16[160,256]{1,0:T(8,128)(2,1)S(1)}, u32[]{:S(2)}, u32[]{:S(2)}) collective-permute-start(bf16[160,256]{1,0:T(8,128)(2,1)S(1)} %get-tuple-element.39), channel_id=1, source_target_pairs={{9,0},{8,1},{13,4},{12,5},{1,8},{0,9},{5,12},{4,13},{11,2},{10,3},... | collective-permute-start | bytes 245768 | tf_op jit(solution)/shard_map/ppermute | solution.py:468
  23.6 4.0 %collective-permute-done.4.block_ref = bf16[160,256]{1,0:T(8,128)(2,1)S(1)} collective-permute-done((bf16[160,256]{1,0:T(8,128)(2,1)S(1)}, bf16[160,256]{1,0:T(8,128)(2,1)S(1)}, u32[]{:S(2)}, u32[]{:S(2)}) %collective-permute-start.4) | collective-permute-done | bytes 81952 | tf_op jit(solution)/shard_map/ppermute | solution.py:468
  27.6 2.4 %collective-permute-start.5 = (bf16[128,256]{1,0:T(8,128)(2,1)S(1)}, bf16[128,256]{1,0:T(8,128)(2,1)S(1)}, u32[]{:S(2)}, u32[]{:S(2)}) collective-permute-start(bf16[128,256]{1,0:T(8,128)(2,1)S(1)} %get-tuple-element.41.refs_5_), channel_id=1, source_target_pairs={{0,2},{2,0},{1,3},{3,1},{4,6},{6,4},{5,7},{7,5},{8,10},{10,8},{9,1... | collective-permute-start | bytes 196616 | tf_op jit(solution)/shard_map/ppermute | solution.py:502
  30.0 1.5 %own.4 = (f32[256,256]{1,0:T(8,128)S(1)}, f32[8,128]{1,0:T(8,128)S(1)}) custom-call(s32[24]{0:T(128)S(1)} %copy-done.2, bf16[24,256,256]{2,1,0:T(8,128)(2,1)S(1)} %bitcast.10, bf16[24,256,256]{2,1,0:T(8,128)(2,1)S(1)} %bitcast.17, bf16[256,256]{1,0:T(8,128)(2,1)S(1)} %get-tuple-element.36.refs_3_.refs_4_), custom_call_target="tpu_custom_call" | custom-call | flops 322122560 | bytes 262144 | tf_op jit(solution)/shard_map/own/pallas_call | solution.py:428
  31.6 1.4 %collective-permute-done.5.refs_6_ = bf16[128,256]{1,0:T(8,128)(2,1)S(1)} collective-permute-done((bf16[128,256]{1,0:T(8,128)(2,1)S(1)}, bf16[128,256]{1,0:T(8,128)(2,1)S(1)}, u32[]{:S(2)}, u32[]{:S(2)}) %collective-permute-start.5) | collective-permute-done | bytes 65568 | tf_op jit(solution)/shard_map/ppermute | solution.py:502
  32.9 1.7 %rest.6 = (bf16[256,256]{1,0:T(8,128)(2,1)S(1)}, f32[8,128]{1,0:T(8,128)S(1)}, f32[8,128]{1,0:T(8,128)S(1)}) custom-call(s32[24]{0:T(128)S(1)} %copy-done.2, bf16[24,256,256]{2,1,0:T(8,128)(2,1)S(1)} %bitcast.11, bf16[24,256,256]{2,1,0:T(8,128)(2,1)S(1)} %bitcast.18, f32[256,256]{1,0:T(8,128)S(1)} %get-tuple-element.37.refs_3_, ...), custom_call_target="tpu_custom_call" | custom-call | flops 644245120 | bytes 262144 | tf_op jit(solution)/shard_map/rest/pallas_call | solution.py:428
  34.6 1.4 %collective-permute-start.8 = (bf16[256,256]{1,0:T(8,128)(2,1)S(1)}, bf16[256,256]{1,0:T(8,128)(2,1)S(1)}, u32[]{:S(2)}, u32[]{:S(2)}) collective-permute-start(bf16[256,256]{1,0:T(8,128)(2,1)S(1)} %get-tuple-element.43.refs_0_), channel_id=1, source_target_pairs={{0,2},{2,0},{1,3},{3,1},{4,6},{6,4},{5,7},{7,5},{8,10},{10,8},{9,1... | collective-permute-start | bytes 393224 | tf_op jit(solution)/shard_map/ppermute | solution.py:509
  36.0 3.6 %collective-permute-done.9 = f32[8,128]{1,0:T(8,128)S(1)} collective-permute-done((f32[8,128]{1,0:T(8,128)S(1)}, f32[8,128]{1,0:T(8,128)S(1)}, u32[]{:S(2)}, u32[]{:S(2)}) %collective-permute-start.9) | collective-permute-done | bytes 4128 | tf_op jit(solution)/shard_map/ppermute | solution.py:483
  39.6 0.9 %collective-permute-done.8.refs_1_ = bf16[256,256]{1,0:T(8,128)(2,1)S(1)} collective-permute-done((bf16[256,256]{1,0:T(8,128)(2,1)S(1)}, bf16[256,256]{1,0:T(8,128)(2,1)S(1)}, u32[]{:S(2)}, u32[]{:S(2)}) %collective-permute-start.8) | collective-permute-done | bytes 131104 | tf_op jit(solution)/shard_map/ppermute | solution.py:509
  42.1 5.1 %collective-permute-done.10.refs_4_ = bf16[128,256]{1,0:T(8,128)(2,1)S(1)} collective-permute-done((bf16[128,256]{1,0:T(8,128)(2,1)S(1)}, bf16[128,256]{1,0:T(8,128)(2,1)S(1)}, u32[]{:S(2)}, u32[]{:S(2)}) %collective-permute-start.10) | collective-permute-done | bytes 65568 | tf_op jit(solution)/shard_map/ppermute | solution.py:468
  47.3 1.7 %own.5.refs_3_ = f32[256,256]{1,0:T(8,128)S(1)} custom-call(s32[24]{0:T(128)S(1)} %copy-done.2, bf16[24,256,256]{2,1,0:T(8,128)(2,1)S(1)} %bitcast.12, bf16[24,256,256]{2,1,0:T(8,128)(2,1)S(1)} %bitcast.19, bf16[256,256]{1,0:T(8,128)(2,1)S(1)} %get-tuple-element.46.refs_3_), custom_call_target="tpu_custom_call" | custom-call | flops 322122560 | bytes 262144 | tf_op jit(solution)/shard_map/own/pallas_call | solution.py:428
  49.0 2.5 %collective-permute-done.11.refs_5_ = bf16[128,256]{1,0:T(8,128)(2,1)S(1)} collective-permute-done((bf16[128,256]{1,0:T(8,128)(2,1)S(1)}, bf16[128,256]{1,0:T(8,128)(2,1)S(1)}, u32[]{:S(2)}, u32[]{:S(2)}) %collective-permute-start.11) | collective-permute-done | bytes 65568 | tf_op jit(solution)/shard_map/ppermute | solution.py:502
  51.5 1.6 %rest.7.refs_0_ = bf16[256,256]{1,0:T(8,128)(2,1)S(1)} custom-call(s32[24]{0:T(128)S(1)} %copy-done.2, bf16[24,256,256]{2,1,0:T(8,128)(2,1)S(1)} %bitcast.13, bf16[24,256,256]{2,1,0:T(8,128)(2,1)S(1)} %bitcast.20, f32[256,256]{1,0:T(8,128)S(1)} %own.5.refs_3_, bf16[128,256]{1,0:T(8,128)(2,1)S(1)} %collective-permute-done.10.refs_4_, ...), custom_call_target="tpu_custom_call" | custom-call | flops 644245120 | bytes 262144 | tf_op jit(solution)/shard_map/rest/pallas_call | solution.py:428
  53.2 4.9 %collective-permute-done.13.refs_1_ = bf16[256,256]{1,0:T(8,128)(2,1)S(1)} collective-permute-done((bf16[256,256]{1,0:T(8,128)(2,1)S(1)}, bf16[256,256]{1,0:T(8,128)(2,1)S(1)}, u32[]{:S(2)}, u32[]{:S(2)}) %collective-permute-start.13) | collective-permute-done | bytes 131104 | tf_op jit(solution)/shard_map/ppermute | solution.py:509
  58.8 8.7 %all_to_all.11 = f32[8,1,128]{2,1,0:T(1,128)S(1)} all-to-all(f32[8,1,128]{2,1,0:T(1,128)S(1)} %bitcast.22), channel_id=1, replica_groups=mesh['groups'=2,'blk'=4,'mpo'=2,'rep'=2] {'blk','rep'}, dimensions={0} | all-to-all | bytes 8192 | tf_op jit(solution)/shard_map/all_to_all | solution.py:514
  67.5 1.4 %final.1 = (bf16[3,1,128,256]{3,2,1,0:T(8,128)(2,1)}, f32[2,3]{1,0:T(2,128)}) custom-call(f32[8,128]{1,0:T(8,128)S(1)} %bitcast.21, f32[256,256]{1,0:T(8,128)S(1)} %get-tuple-element.52.r_ref, f32[256,256]{1,0:T(8,128)S(1)} %get-tuple-element.53.z_ref, f32[256,256]{1,0:T(8,128)S(1)} %get-tuple-element.49.refs_5_.w_ref, ...), custom_call_target="tpu_custom_call" | custom-call | bytes 262144 | tf_op jit(solution)/shard_map/final/pallas_call | solution.py:428
  (29 shorter events, 4.9 us)
Async XLA Ops:
  0.6 0.9 %copy-start.3 = (bf16[1,256,256]{2,1,0:T(8,128)(2,1)S(1)}, bf16[1,256,256]{2,1,0:T(8,128)(2,1)}, u32[]{:S(2)}) copy-start(bf16[1,256,256]{2,1,0:T(8,128)(2,1)} %param.4) | copy-start | bytes 393220
  1.5 9.5 %copy-start = (bf16[24,1,256,256]{3,2,1,0:T(8,128)(2,1)S(1)}, bf16[24,1,256,256]{3,2,1,0:T(8,128)(2,1)}, u32[]{:S(2)}) copy-start(bf16[24,1,256,256]{3,2,1,0:T(8,128)(2,1)} %param.5) | copy-start | bytes 9437188
  1.5 9.5 %copy-start.1 = (bf16[24,1,256,256]{3,2,1,0:T(8,128)(2,1)S(1)}, bf16[24,1,256,256]{3,2,1,0:T(8,128)(2,1)}, u32[]{:S(2)}) copy-start(bf16[24,1,256,256]{3,2,1,0:T(8,128)(2,1)} %param.6) | copy-start | bytes 9437188
  1.5 9.5 %copy-start.2 = (s32[24]{0:T(128)S(1)}, s32[24]{0:T(128)}, u32[]{:S(2)}) copy-start(s32[24]{0:T(128)} %refs_0_.13) | copy-start | bytes 292
  1.6 6.0 %collective-permute-start.1 = (bf16[128,256]{1,0:T(8,128)(2,1)S(1)}, bf16[128,256]{1,0:T(8,128)(2,1)S(1)}, u32[]{:S(2)}, u32[]{:S(2)}) collective-permute-start(bf16[128,256]{1,0:T(8,128)(2,1)S(1)} %get-tuple-element.33), channel_id=1, source_target_pairs={{9,0},{8,1},{13,4},{12,5},{1,8},{0,9},{5,12},{4,13},{11,2},{10,3},... | collective-permute-start | bytes 196616 | tf_op jit(solution)/shard_map/ppermute | solution.py:468
  5.1 7.5 %collective-permute-start = (bf16[256,256]{1,0:T(8,128)(2,1)S(1)}, bf16[256,256]{1,0:T(8,128)(2,1)S(1)}, u32[]{:S(2)}, u32[]{:S(2)}) collective-permute-start(bf16[256,256]{1,0:T(8,128)(2,1)S(1)} %get-tuple-element.28.refs_3_.rows_ref.refs_2_), channel_id=1, source_target_pairs={{12,1},{9,4},{4,9},{1,12},{14,3},{11,6},{6,11},{3,14},{28,17},{25,... | collective-permute-start | bytes 393224 | tf_op jit(solution)/shard_map/ppermute | solution.py:468
  7.6 5.8 %collective-permute-start.2 = (bf16[128,256]{1,0:T(8,128)(2,1)S(1)}, bf16[128,256]{1,0:T(8,128)(2,1)S(1)}, u32[]{:S(2)}, u32[]{:S(2)}) collective-permute-start(bf16[128,256]{1,0:T(8,128)(2,1)S(1)} %hold.1.refs_5_), channel_id=1, source_target_pairs={{0,2},{2,0},{1,3},{3,1},{4,6},{6,4},{5,7},{7,5},{8,10},{10,8},{9,1... | collective-permute-start | bytes 196616 | tf_op jit(solution)/shard_map/ppermute | solution.py:502
  15.0 5.5 %collective-permute-start.3 = (bf16[256,256]{1,0:T(8,128)(2,1)S(1)}, bf16[256,256]{1,0:T(8,128)(2,1)S(1)}, u32[]{:S(2)}, u32[]{:S(2)}) collective-permute-start(bf16[256,256]{1,0:T(8,128)(2,1)S(1)} %get-tuple-element.34.refs_0_), channel_id=1, source_target_pairs={{0,2},{2,0},{1,3},{3,1},{4,6},{6,4},{5,7},{7,5},{8,10},{10,8},{9,1... | collective-permute-start | bytes 393224 | tf_op jit(solution)/shard_map/ppermute | solution.py:509
  20.9 6.7 %collective-permute-start.4 = (bf16[160,256]{1,0:T(8,128)(2,1)S(1)}, bf16[160,256]{1,0:T(8,128)(2,1)S(1)}, u32[]{:S(2)}, u32[]{:S(2)}) collective-permute-start(bf16[160,256]{1,0:T(8,128)(2,1)S(1)} %get-tuple-element.39), channel_id=1, source_target_pairs={{9,0},{8,1},{13,4},{12,5},{1,8},{0,9},{5,12},{4,13},{11,2},{10,3},... | collective-permute-start | bytes 245768 | tf_op jit(solution)/shard_map/ppermute | solution.py:468
  22.9 8.6 %collective-permute-start.6 = (bf16[256,256]{1,0:T(8,128)(2,1)S(1)}, bf16[256,256]{1,0:T(8,128)(2,1)S(1)}, u32[]{:S(2)}, u32[]{:S(2)}) collective-permute-start(bf16[256,256]{1,0:T(8,128)(2,1)S(1)} %get-tuple-element.36.refs_3_.refs_4_), channel_id=1, source_target_pairs={{12,1},{9,4},{4,9},{1,12},{14,3},{11,6},{6,11},{3,14},{28,17},{25,... | collective-permute-start | bytes 393224 | tf_op jit(solution)/shard_map/ppermute | solution.py:468
  27.6 5.3 %collective-permute-start.5 = (bf16[128,256]{1,0:T(8,128)(2,1)S(1)}, bf16[128,256]{1,0:T(8,128)(2,1)S(1)}, u32[]{:S(2)}, u32[]{:S(2)}) collective-permute-start(bf16[128,256]{1,0:T(8,128)(2,1)S(1)} %get-tuple-element.41.refs_5_), channel_id=1, source_target_pairs={{0,2},{2,0},{1,3},{3,1},{4,6},{6,4},{5,7},{7,5},{8,10},{10,8},{9,1... | collective-permute-start | bytes 196616 | tf_op jit(solution)/shard_map/ppermute | solution.py:502
  30.0 1.5 %collective-permute-start.7 = (f32[8,128]{1,0:T(8,128)S(1)}, f32[8,128]{1,0:T(8,128)S(1)}, u32[]{:S(2)}, u32[]{:S(2)}) collective-permute-start(f32[8,128]{1,0:T(8,128)S(1)} %get-tuple-element.42), channel_id=1, source_target_pairs={{0,1},{1,0},{4,5},{5,4},{8,9},{9,8},{12,13},{13,12},{2,3},{3,2},{6... | collective-permute-start | bytes 12296 | tf_op jit(solution)/shard_map/ppermute | solution.py:483
  34.6 5.9 %collective-permute-start.8 = (bf16[256,256]{1,0:T(8,128)(2,1)S(1)}, bf16[256,256]{1,0:T(8,128)(2,1)S(1)}, u32[]{:S(2)}, u32[]{:S(2)}) collective-permute-start(bf16[256,256]{1,0:T(8,128)(2,1)S(1)} %get-tuple-element.43.refs_0_), channel_id=1, source_target_pairs={{0,2},{2,0},{1,3},{3,1},{4,6},{6,4},{5,7},{7,5},{8,10},{10,8},{9,1... | collective-permute-start | bytes 393224 | tf_op jit(solution)/shard_map/ppermute | solution.py:509
  36.0 3.6 %collective-permute-start.9 = (f32[8,128]{1,0:T(8,128)S(1)}, f32[8,128]{1,0:T(8,128)S(1)}, u32[]{:S(2)}, u32[]{:S(2)}) collective-permute-start(f32[8,128]{1,0:T(8,128)S(1)} %get-tuple-element.44), channel_id=1, source_target_pairs={{0,4},{1,5},{4,0},{5,1},{8,12},{9,13},{12,8},{13,9},{2,6},{3,7},{6... | collective-permute-start | bytes 12296 | tf_op jit(solution)/shard_map/ppermute | solution.py:483
  41.4 5.9 %collective-permute-start.10 = (bf16[128,256]{1,0:T(8,128)(2,1)S(1)}, bf16[128,256]{1,0:T(8,128)(2,1)S(1)}, u32[]{:S(2)}, u32[]{:S(2)}) collective-permute-start(bf16[128,256]{1,0:T(8,128)(2,1)S(1)} %get-tuple-element.47), channel_id=1, source_target_pairs={{9,0},{8,1},{13,4},{12,5},{1,8},{0,9},{5,12},{4,13},{11,2},{10,3},... | collective-permute-start | bytes 196616 | tf_op jit(solution)/shard_map/ppermute | solution.py:468
  41.5 10.1 %collective-permute-start.12 = (bf16[256,256]{1,0:T(8,128)(2,1)S(1)}, bf16[256,256]{1,0:T(8,128)(2,1)S(1)}, u32[]{:S(2)}, u32[]{:S(2)}) collective-permute-start(bf16[256,256]{1,0:T(8,128)(2,1)S(1)} %get-tuple-element.46.refs_3_), channel_id=1, source_target_pairs={{12,1},{9,4},{4,9},{1,12},{14,3},{11,6},{6,11},{3,14},{28,17},{25,... | collective-permute-start | bytes 393224 | tf_op jit(solution)/shard_map/ppermute | solution.py:468
  47.3 4.3 %collective-permute-start.11 = (bf16[128,256]{1,0:T(8,128)(2,1)S(1)}, bf16[128,256]{1,0:T(8,128)(2,1)S(1)}, u32[]{:S(2)}, u32[]{:S(2)}) collective-permute-start(bf16[128,256]{1,0:T(8,128)(2,1)S(1)} %collective-permute-done.10.refs_4_), channel_id=1, source_target_pairs={{0,2},{2,0},{1,3},{3,1},{4,6},{6,4},{5,7},{7,5},{8,10},{10,8},{9,1... | collective-permute-start | bytes 196616 | tf_op jit(solution)/shard_map/ppermute | solution.py:502
  53.1 5.0 %collective-permute-start.13 = (bf16[256,256]{1,0:T(8,128)(2,1)S(1)}, bf16[256,256]{1,0:T(8,128)(2,1)S(1)}, u32[]{:S(2)}, u32[]{:S(2)}) collective-permute-start(bf16[256,256]{1,0:T(8,128)(2,1)S(1)} %rest.7.refs_0_), channel_id=1, source_target_pairs={{0,2},{2,0},{1,3},{3,1},{4,6},{6,4},{5,7},{7,5},{8,10},{10,8},{9,1... | collective-permute-start | bytes 393224 | tf_op jit(solution)/shard_map/ppermute | solution.py:509

commit v18 on v17

--- a/solution.py
+++ b/solution.py
@@ -11,7 +11,7 @@
 STEPS = 3
 OFFSETS = (0, NS + 1, NS - 1, -(NS + 1), -(NS - 1))
 EPSILON = 1e-06
-WIDE, WIDEST = 8, 12
+WIDE, WIDEST = 8, 16
 SMALLEST = 1e-30
 TILE = 16
 MIB = 1024 * 1024
@@ -189,7 +189,7 @@
         multiply(group * size, size)
         return carry
 
-    smaller = [wide for wide in (2, 4, WIDE) if wide < size]
+    smaller = [wide for wide in (2, 4, 8, 12) if wide < size]
     groups = (count + size - 1 - smaller[-1]) // size
     lax.fori_loop(0, groups, full, 0)
     rest = count - groups * size

time: 69.8 us -> 68.4 us (0.980)
  starting transfers between devices: 16.9 us -> 21.7 us
  waiting for transfers between devices: 27.9 us -> 23.4 us
  Pallas kernels: 13.7 us -> 12.3 us
    ppermute x3, starting transfers between devices: 3.45 us -> 6.51 us  [gather_parts(): return [t, lax.ppermute(t, 'mpo', [(0, 1), (1, 0)])]]
    ppermute x3, waiting for transfers between devices: 9.39 us -> 7.03 us  [gather_parts(): return [t, lax.ppermute(t, 'mpo', [(0, 1), (1, 0)])]]
    ppermute x3, waiting for transfers between devices: 3.96 us -> 2.26 us  [spread(): first = [piece, lax.ppermute(piece, 'mpo', [(0, 1), (1, 0)])]]
    pallas_call x14, Pallas kernels: 13.7 us -> 12.3 us  [call(): pl.pallas_call(kernel, out_shape=outs, in_specs=[first] + [VMEM] * (len(a...]
    ppermute x3, starting transfers between devices: 5.84 us -> 7.09 us  [spread(): first = [piece, lax.ppermute(piece, 'mpo', [(0, 1), (1, 0)])]]
  transfers between devices with their start and end apart: 14 -> 14, of which waited for: 10 -> 8; matrix products, arithmetic and copies ran while one was open for 0% -> 0% of each run, Pallas kernels for 8% -> 8%
where the time goes in v18:
time: 68.4 us; the launch traced here: 68.2 us
  waiting for transfers between devices  23.4 us (34%)
  starting transfers between devices  21.7 us (32%)
  Pallas kernels  12.3 us (18%)
  blocking collectives  9.11 us (13%)
  local copies, waits for them, and re-layouts  0.91 us (1%)
  between operations  0.79 us (1%)
    pallas_call x14, Pallas kernels, call(): pl.pallas_call(kernel, out_shape=outs, in_specs=[first] + [VMEM] * (len(a...  12.3 us
    ppermute x6, waiting for transfers between devices, shift(): return lax.ppermute(block, ring, pairs)  10.5 us
    all_to_all x1, blocking collectives, exchange(): return lax.all_to_all(rows, ring, 0, 0, tiled=True)  9.11 us
    ppermute x6, starting transfers between devices, shift(): return lax.ppermute(block, ring, pairs)  8.05 us
    ppermute x3, starting transfers between devices, spread(): first = [piece, lax.ppermute(piece, 'mpo', [(0, 1), (1, 0)])]  7.09 us
    ppermute x3, waiting for transfers between devices, gather_parts(): return [t, lax.ppermute(t, 'mpo', [(0, 1), (1, 0)])]  7.03 us
    ppermute x3, starting transfers between devices, gather_parts(): return [t, lax.ppermute(t, 'mpo', [(0, 1), (1, 0)])]  6.51 us
    ppermute x2, waiting for transfers between devices, add_round(): return rows + lax.ppermute(rows, axis, pairs)  3.61 us
  transfers between devices with their start and end apart: 14, of which 8 were waited for; matrix products, arithmetic and copies ran while one was open for 0% of the time, Pallas kernels for 8%

profile of v18, /device:TPU:0, one launch (start us, length us, event | category | flops | bytes accessed | tf_op | source)
XLA Modules:
  0.0 68.2 jit_solution(10586737355663695557)
XLA Ops:
  0.6 0.9 %copy-done.3 = bf16[1,256,256]{2,1,0:T(8,128)(2,1)S(1)} copy-done((bf16[1,256,256]{2,1,0:T(8,128)(2,1)S(1)}, bf16[1,256,256]{2,1,0:T(8,128)(2,1)}, u32[]{:S(2)}) %copy-start.3) | copy-done | bytes 131096
  1.6 3.5 %collective-permute-start.1 = (bf16[128,256]{1,0:T(8,128)(2,1)S(1)}, bf16[128,256]{1,0:T(8,128)(2,1)S(1)}, u32[]{:S(2)}, u32[]{:S(2)}) collective-permute-start(bf16[128,256]{1,0:T(8,128)(2,1)S(1)} %get-tuple-element.33), channel_id=1, source_target_pairs={{9,0},{8,1},{13,4},{12,5},{1,8},{0,9},{5,12},{4,13},{11,2},{10,3},... | collective-permute-start | bytes 196616 | tf_op jit(solution)/shard_map/ppermute | solution.py:468
  5.8 1.8 %collective-permute-done.1.block_ref = bf16[128,256]{1,0:T(8,128)(2,1)S(1)} collective-permute-done((bf16[128,256]{1,0:T(8,128)(2,1)S(1)}, bf16[128,256]{1,0:T(8,128)(2,1)S(1)}, u32[]{:S(2)}, u32[]{:S(2)}) %collective-permute-start.1) | collective-permute-done | bytes 65568 | tf_op jit(solution)/shard_map/ppermute | solution.py:468
  7.6 3.4 %collective-permute-start.2 = (bf16[128,256]{1,0:T(8,128)(2,1)S(1)}, bf16[128,256]{1,0:T(8,128)(2,1)S(1)}, u32[]{:S(2)}, u32[]{:S(2)}) collective-permute-start(bf16[128,256]{1,0:T(8,128)(2,1)S(1)} %hold.1.refs_5_), channel_id=1, source_target_pairs={{0,2},{2,0},{1,3},{3,1},{4,6},{6,4},{5,7},{7,5},{8,10},{10,8},{9,1... | collective-permute-start | bytes 196616 | tf_op jit(solution)/shard_map/ppermute | solution.py:502
  11.0 1.5 %own.3 = (f32[256,256]{1,0:T(8,128)S(1)}, f32[8,128]{1,0:T(8,128)S(1)}) custom-call(s32[24]{0:T(128)S(1)} %copy-done.2, bf16[24,256,256]{2,1,0:T(8,128)(2,1)S(1)} %bitcast.7, bf16[24,256,256]{2,1,0:T(8,128)(2,1)S(1)} %bitcast.14, bf16[256,256]{1,0:T(8,128)(2,1)S(1)} %get-tuple-element.28.refs_3_.rows_ref.refs_2_), custom_call_target="tpu_custom_call" | custom-call | flops 322122560 | bytes 262144 | tf_op jit(solution)/shard_map/own/pallas_call | solution.py:428
  13.4 1.2 %rest.5 = (bf16[256,256]{1,0:T(8,128)(2,1)S(1)}, f32[8,128]{1,0:T(8,128)S(1)}) custom-call(s32[24]{0:T(128)S(1)} %copy-done.2, bf16[24,256,256]{2,1,0:T(8,128)(2,1)S(1)} %bitcast.9, bf16[24,256,256]{2,1,0:T(8,128)(2,1)S(1)} %bitcast.16, f32[256,256]{1,0:T(8,128)S(1)} %get-tuple-element.31.refs_3_, f32[8,128]{1,0:T(8,128)S(1)} %get-tuple-element.32.refs_4_, ...), custom_call_target="tpu_custom_call" | custom-call | flops 322122560 | bytes 262144 | tf_op jit(solution)/shard_map/rest/pallas_call | solution.py:428
  14.6 2.4 %collective-permute-start.3 = (bf16[256,256]{1,0:T(8,128)(2,1)S(1)}, bf16[256,256]{1,0:T(8,128)(2,1)S(1)}, u32[]{:S(2)}, u32[]{:S(2)}) collective-permute-start(bf16[256,256]{1,0:T(8,128)(2,1)S(1)} %get-tuple-element.34.refs_0_), channel_id=1, source_target_pairs={{0,2},{2,0},{1,3},{3,1},{4,6},{6,4},{5,7},{7,5},{8,10},{10,8},{9,1... | collective-permute-start | bytes 393224 | tf_op jit(solution)/shard_map/ppermute | solution.py:509
  17.0 3.4 %collective-permute-done.3.refs_1_ = bf16[256,256]{1,0:T(8,128)(2,1)S(1)} collective-permute-done((bf16[256,256]{1,0:T(8,128)(2,1)S(1)}, bf16[256,256]{1,0:T(8,128)(2,1)S(1)}, u32[]{:S(2)}, u32[]{:S(2)}) %collective-permute-start.3) | collective-permute-done | bytes 131104 | tf_op jit(solution)/shard_map/ppermute | solution.py:509
  20.7 2.5 %collective-permute-start.4 = (bf16[160,256]{1,0:T(8,128)(2,1)S(1)}, bf16[160,256]{1,0:T(8,128)(2,1)S(1)}, u32[]{:S(2)}, u32[]{:S(2)}) collective-permute-start(bf16[160,256]{1,0:T(8,128)(2,1)S(1)} %get-tuple-element.39), channel_id=1, source_target_pairs={{9,0},{8,1},{13,4},{12,5},{1,8},{0,9},{5,12},{4,13},{11,2},{10,3},... | collective-permute-start | bytes 245768 | tf_op jit(solution)/shard_map/ppermute | solution.py:468
  23.9 3.8 %collective-permute-done.4.block_ref = bf16[160,256]{1,0:T(8,128)(2,1)S(1)} collective-permute-done((bf16[160,256]{1,0:T(8,128)(2,1)S(1)}, bf16[160,256]{1,0:T(8,128)(2,1)S(1)}, u32[]{:S(2)}, u32[]{:S(2)}) %collective-permute-start.4) | collective-permute-done | bytes 81952 | tf_op jit(solution)/shard_map/ppermute | solution.py:468
  27.7 2.5 %collective-permute-start.5 = (bf16[128,256]{1,0:T(8,128)(2,1)S(1)}, bf16[128,256]{1,0:T(8,128)(2,1)S(1)}, u32[]{:S(2)}, u32[]{:S(2)}) collective-permute-start(bf16[128,256]{1,0:T(8,128)(2,1)S(1)} %get-tuple-element.41.refs_5_), channel_id=1, source_target_pairs={{0,2},{2,0},{1,3},{3,1},{4,6},{6,4},{5,7},{7,5},{8,10},{10,8},{9,1... | collective-permute-start | bytes 196616 | tf_op jit(solution)/shard_map/ppermute | solution.py:502
  30.3 1.5 %own.4 = (f32[256,256]{1,0:T(8,128)S(1)}, f32[8,128]{1,0:T(8,128)S(1)}) custom-call(s32[24]{0:T(128)S(1)} %copy-done.2, bf16[24,256,256]{2,1,0:T(8,128)(2,1)S(1)} %bitcast.10, bf16[24,256,256]{2,1,0:T(8,128)(2,1)S(1)} %bitcast.17, bf16[256,256]{1,0:T(8,128)(2,1)S(1)} %get-tuple-element.36.refs_3_.refs_4_), custom_call_target="tpu_custom_call" | custom-call | flops 322122560 | bytes 262144 | tf_op jit(solution)/shard_map/own/pallas_call | solution.py:428
  32.6 1.2 %rest.6 = (bf16[256,256]{1,0:T(8,128)(2,1)S(1)}, f32[8,128]{1,0:T(8,128)S(1)}, f32[8,128]{1,0:T(8,128)S(1)}) custom-call(s32[24]{0:T(128)S(1)} %copy-done.2, bf16[24,256,256]{2,1,0:T(8,128)(2,1)S(1)} %bitcast.11, bf16[24,256,256]{2,1,0:T(8,128)(2,1)S(1)} %bitcast.18, f32[256,256]{1,0:T(8,128)S(1)} %get-tuple-element.37.refs_3_, ...), custom_call_target="tpu_custom_call" | custom-call | flops 644245120 | bytes 262144 | tf_op jit(solution)/shard_map/rest/pallas_call | solution.py:428
  33.9 2.4 %collective-permute-start.8 = (bf16[256,256]{1,0:T(8,128)(2,1)S(1)}, bf16[256,256]{1,0:T(8,128)(2,1)S(1)}, u32[]{:S(2)}, u32[]{:S(2)}) collective-permute-start(bf16[256,256]{1,0:T(8,128)(2,1)S(1)} %get-tuple-element.43.refs_0_), channel_id=1, source_target_pairs={{0,2},{2,0},{1,3},{3,1},{4,6},{6,4},{5,7},{7,5},{8,10},{10,8},{9,1... | collective-permute-start | bytes 393224 | tf_op jit(solution)/shard_map/ppermute | solution.py:509
  36.3 3.6 %collective-permute-done.9 = f32[8,128]{1,0:T(8,128)S(1)} collective-permute-done((f32[8,128]{1,0:T(8,128)S(1)}, f32[8,128]{1,0:T(8,128)S(1)}, u32[]{:S(2)}, u32[]{:S(2)}) %collective-permute-start.9) | collective-permute-done | bytes 4128 | tf_op jit(solution)/shard_map/ppermute | solution.py:483
  41.5 4.8 %collective-permute-done.10.refs_4_ = bf16[128,256]{1,0:T(8,128)(2,1)S(1)} collective-permute-done((bf16[128,256]{1,0:T(8,128)(2,1)S(1)}, bf16[128,256]{1,0:T(8,128)(2,1)S(1)}, u32[]{:S(2)}, u32[]{:S(2)}) %collective-permute-start.10) | collective-permute-done | bytes 65568 | tf_op jit(solution)/shard_map/ppermute | solution.py:468
  46.3 1.1 %collective-permute-start.11 = (bf16[128,256]{1,0:T(8,128)(2,1)S(1)}, bf16[128,256]{1,0:T(8,128)(2,1)S(1)}, u32[]{:S(2)}, u32[]{:S(2)}) collective-permute-start(bf16[128,256]{1,0:T(8,128)(2,1)S(1)} %collective-permute-done.10.refs_4_), channel_id=1, source_target_pairs={{0,2},{2,0},{1,3},{3,1},{4,6},{6,4},{5,7},{7,5},{8,10},{10,8},{9,1... | collective-permute-start | bytes 196616 | tf_op jit(solution)/shard_map/ppermute | solution.py:502
  47.4 1.7 %own.5.refs_3_ = f32[256,256]{1,0:T(8,128)S(1)} custom-call(s32[24]{0:T(128)S(1)} %copy-done.2, bf16[24,256,256]{2,1,0:T(8,128)(2,1)S(1)} %bitcast.12, bf16[24,256,256]{2,1,0:T(8,128)(2,1)S(1)} %bitcast.19, bf16[256,256]{1,0:T(8,128)(2,1)S(1)} %get-tuple-element.46.refs_3_), custom_call_target="tpu_custom_call" | custom-call | flops 322122560 | bytes 262144 | tf_op jit(solution)/shard_map/own/pallas_call | solution.py:428
  49.2 1.4 %collective-permute-done.11.refs_5_ = bf16[128,256]{1,0:T(8,128)(2,1)S(1)} collective-permute-done((bf16[128,256]{1,0:T(8,128)(2,1)S(1)}, bf16[128,256]{1,0:T(8,128)(2,1)S(1)}, u32[]{:S(2)}, u32[]{:S(2)}) %collective-permute-start.11) | collective-permute-done | bytes 65568 | tf_op jit(solution)/shard_map/ppermute | solution.py:502
  50.6 1.1 %rest.7.refs_0_ = bf16[256,256]{1,0:T(8,128)(2,1)S(1)} custom-call(s32[24]{0:T(128)S(1)} %copy-done.2, bf16[24,256,256]{2,1,0:T(8,128)(2,1)S(1)} %bitcast.13, bf16[24,256,256]{2,1,0:T(8,128)(2,1)S(1)} %bitcast.20, f32[256,256]{1,0:T(8,128)S(1)} %own.5.refs_3_, bf16[128,256]{1,0:T(8,128)(2,1)S(1)} %collective-permute-done.10.refs_4_, ...), custom_call_target="tpu_custom_call" | custom-call | flops 644245120 | bytes 262144 | tf_op jit(solution)/shard_map/rest/pallas_call | solution.py:428
  51.7 1.7 %collective-permute-start.13 = (bf16[256,256]{1,0:T(8,128)(2,1)S(1)}, bf16[256,256]{1,0:T(8,128)(2,1)S(1)}, u32[]{:S(2)}, u32[]{:S(2)}) collective-permute-start(bf16[256,256]{1,0:T(8,128)(2,1)S(1)} %rest.7.refs_0_), channel_id=1, source_target_pairs={{0,2},{2,0},{1,3},{3,1},{4,6},{6,4},{5,7},{7,5},{8,10},{10,8},{9,1... | collective-permute-start | bytes 393224 | tf_op jit(solution)/shard_map/ppermute | solution.py:509
  53.4 3.6 %collective-permute-done.13.refs_1_ = bf16[256,256]{1,0:T(8,128)(2,1)S(1)} collective-permute-done((bf16[256,256]{1,0:T(8,128)(2,1)S(1)}, bf16[256,256]{1,0:T(8,128)(2,1)S(1)}, u32[]{:S(2)}, u32[]{:S(2)}) %collective-permute-start.13) | collective-permute-done | bytes 131104 | tf_op jit(solution)/shard_map/ppermute | solution.py:509
  57.6 9.1 %all_to_all.11 = f32[8,1,128]{2,1,0:T(1,128)S(1)} all-to-all(f32[8,1,128]{2,1,0:T(1,128)S(1)} %bitcast.22), channel_id=1, replica_groups=mesh['groups'=2,'blk'=4,'mpo'=2,'rep'=2] {'blk','rep'}, dimensions={0} | all-to-all | bytes 8192 | tf_op jit(solution)/shard_map/all_to_all | solution.py:514
  66.8 1.4 %final.1 = (bf16[3,1,128,256]{3,2,1,0:T(8,128)(2,1)}, f32[2,3]{1,0:T(2,128)}) custom-call(f32[8,128]{1,0:T(8,128)S(1)} %bitcast.21, f32[256,256]{1,0:T(8,128)S(1)} %get-tuple-element.52.r_ref, f32[256,256]{1,0:T(8,128)S(1)} %get-tuple-element.53.z_ref, f32[256,256]{1,0:T(8,128)S(1)} %get-tuple-element.49.refs_5_.w_ref, ...), custom_call_target="tpu_custom_call" | custom-call | bytes 262144 | tf_op jit(solution)/shard_map/final/pallas_call | solution.py:428
  (29 shorter events, 5.6 us)
Async XLA Ops:
  0.6 0.9 %copy-start.3 = (bf16[1,256,256]{2,1,0:T(8,128)(2,1)S(1)}, bf16[1,256,256]{2,1,0:T(8,128)(2,1)}, u32[]{:S(2)}) copy-start(bf16[1,256,256]{2,1,0:T(8,128)(2,1)} %param.4) | copy-start | bytes 393220
  1.5 9.5 %copy-start = (bf16[24,1,256,256]{3,2,1,0:T(8,128)(2,1)S(1)}, bf16[24,1,256,256]{3,2,1,0:T(8,128)(2,1)}, u32[]{:S(2)}) copy-start(bf16[24,1,256,256]{3,2,1,0:T(8,128)(2,1)} %param.5) | copy-start | bytes 9437188
  1.5 9.5 %copy-start.1 = (bf16[24,1,256,256]{3,2,1,0:T(8,128)(2,1)S(1)}, bf16[24,1,256,256]{3,2,1,0:T(8,128)(2,1)}, u32[]{:S(2)}) copy-start(bf16[24,1,256,256]{3,2,1,0:T(8,128)(2,1)} %param.6) | copy-start | bytes 9437188
  1.5 9.5 %copy-start.2 = (s32[24]{0:T(128)S(1)}, s32[24]{0:T(128)}, u32[]{:S(2)}) copy-start(s32[24]{0:T(128)} %refs_0_.13) | copy-start | bytes 292
  1.6 6.0 %collective-permute-start.1 = (bf16[128,256]{1,0:T(8,128)(2,1)S(1)}, bf16[128,256]{1,0:T(8,128)(2,1)S(1)}, u32[]{:S(2)}, u32[]{:S(2)}) collective-permute-start(bf16[128,256]{1,0:T(8,128)(2,1)S(1)} %get-tuple-element.33), channel_id=1, source_target_pairs={{9,0},{8,1},{13,4},{12,5},{1,8},{0,9},{5,12},{4,13},{11,2},{10,3},... | collective-permute-start | bytes 196616 | tf_op jit(solution)/shard_map/ppermute | solution.py:468
  5.1 7.5 %collective-permute-start = (bf16[256,256]{1,0:T(8,128)(2,1)S(1)}, bf16[256,256]{1,0:T(8,128)(2,1)S(1)}, u32[]{:S(2)}, u32[]{:S(2)}) collective-permute-start(bf16[256,256]{1,0:T(8,128)(2,1)S(1)} %get-tuple-element.28.refs_3_.rows_ref.refs_2_), channel_id=1, source_target_pairs={{12,1},{9,4},{4,9},{1,12},{14,3},{11,6},{6,11},{3,14},{28,17},{25,... | collective-permute-start | bytes 393224 | tf_op jit(solution)/shard_map/ppermute | solution.py:468
  7.6 5.8 %collective-permute-start.2 = (bf16[128,256]{1,0:T(8,128)(2,1)S(1)}, bf16[128,256]{1,0:T(8,128)(2,1)S(1)}, u32[]{:S(2)}, u32[]{:S(2)}) collective-permute-start(bf16[128,256]{1,0:T(8,128)(2,1)S(1)} %hold.1.refs_5_), channel_id=1, source_target_pairs={{0,2},{2,0},{1,3},{3,1},{4,6},{6,4},{5,7},{7,5},{8,10},{10,8},{9,1... | collective-permute-start | bytes 196616 | tf_op jit(solution)/shard_map/ppermute | solution.py:502
  14.6 5.8 %collective-permute-start.3 = (bf16[256,256]{1,0:T(8,128)(2,1)S(1)}, bf16[256,256]{1,0:T(8,128)(2,1)S(1)}, u32[]{:S(2)}, u32[]{:S(2)}) collective-permute-start(bf16[256,256]{1,0:T(8,128)(2,1)S(1)} %get-tuple-element.34.refs_0_), channel_id=1, source_target_pairs={{0,2},{2,0},{1,3},{3,1},{4,6},{6,4},{5,7},{7,5},{8,10},{10,8},{9,1... | collective-permute-start | bytes 393224 | tf_op jit(solution)/shard_map/ppermute | solution.py:509
  20.7 7.0 %collective-permute-start.4 = (bf16[160,256]{1,0:T(8,128)(2,1)S(1)}, bf16[160,256]{1,0:T(8,128)(2,1)S(1)}, u32[]{:S(2)}, u32[]{:S(2)}) collective-permute-start(bf16[160,256]{1,0:T(8,128)(2,1)S(1)} %get-tuple-element.39), channel_id=1, source_target_pairs={{9,0},{8,1},{13,4},{12,5},{1,8},{0,9},{5,12},{4,13},{11,2},{10,3},... | collective-permute-start | bytes 245768 | tf_op jit(solution)/shard_map/ppermute | solution.py:468
  23.2 8.6 %collective-permute-start.6 = (bf16[256,256]{1,0:T(8,128)(2,1)S(1)}, bf16[256,256]{1,0:T(8,128)(2,1)S(1)}, u32[]{:S(2)}, u32[]{:S(2)}) collective-permute-start(bf16[256,256]{1,0:T(8,128)(2,1)S(1)} %get-tuple-element.36.refs_3_.refs_4_), channel_id=1, source_target_pairs={{12,1},{9,4},{4,9},{1,12},{14,3},{11,6},{6,11},{3,14},{28,17},{25,... | collective-permute-start | bytes 393224 | tf_op jit(solution)/shard_map/ppermute | solution.py:468
  27.7 4.9 %collective-permute-start.5 = (bf16[128,256]{1,0:T(8,128)(2,1)S(1)}, bf16[128,256]{1,0:T(8,128)(2,1)S(1)}, u32[]{:S(2)}, u32[]{:S(2)}) collective-permute-start(bf16[128,256]{1,0:T(8,128)(2,1)S(1)} %get-tuple-element.41.refs_5_), channel_id=1, source_target_pairs={{0,2},{2,0},{1,3},{3,1},{4,6},{6,4},{5,7},{7,5},{8,10},{10,8},{9,1... | collective-permute-start | bytes 196616 | tf_op jit(solution)/shard_map/ppermute | solution.py:502
  30.3 1.5 %collective-permute-start.7 = (f32[8,128]{1,0:T(8,128)S(1)}, f32[8,128]{1,0:T(8,128)S(1)}, u32[]{:S(2)}, u32[]{:S(2)}) collective-permute-start(f32[8,128]{1,0:T(8,128)S(1)} %get-tuple-element.42), channel_id=1, source_target_pairs={{0,1},{1,0},{4,5},{5,4},{8,9},{9,8},{12,13},{13,12},{2,3},{3,2},{6... | collective-permute-start | bytes 12296 | tf_op jit(solution)/shard_map/ppermute | solution.py:483
  33.9 6.0 %collective-permute-start.8 = (bf16[256,256]{1,0:T(8,128)(2,1)S(1)}, bf16[256,256]{1,0:T(8,128)(2,1)S(1)}, u32[]{:S(2)}, u32[]{:S(2)}) collective-permute-start(bf16[256,256]{1,0:T(8,128)(2,1)S(1)} %get-tuple-element.43.refs_0_), channel_id=1, source_target_pairs={{0,2},{2,0},{1,3},{3,1},{4,6},{6,4},{5,7},{7,5},{8,10},{10,8},{9,1... | collective-permute-start | bytes 393224 | tf_op jit(solution)/shard_map/ppermute | solution.py:509
  36.3 3.6 %collective-permute-start.9 = (f32[8,128]{1,0:T(8,128)S(1)}, f32[8,128]{1,0:T(8,128)S(1)}, u32[]{:S(2)}, u32[]{:S(2)}) collective-permute-start(f32[8,128]{1,0:T(8,128)S(1)} %get-tuple-element.44), channel_id=1, source_target_pairs={{0,4},{1,5},{4,0},{5,1},{8,12},{9,13},{12,8},{13,9},{2,6},{3,7},{6... | collective-permute-start | bytes 12296 | tf_op jit(solution)/shard_map/ppermute | solution.py:483
  40.8 5.5 %collective-permute-start.10 = (bf16[128,256]{1,0:T(8,128)(2,1)S(1)}, bf16[128,256]{1,0:T(8,128)(2,1)S(1)}, u32[]{:S(2)}, u32[]{:S(2)}) collective-permute-start(bf16[128,256]{1,0:T(8,128)(2,1)S(1)} %get-tuple-element.47), channel_id=1, source_target_pairs={{9,0},{8,1},{13,4},{12,5},{1,8},{0,9},{5,12},{4,13},{11,2},{10,3},... | collective-permute-start | bytes 196616 | tf_op jit(solution)/shard_map/ppermute | solution.py:468
  40.8 9.7 %collective-permute-start.12 = (bf16[256,256]{1,0:T(8,128)(2,1)S(1)}, bf16[256,256]{1,0:T(8,128)(2,1)S(1)}, u32[]{:S(2)}, u32[]{:S(2)}) collective-permute-start(bf16[256,256]{1,0:T(8,128)(2,1)S(1)} %get-tuple-element.46.refs_3_), channel_id=1, source_target_pairs={{12,1},{9,4},{4,9},{1,12},{14,3},{11,6},{6,11},{3,14},{28,17},{25,... | collective-permute-start | bytes 393224 | tf_op jit(solution)/shard_map/ppermute | solution.py:468
  46.3 4.3 %collective-permute-start.11 = (bf16[128,256]{1,0:T(8,128)(2,1)S(1)}, bf16[128,256]{1,0:T(8,128)(2,1)S(1)}, u32[]{:S(2)}, u32[]{:S(2)}) collective-permute-start(bf16[128,256]{1,0:T(8,128)(2,1)S(1)} %collective-permute-done.10.refs_4_), channel_id=1, source_target_pairs={{0,2},{2,0},{1,3},{3,1},{4,6},{6,4},{5,7},{7,5},{8,10},{10,8},{9,1... | collective-permute-start | bytes 196616 | tf_op jit(solution)/shard_map/ppermute | solution.py:502
  51.7 5.3 %collective-permute-start.13 = (bf16[256,256]{1,0:T(8,128)(2,1)S(1)}, bf16[256,256]{1,0:T(8,128)(2,1)S(1)}, u32[]{:S(2)}, u32[]{:S(2)}) collective-permute-start(bf16[256,256]{1,0:T(8,128)(2,1)S(1)} %rest.7.refs_0_), channel_id=1, source_target_pairs={{0,2},{2,0},{1,3},{3,1},{4,6},{6,4},{5,7},{7,5},{8,10},{10,8},{9,1... | collective-permute-start | bytes 393224 | tf_op jit(solution)/shard_map/ppermute | solution.py:509
